TPU v7x, 32 devices: a whole 2x2x4 slice. The times are simulated.
32 devices in a mesh: seq: 4 (over z), fsdp: 8 (over y, x, core).
Axes of the slice: x: 2, y: 2, z: 4, core: 2. Of those that a mesh axis runs over, the one named last changes fastest.
Arguments:
- inputs: bfloat16 [8, 2048, 1024], P('fsdp', 'seq'), may hold values from -6 to 6
- positions: int32 [8, 2048], P('fsdp', 'seq'), may hold values from 0 to 2047, as said below
- cotangent: bfloat16 [8, 2048, 1024], P('fsdp', 'seq'), may hold values from -6 to 6
- query_weight: bfloat16 [1024, 1024], P('fsdp'), may hold values from -0.1875 to 0.1875
- key_weight: bfloat16 [1024, 512], P('fsdp'), may hold values from -0.1875 to 0.1875
- value_weight: bfloat16 [1024, 512], P('fsdp'), may hold values from -0.1875 to 0.1875
- out_weight: bfloat16 [1024, 1024], P('fsdp'), may hold values from -0.75 to 0.75
- attention_gain: bfloat16 [1024], P('fsdp'), may hold values from 0.099609375 to 1.8984375
- query_gain: bfloat16 [64], P('fsdp'), may hold values from 0.099609375 to 1.8984375
- key_gain: bfloat16 [64], P('fsdp'), may hold values from 0.099609375 to 1.8984375
- feedforward_gain: bfloat16 [1024], P('fsdp'), may hold values from 0.099609375 to 1.8984375
- gate_weight: bfloat16 [1024, 4608], P('fsdp'), may hold values from -0.1875 to 0.1875
- up_weight: bfloat16 [1024, 4608], P('fsdp'), may hold values from -0.1875 to 0.1875
- down_weight: bfloat16 [4608, 1024], P('fsdp'), may hold values from -0.09375 to 0.09375
Outputs:
- output: bfloat16 [8, 2048, 1024], P('fsdp', 'seq')
- input_grad: bfloat16 [8, 2048, 1024], P('fsdp', 'seq')
- query_weight_grad: float32 [1024, 1024], P('fsdp')
- key_weight_grad: float32 [1024, 512], P('fsdp')
- value_weight_grad: float32 [1024, 512], P('fsdp')
- out_weight_grad: float32 [1024, 1024], P('fsdp')
- attention_gain_grad: float32 [1024], P('fsdp')
- query_gain_grad: float32 [64], P('fsdp')
- key_gain_grad: float32 [64], P('fsdp')
- feedforward_gain_grad: float32 [1024], P('fsdp')
- gate_weight_grad: float32 [1024, 4608], P('fsdp')
- up_weight_grad: float32 [1024, 4608], P('fsdp')
- down_weight_grad: float32 [4608, 1024], P('fsdp')
Inputs may be any that keep to these rules, and one draw needn't show every extreme that they name: `positions`: each sequence is a pack of documents; a token's position counts from the first token of its document. In every draw at least one sequence is a single document.
All inputs are finite; a program needn't handle non-finite values.
Results may differ from a plain program's by a relative error of at most 0.018.
Values may be sent and summed in bfloat16 or wider, within the bound.
A program may use at most 192 MiB of HBM per device.

v0:
```python
import jax
import jax.numpy as jnp
from jax import lax
from jax.sharding import PartitionSpec as P

EPSILON = 1e-05
ROPE_BASE = 1000000.0


def rms_scale(values, gain_vector):
    return (
        values
        * lax.rsqrt(jnp.mean(values * values, axis=-1, keepdims=True) + EPSILON)
        * gain_vector
    )


def rotate(values, token_positions):
    half_width = values.shape[-1] // 2
    freqs = ROPE_BASE ** (-jnp.arange(half_width, dtype=jnp.float32) / half_width)
    angles = token_positions.astype(jnp.float32)[:, None] * freqs[None, :]
    cosine = jnp.cos(angles)[:, None, :]
    sine = jnp.sin(angles)[:, None, :]
    first_half = values[..., :half_width]
    second_half = values[..., half_width:]
    return jnp.concatenate(
        [first_half * cosine - second_half * sine, second_half * cosine + first_half * sine],
        axis=-1,
    )


def matmul(left_side, right_side):
    return jnp.dot(left_side, right_side, preferred_element_type=jnp.float32)


def matmul_left_t(left_side, right_side):
    return lax.dot_general(
        left_side, right_side, (((0,), (0,)), ((), ())), preferred_element_type=jnp.float32
    )


def matmul_right_t(left_side, right_side):
    return lax.dot_general(
        left_side, right_side, (((1,), (1,)), ((), ())), preferred_element_type=jnp.float32
    )


def causal_scores(block_queries, key_rows, first_row, block_rows, score_scale):
    seq_len = key_rows.shape[0]
    scores = (
        jnp.einsum("qbgd,kbd->bgqk", block_queries, key_rows, preferred_element_type=jnp.float32)
        * score_scale
    )
    query_index = first_row + jnp.arange(block_rows, dtype=jnp.int32)
    key_index = jnp.arange(seq_len, dtype=jnp.int32)
    allowed = query_index[:, None] >= key_index[None, :]
    return jnp.where(allowed, scores, -1e30)


def attend_sequence(queries, key_rows, value_rows):
    seq_len = queries.shape[0]
    block_rows = min(512, seq_len)
    block_count = seq_len // block_rows
    score_scale = queries.shape[-1] ** (-0.5)

    def one_block(pair):
        block_queries, first_row = pair
        scores = causal_scores(block_queries, key_rows, first_row, block_rows, score_scale)
        row_peak = jnp.max(scores, axis=-1, keepdims=True)
        exp_scores = jnp.exp(scores - row_peak)
        row_total = jnp.sum(exp_scores, axis=-1, keepdims=True)
        prob_low = (exp_scores / row_total).astype(jnp.bfloat16)
        mixed_block = jnp.einsum(
            "bgqk,kbd->qbgd", prob_low, value_rows, preferred_element_type=jnp.float32
        )
        return (mixed_block.astype(jnp.bfloat16), row_peak + jnp.log(row_total))

    blocks = queries.reshape((block_count, block_rows) + queries.shape[1:])
    starts = jnp.arange(block_count, dtype=jnp.int32) * block_rows
    mixed_blocks, log_totals = lax.map(one_block, (blocks, starts))
    return (mixed_blocks.reshape(queries.shape), log_totals)


def attend_back(queries, key_rows, value_rows, log_totals, mixed_grad):
    seq_len = queries.shape[0]
    block_rows = min(512, seq_len)
    block_count = seq_len // block_rows
    score_scale = queries.shape[-1] ** (-0.5)

    def one_block(carry, parts):
        key_total, value_total = carry
        block_queries, block_grad, block_log, first_row = parts
        scores = causal_scores(block_queries, key_rows, first_row, block_rows, score_scale)
        prob_full = jnp.exp(scores - block_log)
        prob_low = prob_full.astype(jnp.bfloat16)
        prob_grad = jnp.einsum(
            "qbgd,kbd->bgqk", block_grad, value_rows, preferred_element_type=jnp.float32
        )
        inner = jnp.sum(prob_full * prob_grad, axis=-1, keepdims=True)
        score_grad = (prob_full * (prob_grad - inner)).astype(jnp.bfloat16)
        query_part = (
            jnp.einsum("bgqk,kbd->qbgd", score_grad, key_rows, preferred_element_type=jnp.float32)
            * score_scale
        )
        key_total = (
            key_total
            + jnp.einsum(
                "bgqk,qbgd->kbd", score_grad, block_queries, preferred_element_type=jnp.float32
            )
            * score_scale
        )
        value_total = value_total + jnp.einsum(
            "bgqk,qbgd->kbd", prob_low, block_grad, preferred_element_type=jnp.float32
        )
        return ((key_total, value_total), query_part.astype(jnp.bfloat16))

    blocks = queries.reshape((block_count, block_rows) + queries.shape[1:])
    grad_blocks = mixed_grad.reshape((block_count, block_rows) + mixed_grad.shape[1:])
    starts = jnp.arange(block_count, dtype=jnp.int32) * block_rows
    zeros_kv = jnp.zeros(key_rows.shape, jnp.float32)
    (key_total, value_total), query_blocks = lax.scan(
        one_block, (zeros_kv, zeros_kv), (blocks, grad_blocks, log_totals, starts)
    )
    return (
        query_blocks.reshape(queries.shape),
        key_total.astype(jnp.bfloat16),
        value_total.astype(jnp.bfloat16),
    )


def per_device(
    inputs,
    positions,
    cotangent,
    query_weight,
    key_weight,
    value_weight,
    out_weight,
    attention_gain,
    query_gain,
    key_gain,
    feedforward_gain,
    gate_weight,
    up_weight,
    down_weight,
):
    seq_local, tok_local, width = inputs.shape
    rows_count = seq_local * tok_local
    query_full, key_full, value_full, out_full, attention_scale, query_scale, key_scale = (
        lax.all_gather(query_weight, "fsdp", axis=0, tiled=True),
        lax.all_gather(key_weight, "fsdp", axis=0, tiled=True),
        lax.all_gather(value_weight, "fsdp", axis=0, tiled=True),
        lax.all_gather(out_weight, "fsdp", axis=0, tiled=True),
        lax.all_gather(attention_gain, "fsdp", axis=0, tiled=True),
        lax.all_gather(query_gain, "fsdp", axis=0, tiled=True),
        lax.all_gather(key_gain, "fsdp", axis=0, tiled=True),
    )
    head_dim = query_scale.shape[0]
    heads_total = query_full.shape[1] // head_dim
    kv_total = key_full.shape[1] // head_dim
    group_size = heads_total // kv_total
    rows_in = inputs.reshape(rows_count, width).astype(jnp.float32)
    flat_positions = positions.reshape(rows_count)
    normed, norm_pull = jax.vjp(rms_scale, rows_in, attention_scale.astype(jnp.float32))
    normed_low = normed.astype(jnp.bfloat16)
    query_proj = matmul(normed_low, query_full)
    key_proj = matmul(normed_low, key_full)
    value_low = matmul(normed_low, value_full).astype(jnp.bfloat16)

    def prepare(query_in, key_in, query_gain_in, key_gain_in):
        query_heads = rotate(
            rms_scale(query_in.reshape(rows_count, heads_total, head_dim), query_gain_in),
            flat_positions,
        )
        key_heads = rotate(
            rms_scale(key_in.reshape(rows_count, kv_total, head_dim), key_gain_in), flat_positions
        )
        return (query_heads.reshape(rows_count, -1), key_heads.reshape(rows_count, -1))

    (query_rot, key_rot), prepare_pull = jax.vjp(
        prepare,
        query_proj,
        key_proj,
        query_scale.astype(jnp.float32),
        key_scale.astype(jnp.float32),
    )
    query_send = query_rot.astype(jnp.bfloat16).reshape(seq_local, tok_local, -1)
    key_send = key_rot.astype(jnp.bfloat16).reshape(seq_local, tok_local, -1)
    value_send = value_low.reshape(seq_local, tok_local, -1)
    query_heads, key_heads, value_heads = (
        lax.all_to_all(query_send, "seq", split_axis=2, concat_axis=1, tiled=True),
        lax.all_to_all(key_send, "seq", split_axis=2, concat_axis=1, tiled=True),
        lax.all_to_all(value_send, "seq", split_axis=2, concat_axis=1, tiled=True),
    )
    seq_len = query_heads.shape[1]
    kv_local = key_heads.shape[2] // head_dim
    query_grid = query_heads.reshape(seq_local, seq_len, kv_local, group_size, head_dim)
    key_grid = key_heads.reshape(seq_local, seq_len, kv_local, head_dim)
    value_grid = value_heads.reshape(seq_local, seq_len, kv_local, head_dim)
    mixed_heads, log_totals = lax.map(
        lambda triple: attend_sequence(triple[0], triple[1], triple[2]),
        (query_grid, key_grid, value_grid),
    )
    mixed_tokens = lax.all_to_all(
        mixed_heads.reshape(seq_local, seq_len, -1), "seq", split_axis=1, concat_axis=2, tiled=True
    )
    mixed_rows = mixed_tokens.reshape(rows_count, -1)
    middle = rows_in + matmul(mixed_rows, out_full)
    feed_scale, gate_full, up_full, down_full = (
        lax.all_gather(feedforward_gain, "fsdp", axis=0, tiled=True),
        lax.all_gather(gate_weight, "fsdp", axis=0, tiled=True),
        lax.all_gather(up_weight, "fsdp", axis=0, tiled=True),
        lax.all_gather(down_weight, "fsdp", axis=0, tiled=True),
    )
    normed_two, norm_two_pull = jax.vjp(rms_scale, middle, feed_scale.astype(jnp.float32))
    normed_two_low = normed_two.astype(jnp.bfloat16)
    gate_value = matmul(normed_two_low, gate_full)
    up_value = matmul(normed_two_low, up_full)

    def activate(gate_in, up_in):
        return jax.nn.silu(gate_in) * up_in

    hidden, activate_pull = jax.vjp(activate, gate_value, up_value)
    hidden_low = hidden.astype(jnp.bfloat16)
    result_rows = middle + matmul(hidden_low, down_full)
    output = result_rows.astype(jnp.bfloat16).reshape(inputs.shape)
    query_full, key_full, value_full, out_full = (
        lax.all_gather(query_weight, "fsdp", axis=0, tiled=True),
        lax.all_gather(key_weight, "fsdp", axis=0, tiled=True),
        lax.all_gather(value_weight, "fsdp", axis=0, tiled=True),
        lax.all_gather(out_weight, "fsdp", axis=0, tiled=True),
    )
    gate_full, up_full, down_full = (
        lax.all_gather(gate_weight, "fsdp", axis=0, tiled=True),
        lax.all_gather(up_weight, "fsdp", axis=0, tiled=True),
        lax.all_gather(down_weight, "fsdp", axis=0, tiled=True),
    )
    grad_rows = cotangent.reshape(rows_count, width)
    down_grad = matmul_left_t(hidden_low, grad_rows)
    hidden_grad = matmul_right_t(grad_rows, down_full)
    gate_grad, up_grad = activate_pull(hidden_grad)
    gate_grad_low = gate_grad.astype(jnp.bfloat16)
    up_grad_low = up_grad.astype(jnp.bfloat16)
    gate_weight_grad = matmul_left_t(normed_two_low, gate_grad_low)
    up_weight_grad = matmul_left_t(normed_two_low, up_grad_low)
    normed_two_grad = matmul_right_t(gate_grad_low, gate_full) + matmul_right_t(
        up_grad_low, up_full
    )
    middle_part, feed_gain_grad = norm_two_pull(normed_two_grad)
    middle_grad = grad_rows.astype(jnp.float32) + middle_part
    middle_low = middle_grad.astype(jnp.bfloat16)
    out_weight_grad = matmul_left_t(mixed_rows, middle_low)
    mixed_grad = matmul_right_t(middle_low, out_full).astype(jnp.bfloat16)
    mixed_grad_heads = lax.all_to_all(
        mixed_grad.reshape(seq_local, tok_local, -1), "seq", split_axis=2, concat_axis=1, tiled=True
    )
    grid_grad = mixed_grad_heads.reshape(seq_local, seq_len, kv_local, group_size, head_dim)
    query_back, key_back, value_back = lax.map(
        lambda quintet: attend_back(quintet[0], quintet[1], quintet[2], quintet[3], quintet[4]),
        (query_grid, key_grid, value_grid, log_totals, grid_grad),
    )
    query_tok, key_tok, value_tok = (
        lax.all_to_all(
            query_back.reshape(seq_local, seq_len, -1),
            "seq",
            split_axis=1,
            concat_axis=2,
            tiled=True,
        ),
        lax.all_to_all(
            key_back.reshape(seq_local, seq_len, -1), "seq", split_axis=1, concat_axis=2, tiled=True
        ),
        lax.all_to_all(
            value_back.reshape(seq_local, seq_len, -1),
            "seq",
            split_axis=1,
            concat_axis=2,
            tiled=True,
        ),
    )
    query_proj_grad, key_proj_grad, query_gain_grad, key_gain_grad = prepare_pull(
        (
            query_tok.reshape(rows_count, -1).astype(jnp.float32),
            key_tok.reshape(rows_count, -1).astype(jnp.float32),
        )
    )
    query_proj_low = query_proj_grad.astype(jnp.bfloat16)
    key_proj_low = key_proj_grad.astype(jnp.bfloat16)
    value_tok_rows = value_tok.reshape(rows_count, -1)
    query_weight_grad = matmul_left_t(normed_low, query_proj_low)
    key_weight_grad = matmul_left_t(normed_low, key_proj_low)
    value_weight_grad = matmul_left_t(normed_low, value_tok_rows)
    normed_grad = (
        matmul_right_t(query_proj_low, query_full)
        + matmul_right_t(key_proj_low, key_full)
        + matmul_right_t(value_tok_rows, value_full)
    )
    input_part, attention_gain_grad = norm_pull(normed_grad)
    input_grad = (middle_grad + input_part).astype(jnp.bfloat16).reshape(inputs.shape)
    (
        query_shard,
        key_shard,
        value_shard,
        out_shard,
        attention_gain_shard,
        query_gain_shard,
        key_gain_shard,
    ) = (
        lax.psum_scatter(query_weight_grad, "fsdp", scatter_dimension=0, tiled=True),
        lax.psum_scatter(key_weight_grad, "fsdp", scatter_dimension=0, tiled=True),
        lax.psum_scatter(value_weight_grad, "fsdp", scatter_dimension=0, tiled=True),
        lax.psum_scatter(out_weight_grad, "fsdp", scatter_dimension=0, tiled=True),
        lax.psum_scatter(attention_gain_grad, "fsdp", scatter_dimension=0, tiled=True),
        lax.psum_scatter(query_gain_grad, "fsdp", scatter_dimension=0, tiled=True),
        lax.psum_scatter(key_gain_grad, "fsdp", scatter_dimension=0, tiled=True),
    )
    feed_gain_shard, gate_shard, up_shard, down_shard = (
        lax.psum_scatter(feed_gain_grad, "fsdp", scatter_dimension=0, tiled=True),
        lax.psum_scatter(gate_weight_grad, "fsdp", scatter_dimension=0, tiled=True),
        lax.psum_scatter(up_weight_grad, "fsdp", scatter_dimension=0, tiled=True),
        lax.psum_scatter(down_grad, "fsdp", scatter_dimension=0, tiled=True),
    )
    (
        query_total,
        key_total,
        value_total,
        out_total,
        attention_gain_total,
        query_gain_total,
        key_gain_total,
        feed_gain_total,
        gate_total,
        up_total,
        down_total,
    ) = (
        lax.psum(query_shard.astype(jnp.bfloat16), "seq").astype(jnp.float32),
        lax.psum(key_shard.astype(jnp.bfloat16), "seq").astype(jnp.float32),
        lax.psum(value_shard.astype(jnp.bfloat16), "seq").astype(jnp.float32),
        lax.psum(out_shard.astype(jnp.bfloat16), "seq").astype(jnp.float32),
        lax.psum(attention_gain_shard.astype(jnp.bfloat16), "seq").astype(jnp.float32),
        lax.psum(query_gain_shard.astype(jnp.bfloat16), "seq").astype(jnp.float32),
        lax.psum(key_gain_shard.astype(jnp.bfloat16), "seq").astype(jnp.float32),
        lax.psum(feed_gain_shard.astype(jnp.bfloat16), "seq").astype(jnp.float32),
        lax.psum(gate_shard.astype(jnp.bfloat16), "seq").astype(jnp.float32),
        lax.psum(up_shard.astype(jnp.bfloat16), "seq").astype(jnp.float32),
        lax.psum(down_shard.astype(jnp.bfloat16), "seq").astype(jnp.float32),
    )
    return (
        output,
        input_grad,
        query_total,
        key_total,
        value_total,
        out_total,
        attention_gain_total,
        query_gain_total,
        key_gain_total,
        feed_gain_total,
        gate_total,
        up_total,
        down_total,
    )


def solution(mesh):
    in_specs = (
        P("fsdp", "seq", None),
        P("fsdp", "seq"),
        P("fsdp", "seq", None),
        P("fsdp", None),
        P("fsdp", None),
        P("fsdp", None),
        P("fsdp", None),
        P("fsdp"),
        P("fsdp"),
        P("fsdp"),
        P("fsdp"),
        P("fsdp", None),
        P("fsdp", None),
        P("fsdp", None),
    )
    out_specs = (
        P("fsdp", "seq", None),
        P("fsdp", "seq", None),
        P("fsdp", None),
        P("fsdp", None),
        P("fsdp", None),
        P("fsdp", None),
        P("fsdp"),
        P("fsdp"),
        P("fsdp"),
        P("fsdp"),
        P("fsdp", None),
        P("fsdp", None),
        P("fsdp", None),
    )
    return jax.shard_map(
        per_device, mesh=mesh, in_specs=in_specs, out_specs=out_specs, check_vma=False
    )
```

profile of v0, /device:TPU:0, one launch (start us, length us, event | category | flops | bytes accessed | tf_op | source)
XLA Modules:
  0.0 1398.7 jit_solution(8657508417507413299)
XLA Ops:
  11.2 10.2 all-gather
  23.2 13.3 all-reduce.11
  47.0 5.1 all-to-all-start.1
  52.1 9.5 all-gather.14.cloned.1.call-done
  69.6 21.9 %all-gather.10.cloned.1.call-done = bf16[1024,1024]{1,0:T(8,128)(2,1)} async-done(((bf16[128,1024]{1,0:T(8,128)(2,1)}), bf16[1024,1024]{1,0:T(8,128)(2,1)}) %all-gather.10.cloned.1.call-update) | async-done | bytes 2097168 | tf_op jit(solution)/shard_map/all_gather | solution.py:150
  98.4 5.0 all-to-all-start.2
  106.2 7.0 reduce
  131.7 15.6 %all-to-all-done = bf16[4,2,65536]{2,1,0:T(2,128)(2,1)S(1)} async-done(((bf16[4,2,65536]{2,1,0:T(2,128)(2,1)}), bf16[4,2,65536]{2,1,0:T(2,128)(2,1)S(1)}, u32[]{:S(2)}, u32[]{:S(2)}) %all-to-all-start) | async-done | bytes 1048608 | tf_op jit(solution)/shard_map/all_to_all | solution.py:191
  152.5 62.2 %while.47 = (s32[]{:T(128)}, bf16[4,512,2,2,64]{1,4,3,2,0:T(8,128)(2,1)}, f32[4,2,2,512,1]{3,2,1,4,0:T(2,128)}, s32[4]{0:T(128)S(1)}, bf16[4,512,2,2,64]{1,4,3,2...) while((s32[]{:T(128)}, ...), condition=%wide.region_6.7_spmd, body=%wide.region_3.6_spmd.sunk | while | flops 1125251584 | bytes 56168568 | solution.py:80
  161.8 5.6 fusion.169
  177.4 5.6 fusion.169
  192.9 5.6 fusion.169
  208.4 5.6 fusion.169
  214.7 6.1 copy.135
  220.8 8.6 reshape.431
  229.4 11.6 reduce.3
  246.2 8.7 all-gather.1
  254.9 16.5 %all-to-all-done.3 = bf16[4,2,65536]{2,1,0:T(2,128)(2,1)S(1)} async-done(((bf16[4,2,65536]{2,1,0:T(2,128)(2,1)}), bf16[4,2,65536]{2,1,0:T(2,128)(2,1)S(1)}, u32[]{:S(2)}, u32[]{:S(2)}) %all-to-all-start.3) | async-done | bytes 1048608 | tf_op jit(solution)/shard_map/all_to_all | solution.py:204
  283.9 11.5 fusion.109
  295.4 11.4 fusion.110
  306.7 20.6 %multiply_convert_fusion = (bf16[512,4608]{1,0:T(8,128)(2,1)}, bf16[512,4608]{1,0:T(8,128)(2,1)}, bf16[512,4608]{1,0:T(8,128)(2,1)}) fusion(f32[512,4608]{1,0:T(8,128)} %fusion.109, f32[512,4608]{1,0:T(8,128)} %fusion.110, bf16[4608,1024]{1,0:T(8,128)(2,1)} %all-gather.22.cloned.1.call-done, bf16[1,512,1024]{2,1,0:T(8,128)(2,1)S(1)} %copy-done.36), kind=kOutput, calls=%fused_computation.67 | convolution fusion | flops 4869586944 | bytes 43515904 | tf_op jit(solution)/shard_map/dot_general | solution.py:43
  327.3 9.2 fusion.111
  336.5 9.0 multiply_reduce_fusion
  354.3 8.0 reduce.4
  370.3 24.9 %all-to-all-done.4 = bf16[4,2,65536]{2,1,0:T(2,128)(2,1)} async-done(((bf16[4,2,65536]{2,1,0:T(2,128)(2,1)}), bf16[4,2,65536]{2,1,0:T(2,128)(2,1)}, u32[]{:S(2)}, u32[]{:S(2)}) %all-to-all-start.4) | async-done | bytes 1048608 | tf_op jit(solution)/shard_map/all_to_all | solution.py:254
  400.4 195.2 %while.48 = (s32[]{:T(128)}, f32[2048,2,64]{0,2,1:T(8,128)}, f32[2048,2,64]{0,2,1:T(8,128)}, bf16[4,512,2,2,64]{1,4,3,2,0:T(8,128)(2,1)}, bf16[4,512,2,2,64]{1,4...) while((s32[]{:T(128)}, f32[2048,2,64]{0,2,1:T(8,128)}, ...), condition=%wide.region_11.12_spmd.clone, body=%wide.region_9.11_spmd.clone.sunk | while | flops 2749889024 | bytes 242020752 | solution.py:121
  407.3 11.5 fusion.179
  418.8 10.9 fusion.180
  429.7 6.2 fusion.181
  435.9 8.4 fusion.182
  444.3 4.8 fusion.183
  455.8 11.5 fusion.179
  467.3 10.9 fusion.180
  478.3 6.4 fusion.181
  484.7 8.4 fusion.182
  493.1 4.8 fusion.183
  504.6 11.5 fusion.179
  516.1 10.9 fusion.180
  527.0 6.4 fusion.181
  533.4 8.4 fusion.182
  541.9 4.8 fusion.183
  553.4 11.5 fusion.179
  564.9 10.9 fusion.180
  575.8 6.4 fusion.181
  582.2 8.4 fusion.182
  597.7 11.5 reduce.7
  609.3 16.4 %all_to_all.108 = bf16[4,2,32768]{2,1,0:T(2,128)(2,1)S(1)} all-to-all(bf16[4,2,32768]{2,1,0:T(2,128)(2,1)S(1)} %reshape.449), channel_id=1, replica_groups=mesh['seq'=4,'fsdp'=8] {'seq'}, dimensions={0} | all-to-all | bytes 1048576 | tf_op jit(solution)/shard_map/all_to_all | solution.py:270
  632.9 11.5 reduce.5
  644.5 16.6 %all_to_all.109 = bf16[4,2,32768]{2,1,0:T(2,128)(2,1)S(1)} all-to-all(bf16[4,2,32768]{2,1,0:T(2,128)(2,1)S(1)} %reshape.451), channel_id=1, replica_groups=mesh['seq'=4,'fsdp'=8] {'seq'}, dimensions={0} | all-to-all | bytes 1048576 | tf_op jit(solution)/shard_map/all_to_all | solution.py:273
  670.8 5.9 copy.136
  676.7 8.7 reshape.432
  685.4 12.6 reduce.6
  701.5 29.3 %all_to_all.110 = bf16[4,2,65536]{2,1,0:T(2,128)(2,1)} all-to-all(bf16[4,2,65536]{2,1,0:T(2,128)(2,1)} %reshape.447), channel_id=1, replica_groups=mesh['seq'=4,'fsdp'=8] {'seq'}, dimensions={0} | all-to-all | bytes 2097152 | tf_op jit(solution)/shard_map/all_to_all | solution.py:263
  749.7 11.2 fusion.114
  761.0 11.5 fusion.115
  772.6 12.0 fusion.80
  790.0 35.5 %reduce-scatter.8.cloned.1.call-done = f32[128,1024]{1,0:T(8,128)} async-done(((f32[1024,1024]{1,0:T(8,128)}), f32[128,1024]{1,0:T(8,128)}) %reduce-scatter.8.cloned.1.call-update) | async-done | bytes 524304 | tf_op jit(solution)/shard_map/reduce_scatter | solution.py:309
  827.3 127.8 %reduce-scatter.16.cloned.1.call-done = f32[128,4608]{1,0:T(8,128)} async-done(((f32[1024,4608]{1,0:T(8,128)}), f32[128,4608]{1,0:T(8,128)}) %reduce-scatter.16.cloned.1.call-update) | async-done | bytes 2359312 | tf_op jit(solution)/shard_map/reduce_scatter | solution.py:319
  957.9 126.9 %reduce-scatter.18.cloned.1.call-done = f32[128,4608]{1,0:T(8,128)} async-done(((f32[1024,4608]{1,0:T(8,128)}), f32[128,4608]{1,0:T(8,128)}) %reduce-scatter.18.cloned.1.call-update) | async-done | bytes 2359312 | tf_op jit(solution)/shard_map/reduce_scatter | solution.py:320
  1087.6 126.8 %reduce-scatter.20.cloned.1.call-done = f32[576,1024]{1,0:T(8,128)} async-done(((f32[4608,1024]{1,0:T(8,128)}), f32[576,1024]{1,0:T(8,128)}) %reduce-scatter.20.cloned.1.call-update) | async-done | bytes 2359312 | tf_op jit(solution)/shard_map/reduce_scatter | solution.py:321
  1218.7 10.2 fusion.75
  1234.7 24.6 %all-reduce.10 = (bf16[1024]{0:T(1024)(128)(2,1)S(1)}, bf16[64]{0:T(256)(128)(2,1)S(1)}, bf16[64]{0:T(256)(128)(2,1)S(1)}, bf16[1024]{0:T(1024)(128)(2,1)S(1)}) all-reduce(f32[1024]{0:T(1024)S(1)} %get-tuple-element.192, f32[64]{0:T(128)S(1)} %get-tuple-element.190, ...), channel_id=6, replica_groups=mesh['seq'=4,'fsdp'=8] {'fsdp'}, use_global_device_ids=true, to_apply=%region_24.25.clone | all-reduce | flops 2176 | bytes 13056
  1259.6 12.4 all-reduce.12
  1277.2 102.7 %all-reduce.16.cloned.1.call-done = (bf16[128,1024]{1,0:T(8,128)(2,1)}, bf16[128,512]{1,0:T(8,128)(2,1)}, bf16[128,512]{1,0:T(8,128)(2,1)}, bf16[128,1024]{1,0:T...) async-done(((bf16[128,1024]{1,0:T(8,128)(2,1)}, bf16[128,512]{1,0:T(8,128)(2,1)}, bf16[128,512]{1,0:T(8,128)(2,1)}, ...) | async-done | bytes 4325392 | tf_op jit(solution)/shard_map/psum | solution.py:336
  (389 shorter events, 247.2 us)
Async XLA Ops:
  7.2 14.3 %copy-start.58 = (u32[32]{0:T(128)S(1)}, u32[32]{0:T(128)}, u32[]{:S(2)}) copy-start(u32[32]{0:T(128)} %constant.129) | copy-start | bytes 388
  7.2 14.2 %copy-start.59 = (s32[1,512]{1,0:T(1,128)S(1)}, s32[1,512]{1,0:T(1,128)}, u32[]{:S(2)}) copy-start(s32[1,512]{1,0:T(1,128)} %param.19) | copy-start | bytes 6148
  7.2 15.5 %copy-start.62 = (bf16[8]{0:T(256)(128)(2,1)S(1)}, bf16[8]{0:T(256)(128)(2,1)}, u32[]{:S(2)}) copy-start(bf16[8]{0:T(256)(128)(2,1)} %param.26) | copy-start | bytes 52
  7.2 15.8 %copy-start.63 = (bf16[8]{0:T(256)(128)(2,1)S(1)}, bf16[8]{0:T(256)(128)(2,1)}, u32[]{:S(2)}) copy-start(bf16[8]{0:T(256)(128)(2,1)} %param.27) | copy-start | bytes 52
  7.2 29.3 %copy-start.3 = (bf16[1,512,1024]{2,1,0:T(8,128)(2,1)S(1)}, bf16[1,512,1024]{2,1,0:T(8,128)(2,1)}, u32[]{:S(2)}) copy-start(bf16[1,512,1024]{2,1,0:T(8,128)(2,1)} %param.18) | copy-start | bytes 3145732
  7.2 30.0 %all-gather.12.cloned.1.call-start = ((), (), s32[]{:S(2)}) async-start(), calls=%async_computation.16 | async-start | bytes 1179648 | tf_op jit(solution)/shard_map/all_gather | solution.py:151
  8.0 53.7 %all-gather.14.cloned.1.call-start = ((), (), s32[]{:S(2)}) async-start(), calls=%async_computation.17 | async-start | bytes 1179648 | tf_op jit(solution)/shard_map/all_gather | solution.py:152
  8.7 82.8 %all-gather.10.cloned.1.call-start = ((), (), s32[]{:S(2)}) async-start(), calls=%async_computation.15 | async-start | bytes 2359296 | tf_op jit(solution)/shard_map/all_gather | solution.py:150
  9.5 269.4 %all-gather.16.cloned.1.call-start = ((), (), s32[]{:S(2)}) async-start(), calls=%async_computation.18 | async-start | bytes 2359296 | tf_op jit(solution)/shard_map/all_gather | solution.py:153
  10.0 273.8 %all-gather.18.cloned.1.call-start = ((), (), s32[]{:S(2)}) async-start(), calls=%async_computation.19 | async-start | bytes 10616832 | tf_op jit(solution)/shard_map/all_gather | solution.py:211
  10.6 284.7 %all-gather.20.cloned.1.call-start = ((), (), s32[]{:S(2)}) async-start(), calls=%async_computation.20 | async-start | bytes 10616832 | tf_op jit(solution)/shard_map/all_gather | solution.py:212
  21.4 74.0 %copy-start.45 = (f32[8,1,128]{2,1,0:T(1,128)}, f32[8,1,128]{2,1,0:T(1,128)S(1)}, u32[]{:S(2)}) copy-start(f32[8,1,128]{2,1,0:T(1,128)S(1)} %convert_element_type.302) | copy-start | bytes 12292
  36.9 58.6 %copy-start.49 = (f32[512]{0:T(512)}, f32[512]{0:T(512)S(1)}, u32[]{:S(2)}) copy-start(f32[512]{0:T(512)S(1)} %fusion.101) | copy-start | bytes 6148
  37.2 66.8 %copy-start.25 = (f32[512,32]{0,1:T(8,128)}, f32[512,32]{0,1:T(8,128)S(1)}, u32[]{:S(2)}) copy-start(f32[512,32]{0,1:T(8,128)S(1)} %get-tuple-element.262) | copy-start | bytes 196612
  37.2 66.8 %copy-start.27 = (f32[512,32]{0,1:T(8,128)}, f32[512,32]{0,1:T(8,128)S(1)}, u32[]{:S(2)}) copy-start(f32[512,32]{0,1:T(8,128)S(1)} %get-tuple-element.263) | copy-start | bytes 196612
  47.0 51.4 %all-to-all-start.1 = ((bf16[4,2,32768]{2,1,0:T(2,128)(2,1)}), bf16[4,2,32768]{2,1,0:T(2,128)(2,1)}, u32[]{:S(2)}, u32[]{:S(2)}) async-start(bf16[4,2,32768]{2,1,0:T(2,128)(2,1)} %reshape.439), calls=%async_computation.1 | async-start | bytes 1048576 | tf_op jit(solution)/shard_map/all_to_all | solution.py:192
  52.1 51.4 %copy-start.53 = (f32[64]{0:T(128)}, f32[64]{0:T(128)S(1)}, u32[]{:S(2)}) copy-start(f32[64]{0:T(128)S(1)} %convert_element_type.241) | copy-start | bytes 772
  98.4 5.6 copy-start.7
  98.4 5.6 copy-start.43
  98.4 20.0 %all-to-all-start.2 = ((bf16[4,2,32768]{2,1,0:T(2,128)(2,1)}), bf16[4,2,32768]{2,1,0:T(2,128)(2,1)}, u32[]{:S(2)}, u32[]{:S(2)}) async-start(bf16[4,2,32768]{2,1,0:T(2,128)(2,1)} %reshape.441), calls=%async_computation.2 | async-start | bytes 1048576 | tf_op jit(solution)/shard_map/all_to_all | solution.py:193
  118.5 28.8 %all-to-all-start = ((bf16[4,2,65536]{2,1,0:T(2,128)(2,1)}), bf16[4,2,65536]{2,1,0:T(2,128)(2,1)S(1)}, u32[]{:S(2)}, u32[]{:S(2)}) async-start(bf16[4,2,65536]{2,1,0:T(2,128)(2,1)} %reshape.437), calls=%async_computation | async-start | bytes 2097152 | tf_op jit(solution)/shard_map/all_to_all | solution.py:191
  122.0 184.7 %all-gather.22.cloned.1.call-start = ((), (), s32[]{:S(2)}) async-start(), calls=%async_computation.21 | async-start | bytes 10616832 | tf_op jit(solution)/shard_map/all_gather | solution.py:213
  214.7 14.7 %copy-start.6 = (bf16[2048,2,64]{0,2,1:T(8,128)(2,1)}, bf16[2048,2,64]{0,2,1:T(8,128)(2,1)S(1)}, u32[]{:S(2)}) copy-start(bf16[2048,2,64]{0,2,1:T(8,128)(2,1)S(1)} %get-tuple-element.481) | copy-start | bytes 1572868
  214.7 14.7 %copy-start.13 = (bf16[4,512,2,2,64]{1,4,3,2,0:T(8,128)(2,1)}, bf16[4,512,2,2,64]{1,4,3,2,0:T(8,128)(2,1)S(1)}, u32[]{:S(2)}) copy-start(bf16[4,512,2,2,64]{1,4,3,2,0:T(8,128)(2,1)S(1)} %get-tuple-element.484) | copy-start | bytes 3145732
  241.0 5.2 copy-start.61
  242.7 28.8 %all-to-all-start.3 = ((bf16[4,2,65536]{2,1,0:T(2,128)(2,1)}), bf16[4,2,65536]{2,1,0:T(2,128)(2,1)S(1)}, u32[]{:S(2)}, u32[]{:S(2)}) async-start(bf16[4,2,65536]{2,1,0:T(2,128)(2,1)} %reshape.443), calls=%async_computation.3 | async-start | bytes 2097152 | tf_op jit(solution)/shard_map/all_to_all | solution.py:204
  273.9 5.0 copy-start.4
  283.9 11.5 copy-start.15
  295.3 11.4 copy-start.36
  327.3 9.2 copy-start.12
  327.3 9.2 copy-start.21
  366.0 29.3 %all-to-all-start.4 = ((bf16[4,2,65536]{2,1,0:T(2,128)(2,1)}), bf16[4,2,65536]{2,1,0:T(2,128)(2,1)}, u32[]{:S(2)}, u32[]{:S(2)}) async-start(bf16[4,2,65536]{2,1,0:T(2,128)(2,1)} %reshape.445), calls=%async_computation.4 | async-start | bytes 2097152 | tf_op jit(solution)/shard_map/all_to_all | solution.py:254
  370.3 414.6 %reduce-scatter.10.cloned.1.call-start = ((), (), s32[]{:S(2)}) async-start(), calls=%async_computation.23 | async-start | bytes 2359296 | tf_op jit(solution)/shard_map/reduce_scatter | solution.py:310
  404.1 14.7 %copy-start = (f32[2,512,2,2048]{3,1,2,0:T(8,128)}, f32[2,512,2,2048]{3,1,2,0:T(8,128)S(1)}, u32[]{:S(2)}) copy-start(f32[2,512,2,2048]{3,1,2,0:T(8,128)S(1)} %fusion.178) | copy-start | bytes 50331652 | tf_op jit(solution)/shard_map/while/body/eval_jaxpr/while
  429.7 6.2 copy-start.33
  429.7 14.6 %slice-start = ((s8[8388608]{0:T(1024)(128)(4,1)}), s8[4194304]{0:T(1024)(128)(4,1)S(1)}, s32[]{:S(2)}) async-start(s8[8388608]{0:T(1024)(128)(4,1)} %bitcast.353), calls=%async_computation.30 | async-start | bytes 8388608 | tf_op jit(solution)/shard_map/while/body/eval_jaxpr/while
  435.9 8.4 slice-start.1
  444.3 4.8 copy-start.34
  452.6 14.7 %copy-start = (f32[2,512,2,2048]{3,1,2,0:T(8,128)}, f32[2,512,2,2048]{3,1,2,0:T(8,128)S(1)}, u32[]{:S(2)}) copy-start(f32[2,512,2,2048]{3,1,2,0:T(8,128)S(1)} %fusion.178) | copy-start | bytes 50331652 | tf_op jit(solution)/shard_map/while/body/eval_jaxpr/while
  478.3 6.4 copy-start.33
  478.3 14.8 %slice-start = ((s8[8388608]{0:T(1024)(128)(4,1)}), s8[4194304]{0:T(1024)(128)(4,1)S(1)}, s32[]{:S(2)}) async-start(s8[8388608]{0:T(1024)(128)(4,1)} %bitcast.353), calls=%async_computation.30 | async-start | bytes 8388608 | tf_op jit(solution)/shard_map/while/body/eval_jaxpr/while
  484.7 8.4 slice-start.1
  493.0 4.8 copy-start.34
  501.4 14.7 %copy-start = (f32[2,512,2,2048]{3,1,2,0:T(8,128)}, f32[2,512,2,2048]{3,1,2,0:T(8,128)S(1)}, u32[]{:S(2)}) copy-start(f32[2,512,2,2048]{3,1,2,0:T(8,128)S(1)} %fusion.178) | copy-start | bytes 50331652 | tf_op jit(solution)/shard_map/while/body/eval_jaxpr/while
  527.0 6.4 copy-start.33
  527.0 14.8 %slice-start = ((s8[8388608]{0:T(1024)(128)(4,1)}), s8[4194304]{0:T(1024)(128)(4,1)S(1)}, s32[]{:S(2)}) async-start(s8[8388608]{0:T(1024)(128)(4,1)} %bitcast.353), calls=%async_computation.30 | async-start | bytes 8388608 | tf_op jit(solution)/shard_map/while/body/eval_jaxpr/while
  533.4 8.4 slice-start.1
  541.8 4.9 copy-start.34
  550.2 14.7 %copy-start = (f32[2,512,2,2048]{3,1,2,0:T(8,128)}, f32[2,512,2,2048]{3,1,2,0:T(8,128)S(1)}, u32[]{:S(2)}) copy-start(f32[2,512,2,2048]{3,1,2,0:T(8,128)S(1)} %fusion.178) | copy-start | bytes 50331652 | tf_op jit(solution)/shard_map/while/body/eval_jaxpr/while
  575.8 6.4 copy-start.33
  575.8 14.8 %slice-start = ((s8[8388608]{0:T(1024)(128)(4,1)}), s8[4194304]{0:T(1024)(128)(4,1)S(1)}, s32[]{:S(2)}) async-start(s8[8388608]{0:T(1024)(128)(4,1)} %bitcast.353), calls=%async_computation.30 | async-start | bytes 8388608 | tf_op jit(solution)/shard_map/while/body/eval_jaxpr/while
  582.2 8.4 slice-start.1
  590.6 4.8 copy-start.34
  631.6 155.0 %reduce-scatter.12.cloned.1.call-start = ((), (), s32[]{:S(2)}) async-start(), calls=%async_computation.24 | async-start | bytes 2359296 | tf_op jit(solution)/shard_map/reduce_scatter | solution.py:311
  666.2 122.0 %reduce-scatter.14.cloned.1.call-start = ((), (), s32[]{:S(2)}) async-start(), calls=%async_computation.25 | async-start | bytes 4718592 | tf_op jit(solution)/shard_map/reduce_scatter | solution.py:312
  670.7 154.8 %reduce-scatter.8.cloned.1.call-start = ((), (), s32[]{:S(2)}) async-start(), calls=%async_computation.22 | async-start | bytes 4718592 | tf_op jit(solution)/shard_map/reduce_scatter | solution.py:309
  749.6 205.5 %reduce-scatter.16.cloned.1.call-start = ((), (), s32[]{:S(2)}) async-start(), calls=%async_computation.26 | async-start | bytes 21233664 | tf_op jit(solution)/shard_map/reduce_scatter | solution.py:319
  760.9 323.9 %reduce-scatter.18.cloned.1.call-start = ((), (), s32[]{:S(2)}) async-start(), calls=%async_computation.27 | async-start | bytes 21233664 | tf_op jit(solution)/shard_map/reduce_scatter | solution.py:320
  772.5 441.9 %reduce-scatter.20.cloned.1.call-start = ((), (), s32[]{:S(2)}) async-start(), calls=%async_computation.28 | async-start | bytes 21233664 | tf_op jit(solution)/shard_map/reduce_scatter | solution.py:321
  784.6 595.4 %all-reduce.16.cloned.1.call-start = ((), (), s32[]{:S(2)}) async-start(), calls=%async_computation.29 | async-start | bytes 8650752 | tf_op jit(solution)/shard_map/psum | solution.py:336
  1218.7 10.2 copy-start.20
  1218.7 10.2 copy-start.22
  1232.2 41.9 %copy-start.52 = (f32[512]{0:T(512)S(1)}, f32[512]{0:T(512)}, u32[]{:S(2)}) copy-start(f32[512]{0:T(512)} %copy-done.51) | copy-start | bytes 6148
  1380.0 7.0 copy-start.31
  (43 other events, 93.4 us)
Sparse Core Ops, SparseCore 0:
  10.0 26.2 all-gather.11
  38.1 23.4 all-gather.13
  63.6 27.8 all-gather.9
  93.2 27.8 all-gather.15
  122.9 58.8 all-gather.17
  183.5 58.8 all-gather.19
  244.3 58.8 all-gather.21
  631.7 39.1 reduce-scatter.9
  674.6 41.2 reduce-scatter.11
  719.0 51.3 reduce-scatter.13
  774.1 51.3 reduce-scatter.7
  829.0 126.0 reduce-scatter.15
  958.7 126.0 reduce-scatter.17
  1088.3 126.1 reduce-scatter.19
  1218.4 161.5 all-reduce.15
where the time goes:
time: 1410 us; the launch traced here: 1400 us
  waiting for transfers between devices  616 us (44%)
  matrix products  309 us (22%)
  other arithmetic  187 us (13%)
  blocking collectives  131 us (9%)
  local copies, waits for them, and re-layouts  115 us (8%)
  starting transfers between devices  22.3 us (2%)
  between operations  17.2 us (1%)
    reduce_scatter x1, waiting for transfers between devices, per_device(): lax.psum_scatter(gate_weight_grad, 'fsdp', scatter_dimension=0, tiled=True)  128 us
    reduce_scatter x1, waiting for transfers between devices, per_device(): lax.psum_scatter(up_weight_grad, 'fsdp', scatter_dimension=0, tiled=True)  127 us
    reduce_scatter x1, waiting for transfers between devices, per_device(): lax.psum_scatter(down_grad, 'fsdp', scatter_dimension=0, tiled=True)  127 us
    psum x1, waiting for transfers between devices, per_device(): lax.psum(query_shard.astype(jnp.bfloat16), 'seq').astype(jnp.float32)  103 us
    unnamed x10, other arithmetic  70 us
    unnamed x150, local copies, waits for them, and re-layouts  49.2 us
    dot_general x7, matrix products, matmul_left_t(): lax.dot_general(left_side, right_side, (((0,), (0,)), ((), ())), preferre...  48.5 us
    dot_general x4, matrix products, one_block(): jnp.einsum('qbgd,kbd->bgqk', block_grad, value_rows, preferred_element_ty...  46.2 us
  transfers between devices with their start and end apart: 20, of which 11 were waited for; matrix products, arithmetic and copies ran while one was open for 22% of the time, Pallas kernels for 0%

commit v1 on v0

v1 whole, which is shorter than its diff:
```python
import functools

import jax
import jax.numpy as jnp
from jax import lax
from jax.experimental import pallas as pl
from jax.experimental.pallas import tpu as pltpu
from jax.sharding import PartitionSpec as P

EPSILON = 1e-05
ROPE_BASE = 1000000.0
LOG2E = 1.4426950408889634
BF = jnp.bfloat16
F32 = jnp.float32
VMEM = pl.BlockSpec(memory_space=pltpu.VMEM)
SMEM = pl.BlockSpec(memory_space=pltpu.SMEM)
ANY = pl.BlockSpec(memory_space=pl.ANY)
VMEM_BYTES = 58 * 2**20


def dot_nn(a, b):
    return lax.dot_general(a, b, (((1,), (0,)), ((), ())), preferred_element_type=F32)


def dot_nt(a, b):
    return lax.dot_general(a, b, (((1,), (1,)), ((), ())), preferred_element_type=F32)


def dot_tn(a, b):
    return lax.dot_general(a, b, (((0,), (0,)), ((), ())), preferred_element_type=F32)


def shape_of(shape, dtype):
    return jax.ShapeDtypeStruct(shape, dtype)


def call(kernel, outs, in_specs, out_specs, scratch, flops, moved, **more):
    return pl.pallas_call(
        kernel,
        out_shape=outs,
        in_specs=in_specs,
        out_specs=out_specs,
        scratch_shapes=scratch,
        compiler_params=pltpu.CompilerParams(vmem_limit_bytes=VMEM_BYTES),
        cost_estimate=pl.CostEstimate(flops=flops, bytes_accessed=moved, transcendentals=0),
        **more,
    )


def row_norm(values):
    return lax.rsqrt(jnp.mean(values * values, axis=-1, keepdims=True) + EPSILON)


def piece_offset(me, at, count, rows):
    if count == 1:
        return 0
    return pl.multiple_of((me ^ at) * rows, rows)


def start_pieces(me, pieces, whole, sems, first, rows=None, base=0, stride=None, cols=None, to_cols=None):
    copies = []
    for at, piece in enumerate(pieces):
        count = piece.shape[0] if rows is None else rows
        if len(pieces) == 1:
            count, offset = whole.shape[0], 0
        else:
            offset = piece_offset(me, at, len(pieces), count if stride is None else stride) + base
        source = piece.at[pl.ds(0, count)] if cols is None else piece.at[pl.ds(0, count), pl.ds(*cols)]
        target = whole.at[pl.ds(offset, count)] if to_cols is None else whole.at[pl.ds(offset, count), pl.ds(*to_cols)]
        copy = pltpu.make_async_copy(source, target, sems.at[first + at])
        copy.start()
        copies.append(copy)
    return copies


def wait_all(copies):
    for copy in copies:
        copy.wait()


def head_mask(width, head_dim):
    rows = lax.broadcasted_iota(jnp.int32, (width, width), 0) // head_dim
    cols = lax.broadcasted_iota(jnp.int32, (width, width), 1) // head_dim
    return (rows == cols).astype(BF)


def head_sum(values, mask):
    high = values.astype(BF)
    rest = (values - high.astype(F32)).astype(BF)
    return dot_nn(high, mask) + dot_nn(rest, mask)


def partner(values, head_dim):
    half = head_dim // 2
    width = values.shape[-1]
    lane = lax.broadcasted_iota(jnp.int32, values.shape, 1)
    after = pltpu.roll(values, width - half, 1)
    before = pltpu.roll(values, half, 1)
    return jnp.where(lane % head_dim < half, after, before)


def pre_kernel(dims, ids, x_ref, gain_ref, head_gain_ref, cos_ref, sin_ref, *refs):
    nz, np_a, head_dim, q_cols, k_cols, v_cols = dims
    a_pieces, b_pieces = refs[:np_a], refs[np_a : 2 * np_a]
    refs = refs[2 * np_a :]
    normed_t_ref, proj_ref = refs[:2]
    blocks = refs[2 : 2 + nz]
    w_qk, w_v, qkv, sems = refs[2 + nz :]
    z, me = ids[0], ids[1]
    rows = w_qk.shape[0] // np_a
    copies = start_pieces(me, a_pieces, w_qk, sems, 0, rows=rows)
    copies += start_pieces(me, b_pieces, w_v, sems, np_a, rows=rows, cols=(0, v_cols))
    x = x_ref[...].astype(F32)
    normed = (x * row_norm(x) * gain_ref[...]).astype(BF)
    normed_t_ref[...] = normed.T
    width = 256
    mask = head_mask(width, head_dim)
    cos = jnp.concatenate([cos_ref[...]] * (width // 128), axis=1)
    sin = jnp.concatenate([sin_ref[...]] * (width // 128), axis=1)
    wait_all(copies)
    for start in range(0, q_cols + k_cols, width):
        cols = slice(start, start + width)
        proj = dot_nn(normed, w_qk[:, cols])
        proj_ref[:, cols] = proj
        scale = lax.rsqrt(head_sum(proj * proj, mask) * (1.0 / head_dim) + EPSILON)
        values = proj * scale * head_gain_ref[:, cols]
        qkv[:, cols] = (values * cos + partner(values, head_dim) * sin).astype(BF)
    qkv[:, q_cols + k_cols :] = dot_nn(normed, w_v[...]).astype(BF)
    pack_blocks(z, nz, qkv, blocks, (q_cols, k_cols, v_cols))


def pack_blocks(z, nz, source, blocks, widths):
    for j, block in enumerate(blocks):
        owner = z ^ j
        base, at = 0, 0
        for width in widths:
            part = width // nz
            block[:, at : at + part] = source[:, pl.ds(pl.multiple_of(base + owner * part, part), part)]
            base, at = base + width, at + part


def load_heads(z, nz, blocks, scratch, sems, first):
    copies = []
    tokens = blocks[0].shape[0]
    for j in range(nz):
        copy = pltpu.make_async_copy(
            blocks[j], scratch.at[pl.ds(pl.multiple_of((z ^ j) * tokens, tokens), tokens)], sems.at[first + j]
        )
        copy.start()
        copies.append(copy)
    return copies


def split_heads(scratch, first, heads):
    head_dim = heads.shape[-1]
    for h in range(heads.shape[0]):
        heads[h] = scratch[:, first + h * head_dim : first + (h + 1) * head_dim]


def attend_kernel(dims, ids, *refs):
    nz, rows = dims
    blocks, outs = refs[:nz], refs[nz : 2 * nz]
    full_ref, log_ref, scratch, queries, keys, values, sems = refs[2 * nz :]
    z = ids[0]
    wait_all(load_heads(z, nz, blocks, scratch, sems, 0))
    heads, seq_len, head_dim = queries.shape
    kv_heads = keys.shape[0]
    group = heads // kv_heads
    split_heads(scratch, 0, queries)
    split_heads(scratch, heads * head_dim, keys)
    split_heads(scratch, (heads + kv_heads) * head_dim, values)
    scale = head_dim**-0.5 * LOG2E
    for r in range(seq_len // rows):
        span = slice(r * rows, (r + 1) * rows)
        reach = (r + 1) * rows

        def one_head(h, _):
            b = lax.div(h, group)
            scores = dot_nt(queries[h, span], keys[b, :reach]) * scale
            row = lax.broadcasted_iota(jnp.int32, scores.shape, 0) + r * rows
            col = lax.broadcasted_iota(jnp.int32, scores.shape, 1)
            probs = jnp.exp2(jnp.where(row >= col, scores, -1e30))
            total = jnp.sum(probs, axis=1, keepdims=True)
            full_ref[h, span] = dot_nn(probs.astype(BF), values[b, :reach]) * (1.0 / total)
            log_ref[h, :, span] = jnp.broadcast_to(jnp.log2(total), (rows, 128)).T[0:8]
            return 0

        lax.fori_loop(0, heads, one_head, 0)
    tokens = outs[0].shape[0]
    for j in range(nz):
        first = pl.multiple_of((z ^ j) * tokens, tokens)
        for h in range(heads):
            outs[j][:, h * head_dim : (h + 1) * head_dim] = full_ref[h, pl.ds(first, tokens)].astype(BF)


def attend_back_kernel(dims, ids, *refs):
    nz, rows, chunk = dims
    blocks, grads = refs[:nz], refs[nz : 2 * nz]
    full_ref, log_ref = refs[2 * nz : 2 * nz + 2]
    outs = refs[2 * nz + 2 : 3 * nz + 2]
    scratch, grad_scratch, queries, keys, values, grad, delta, q_grad, k_grad, v_grad, sems = refs[3 * nz + 2 :]
    z = ids[0]
    copies = load_heads(z, nz, blocks, scratch, sems, 0)
    copies += load_heads(z, nz, grads, grad_scratch, sems, nz)
    wait_all(copies)
    heads, seq_len, head_dim = queries.shape
    kv_heads = keys.shape[0]
    group = heads // kv_heads
    split_heads(scratch, 0, queries)
    split_heads(scratch, heads * head_dim, keys)
    split_heads(scratch, (heads + kv_heads) * head_dim, values)
    split_heads(grad_scratch, 0, grad)
    factor = head_dim**-0.5
    scale = factor * LOG2E
    ones = jnp.ones((8, head_dim), F32)
    for h in range(heads):
        product = grad[h].astype(F32) * full_ref[h]
        delta[h] = lax.dot_general(
            ones, product, (((1,), (1,)), ((), ())), preferred_element_type=F32, precision=lax.Precision.HIGHEST
        )
        q_grad[h] = jnp.zeros((seq_len, head_dim), F32)
    for at in range(seq_len // rows):
        span = slice(at * rows, (at + 1) * rows)

        def one_head(b, _):
            key, value = keys[b, span], values[b, span]
            key_total = jnp.zeros((rows, head_dim), F32)
            value_total = jnp.zeros((rows, head_dim), F32)
            for g in range(group):
                h = b * group + g
                for first in range(at * rows, seq_len, chunk):
                    last = min(first + chunk, seq_len)
                    part = slice(first, last)
                    query, out_grad = queries[h, part], grad[h, part]
                    scores = dot_nt(key, query) * scale - log_ref[h, 0:1, part]
                    if first == at * rows:
                        key_at = lax.broadcasted_iota(jnp.int32, scores.shape, 0) + at * rows
                        query_at = lax.broadcasted_iota(jnp.int32, scores.shape, 1) + first
                        scores = jnp.where(query_at >= key_at, scores, -1e30)
                    probs = jnp.exp2(scores)
                    prob_grad = dot_nt(value, out_grad)
                    score_grad = (probs * (prob_grad - delta[h, 0:1, part])).astype(BF)
                    value_total = value_total + dot_nn(probs.astype(BF), out_grad)
                    key_total = key_total + dot_nn(score_grad, query)
                    q_grad[h, part] = q_grad[h, part] + dot_tn(score_grad, key)
            k_grad[b, span] = (key_total * factor).astype(BF)
            v_grad[b, span] = value_total.astype(BF)
            return 0

        lax.fori_loop(0, kv_heads, one_head, 0)
    tokens = outs[0].shape[0]
    for j in range(nz):
        here = pl.ds(pl.multiple_of((z ^ j) * tokens, tokens), tokens)
        parts = [(q_grad[h, here] * factor).astype(BF) for h in range(heads)]
        parts += [k_grad[b, here] for b in range(kv_heads)] + [v_grad[b, here] for b in range(kv_heads)]
        outs[j][...] = jnp.concatenate(parts, axis=1)


def load_columns(z, nz, blocks, whole, sems, first):
    copies = []
    width = blocks[0].shape[1]
    for j in range(nz):
        copy = pltpu.make_async_copy(
            blocks[j], whole.at[:, pl.ds(pl.multiple_of((z ^ j) * width, width), width)], sems.at[first + j]
        )
        copy.start()
        copies.append(copy)
    return copies


def norm_back(rows, gain, gradient):
    q = row_norm(rows)
    n = rows * q
    u = gradient * gain
    return q * (u - n * jnp.mean(u * n, axis=-1, keepdims=True)), jnp.sum(gradient * n, axis=0, keepdims=True)


def feed_kernel(dims, ids, x_ref, dy_ref, gain_ref, *refs):
    nz, n_out, n_ff, n_down, out_cols, width, groups = dims
    mixed_blocks, refs = refs[:nz], refs[nz:]
    out_pieces, refs = refs[:n_out], refs[n_out:]
    gate_pieces, refs = refs[:n_ff], refs[n_ff:]
    up_pieces, refs = refs[:n_ff], refs[n_ff:]
    down_pieces, refs = refs[:n_down], refs[n_down:]
    output_ref, middle_grad_ref, middle_low_ref, mixed_t_ref, normed_t_ref, gain_grad_ref = refs[:6]
    grad_blocks, refs = refs[6 : 6 + nz], refs[6 + nz :]
    hidden_hbm, gate_grad_hbm, up_grad_hbm = refs[:3]
    w_out, w_gate, w_up, w_down, mixed, middle, normed, back = refs[3:11]
    hidden_slot, gate_slot, up_slot, sems, slot_sems = refs[11:]
    z, me = ids[0], ids[1]
    at = 0
    early = load_columns(z, nz, mixed_blocks, mixed, sems, at)
    at += nz
    early += start_pieces(me, out_pieces, w_out, sems, at, rows=w_out.shape[0] // n_out, cols=out_cols)
    at += n_out
    if n_down == 1:
        down_copies = start_pieces(me, down_pieces, w_down, sems, at)
    else:
        half = n_down // 2
        rows = down_pieces[0].shape[0]
        down_copies = start_pieces(me, down_pieces[:half], w_down, sems, at, stride=2 * rows)
        down_copies += start_pieces(me, down_pieces[half:], w_down, sems, at + half, stride=2 * rows, base=rows)
    at += n_down
    hidden_cols = w_gate.shape[1]
    group_cols = hidden_cols // groups
    group_copies = []
    for g in range(groups):
        cols = (g * group_cols, group_cols)
        copies = start_pieces(me, gate_pieces, w_gate, sems, at, cols=cols, to_cols=cols)
        copies += start_pieces(me, up_pieces, w_up, sems, at + n_ff, cols=cols, to_cols=cols)
        at += 2 * n_ff
        group_copies.append(copies)
    wait_all(early)
    x = x_ref[...].astype(F32)
    mixed_rows = mixed[...]
    mixed_t_ref[...] = mixed_rows.T
    middle_rows = x + dot_nn(mixed_rows, w_out[...])
    normed_rows = (middle_rows * row_norm(middle_rows) * gain_ref[...]).astype(BF)
    normed[...] = normed_rows
    normed_t_ref[...] = normed_rows.T
    middle[...] = middle_rows
    back[...] = jnp.zeros(back.shape, F32)
    wait_all(down_copies)

    def slot_copies(slot, f):
        here = pl.ds(pl.multiple_of(f * width, width), width)
        return (
            pltpu.make_async_copy(hidden_slot.at[slot], hidden_hbm.at[here], slot_sems.at[slot, 0]),
            pltpu.make_async_copy(gate_slot.at[slot], gate_grad_hbm.at[:, here], slot_sems.at[slot, 1]),
            pltpu.make_async_copy(up_slot.at[slot], up_grad_hbm.at[:, here], slot_sems.at[slot, 2]),
        )

    def one_block(f, _):
        slot = lax.rem(f, 2)
        here = pl.ds(pl.multiple_of(f * width, width), width)

        @pl.when(f >= 2)
        def _():
            wait_all(slot_copies(slot, f - 2))

        gate = dot_nn(normed[...], w_gate[:, here])
        up = dot_nn(normed[...], w_up[:, here])
        hidden_grad = dot_nt(dy_ref[...], w_down[here])
        s = 1.0 / (1.0 + jnp.exp(-gate))
        silu = gate * s
        hidden = (silu * up).astype(BF)
        gate_grad = (hidden_grad * up * (s * (1.0 + gate * (1.0 - s)))).astype(BF)
        up_grad = (hidden_grad * silu).astype(BF)
        hidden_slot[slot] = hidden.T
        gate_slot[slot] = gate_grad
        up_slot[slot] = up_grad
        for copy in slot_copies(slot, f):
            copy.start()
        middle[...] = middle[...] + dot_nn(hidden, w_down[here])
        back[...] = back[...] + (dot_nt(gate_grad, w_gate[:, here]) + dot_nt(up_grad, w_up[:, here]))
        return 0

    blocks = hidden_cols // width
    per_group = blocks // groups
    for g in range(groups):
        wait_all(group_copies[g])
        lax.fori_loop(g * per_group, (g + 1) * per_group, one_block, 0)
    output_ref[...] = middle[...].astype(BF)
    middle_rows = x_ref[...].astype(F32) + dot_nn(mixed[...], w_out[...])
    part, gain_sum = norm_back(middle_rows, gain_ref[...], back[...])
    gain_grad_ref[...] = gain_sum
    middle_grad = dy_ref[...].astype(F32) + part
    middle_grad_ref[...] = middle_grad
    middle_low = middle_grad.astype(BF)
    middle_low_ref[...] = middle_low
    mixed[...] = dot_nt(middle_low, w_out[...]).astype(BF)
    pack_blocks(z, nz, mixed, grad_blocks, (mixed.shape[1],))
    for f in (blocks - 2, blocks - 1):
        wait_all(slot_copies(f % 2, f))


def weight_grad_kernel(dims, ids, left_ref, right_ref, *refs):
    chips, parts = dims
    if chips == 0:
        refs[0][...] = dot_nn(left_ref[...], right_ref[...]).astype(BF)
        return
    outs, (ordered,) = refs[:-1], refs[-1:]
    me = ids[1]
    chip, core = lax.div(me, 2), lax.rem(me, 2)
    rows = left_ref.shape[0] // (2 * chips)

    @pl.when(pl.program_id(0) == 0)
    def _():
        for side in range(2):
            owner_core = 1 - core if side == 0 else core
            for r in range(chips):
                owner = (chip ^ r) * 2 + owner_core
                to = (side * chips + r) * rows
                ordered[to : to + rows] = left_ref[pl.ds(pl.multiple_of(owner * rows, rows), rows)]

    right = right_ref[...]
    part = rows // parts
    for side in range(2):
        got = dot_nn(ordered[side * chips * rows : (side + 1) * chips * rows], right).astype(BF)
        for r in range(chips):
            for p in range(parts):
                first = r * rows + p * part
                outs[side * parts + p][r] = got[first : first + part]


def weight_grad(ids, left, right, chips, parts=1, width=512):
    rows, tokens = left.shape
    cols = right.shape[1]
    width = min(width, cols)
    if chips:
        part = rows // (2 * chips * parts)
        outs = [shape_of((chips, part, cols), BF)] * (2 * parts)
        out_specs = [pl.BlockSpec((chips, part, width), lambda n: (0, 0, n))] * (2 * parts)
        scratch = [pltpu.VMEM((rows, tokens), BF)]
    else:
        outs = [shape_of((rows, cols), BF)]
        out_specs = [pl.BlockSpec((rows, width), lambda n: (0, n))]
        scratch = []
    return call(
        functools.partial(weight_grad_kernel, (chips, parts)),
        outs,
        [SMEM, pl.BlockSpec((rows, tokens), lambda n: (0, 0)), pl.BlockSpec((tokens, width), lambda n: (0, n))],
        out_specs,
        scratch,
        2 * rows * tokens * cols,
        2 * (rows * tokens + tokens * cols + rows * cols),
        grid=(cols // width,),
    )(ids, left, right)


def post_kernel(dims, ids, x_ref, middle_grad_ref, gain_ref, head_gain_ref, cos_ref, sin_ref, proj_ref, *refs):
    nz, np_a, head_dim, q_cols, k_cols, v_cols = dims
    blocks, refs = refs[:nz], refs[nz:]
    a_pieces, b_pieces, refs = refs[:np_a], refs[np_a : 2 * np_a], refs[2 * np_a :]
    input_grad_ref, first_ref, second_ref, gain_grad_ref, head_gain_grad_ref = refs[:5]
    w_qk, w_v, qkv, sems = refs[5:]
    z, me = ids[0], ids[1]
    rows = w_qk.shape[0] // np_a
    copies = start_pieces(me, a_pieces, w_qk, sems, 0, rows=rows)
    copies += start_pieces(me, b_pieces, w_v, sems, np_a, rows=rows, cols=(0, v_cols))
    block_copies = []
    for j in range(nz):
        base, at = 0, 0
        for i, width in enumerate((q_cols, k_cols, v_cols)):
            part = width // nz
            to = pl.multiple_of(base + (z ^ j) * part, part)
            copy = pltpu.make_async_copy(
                blocks[j].at[:, pl.ds(at, part)], qkv.at[:, pl.ds(to, part)], sems.at[2 * np_a + 3 * j + i]
            )
            copy.start()
            block_copies.append(copy)
            base, at = base + width, at + part
    wait_all(block_copies)
    width = 256
    mask = head_mask(width, head_dim)
    cos = jnp.concatenate([cos_ref[...]] * (width // 128), axis=1)
    sin = jnp.concatenate([sin_ref[...]] * (width // 128), axis=1)
    for start in range(0, q_cols + k_cols, width):
        cols = slice(start, start + width)
        rotated = qkv[:, cols].astype(F32)
        gradient = rotated * cos - partner(rotated, head_dim) * sin
        proj = proj_ref[:, cols]
        scale = lax.rsqrt(head_sum(proj * proj, mask) * (1.0 / head_dim) + EPSILON)
        n = proj * scale
        u = gradient * head_gain_ref[:, cols]
        head_gain_grad_ref[:, cols] = jnp.sum(gradient * n, axis=0, keepdims=True)
        low = (scale * (u - n * (head_sum(u * n, mask) * (1.0 / head_dim)))).astype(BF)
        qkv[:, cols] = low
    first_ref[...] = qkv[:, :q_cols]
    second_ref[...] = qkv[:, q_cols:]
    wait_all(copies)
    normed_grad = dot_nt(qkv[:, : q_cols + k_cols], w_qk[...]) + dot_nt(qkv[:, q_cols + k_cols :], w_v[...])
    part, gain_sum = norm_back(x_ref[...].astype(F32), gain_ref[...], normed_grad)
    gain_grad_ref[...] = gain_sum
    input_grad_ref[...] = (middle_grad_ref[...] + part).astype(BF)


def add(a, b):
    return (a.astype(F32) + b.astype(F32)).astype(a.dtype)


def swap(values, axis, size, bit):
    return lax.ppermute(values, axis, [(i, i ^ bit) for i in range(size)])


def gather_plane(first, second):
    near = {0: first, 2: swap(first, "fsdp", 8, 2), 4: swap(first, "fsdp", 8, 4)}
    near[6] = swap(near[2], "fsdp", 8, 4)
    far = {0: second, 4: swap(second, "fsdp", 8, 4), 2: swap(second, "fsdp", 8, 2)}
    far[6] = swap(far[4], "fsdp", 8, 2)
    both = []
    for blocks in (near, far):
        whole = dict(blocks)
        for b in (0, 2, 4, 6):
            whole[b + 1] = swap(blocks[b], "fsdp", 8, 1)
        both.append([whole[b] for b in range(8)])
    return both


def reduce_plane(theirs, mine, x_first):
    got = swap(theirs, "fsdp", 8, 1)
    if x_first:
        away, kept, bits = (1, 3), (0, 2), (2, 4)
    else:
        away, kept, bits = (2, 3), (0, 1), (4, 2)
    send = jnp.stack([add(mine[r], got[r]) for r in away])
    keep = [add(mine[r], got[r]) for r in kept]
    back = swap(send, "fsdp", 8, bits[0])
    last = swap(add(keep[1], back[1]), "fsdp", 8, bits[1])
    return add(add(keep[0], back[0]), last)


def sum_line(values):
    size = lax.axis_size("seq")
    if size != 4:
        return lax.psum(values, "seq")
    z = lax.axis_index("seq")
    inner = add(values, lax.ppermute(values, "seq", [(0, 1), (3, 2)]))
    total = add(inner, lax.ppermute(inner, "seq", [(1, 2), (2, 1)]))
    outer = lax.ppermute(total, "seq", [(1, 0), (2, 3)])
    return jnp.where((z == 1) | (z == 2), total, outer)


def flip_to_order(values, me):
    grid = values.reshape((2, 2, 2) + values.shape[1:])
    for axis, bit in enumerate((4, 2, 1)):
        grid = jnp.where((me & bit) != 0, jnp.flip(grid, axis), grid)
    return grid.reshape(values.shape)


def per_device(
    inputs,
    positions,
    cotangent,
    query_weight,
    key_weight,
    value_weight,
    out_weight,
    attention_gain,
    query_gain,
    key_gain,
    feedforward_gain,
    gate_weight,
    up_weight,
    down_weight,
):
    seqs, tokens, model = inputs.shape
    assert seqs == 1
    fsdp, nz = lax.axis_size("fsdp"), lax.axis_size("seq")
    me, z = lax.axis_index("fsdp"), lax.axis_index("seq")
    plane = fsdp == 8
    ids = jnp.stack([z, me]).astype(jnp.int32)
    x = inputs.reshape(tokens, model)
    dy = cotangent.reshape(tokens, model)
    head_dim = query_gain.shape[0] * fsdp
    q_cols, k_cols, v_cols = query_weight.shape[1], key_weight.shape[1], value_weight.shape[1]
    heads, kv_heads = q_cols // head_dim // nz, k_cols // head_dim // nz
    hidden_cols = gate_weight.shape[1]
    seq_len = tokens * nz

    gains = jnp.concatenate([attention_gain, query_gain, key_gain, feedforward_gain])
    shard_rows = query_weight.shape[0]
    first = jnp.concatenate([query_weight, key_weight], axis=1)
    second = jnp.concatenate([value_weight, out_weight], axis=1)
    if plane:
        gain_rows = jnp.zeros((16, first.shape[1]), BF).at[0, : gains.shape[0]].set(gains)
        qk_pieces, vo_pieces = gather_plane(jnp.concatenate([first, gain_rows]), second)
        gate_pieces, up_pieces = gather_plane(gate_weight, up_weight)
        half = down_weight.shape[0] // 2
        upper, lower = gather_plane(down_weight[:half], down_weight[half:])
        down_pieces = upper + lower
        gains_all = flip_to_order(jnp.stack([p[shard_rows, : gains.shape[0]] for p in qk_pieces]), me)
    else:
        gather = functools.partial(lax.all_gather, axis_name="fsdp", axis=0, tiled=True)
        qk_pieces, vo_pieces = [gather(first)], [gather(second)]
        gate_pieces, up_pieces, down_pieces = [gather(gate_weight)], [gather(up_weight)], [gather(down_weight)]
        gains_all = lax.all_gather(gains, "fsdp", axis=0)
    gains_all = gains_all.astype(F32)
    n_a, n_h = attention_gain.shape[0], query_gain.shape[0]
    cuts = (n_a, n_a + n_h, n_a + 2 * n_h)
    attention_scale = gains_all[:, : cuts[0]].reshape(1, -1)
    query_scale = gains_all[:, cuts[0] : cuts[1]].reshape(1, -1)
    key_scale = gains_all[:, cuts[1] : cuts[2]].reshape(1, -1)
    feed_scale = gains_all[:, cuts[2] :].reshape(1, -1)
    head_scale = jnp.concatenate(
        [jnp.tile(query_scale, (1, q_cols // head_dim)), jnp.tile(key_scale, (1, k_cols // head_dim))], axis=1
    )

    half_dim = head_dim // 2
    freqs = ROPE_BASE ** (-jnp.arange(half_dim, dtype=F32) / half_dim)
    angles = positions.reshape(tokens).astype(F32)[:, None] * freqs[None, :]
    cosine, sine = jnp.cos(angles), jnp.sin(angles)
    cosine = jnp.tile(cosine, (1, 128 // half_dim))
    sine = jnp.tile(jnp.concatenate([-sine, sine], axis=1), (1, 128 // head_dim))

    np_a = len(qk_pieces)
    dims = (nz, np_a, head_dim, q_cols, k_cols, v_cols)
    block_cols = (q_cols + k_cols + v_cols) // nz
    qkv_scratch = [
        pltpu.VMEM((model, q_cols + k_cols), BF),
        pltpu.VMEM((model, v_cols), BF),
        pltpu.VMEM((tokens, q_cols + k_cols + v_cols), BF),
    ]
    proj_flops = 2 * tokens * model * (q_cols + k_cols + v_cols)
    normed_t, proj, *blocks = call(
        functools.partial(pre_kernel, dims),
        [shape_of((model, tokens), BF), shape_of((tokens, q_cols + k_cols), F32)]
        + [shape_of((tokens, block_cols), BF)] * nz,
        [SMEM] + [VMEM] * 5 + [ANY] * (2 * np_a),
        [VMEM] * (2 + nz),
        qkv_scratch + [pltpu.SemaphoreType.DMA((2 * np_a,))],
        proj_flops,
        12 * 2**20,
    )(ids, x, attention_scale, head_scale, cosine, sine, *qk_pieces, *vo_pieces)
    blocks = [blocks[0]] + [swap(blocks[j], "seq", nz, j) for j in range(1, nz)]

    mixed_cols = heads * head_dim
    head_scratch = [
        pltpu.VMEM((heads, seq_len, head_dim), BF),
        pltpu.VMEM((kv_heads, seq_len, head_dim), BF),
        pltpu.VMEM((kv_heads, seq_len, head_dim), BF),
    ]
    attend_flops = 2 * heads * seq_len * seq_len * head_dim
    *mixed, full, logs = call(
        functools.partial(attend_kernel, (nz, min(256, seq_len))),
        [shape_of((tokens, mixed_cols), BF)] * nz
        + [shape_of((heads, seq_len, head_dim), F32), shape_of((heads, 8, seq_len), F32)],
        [SMEM] + [ANY] * nz,
        [VMEM] * (nz + 2),
        [pltpu.VMEM((seq_len, block_cols), BF)] + head_scratch + [pltpu.SemaphoreType.DMA((nz,))],
        4 * attend_flops,
        8 * 2**20,
    )(ids, *blocks)
    mixed = [mixed[0]] + [swap(mixed[j], "seq", nz, j) for j in range(1, nz)]

    n_ff, n_down = len(gate_pieces), len(down_pieces)
    width = 512
    groups = 3
    rows_model = lambda kind: shape_of((tokens, model), kind)
    feed_out = call(
        functools.partial(feed_kernel, (nz, np_a, n_ff, n_down, (v_cols, model), width, groups)),
        [
            rows_model(BF),
            rows_model(F32),
            rows_model(BF),
            shape_of((model, tokens), BF),
            shape_of((model, tokens), BF),
            shape_of((1, model), F32),
        ]
        + [shape_of((tokens, mixed_cols), BF)] * nz
        + [shape_of((hidden_cols, tokens), BF)]
        + [shape_of((tokens, hidden_cols), BF)] * 2,
        [SMEM] + [VMEM] * 3 + [ANY] * (nz + np_a + 2 * n_ff + n_down),
        [VMEM] * (6 + nz) + [ANY] * 3,
        [
            pltpu.VMEM((q_cols, model), BF),
            pltpu.VMEM((model, hidden_cols), BF),
            pltpu.VMEM((model, hidden_cols), BF),
            pltpu.VMEM((hidden_cols, model), BF),
            pltpu.VMEM((tokens, q_cols), BF),
            pltpu.VMEM((tokens, model), F32),
            pltpu.VMEM((tokens, model), BF),
            pltpu.VMEM((tokens, model), F32),
            pltpu.VMEM((2, width, tokens), BF),
            pltpu.VMEM((2, tokens, width), BF),
            pltpu.VMEM((2, tokens, width), BF),
            pltpu.SemaphoreType.DMA((nz + np_a + n_down + 2 * n_ff * groups,)),
            pltpu.SemaphoreType.DMA((2, 3)),
        ],
        12 * tokens * model * hidden_cols,
        50 * 2**20,
    )(ids, x, dy, feed_scale, *mixed, *vo_pieces, *gate_pieces, *up_pieces, *down_pieces)
    output, middle_grad, middle_low, mixed_t, normed_two_t, feed_gain_part = feed_out[:6]
    mixed_grad = feed_out[6 : 6 + nz]
    hidden_t, gate_grad, up_grad = feed_out[6 + nz :]
    mixed_grad = [mixed_grad[0]] + [swap(mixed_grad[j], "seq", nz, j) for j in range(1, nz)]

    chips = 4 if plane else 0

    def scatter(values):
        return lax.psum_scatter(values, "fsdp", scatter_dimension=0, tiled=True)

    if plane:
        down_tu, down_tl, down_mu, down_ml = weight_grad(ids, hidden_t, dy, chips, parts=2, width=256)
        gate_t, gate_m = weight_grad(ids, normed_two_t, gate_grad, chips)
        up_t, up_m = weight_grad(ids, normed_two_t, up_grad, chips)
        out_t, out_m = weight_grad(ids, mixed_t, middle_low, chips)
        down_shard = jnp.concatenate(
            [sum_line(reduce_plane(down_tu, down_mu, True)), sum_line(reduce_plane(down_tl, down_ml, False))]
        )
        gate_shard = sum_line(reduce_plane(gate_t, gate_m, True))
        up_shard = sum_line(reduce_plane(up_t, up_m, False))
        out_shard = sum_line(reduce_plane(out_t, out_m, True))
    else:
        down_shard = sum_line(scatter(weight_grad(ids, hidden_t, dy, chips, width=256)[0]))
        gate_shard = sum_line(scatter(weight_grad(ids, normed_two_t, gate_grad, chips)[0]))
        up_shard = sum_line(scatter(weight_grad(ids, normed_two_t, up_grad, chips)[0]))
        out_shard = sum_line(scatter(weight_grad(ids, mixed_t, middle_low, chips)[0]))

    grads = call(
        functools.partial(attend_back_kernel, (nz, min(256, seq_len), min(1024, seq_len))),
        [shape_of((tokens, block_cols), BF)] * nz,
        [SMEM] + [ANY] * (2 * nz) + [VMEM] * 2,
        [VMEM] * nz,
        [pltpu.VMEM((seq_len, block_cols), BF), pltpu.VMEM((seq_len, mixed_cols), BF)]
        + head_scratch
        + [
            pltpu.VMEM((heads, seq_len, head_dim), BF),
            pltpu.VMEM((heads, 8, seq_len), F32),
            pltpu.VMEM((heads, seq_len, head_dim), F32),
            pltpu.VMEM((kv_heads, seq_len, head_dim), BF),
            pltpu.VMEM((kv_heads, seq_len, head_dim), BF),
            pltpu.SemaphoreType.DMA((2 * nz,)),
        ],
        10 * attend_flops,
        20 * 2**20,
    )(ids, *blocks, *mixed_grad, full, logs)
    grads = [grads[0]] + [swap(grads[j], "seq", nz, j) for j in range(1, nz)]

    input_grad, q_grad, kv_grad, attention_gain_part, head_gain_part = call(
        functools.partial(post_kernel, dims),
        [
            rows_model(BF),
            shape_of((tokens, q_cols), BF),
            shape_of((tokens, k_cols + v_cols), BF),
            shape_of((1, model), F32),
            shape_of((1, q_cols + k_cols), F32),
        ],
        [SMEM] + [VMEM] * 7 + [ANY] * (nz + 2 * np_a),
        [VMEM] * 5,
        qkv_scratch + [pltpu.SemaphoreType.DMA((2 * np_a + 3 * nz,))],
        proj_flops,
        14 * 2**20,
    )(ids, x, middle_grad, attention_scale, head_scale, cosine, sine, proj, *grads, *qk_pieces, *vo_pieces)
    if plane:
        q_t, q_m = weight_grad(ids, normed_t, q_grad, chips)
        kv_t, kv_m = weight_grad(ids, normed_t, kv_grad, chips)
        q_shard = sum_line(reduce_plane(q_t, q_m, True))
        kv_shard = sum_line(reduce_plane(kv_t, kv_m, False))
    else:
        q_shard = sum_line(scatter(weight_grad(ids, normed_t, q_grad, chips)[0]))
        kv_shard = sum_line(scatter(weight_grad(ids, normed_t, kv_grad, chips)[0]))

    q_part = head_gain_part[:, :q_cols].reshape(-1, head_dim).sum(axis=0)
    k_part = head_gain_part[:, q_cols:].reshape(-1, head_dim).sum(axis=0)
    gain_parts = jnp.concatenate(
        [v.reshape(fsdp, -1) for v in (attention_gain_part, q_part, k_part, feed_gain_part)], axis=1
    )
    if plane:
        ordered = flip_to_order(gain_parts, me).reshape(4, 2, 1, -1)
        gain_shard = sum_line(reduce_plane(ordered[:, 1], ordered[:, 0], True)).reshape(-1)
    else:
        gain_shard = sum_line(scatter(gain_parts).reshape(-1))
    wide = lambda v: v.astype(F32)
    return (
        output.reshape(inputs.shape),
        input_grad.reshape(inputs.shape),
        wide(q_shard),
        wide(kv_shard[:, :k_cols]),
        wide(kv_shard[:, k_cols:]),
        wide(out_shard),
        gain_shard[: cuts[0]],
        gain_shard[cuts[0] : cuts[1]],
        gain_shard[cuts[1] : cuts[2]],
        gain_shard[cuts[2] :],
        wide(gate_shard),
        wide(up_shard),
        wide(down_shard),
    )


def solution(mesh):
    tokens, rows, row = P("fsdp", "seq", None), P("fsdp", None), P("fsdp")
    in_specs = (tokens, P("fsdp", "seq"), tokens) + (rows,) * 4 + (row,) * 4 + (rows,) * 3
    out_specs = (tokens, tokens) + (rows,) * 4 + (row,) * 4 + (rows,) * 3
    return jax.shard_map(per_device, mesh=mesh, in_specs=in_specs, out_specs=out_specs, check_vma=False)
```

time: 1410 us -> 770 us (0.55)
  matrix products: 309 us -> 0 us
  waiting for transfers between devices: 616 us -> 395 us
  Pallas kernels: 0 us -> 180 us
  other arithmetic: 187 us -> 26.7 us
  blocking collectives: 131 us -> 0 us
  starting transfers between devices: 22.3 us -> 144 us
  local copies, waits for them, and re-layouts: 115 us -> 17.3 us
  between operations: 17.2 us -> 2.26 us
    reduce_scatter x7 -> x0, waiting for transfers between devices: 417 us -> none  [the longest x1 128 us: per_device(): lax.psum_scatter(gate_weight_grad, 'fsdp', scatter_dimension=0, tiled=True)]
    ppermute x0 -> x102, waiting for transfers between devices: none -> 395 us  [the longest x78 256 us: swap(): return lax.ppermute(values, axis, [(i, i ^ bit) for i in range(size)])]
    dot_general x49 -> x0, matrix products: 309 us -> none  [the longest x7 48.5 us: matmul_left_t(): lax.dot_general(left_side, right_side, (((0,), (0,)), ((), ())), preferre...]
    pallas_call x0 -> x11, Pallas kernels: none -> 180 us  [the longest x1 47.9 us: per_device(): call(functools.partial(feed_kernel, (nz, np_a, n_ff, n_down, (v_cols, mod...]
    ppermute x0 -> x102, starting transfers between devices: none -> 144 us  [the longest x78 84.3 us: swap(): return lax.ppermute(values, axis, [(i, i ^ bit) for i in range(size)])]
    psum x1 -> x0, waiting for transfers between devices: 103 us -> none  [per_device(): lax.psum(query_shard.astype(jnp.bfloat16), 'seq').astype(jnp.float32)]
    unnamed x10 -> x3, other arithmetic: 70 us -> 0.01 us
    all_to_all x3 -> x0, blocking collectives: 62.2 us -> none  [the longest x1 29.3 us: per_device(): lax.all_to_all(query_back.reshape(seq_local, seq_len, -1), 'seq', split_a...]
  transfers between devices with their start and end apart: 20 -> 102, of which waited for: 11 -> 48; matrix products, arithmetic and copies ran while one was open for 22% -> 4% of each run, Pallas kernels for 0% -> 10%
where the time goes in v1:
time: 770 us; the launch traced here: 766 us
  waiting for transfers between devices  395 us (51%)
  Pallas kernels  180 us (23%)
  starting transfers between devices  144 us (19%)
  other arithmetic  26.7 us (3%)
  local copies, waits for them, and re-layouts  17.3 us (2%)
    ppermute x78, waiting for transfers between devices, swap(): return lax.ppermute(values, axis, [(i, i ^ bit) for i in range(size)])  256 us
    ppermute x78, starting transfers between devices, swap(): return lax.ppermute(values, axis, [(i, i ^ bit) for i in range(size)])  84.3 us
    ppermute x8, waiting for transfers between devices, sum_line(): outer = lax.ppermute(total, 'seq', [(1, 0), (2, 3)])  72.4 us
    ppermute x8, waiting for transfers between devices, sum_line(): inner = add(values, lax.ppermute(values, 'seq', [(0, 1), (3, 2)]))  67.2 us
    pallas_call x1, Pallas kernels, per_device(): call(functools.partial(feed_kernel, (nz, np_a, n_ff, n_down, (v_cols, mod...  47.9 us
    ppermute x8, starting transfers between devices, sum_line(): inner = add(values, lax.ppermute(values, 'seq', [(0, 1), (3, 2)]))  43.6 us
    pallas_call x6, Pallas kernels, weight_grad(): call(functools.partial(weight_grad_kernel, (chips, parts)), outs, [SMEM,...  43.3 us
    pallas_call x1, Pallas kernels, per_device(): call(functools.partial(attend_back_kernel, (nz, min(256, seq_len), min(10...  40.7 us
  transfers between devices with their start and end apart: 102, of which 48 were waited for; matrix products, arithmetic and copies ran while one was open for 4% of the time, Pallas kernels for 10%

profile of v1, /device:TPU:0, one launch (start us, length us, event | category | flops | bytes accessed | tf_op | source)
XLA Modules:
  0.0 765.7 jit_solution(9750996588758628365)
XLA Ops:
  2.6 3.0 collective-permute-start.10
  9.7 5.9 collective-permute-done.10.refs_12_.refs_8_.refs_16_
  19.7 5.4 collective-permute-done.3.refs_4_.refs_8_
  25.1 2.1 collective-permute-done.1.refs_2_.refs_6_
  29.2 8.6 %collective-permute-done.44.refs_40_ = bf16[288,1024]{1,0:T(8,128)(2,1)} collective-permute-done((bf16[288,1024]{1,0:T(8,128)(2,1)S(1)}, bf16[288,1024]{1,0:T(8,128)(2,1)}, u32[]{:S(2)}, u32[]{:S(2)}) %collective-permute-start.44) | collective-permute-done | bytes 589856 | tf_op jit(solution)/shard_map/ppermute | solution.py:483
  41.4 8.2 %collective-permute-done.37.refs_32_ = bf16[288,1024]{1,0:T(8,128)(2,1)} collective-permute-done((bf16[288,1024]{1,0:T(8,128)(2,1)S(1)}, bf16[288,1024]{1,0:T(8,128)(2,1)}, u32[]{:S(2)}, u32[]{:S(2)}) %collective-permute-start.37) | collective-permute-done | bytes 589856 | tf_op jit(solution)/shard_map/ppermute | solution.py:483
  54.2 6.8 collective-permute-done.12.refs_14_.refs_10_.refs_18_
  66.2 7.5 collective-permute-done.46.refs_42_
  83.8 6.3 collective-permute-done.39.refs_34_
  92.2 6.8 collective-permute-done.21.refs_14_
  100.1 11.4 %shard_map.237 = (bf16[1024,512]{1,0:T(8,128)(2,1)}, f32[512,1536]{1,0:T(8,128)}, bf16[512,512]{1,0:T(8,128)(2,1)}, bf16[512,512]{1,0:T(8,128)(2,1)}, bf16[512,5...) custom-call(s32[2]{0:T(128)} %pad_add_fusion.ids, bf16[512,1024]{1,0:T(8,128)(2,1)} %bitcast.115, f32[1,1024]{1,0:T(1,128)} %bitcast.124, ...), custom_call_target="tpu_custom_call" | custom-call | flops 2147483648 | bytes 12582912 | tf_op jit(solution)/shard_map/pallas_call | solution.py:605
  111.5 2.1 collective-permute-start.14
  115.5 2.6 collective-permute-start.15
  118.0 4.7 collective-permute-done.28.refs_22_
  122.7 3.6 collective-permute-start.16
  126.9 13.9 %collective-permute-done.30.refs_24_ = bf16[128,4608]{1,0:T(8,128)(2,1)} collective-permute-done((bf16[128,4608]{1,0:T(8,128)(2,1)}, bf16[128,4608]{1,0:T(8,128)(2,1)}, u32[]{:S(2)}, u32[]{:S(2)}) %collective-permute-start.30) | collective-permute-done | bytes 1179680 | tf_op jit(solution)/shard_map/ppermute | solution.py:483
  141.5 12.4 %collective-permute-done.15.refs_2_ = bf16[512,512]{1,0:T(8,128)(2,1)S(1)} collective-permute-done((bf16[512,512]{1,0:T(8,128)(2,1)}, bf16[512,512]{1,0:T(8,128)(2,1)S(1)}, u32[]{:S(2)}, u32[]{:S(2)}) %collective-permute-start.15) | collective-permute-done | bytes 524320 | tf_op jit(solution)/shard_map/ppermute | solution.py:483
  156.2 22.9 %shard_map.238 = (bf16[512,256]{1,0:T(8,128)(2,1)}, bf16[512,256]{1,0:T(8,128)(2,1)}, bf16[512,256]{1,0:T(8,128)(2,1)}, bf16[512,256]{1,0:T(8,128)(2,1)}, f32[4,2048,64]{2,1,0:T(8,128)}, /*index=5*/f32[4,8,2048]{2,1,0:T(8,128)}) custom-call(s32[2]{0:T(128)} %pad_add_fusion.ids, bf16[512,512]{1,0:T(8,128)(2,1)} %get-tuple-element.73.refs_0_, ...), custom_call_target="tpu_custom_call" | custom-call | flops 8589934592 | bytes 8388608 | tf_op jit(solution)/shard_map/pallas_call | solution.py:624
  179.1 9.6 %collective-permute-start.17 = (bf16[512,256]{1,0:T(8,128)(2,1)}, bf16[512,256]{1,0:T(8,128)(2,1)S(1)}, u32[]{:S(2)}, u32[]{:S(2)}) collective-permute-start(bf16[512,256]{1,0:T(8,128)(2,1)} %get-tuple-element.78), channel_id=1, source_target_pairs={{0,8},{8,0},{16,24},{24,16},{1,9},{9,1},{17,25},{25,17},{2,10},{10... | collective-permute-start | bytes 786440 | tf_op jit(solution)/shard_map/ppermute | solution.py:483
  190.6 9.0 %collective-permute-done.17.refs_1_ = bf16[512,256]{1,0:T(8,128)(2,1)S(1)} collective-permute-done((bf16[512,256]{1,0:T(8,128)(2,1)}, bf16[512,256]{1,0:T(8,128)(2,1)S(1)}, u32[]{:S(2)}, u32[]{:S(2)}) %collective-permute-start.17) | collective-permute-done | bytes 262176 | tf_op jit(solution)/shard_map/ppermute | solution.py:483
  201.0 7.6 collective-permute-done.19.refs_3_
  211.6 3.4 collective-permute-done.29.refs_23_
  217.6 47.9 %shard_map.239 = (bf16[512,1024]{1,0:T(8,128)(2,1)}, f32[512,1024]{1,0:T(8,128)}, bf16[512,1024]{1,0:T(8,128)(2,1)}, bf16[1024,512]{1,0:T(8,128)(2,1)}, bf16[102...) custom-call(s32[2]{0:T(128)} %pad_add_fusion.ids, ...), custom_call_target="tpu_custom_call" | custom-call | flops 28991029248 | bytes 52428800 | tf_op jit(solution)/shard_map/pallas_call | solution.py:640
  265.5 5.8 collective-permute-start.48
  274.3 9.1 %collective-permute-done.48.refs_5_ = bf16[512,256]{1,0:T(8,128)(2,1)S(1)} collective-permute-done((bf16[512,256]{1,0:T(8,128)(2,1)}, bf16[512,256]{1,0:T(8,128)(2,1)S(1)}, u32[]{:S(2)}, u32[]{:S(2)}) %collective-permute-start.48) | collective-permute-done | bytes 262176 | tf_op jit(solution)/shard_map/ppermute | solution.py:483
  283.4 9.4 %collective-permute-done.49.refs_6_ = bf16[512,256]{1,0:T(8,128)(2,1)S(1)} collective-permute-done((bf16[512,256]{1,0:T(8,128)(2,1)}, bf16[512,256]{1,0:T(8,128)(2,1)S(1)}, u32[]{:S(2)}, u32[]{:S(2)}) %collective-permute-start.49) | collective-permute-done | bytes 262176 | tf_op jit(solution)/shard_map/ppermute | solution.py:483
  293.6 40.7 %shard_map.240 = (bf16[512,512]{1,0:T(8,128)(2,1)}, bf16[512,512]{1,0:T(8,128)(2,1)}, bf16[512,512]{1,0:T(8,128)(2,1)}, bf16[512,512]{1,0:T(8,128)(2,1)}) custom-call(s32[2]{0:T(128)} %pad_add_fusion.ids, bf16[512,512]{1,0:T(8,128)(2,1)} %get-tuple-element.73.refs_0_, bf16[512,512]{1,0:T(8,128)(2,1)} %copy-done.43, bf16[512,512]{1,0:T(8,128)(2,1)} %copy-done.44, ...), custom_call_target="tpu_custom_call" | custom-call | flops 21474836480 | bytes 20971520 | tf_op jit(solution)/shard_map/pallas_call | solution.py:700
  334.3 5.1 collective-permute-start.51
  342.4 18.6 %collective-permute-done.51.refs_1_ = bf16[512,512]{1,0:T(8,128)(2,1)S(1)} collective-permute-done((bf16[512,512]{1,0:T(8,128)(2,1)}, bf16[512,512]{1,0:T(8,128)(2,1)S(1)}, u32[]{:S(2)}, u32[]{:S(2)}) %collective-permute-start.51) | collective-permute-done | bytes 524320 | tf_op jit(solution)/shard_map/ppermute | solution.py:483
  361.0 16.8 %collective-permute-done.52.refs_2_ = bf16[512,512]{1,0:T(8,128)(2,1)S(1)} collective-permute-done((bf16[512,512]{1,0:T(8,128)(2,1)}, bf16[512,512]{1,0:T(8,128)(2,1)S(1)}, u32[]{:S(2)}, u32[]{:S(2)}) %collective-permute-start.52) | collective-permute-done | bytes 524320 | tf_op jit(solution)/shard_map/ppermute | solution.py:483
  378.8 13.7 %shard_map.241 = (bf16[512,1024]{1,0:T(8,128)(2,1)}, bf16[512,1024]{1,0:T(8,128)(2,1)}, bf16[512,1024]{1,0:T(8,128)(2,1)}, f32[1,1024]{1,0:T(1,128)}, f32[1,1536]{1,0:T(1,128)}) custom-call(s32[2]{0:T(128)} %pad_add_fusion.ids, bf16[512,1024]{1,0:T(8,128)(2,1)} %bitcast.117, f32[512,1024]{1,0:T(8,128)} %get-tuple-element.82.middle_grad_ref, ...), custom_call_target="tpu_custom_call" | custom-call | flops 2147483648 | bytes 14680064 | tf_op jit(solution)/shard_map/pallas_call | solution.py:720
  395.3 3.9 shard_map.244
  400.3 9.8 %shard_map.247 = (bf16[4,288,1024]{2,1,0:T(8,128)(2,1)}, bf16[4,288,1024]{2,1,0:T(8,128)(2,1)}, bf16[4,288,1024]{2,1,0:T(8,128)(2,1)}, bf16[4,288,1024]{2,1,0:T(8,128)(2,1)}) custom-call(s32[2]{0:T(128)} %pad_add_fusion.ids, bf16[4608,512]{1,0:T(8,128)(2,1)} %get-tuple-element.116.left_ref, bf16[512,1024]{1,0:T(8,128)(2,1)} %bitcast.133), custom_call_target="tpu_custom_call" | custom-call | flops 4831838208 | bytes 15204352 | tf_op jit(solution)/shard_map/pallas_call | solution.py:419
  410.7 11.0 %shard_map.246 = (bf16[4,128,4608]{2,1,0:T(8,128)(2,1)}, bf16[4,128,4608]{2,1,0:T(8,128)(2,1)}) custom-call(s32[2]{0:T(128)} %pad_add_fusion.ids, bf16[1024,512]{1,0:T(8,128)(2,1)} %get-tuple-element.109.left_ref, bf16[512,4608]{1,0:T(8,128)(2,1)} %get-tuple-element.113.right_ref), custom_call_target="tpu_custom_call" | custom-call | flops 4831838208 | bytes 15204352 | tf_op jit(solution)/shard_map/pallas_call | solution.py:419
  421.7 11.3 %collective-permute-start.75 = (f32[1,272]{1,0:T(1,128)S(1)}, f32[1,272]{1,0:T(1,128)S(1)}, u32[]{:S(2)}, u32[]{:S(2)}) collective-permute-start(f32[1,272]{1,0:T(1,128)S(1)} %fusion.28), channel_id=1, source_target_pairs={{0,8},{24,16},{1,9},{25,17},{2,10},{26,18},{3,11},{27,19},{4,12},{... | collective-permute-start | bytes 3272 | tf_op jit(solution)/shard_map/ppermute | solution.py:518
  433.0 11.0 %shard_map.245 = (bf16[4,128,4608]{2,1,0:T(8,128)(2,1)}, bf16[4,128,4608]{2,1,0:T(8,128)(2,1)}) custom-call(s32[2]{0:T(128)} %pad_add_fusion.ids, bf16[1024,512]{1,0:T(8,128)(2,1)} %get-tuple-element.109.left_ref, bf16[512,4608]{1,0:T(8,128)(2,1)} %get-tuple-element.110.right_ref), custom_call_target="tpu_custom_call" | custom-call | flops 4831838208 | bytes 15204352 | tf_op jit(solution)/shard_map/pallas_call | solution.py:419
  444.7 3.8 shard_map.243
  454.0 3.8 shard_map.242
  458.7 8.5 %collective-permute-done.67 = bf16[2,128,1024]{2,1,0:T(8,128)(2,1)} collective-permute-done((bf16[2,128,1024]{2,1,0:T(8,128)(2,1)}, bf16[2,128,1024]{2,1,0:T(8,128)(2,1)}, u32[]{:S(2)}, u32[]{:S(2)}) %collective-permute-start.67) | collective-permute-done | bytes 524320 | tf_op jit(solution)/shard_map/ppermute | solution.py:483
  470.8 6.8 collective-permute-done.68
  478.9 4.7 collective-permute-start.69
  488.6 7.4 collective-permute-done.55
  497.7 2.1 collective-permute-start.56
  505.1 2.1 collective-permute-start.97
  507.5 3.6 collective-permute-start.63
  512.2 2.7 collective-permute-done.63
  515.0 4.4 collective-permute-start.57
  519.4 7.9 %collective-permute-done.91 = bf16[2,288,1024]{2,1,0:T(8,128)(2,1)S(1)} collective-permute-done((bf16[2,288,1024]{2,1,0:T(8,128)(2,1)S(1)}, bf16[2,288,1024]{2,1,0:T(8,128)(2,1)S(1)}, u32[]{:S(2)}, u32[]{:S(2)}) %collective-permute-start.91) | collective-permute-done | bytes 1179680 | tf_op jit(solution)/shard_map/ppermute | solution.py:483
  528.3 2.9 collective-permute-done.97
  533.2 2.1 collective-permute-start.98
  536.2 5.9 collective-permute-done.92
  543.8 9.8 %collective-permute-start.93 = (bf16[288,1024]{1,0:T(8,128)(2,1)S(1)}, bf16[288,1024]{1,0:T(8,128)(2,1)S(1)}, u32[]{:S(2)}, u32[]{:S(2)}) collective-permute-start(bf16[288,1024]{1,0:T(8,128)(2,1)S(1)} %fusion.7), channel_id=1, source_target_pairs={{0,8},{24,16},{1,9},{25,17},{2,10},{26,18},{3,11},{27,19},{4,12},{... | collective-permute-start | bytes 1769480 | tf_op jit(solution)/shard_map/ppermute | solution.py:518
  556.8 10.5 %collective-permute-done.93 = bf16[288,1024]{1,0:T(8,128)(2,1)S(1)} collective-permute-done((bf16[288,1024]{1,0:T(8,128)(2,1)S(1)}, bf16[288,1024]{1,0:T(8,128)(2,1)S(1)}, u32[]{:S(2)}, u32[]{:S(2)}) %collective-permute-start.93) | collective-permute-done | bytes 589856 | tf_op jit(solution)/shard_map/ppermute | solution.py:518
  568.2 8.0 %collective-permute-done.99 = bf16[288,1024]{1,0:T(8,128)(2,1)S(1)} collective-permute-done((bf16[288,1024]{1,0:T(8,128)(2,1)S(1)}, bf16[288,1024]{1,0:T(8,128)(2,1)S(1)}, u32[]{:S(2)}, u32[]{:S(2)}) %collective-permute-start.99) | collective-permute-done | bytes 589856 | tf_op jit(solution)/shard_map/ppermute | solution.py:518
  586.4 16.1 %collective-permute-done.95 = bf16[288,1024]{1,0:T(8,128)(2,1)S(1)} collective-permute-done((bf16[288,1024]{1,0:T(8,128)(2,1)S(1)}, bf16[288,1024]{1,0:T(8,128)(2,1)S(1)}, u32[]{:S(2)}, u32[]{:S(2)}) %collective-permute-start.95) | collective-permute-done | bytes 589856 | tf_op jit(solution)/shard_map/ppermute | solution.py:520
  602.6 8.3 %collective-permute-done.101 = bf16[288,1024]{1,0:T(8,128)(2,1)S(1)} collective-permute-done((bf16[288,1024]{1,0:T(8,128)(2,1)S(1)}, bf16[288,1024]{1,0:T(8,128)(2,1)S(1)}, u32[]{:S(2)}, u32[]{:S(2)}) %collective-permute-start.101) | collective-permute-done | bytes 589856 | tf_op jit(solution)/shard_map/ppermute | solution.py:520
  612.7 15.1 %collective-permute-done.79 = bf16[2,128,4608]{2,1,0:T(8,128)(2,1)S(1)} collective-permute-done((bf16[2,128,4608]{2,1,0:T(8,128)(2,1)S(1)}, bf16[2,128,4608]{2,1,0:T(8,128)(2,1)S(1)}, u32[]{:S(2)}, u32[]{:S(2)}) %collective-permute-start.79) | collective-permute-done | bytes 2359328 | tf_op jit(solution)/shard_map/ppermute | solution.py:483
  629.4 4.0 collective-permute-done.85
  634.0 21.2 %collective-permute-done.80 = bf16[128,4608]{1,0:T(8,128)(2,1)S(1)} collective-permute-done((bf16[128,4608]{1,0:T(8,128)(2,1)S(1)}, bf16[128,4608]{1,0:T(8,128)(2,1)S(1)}, u32[]{:S(2)}, u32[]{:S(2)}) %collective-permute-start.80) | collective-permute-done | bytes 1179680 | tf_op jit(solution)/shard_map/ppermute | solution.py:483
  655.7 7.1 collective-permute-start.81
  664.8 24.4 %collective-permute-done.81 = bf16[128,4608]{1,0:T(8,128)(2,1)S(1)} collective-permute-done((bf16[128,4608]{1,0:T(8,128)(2,1)S(1)}, bf16[128,4608]{1,0:T(8,128)(2,1)S(1)}, u32[]{:S(2)}, u32[]{:S(2)}) %collective-permute-start.81) | collective-permute-done | bytes 1179680 | tf_op jit(solution)/shard_map/ppermute | solution.py:518
  690.2 20.2 %collective-permute-done.87 = bf16[128,4608]{1,0:T(8,128)(2,1)S(1)} collective-permute-done((bf16[128,4608]{1,0:T(8,128)(2,1)S(1)}, bf16[128,4608]{1,0:T(8,128)(2,1)S(1)}, u32[]{:S(2)}, u32[]{:S(2)}) %collective-permute-start.87) | collective-permute-done | bytes 1179680 | tf_op jit(solution)/shard_map/ppermute | solution.py:518
  714.5 26.5 %collective-permute-done.83 = bf16[128,4608]{1,0:T(8,128)(2,1)S(1)} collective-permute-done((bf16[128,4608]{1,0:T(8,128)(2,1)S(1)}, bf16[128,4608]{1,0:T(8,128)(2,1)S(1)}, u32[]{:S(2)}, u32[]{:S(2)}) %collective-permute-start.83) | collective-permute-done | bytes 1179680 | tf_op jit(solution)/shard_map/ppermute | solution.py:520
  742.6 21.4 %collective-permute-done.89 = bf16[128,4608]{1,0:T(8,128)(2,1)S(1)} collective-permute-done((bf16[128,4608]{1,0:T(8,128)(2,1)S(1)}, bf16[128,4608]{1,0:T(8,128)(2,1)S(1)}, u32[]{:S(2)}, u32[]{:S(2)}) %collective-permute-start.89) | collective-permute-done | bytes 1179680 | tf_op jit(solution)/shard_map/ppermute | solution.py:520
  (379 shorter events, 124.7 us)
Async XLA Ops:
  9.0 16.1 %collective-permute-start.3 = (bf16[144,1536]{1,0:T(8,128)(2,1)S(1)}, bf16[144,1536]{1,0:T(8,128)(2,1)S(1)}, u32[]{:S(2)}, u32[]{:S(2)}) collective-permute-start(bf16[144,1536]{1,0:T(8,128)(2,1)S(1)} %fusion.16.refs_0_.refs_4_), channel_id=1, source_target_pairs={{0,4},{1,5},{2,6},{3,7},{4,0},{5,1},{6,2},{7,3},{8,12},{9,13},{10,... | collective-permute-start | bytes 1327112 | tf_op jit(solution)/shard_map/ppermute | solution.py:483
  9.6 17.6 %collective-permute-start.1 = (bf16[144,1536]{1,0:T(8,128)(2,1)S(1)}, bf16[144,1536]{1,0:T(8,128)(2,1)S(1)}, u32[]{:S(2)}, u32[]{:S(2)}) collective-permute-start(bf16[144,1536]{1,0:T(8,128)(2,1)S(1)} %fusion.16.refs_0_.refs_4_), channel_id=1, source_target_pairs={{0,2},{1,3},{2,0},{3,1},{4,6},{5,7},{6,4},{7,5},{8,10},{9,11},{10,... | collective-permute-start | bytes 1327112 | tf_op jit(solution)/shard_map/ppermute | solution.py:483
  17.7 20.1 %collective-permute-start.44 = (bf16[288,1024]{1,0:T(8,128)(2,1)S(1)}, bf16[288,1024]{1,0:T(8,128)(2,1)}, u32[]{:S(2)}, u32[]{:S(2)}) collective-permute-start(bf16[288,1024]{1,0:T(8,128)(2,1)S(1)} %get-tuple-element.135.refs_36_), channel_id=1, source_target_pairs={{0,4},{1,5},{2,6},{3,7},{4,0},{5,1},{6,2},{7,3},{8,12},{9,13},{10,... | collective-permute-start | bytes 1769480 | tf_op jit(solution)/shard_map/ppermute | solution.py:483
  17.9 21.9 %collective-permute-start.42 = (bf16[288,1024]{1,0:T(8,128)(2,1)S(1)}, bf16[288,1024]{1,0:T(8,128)(2,1)S(1)}, u32[]{:S(2)}, u32[]{:S(2)}) collective-permute-start(bf16[288,1024]{1,0:T(8,128)(2,1)S(1)} %get-tuple-element.135.refs_36_), channel_id=1, source_target_pairs={{0,2},{1,3},{2,0},{3,1},{4,6},{5,7},{6,4},{7,5},{8,10},{9,11},{10,... | collective-permute-start | bytes 1769480 | tf_op jit(solution)/shard_map/ppermute | solution.py:483
  25.1 16.2 %collective-permute-start.41 = (bf16[288,1024]{1,0:T(8,128)(2,1)S(1)}, bf16[288,1024]{1,0:T(8,128)(2,1)S(1)}, u32[]{:S(2)}, u32[]{:S(2)}) collective-permute-start(bf16[288,1024]{1,0:T(8,128)(2,1)S(1)} %get-tuple-element.135.refs_36_), channel_id=1, source_target_pairs={{0,1},{1,0},{2,3},{3,2},{4,5},{5,4},{6,7},{7,6},{8,9},{9,8},{10,11... | collective-permute-start | bytes 1769480 | tf_op jit(solution)/shard_map/ppermute | solution.py:483
  27.2 22.5 %collective-permute-start.37 = (bf16[288,1024]{1,0:T(8,128)(2,1)S(1)}, bf16[288,1024]{1,0:T(8,128)(2,1)}, u32[]{:S(2)}, u32[]{:S(2)}) collective-permute-start(bf16[288,1024]{1,0:T(8,128)(2,1)S(1)} %get-tuple-element.136.refs_28_), channel_id=1, source_target_pairs={{0,4},{1,5},{2,6},{3,7},{4,0},{5,1},{6,2},{7,3},{8,12},{9,13},{10,... | collective-permute-start | bytes 1769480 | tf_op jit(solution)/shard_map/ppermute | solution.py:483
  27.3 25.3 %collective-permute-start.35 = (bf16[288,1024]{1,0:T(8,128)(2,1)S(1)}, bf16[288,1024]{1,0:T(8,128)(2,1)}, u32[]{:S(2)}, u32[]{:S(2)}) collective-permute-start(bf16[288,1024]{1,0:T(8,128)(2,1)S(1)} %get-tuple-element.136.refs_28_), channel_id=1, source_target_pairs={{0,2},{1,3},{2,0},{3,1},{4,6},{5,7},{6,4},{7,5},{8,10},{9,11},{10,... | collective-permute-start | bytes 1769480 | tf_op jit(solution)/shard_map/ppermute | solution.py:483
  37.8 14.7 %collective-permute-start.34 = (bf16[288,1024]{1,0:T(8,128)(2,1)S(1)}, bf16[288,1024]{1,0:T(8,128)(2,1)S(1)}, u32[]{:S(2)}, u32[]{:S(2)}) collective-permute-start(bf16[288,1024]{1,0:T(8,128)(2,1)S(1)} %get-tuple-element.136.refs_28_), channel_id=1, source_target_pairs={{0,1},{1,0},{2,3},{3,2},{4,5},{5,4},{6,7},{7,6},{8,9},{9,8},{10,11... | collective-permute-start | bytes 1769480 | tf_op jit(solution)/shard_map/ppermute | solution.py:483
  39.8 21.1 %collective-permute-start.12 = (bf16[128,1536]{1,0:T(8,128)(2,1)S(1)}, bf16[128,1536]{1,0:T(8,128)(2,1)S(1)}, u32[]{:S(2)}, u32[]{:S(2)}) collective-permute-start(bf16[128,1536]{1,0:T(8,128)(2,1)S(1)} %collective-permute-done.10.refs_12_.refs_8_.refs_16_), channel_id=1, source_target_pairs={{0,2},{1,3},{2,0},{3,1},{4,6},{5,7},{6,4},{7,5},{8,10},{9,11},{10,... | collective-permute-start | bytes 1179656 | tf_op jit(solution)/shard_map/ppermute | solution.py:483
  41.3 19.6 %collective-permute-start.11 = (bf16[128,1536]{1,0:T(8,128)(2,1)S(1)}, bf16[128,1536]{1,0:T(8,128)(2,1)S(1)}, u32[]{:S(2)}, u32[]{:S(2)}) collective-permute-start(bf16[128,1536]{1,0:T(8,128)(2,1)S(1)} %collective-permute-done.10.refs_12_.refs_8_.refs_16_), channel_id=1, source_target_pairs={{0,1},{1,0},{2,3},{3,2},{4,5},{5,4},{6,7},{7,6},{8,9},{9,8},{10,11... | collective-permute-start | bytes 1179656 | tf_op jit(solution)/shard_map/ppermute | solution.py:483
  52.6 21.1 %collective-permute-start.46 = (bf16[288,1024]{1,0:T(8,128)(2,1)}, bf16[288,1024]{1,0:T(8,128)(2,1)}, u32[]{:S(2)}, u32[]{:S(2)}) collective-permute-start(bf16[288,1024]{1,0:T(8,128)(2,1)} %collective-permute-done.44.refs_40_), channel_id=1, source_target_pairs={{0,2},{1,3},{2,0},{3,1},{4,6},{5,7},{6,4},{7,5},{8,10},{9,11},{10,... | collective-permute-start | bytes 1769480 | tf_op jit(solution)/shard_map/ppermute | solution.py:483
  62.7 18.5 %collective-permute-start.45 = (bf16[288,1024]{1,0:T(8,128)(2,1)}, bf16[288,1024]{1,0:T(8,128)(2,1)}, u32[]{:S(2)}, u32[]{:S(2)}) collective-permute-start(bf16[288,1024]{1,0:T(8,128)(2,1)} %collective-permute-done.44.refs_40_), channel_id=1, source_target_pairs={{0,1},{1,0},{2,3},{3,2},{4,5},{5,4},{6,7},{7,6},{8,9},{9,8},{10,11... | collective-permute-start | bytes 1769480 | tf_op jit(solution)/shard_map/ppermute | solution.py:483
  63.9 35.0 %collective-permute-start.21 = (bf16[128,4608]{1,0:T(8,128)(2,1)}, bf16[128,4608]{1,0:T(8,128)(2,1)}, u32[]{:S(2)}, u32[]{:S(2)}) collective-permute-start(bf16[128,4608]{1,0:T(8,128)(2,1)} %refs_12_.1), channel_id=1, source_target_pairs={{0,2},{1,3},{2,0},{3,1},{4,6},{5,7},{6,4},{7,5},{8,10},{9,11},{10,... | collective-permute-start | bytes 3538952 | tf_op jit(solution)/shard_map/ppermute | solution.py:483
  66.1 15.6 %collective-permute-start.43 = (bf16[288,1024]{1,0:T(8,128)(2,1)}, bf16[288,1024]{1,0:T(8,128)(2,1)}, u32[]{:S(2)}, u32[]{:S(2)}) collective-permute-start(bf16[288,1024]{1,0:T(8,128)(2,1)} %copy-done.38), channel_id=1, source_target_pairs={{0,1},{1,0},{2,3},{3,2},{4,5},{5,4},{6,7},{7,6},{8,9},{9,8},{10,11... | collective-permute-start | bytes 1769480 | tf_op jit(solution)/shard_map/ppermute | solution.py:483
  73.7 16.5 %collective-permute-start.39 = (bf16[288,1024]{1,0:T(8,128)(2,1)}, bf16[288,1024]{1,0:T(8,128)(2,1)}, u32[]{:S(2)}, u32[]{:S(2)}) collective-permute-start(bf16[288,1024]{1,0:T(8,128)(2,1)} %collective-permute-done.35.refs_30_), channel_id=1, source_target_pairs={{0,4},{1,5},{2,6},{3,7},{4,0},{5,1},{6,2},{7,3},{8,12},{9,13},{10,... | collective-permute-start | bytes 1769480 | tf_op jit(solution)/shard_map/ppermute | solution.py:483
  81.7 29.8 %collective-permute-start.20 = (bf16[128,4608]{1,0:T(8,128)(2,1)}, bf16[128,4608]{1,0:T(8,128)(2,1)}, u32[]{:S(2)}, u32[]{:S(2)}) collective-permute-start(bf16[128,4608]{1,0:T(8,128)(2,1)} %refs_12_.1), channel_id=1, source_target_pairs={{0,1},{1,0},{2,3},{3,2},{4,5},{5,4},{6,7},{7,6},{8,9},{9,8},{10,11... | collective-permute-start | bytes 3538952 | tf_op jit(solution)/shard_map/ppermute | solution.py:483
  81.9 33.6 %collective-permute-start.23 = (bf16[128,4608]{1,0:T(8,128)(2,1)}, bf16[128,4608]{1,0:T(8,128)(2,1)}, u32[]{:S(2)}, u32[]{:S(2)}) collective-permute-start(bf16[128,4608]{1,0:T(8,128)(2,1)} %refs_12_.1), channel_id=1, source_target_pairs={{0,4},{1,5},{2,6},{3,7},{4,0},{5,1},{6,2},{7,3},{8,12},{9,13},{10,... | collective-permute-start | bytes 3538952 | tf_op jit(solution)/shard_map/ppermute | solution.py:483
  90.2 32.6 %collective-permute-start.28 = (bf16[128,4608]{1,0:T(8,128)(2,1)}, bf16[128,4608]{1,0:T(8,128)(2,1)}, u32[]{:S(2)}, u32[]{:S(2)}) collective-permute-start(bf16[128,4608]{1,0:T(8,128)(2,1)} %refs_20_.1), channel_id=1, source_target_pairs={{0,2},{1,3},{2,0},{3,1},{4,6},{5,7},{6,4},{7,5},{8,10},{9,11},{10,... | collective-permute-start | bytes 3538952 | tf_op jit(solution)/shard_map/ppermute | solution.py:483
  92.1 34.3 %collective-permute-start.27 = (bf16[128,4608]{1,0:T(8,128)(2,1)}, bf16[128,4608]{1,0:T(8,128)(2,1)S(1)}, u32[]{:S(2)}, u32[]{:S(2)}) collective-permute-start(bf16[128,4608]{1,0:T(8,128)(2,1)} %refs_20_.1), channel_id=1, source_target_pairs={{0,1},{1,0},{2,3},{3,2},{4,5},{5,4},{6,7},{7,6},{8,9},{9,8},{10,11... | collective-permute-start | bytes 3538952 | tf_op jit(solution)/shard_map/ppermute | solution.py:483
  98.9 41.8 %collective-permute-start.30 = (bf16[128,4608]{1,0:T(8,128)(2,1)}, bf16[128,4608]{1,0:T(8,128)(2,1)}, u32[]{:S(2)}, u32[]{:S(2)}) collective-permute-start(bf16[128,4608]{1,0:T(8,128)(2,1)} %refs_20_.1), channel_id=1, source_target_pairs={{0,4},{1,5},{2,6},{3,7},{4,0},{5,1},{6,2},{7,3},{8,12},{9,13},{10,... | collective-permute-start | bytes 3538952 | tf_op jit(solution)/shard_map/ppermute | solution.py:483
  111.5 29.2 %collective-permute-start.14 = (bf16[512,512]{1,0:T(8,128)(2,1)}, bf16[512,512]{1,0:T(8,128)(2,1)S(1)}, u32[]{:S(2)}, u32[]{:S(2)}) collective-permute-start(bf16[512,512]{1,0:T(8,128)(2,1)} %get-tuple-element.74), channel_id=1, source_target_pairs={{0,8},{8,0},{16,24},{24,16},{1,9},{9,1},{17,25},{25,17},{2,10},{10... | collective-permute-start | bytes 1572872 | tf_op jit(solution)/shard_map/ppermute | solution.py:483
  115.5 38.4 %collective-permute-start.15 = (bf16[512,512]{1,0:T(8,128)(2,1)}, bf16[512,512]{1,0:T(8,128)(2,1)S(1)}, u32[]{:S(2)}, u32[]{:S(2)}) collective-permute-start(bf16[512,512]{1,0:T(8,128)(2,1)} %get-tuple-element.75), channel_id=1, source_target_pairs={{0,16},{8,24},{16,0},{24,8},{1,17},{9,25},{17,1},{25,9},{2,18},{10... | collective-permute-start | bytes 1572872 | tf_op jit(solution)/shard_map/ppermute | solution.py:483
  122.7 31.9 %collective-permute-start.16 = (bf16[512,512]{1,0:T(8,128)(2,1)}, bf16[512,512]{1,0:T(8,128)(2,1)}, u32[]{:S(2)}, u32[]{:S(2)}) collective-permute-start(bf16[512,512]{1,0:T(8,128)(2,1)} %get-tuple-element.76), channel_id=1, source_target_pairs={{0,24},{8,16},{16,8},{24,0},{1,25},{9,17},{17,9},{25,1},{2,26},{10... | collective-permute-start | bytes 1572872 | tf_op jit(solution)/shard_map/ppermute | solution.py:483
  126.4 82.2 %collective-permute-start.25 = (bf16[128,4608]{1,0:T(8,128)(2,1)}, bf16[128,4608]{1,0:T(8,128)(2,1)S(1)}, u32[]{:S(2)}, u32[]{:S(2)}) collective-permute-start(bf16[128,4608]{1,0:T(8,128)(2,1)} %collective-permute-done.21.refs_14_), channel_id=1, source_target_pairs={{0,4},{1,5},{2,6},{3,7},{4,0},{5,1},{6,2},{7,3},{8,12},{9,13},{10,... | collective-permute-start | bytes 3538952 | tf_op jit(solution)/shard_map/ppermute | solution.py:483
  140.7 68.4 %collective-permute-start.22 = (bf16[128,4608]{1,0:T(8,128)(2,1)}, bf16[128,4608]{1,0:T(8,128)(2,1)S(1)}, u32[]{:S(2)}, u32[]{:S(2)}) collective-permute-start(bf16[128,4608]{1,0:T(8,128)(2,1)} %collective-permute-done.21.refs_14_), channel_id=1, source_target_pairs={{0,1},{1,0},{2,3},{3,2},{4,5},{5,4},{6,7},{7,6},{8,9},{9,8},{10,11... | collective-permute-start | bytes 3538952 | tf_op jit(solution)/shard_map/ppermute | solution.py:483
  140.7 38.3 %collective-permute-start.47 = (bf16[288,1024]{1,0:T(8,128)(2,1)}, bf16[288,1024]{1,0:T(8,128)(2,1)S(1)}, u32[]{:S(2)}, u32[]{:S(2)}) collective-permute-start(bf16[288,1024]{1,0:T(8,128)(2,1)} %collective-permute-done.46.refs_42_), channel_id=1, source_target_pairs={{0,1},{1,0},{2,3},{3,2},{4,5},{5,4},{6,7},{7,6},{8,9},{9,8},{10,11... | collective-permute-start | bytes 1769480 | tf_op jit(solution)/shard_map/ppermute | solution.py:483
  153.9 34.7 %collective-permute-start.40 = (bf16[288,1024]{1,0:T(8,128)(2,1)}, bf16[288,1024]{1,0:T(8,128)(2,1)S(1)}, u32[]{:S(2)}, u32[]{:S(2)}) collective-permute-start(bf16[288,1024]{1,0:T(8,128)(2,1)} %collective-permute-done.39.refs_34_), channel_id=1, source_target_pairs={{0,1},{1,0},{2,3},{3,2},{4,5},{5,4},{6,7},{7,6},{8,9},{9,8},{10,11... | collective-permute-start | bytes 1769480 | tf_op jit(solution)/shard_map/ppermute | solution.py:483
  154.7 54.5 %collective-permute-start.32 = (bf16[128,4608]{1,0:T(8,128)(2,1)}, bf16[128,4608]{1,0:T(8,128)(2,1)S(1)}, u32[]{:S(2)}, u32[]{:S(2)}) collective-permute-start(bf16[128,4608]{1,0:T(8,128)(2,1)} %collective-permute-done.30.refs_24_), channel_id=1, source_target_pairs={{0,2},{1,3},{2,0},{3,1},{4,6},{5,7},{6,4},{7,5},{8,10},{9,11},{10,... | collective-permute-start | bytes 3538952 | tf_op jit(solution)/shard_map/ppermute | solution.py:483
  179.1 20.6 %collective-permute-start.17 = (bf16[512,256]{1,0:T(8,128)(2,1)}, bf16[512,256]{1,0:T(8,128)(2,1)S(1)}, u32[]{:S(2)}, u32[]{:S(2)}) collective-permute-start(bf16[512,256]{1,0:T(8,128)(2,1)} %get-tuple-element.78), channel_id=1, source_target_pairs={{0,8},{8,0},{16,24},{24,16},{1,9},{9,1},{17,25},{25,17},{2,10},{10... | collective-permute-start | bytes 786440 | tf_op jit(solution)/shard_map/ppermute | solution.py:483
  200.9 14.1 %collective-permute-start.31 = (bf16[128,4608]{1,0:T(8,128)(2,1)}, bf16[128,4608]{1,0:T(8,128)(2,1)S(1)}, u32[]{:S(2)}, u32[]{:S(2)}) collective-permute-start(bf16[128,4608]{1,0:T(8,128)(2,1)} %collective-permute-done.30.refs_24_), channel_id=1, source_target_pairs={{0,1},{1,0},{2,3},{3,2},{4,5},{5,4},{6,7},{7,6},{8,9},{9,8},{10,11... | collective-permute-start | bytes 3538952 | tf_op jit(solution)/shard_map/ppermute | solution.py:483
  265.5 17.9 %collective-permute-start.48 = (bf16[512,256]{1,0:T(8,128)(2,1)}, bf16[512,256]{1,0:T(8,128)(2,1)S(1)}, u32[]{:S(2)}, u32[]{:S(2)}) collective-permute-start(bf16[512,256]{1,0:T(8,128)(2,1)} %get-tuple-element.85), channel_id=1, source_target_pairs={{0,8},{8,0},{16,24},{24,16},{1,9},{9,1},{17,25},{25,17},{2,10},{10... | collective-permute-start | bytes 786440 | tf_op jit(solution)/shard_map/ppermute | solution.py:483
  271.3 21.5 %collective-permute-start.49 = (bf16[512,256]{1,0:T(8,128)(2,1)}, bf16[512,256]{1,0:T(8,128)(2,1)S(1)}, u32[]{:S(2)}, u32[]{:S(2)}) collective-permute-start(bf16[512,256]{1,0:T(8,128)(2,1)} %get-tuple-element.86), channel_id=1, source_target_pairs={{0,16},{8,24},{16,0},{24,8},{1,17},{9,25},{17,1},{25,9},{2,18},{10... | collective-permute-start | bytes 786440 | tf_op jit(solution)/shard_map/ppermute | solution.py:483
  273.4 19.5 %collective-permute-start.50 = (bf16[512,256]{1,0:T(8,128)(2,1)}, bf16[512,256]{1,0:T(8,128)(2,1)S(1)}, u32[]{:S(2)}, u32[]{:S(2)}) collective-permute-start(bf16[512,256]{1,0:T(8,128)(2,1)} %get-tuple-element.87), channel_id=1, source_target_pairs={{0,24},{8,16},{16,8},{24,0},{1,25},{9,17},{17,9},{25,1},{2,26},{10... | collective-permute-start | bytes 786440 | tf_op jit(solution)/shard_map/ppermute | solution.py:483
  334.3 26.7 %collective-permute-start.51 = (bf16[512,512]{1,0:T(8,128)(2,1)}, bf16[512,512]{1,0:T(8,128)(2,1)S(1)}, u32[]{:S(2)}, u32[]{:S(2)}) collective-permute-start(bf16[512,512]{1,0:T(8,128)(2,1)} %get-tuple-element.91), channel_id=1, source_target_pairs={{0,8},{8,0},{16,24},{24,16},{1,9},{9,1},{17,25},{25,17},{2,10},{10... | collective-permute-start | bytes 1572872 | tf_op jit(solution)/shard_map/ppermute | solution.py:483
  339.4 38.4 %collective-permute-start.52 = (bf16[512,512]{1,0:T(8,128)(2,1)}, bf16[512,512]{1,0:T(8,128)(2,1)S(1)}, u32[]{:S(2)}, u32[]{:S(2)}) collective-permute-start(bf16[512,512]{1,0:T(8,128)(2,1)} %get-tuple-element.92), channel_id=1, source_target_pairs={{0,16},{8,24},{16,0},{24,8},{1,17},{9,25},{17,1},{25,9},{2,18},{10... | collective-permute-start | bytes 1572872 | tf_op jit(solution)/shard_map/ppermute | solution.py:483
  341.0 36.8 %collective-permute-start.53 = (bf16[512,512]{1,0:T(8,128)(2,1)}, bf16[512,512]{1,0:T(8,128)(2,1)S(1)}, u32[]{:S(2)}, u32[]{:S(2)}) collective-permute-start(bf16[512,512]{1,0:T(8,128)(2,1)} %get-tuple-element.93), channel_id=1, source_target_pairs={{0,24},{8,16},{16,8},{24,0},{1,25},{9,17},{17,9},{25,1},{2,26},{10... | collective-permute-start | bytes 1572872 | tf_op jit(solution)/shard_map/ppermute | solution.py:483
  399.2 51.1 %collective-permute-start.66 = (bf16[4,128,1024]{2,1,0:T(8,128)(2,1)}, bf16[4,128,1024]{2,1,0:T(8,128)(2,1)}, u32[]{:S(2)}, u32[]{:S(2)}) collective-permute-start(bf16[4,128,1024]{2,1,0:T(8,128)(2,1)} %get-tuple-element.105), channel_id=1, source_target_pairs={{0,1},{1,0},{2,3},{3,2},{4,5},{5,4},{6,7},{7,6},{8,9},{9,8},{10,11... | collective-permute-start | bytes 3145736 | tf_op jit(solution)/shard_map/ppermute | solution.py:483
  410.1 89.8 %collective-permute-start.90 = (bf16[4,288,1024]{2,1,0:T(8,128)(2,1)}, bf16[4,288,1024]{2,1,0:T(8,128)(2,1)S(1)}, u32[]{:S(2)}, u32[]{:S(2)}) collective-permute-start(bf16[4,288,1024]{2,1,0:T(8,128)(2,1)} %get-tuple-element.118), channel_id=1, source_target_pairs={{0,1},{1,0},{2,3},{3,2},{4,5},{5,4},{6,7},{7,6},{8,9},{9,8},{10,11... | collective-permute-start | bytes 7077896 | tf_op jit(solution)/shard_map/ppermute | solution.py:483
  410.1 91.7 %collective-permute-start.96 = (bf16[4,288,1024]{2,1,0:T(8,128)(2,1)}, bf16[4,288,1024]{2,1,0:T(8,128)(2,1)S(1)}, u32[]{:S(2)}, u32[]{:S(2)}) collective-permute-start(bf16[4,288,1024]{2,1,0:T(8,128)(2,1)} %get-tuple-element.120), channel_id=1, source_target_pairs={{0,1},{1,0},{2,3},{3,2},{4,5},{5,4},{6,7},{7,6},{8,9},{9,8},{10,11... | collective-permute-start | bytes 7077896 | tf_op jit(solution)/shard_map/ppermute | solution.py:483
  421.7 22.3 %collective-permute-start.75 = (f32[1,272]{1,0:T(1,128)S(1)}, f32[1,272]{1,0:T(1,128)S(1)}, u32[]{:S(2)}, u32[]{:S(2)}) collective-permute-start(f32[1,272]{1,0:T(1,128)S(1)} %fusion.28), channel_id=1, source_target_pairs={{0,8},{24,16},{1,9},{25,17},{2,10},{26,18},{3,11},{27,19},{4,12},{... | collective-permute-start | bytes 3272 | tf_op jit(solution)/shard_map/ppermute | solution.py:518
  448.5 21.9 %collective-permute-start.60 = (bf16[4,128,1024]{2,1,0:T(8,128)(2,1)}, bf16[4,128,1024]{2,1,0:T(8,128)(2,1)S(1)}, u32[]{:S(2)}, u32[]{:S(2)}) collective-permute-start(bf16[4,128,1024]{2,1,0:T(8,128)(2,1)} %get-tuple-element.101), channel_id=1, source_target_pairs={{0,1},{1,0},{2,3},{3,2},{4,5},{5,4},{6,7},{7,6},{8,9},{9,8},{10,11... | collective-permute-start | bytes 3145736 | tf_op jit(solution)/shard_map/ppermute | solution.py:483
  452.5 14.6 %collective-permute-start.67 = (bf16[2,128,1024]{2,1,0:T(8,128)(2,1)}, bf16[2,128,1024]{2,1,0:T(8,128)(2,1)}, u32[]{:S(2)}, u32[]{:S(2)}) collective-permute-start(bf16[2,128,1024]{2,1,0:T(8,128)(2,1)} %pad_maximum_fusion.6), channel_id=1, source_target_pairs={{0,2},{1,3},{2,0},{3,1},{4,6},{5,7},{6,4},{7,5},{8,10},{9,11},{10,... | collective-permute-start | bytes 1572872 | tf_op jit(solution)/shard_map/ppermute | solution.py:483
  457.8 25.8 %collective-permute-start.54 = (bf16[4,128,1024]{2,1,0:T(8,128)(2,1)}, bf16[4,128,1024]{2,1,0:T(8,128)(2,1)S(1)}, u32[]{:S(2)}, u32[]{:S(2)}) collective-permute-start(bf16[4,128,1024]{2,1,0:T(8,128)(2,1)} %get-tuple-element.98), channel_id=1, source_target_pairs={{0,1},{1,0},{2,3},{3,2},{4,5},{5,4},{6,7},{7,6},{8,9},{9,8},{10,11... | collective-permute-start | bytes 3145736 | tf_op jit(solution)/shard_map/ppermute | solution.py:483
  470.7 17.1 %collective-permute-start.61 = (bf16[2,128,1024]{2,1,0:T(8,128)(2,1)S(1)}, bf16[2,128,1024]{2,1,0:T(8,128)(2,1)S(1)}, u32[]{:S(2)}, u32[]{:S(2)}) collective-permute-start(bf16[2,128,1024]{2,1,0:T(8,128)(2,1)S(1)} %pad_maximum_fusion.5), channel_id=1, source_target_pairs={{0,4},{1,5},{2,6},{3,7},{4,0},{5,1},{6,2},{7,3},{8,12},{9,13},{10,... | collective-permute-start | bytes 1572872 | tf_op jit(solution)/shard_map/ppermute | solution.py:483
  487.5 89.8 %collective-permute-start.78 = (bf16[4,128,4608]{2,1,0:T(8,128)(2,1)}, bf16[4,128,4608]{2,1,0:T(8,128)(2,1)S(1)}, u32[]{:S(2)}, u32[]{:S(2)}) collective-permute-start(bf16[4,128,4608]{2,1,0:T(8,128)(2,1)} %get-tuple-element.112), channel_id=1, source_target_pairs={{0,1},{1,0},{2,3},{3,2},{4,5},{5,4},{6,7},{7,6},{8,9},{9,8},{10,11... | collective-permute-start | bytes 14155784 | tf_op jit(solution)/shard_map/ppermute | solution.py:483
  501.8 25.5 %collective-permute-start.91 = (bf16[2,288,1024]{2,1,0:T(8,128)(2,1)S(1)}, bf16[2,288,1024]{2,1,0:T(8,128)(2,1)S(1)}, u32[]{:S(2)}, u32[]{:S(2)}) collective-permute-start(bf16[2,288,1024]{2,1,0:T(8,128)(2,1)S(1)} %pad_maximum_fusion.2), channel_id=1, source_target_pairs={{0,2},{1,3},{2,0},{3,1},{4,6},{5,7},{6,4},{7,5},{8,10},{9,11},{10,... | collective-permute-start | bytes 3538952 | tf_op jit(solution)/shard_map/ppermute | solution.py:483
  505.1 26.0 %collective-permute-start.97 = (bf16[2,288,1024]{2,1,0:T(8,128)(2,1)S(1)}, bf16[2,288,1024]{2,1,0:T(8,128)(2,1)S(1)}, u32[]{:S(2)}, u32[]{:S(2)}) collective-permute-start(bf16[2,288,1024]{2,1,0:T(8,128)(2,1)S(1)} %pad_maximum_fusion.3), channel_id=1, source_target_pairs={{0,4},{1,5},{2,6},{3,7},{4,0},{5,1},{6,2},{7,3},{8,12},{9,13},{10,... | collective-permute-start | bytes 3538952 | tf_op jit(solution)/shard_map/ppermute | solution.py:483
  511.3 68.4 %collective-permute-start.84 = (bf16[4,128,4608]{2,1,0:T(8,128)(2,1)S(1)}, bf16[4,128,4608]{2,1,0:T(8,128)(2,1)S(1)}, u32[]{:S(2)}, u32[]{:S(2)}) collective-permute-start(bf16[4,128,4608]{2,1,0:T(8,128)(2,1)S(1)} %bitcast.131), channel_id=1, source_target_pairs={{0,1},{1,0},{2,3},{3,2},{4,5},{5,4},{6,7},{7,6},{8,9},{9,8},{10,11... | collective-permute-start | bytes 14155784 | tf_op jit(solution)/shard_map/ppermute | solution.py:483
  515.0 18.3 %collective-permute-start.57 = (bf16[128,1024]{1,0:T(8,128)(2,1)S(1)}, bf16[128,1024]{1,0:T(8,128)(2,1)S(1)}, u32[]{:S(2)}, u32[]{:S(2)}) collective-permute-start(bf16[128,1024]{1,0:T(8,128)(2,1)S(1)} %fusion.15), channel_id=1, source_target_pairs={{0,8},{24,16},{1,9},{25,17},{2,10},{26,18},{3,11},{27,19},{4,12},{... | collective-permute-start | bytes 786440 | tf_op jit(solution)/shard_map/ppermute | solution.py:518
  535.4 18.6 %collective-permute-start.58 = (bf16[128,1024]{1,0:T(8,128)(2,1)S(1)}, bf16[128,1024]{1,0:T(8,128)(2,1)S(1)}, u32[]{:S(2)}, u32[]{:S(2)}) collective-permute-start(bf16[128,1024]{1,0:T(8,128)(2,1)S(1)} %add_convert_fusion.51), channel_id=1, source_target_pairs={{8,16},{16,8},{9,17},{17,9},{10,18},{18,10},{11,19},{19,11},{12,20... | collective-permute-start | bytes 786440 | tf_op jit(solution)/shard_map/ppermute | solution.py:519
  543.8 23.5 %collective-permute-start.93 = (bf16[288,1024]{1,0:T(8,128)(2,1)S(1)}, bf16[288,1024]{1,0:T(8,128)(2,1)S(1)}, u32[]{:S(2)}, u32[]{:S(2)}) collective-permute-start(bf16[288,1024]{1,0:T(8,128)(2,1)S(1)} %fusion.7), channel_id=1, source_target_pairs={{0,8},{24,16},{1,9},{25,17},{2,10},{26,18},{3,11},{27,19},{4,12},{... | collective-permute-start | bytes 1769480 | tf_op jit(solution)/shard_map/ppermute | solution.py:518
  554.0 22.2 %collective-permute-start.99 = (bf16[288,1024]{1,0:T(8,128)(2,1)S(1)}, bf16[288,1024]{1,0:T(8,128)(2,1)S(1)}, u32[]{:S(2)}, u32[]{:S(2)}) collective-permute-start(bf16[288,1024]{1,0:T(8,128)(2,1)S(1)} %fusion.6), channel_id=1, source_target_pairs={{0,8},{24,16},{1,9},{25,17},{2,10},{26,18},{3,11},{27,19},{4,12},{... | collective-permute-start | bytes 1769480 | tf_op jit(solution)/shard_map/ppermute | solution.py:518
  555.4 30.2 %collective-permute-start.59 = (bf16[128,1024]{1,0:T(8,128)(2,1)S(1)}, bf16[128,1024]{1,0:T(8,128)(2,1)S(1)}, u32[]{:S(2)}, u32[]{:S(2)}) collective-permute-start(bf16[128,1024]{1,0:T(8,128)(2,1)S(1)} %add_convert_fusion.50), channel_id=1, source_target_pairs={{8,0},{16,24},{9,1},{17,25},{10,2},{18,26},{11,3},{19,27},{12,4},{... | collective-permute-start | bytes 786440 | tf_op jit(solution)/shard_map/ppermute | solution.py:520
  578.1 49.6 %collective-permute-start.79 = (bf16[2,128,4608]{2,1,0:T(8,128)(2,1)S(1)}, bf16[2,128,4608]{2,1,0:T(8,128)(2,1)S(1)}, u32[]{:S(2)}, u32[]{:S(2)}) collective-permute-start(bf16[2,128,4608]{2,1,0:T(8,128)(2,1)S(1)} %pad_maximum_fusion), channel_id=1, source_target_pairs={{0,2},{1,3},{2,0},{3,1},{4,6},{5,7},{6,4},{7,5},{8,10},{9,11},{10,... | collective-permute-start | bytes 7077896 | tf_op jit(solution)/shard_map/ppermute | solution.py:483
  580.5 52.8 %collective-permute-start.85 = (bf16[2,128,4608]{2,1,0:T(8,128)(2,1)S(1)}, bf16[2,128,4608]{2,1,0:T(8,128)(2,1)S(1)}, u32[]{:S(2)}, u32[]{:S(2)}) collective-permute-start(bf16[2,128,4608]{2,1,0:T(8,128)(2,1)S(1)} %pad_maximum_fusion.1), channel_id=1, source_target_pairs={{0,4},{1,5},{2,6},{3,7},{4,0},{5,1},{6,2},{7,3},{8,12},{9,13},{10,... | collective-permute-start | bytes 7077896 | tf_op jit(solution)/shard_map/ppermute | solution.py:483
  581.7 20.8 %collective-permute-start.95 = (bf16[288,1024]{1,0:T(8,128)(2,1)S(1)}, bf16[288,1024]{1,0:T(8,128)(2,1)S(1)}, u32[]{:S(2)}, u32[]{:S(2)}) collective-permute-start(bf16[288,1024]{1,0:T(8,128)(2,1)S(1)} %add_convert_fusion.26), channel_id=1, source_target_pairs={{8,0},{16,24},{9,1},{17,25},{10,2},{18,26},{11,3},{19,27},{12,4},{... | collective-permute-start | bytes 1769480 | tf_op jit(solution)/shard_map/ppermute | solution.py:520
  583.3 27.7 %collective-permute-start.101 = (bf16[288,1024]{1,0:T(8,128)(2,1)S(1)}, bf16[288,1024]{1,0:T(8,128)(2,1)S(1)}, u32[]{:S(2)}, u32[]{:S(2)}) collective-permute-start(bf16[288,1024]{1,0:T(8,128)(2,1)S(1)} %add_convert_fusion.20), channel_id=1, source_target_pairs={{8,0},{16,24},{9,1},{17,25},{10,2},{18,26},{11,3},{19,27},{12,4},{... | collective-permute-start | bytes 1769480 | tf_op jit(solution)/shard_map/ppermute | solution.py:520
  628.2 27.0 %collective-permute-start.80 = (bf16[128,4608]{1,0:T(8,128)(2,1)S(1)}, bf16[128,4608]{1,0:T(8,128)(2,1)S(1)}, u32[]{:S(2)}, u32[]{:S(2)}) collective-permute-start(bf16[128,4608]{1,0:T(8,128)(2,1)S(1)} %fusion.3), channel_id=1, source_target_pairs={{0,4},{1,5},{2,6},{3,7},{4,0},{5,1},{6,2},{7,3},{8,12},{9,13},{10,... | collective-permute-start | bytes 3538952 | tf_op jit(solution)/shard_map/ppermute | solution.py:483
  633.8 29.0 %collective-permute-start.86 = (bf16[128,4608]{1,0:T(8,128)(2,1)S(1)}, bf16[128,4608]{1,0:T(8,128)(2,1)S(1)}, u32[]{:S(2)}, u32[]{:S(2)}) collective-permute-start(bf16[128,4608]{1,0:T(8,128)(2,1)S(1)} %fusion.5), channel_id=1, source_target_pairs={{0,2},{1,3},{2,0},{3,1},{4,6},{5,7},{6,4},{7,5},{8,10},{9,11},{10,... | collective-permute-start | bytes 3538952 | tf_op jit(solution)/shard_map/ppermute | solution.py:483
  655.7 33.4 %collective-permute-start.81 = (bf16[128,4608]{1,0:T(8,128)(2,1)S(1)}, bf16[128,4608]{1,0:T(8,128)(2,1)S(1)}, u32[]{:S(2)}, u32[]{:S(2)}) collective-permute-start(bf16[128,4608]{1,0:T(8,128)(2,1)S(1)} %fusion.1), channel_id=1, source_target_pairs={{0,8},{24,16},{1,9},{25,17},{2,10},{26,18},{3,11},{27,19},{4,12},{... | collective-permute-start | bytes 3538952 | tf_op jit(solution)/shard_map/ppermute | solution.py:518
  663.4 46.9 %collective-permute-start.87 = (bf16[128,4608]{1,0:T(8,128)(2,1)S(1)}, bf16[128,4608]{1,0:T(8,128)(2,1)S(1)}, u32[]{:S(2)}, u32[]{:S(2)}) collective-permute-start(bf16[128,4608]{1,0:T(8,128)(2,1)S(1)} %fusion), channel_id=1, source_target_pairs={{0,8},{24,16},{1,9},{25,17},{2,10},{26,18},{3,11},{27,19},{4,12},{... | collective-permute-start | bytes 3538952 | tf_op jit(solution)/shard_map/ppermute | solution.py:518
  689.4 21.9 %collective-permute-start.82 = (bf16[128,4608]{1,0:T(8,128)(2,1)S(1)}, bf16[128,4608]{1,0:T(8,128)(2,1)S(1)}, u32[]{:S(2)}, u32[]{:S(2)}) collective-permute-start(bf16[128,4608]{1,0:T(8,128)(2,1)S(1)} %add_convert_fusion.11), channel_id=1, source_target_pairs={{8,16},{16,8},{9,17},{17,9},{10,18},{18,10},{11,19},{19,11},{12,20... | collective-permute-start | bytes 3538952 | tf_op jit(solution)/shard_map/ppermute | solution.py:519
  711.6 29.4 %collective-permute-start.83 = (bf16[128,4608]{1,0:T(8,128)(2,1)S(1)}, bf16[128,4608]{1,0:T(8,128)(2,1)S(1)}, u32[]{:S(2)}, u32[]{:S(2)}) collective-permute-start(bf16[128,4608]{1,0:T(8,128)(2,1)S(1)} %add_convert_fusion.10), channel_id=1, source_target_pairs={{8,0},{16,24},{9,1},{17,25},{10,2},{18,26},{11,3},{19,27},{12,4},{... | collective-permute-start | bytes 3538952 | tf_op jit(solution)/shard_map/ppermute | solution.py:520
  713.2 50.8 %collective-permute-start.89 = (bf16[128,4608]{1,0:T(8,128)(2,1)S(1)}, bf16[128,4608]{1,0:T(8,128)(2,1)S(1)}, u32[]{:S(2)}, u32[]{:S(2)}) collective-permute-start(bf16[128,4608]{1,0:T(8,128)(2,1)S(1)} %add_convert_fusion.4), channel_id=1, source_target_pairs={{8,0},{16,24},{9,1},{17,25},{10,2},{18,26},{11,3},{19,27},{12,4},{... | collective-permute-start | bytes 3538952 | tf_op jit(solution)/shard_map/ppermute | solution.py:520
  (94 other events, 1434.3 us)

commit v2 on v1

--- a/solution.py
+++ b/solution.py
@@ -34,14 +34,15 @@
     return jax.ShapeDtypeStruct(shape, dtype)
 
 
-def call(kernel, outs, in_specs, out_specs, scratch, flops, moved, **more):
+def call(kernel, outs, in_specs, out_specs, scratch, flops, moved, collective=None, **more):
+    params = {} if collective is None else {"collective_id": collective, "has_side_effects": True}
     return pl.pallas_call(
         kernel,
         out_shape=outs,
         in_specs=in_specs,
         out_specs=out_specs,
         scratch_shapes=scratch,
-        compiler_params=pltpu.CompilerParams(vmem_limit_bytes=VMEM_BYTES),
+        compiler_params=pltpu.CompilerParams(vmem_limit_bytes=VMEM_BYTES, **params),
         cost_estimate=pl.CostEstimate(flops=flops, bytes_accessed=moved, transcendentals=0),
         **more,
     )
@@ -51,26 +52,15 @@
     return lax.rsqrt(jnp.mean(values * values, axis=-1, keepdims=True) + EPSILON)
 
 
-def piece_offset(me, at, count, rows):
-    if count == 1:
-        return 0
-    return pl.multiple_of((me ^ at) * rows, rows)
-
-
-def start_pieces(me, pieces, whole, sems, first, rows=None, base=0, stride=None, cols=None, to_cols=None):
-    copies = []
-    for at, piece in enumerate(pieces):
-        count = piece.shape[0] if rows is None else rows
-        if len(pieces) == 1:
-            count, offset = whole.shape[0], 0
-        else:
-            offset = piece_offset(me, at, len(pieces), count if stride is None else stride) + base
-        source = piece.at[pl.ds(0, count)] if cols is None else piece.at[pl.ds(0, count), pl.ds(*cols)]
-        target = whole.at[pl.ds(offset, count)] if to_cols is None else whole.at[pl.ds(offset, count), pl.ds(*to_cols)]
-        copy = pltpu.make_async_copy(source, target, sems.at[first + at])
+class Fetch:
+    def __init__(self, sems):
+        self.sems, self.used = sems, 0
+
+    def start(self, source, target):
+        copy = pltpu.make_async_copy(source, target, self.sems.at[self.used])
         copy.start()
-        copies.append(copy)
-    return copies
+        self.used += 1
+        return copy
 
 
 def wait_all(copies):
@@ -97,36 +87,6 @@
     after = pltpu.roll(values, width - half, 1)
     before = pltpu.roll(values, half, 1)
     return jnp.where(lane % head_dim < half, after, before)
-
-
-def pre_kernel(dims, ids, x_ref, gain_ref, head_gain_ref, cos_ref, sin_ref, *refs):
-    nz, np_a, head_dim, q_cols, k_cols, v_cols = dims
-    a_pieces, b_pieces = refs[:np_a], refs[np_a : 2 * np_a]
-    refs = refs[2 * np_a :]
-    normed_t_ref, proj_ref = refs[:2]
-    blocks = refs[2 : 2 + nz]
-    w_qk, w_v, qkv, sems = refs[2 + nz :]
-    z, me = ids[0], ids[1]
-    rows = w_qk.shape[0] // np_a
-    copies = start_pieces(me, a_pieces, w_qk, sems, 0, rows=rows)
-    copies += start_pieces(me, b_pieces, w_v, sems, np_a, rows=rows, cols=(0, v_cols))
-    x = x_ref[...].astype(F32)
-    normed = (x * row_norm(x) * gain_ref[...]).astype(BF)
-    normed_t_ref[...] = normed.T
-    width = 256
-    mask = head_mask(width, head_dim)
-    cos = jnp.concatenate([cos_ref[...]] * (width // 128), axis=1)
-    sin = jnp.concatenate([sin_ref[...]] * (width // 128), axis=1)
-    wait_all(copies)
-    for start in range(0, q_cols + k_cols, width):
-        cols = slice(start, start + width)
-        proj = dot_nn(normed, w_qk[:, cols])
-        proj_ref[:, cols] = proj
-        scale = lax.rsqrt(head_sum(proj * proj, mask) * (1.0 / head_dim) + EPSILON)
-        values = proj * scale * head_gain_ref[:, cols]
-        qkv[:, cols] = (values * cos + partner(values, head_dim) * sin).astype(BF)
-    qkv[:, q_cols + k_cols :] = dot_nn(normed, w_v[...]).astype(BF)
-    pack_blocks(z, nz, qkv, blocks, (q_cols, k_cols, v_cols))
 
 
 def pack_blocks(z, nz, source, blocks, widths):
@@ -137,6 +97,245 @@
             part = width // nz
             block[:, at : at + part] = source[:, pl.ds(pl.multiple_of(base + owner * part, part), part)]
             base, at = base + width, at + part
+
+
+class Links:
+    def __init__(self, send_sems, recv_sems):
+        self.sems, self.used, self.started = (send_sems, recv_sems), 0, []
+
+    def copy(self, source, target, device):
+        copy = pltpu.make_async_remote_copy(
+            src_ref=source,
+            dst_ref=target,
+            send_sem=self.sems[0].at[self.used],
+            recv_sem=self.sems[1].at[self.used],
+            device_id=device,
+            device_id_type=pl.DeviceIdType.MESH,
+        )
+        self.used += 1
+        return copy
+
+    def start(self, source, target, device):
+        copy = self.copy(source, target, device)
+        copy.start()
+        self.started.append(copy)
+        return copy
+
+    def wait_sends(self):
+        for copy in self.started:
+            copy.wait_send()
+
+
+def enter(me, z, nz, plane):
+    barrier = pltpu.get_barrier_semaphore()
+    peers = [{"seq": z ^ j} for j in range(1, nz)]
+    if plane:
+        peers += [{"fsdp": me ^ bit} for bit in (1, 2, 4)]
+    for peer in peers:
+        pl.semaphore_signal(barrier, inc=1, device_id=peer, device_id_type=pl.DeviceIdType.MESH)
+    pl.semaphore_wait(barrier, len(peers))
+
+
+class Gather:
+    def __init__(self, links, me, own, whole, x_first):
+        self.links, self.me, self.own, self.whole = links, me, own, whole
+        self.rows = own.shape[0]
+        self.near, self.other = (2, 4) if x_first else (4, 2)
+
+    def block(self, b):
+        return self.whole.at[pl.ds(pl.multiple_of((self.me ^ b) * self.rows, self.rows), self.rows)]
+
+    def pass_on(self, b, bit):
+        source = self.own if b == 0 else self.block(b)
+        return self.links.start(source, self.block(b), {"fsdp": self.me ^ bit})
+
+    def begin(self):
+        self.first = self.pass_on(0, self.near)
+        self.second = self.pass_on(0, self.other)
+        self.to_core = [self.pass_on(0, 1)]
+
+    def forward_first(self):
+        self.first.wait_recv()
+        self.far = self.pass_on(self.near, self.other)
+        self.to_core.append(self.pass_on(self.near, 1))
+
+    def forward_second(self):
+        self.second.wait_recv()
+        self.to_core.append(self.pass_on(self.other, 1))
+
+    def forward_far(self):
+        self.far.wait_recv()
+        self.to_core.append(self.pass_on(self.near + self.other, 1))
+
+    def end(self):
+        for copy in self.to_core:
+            copy.wait_recv()
+
+
+def forward_first(gathers):
+    for gather in gathers:
+        gather.forward_first()
+    for gather in gathers:
+        gather.forward_second()
+
+
+def forward_far(gathers):
+    for gather in gathers:
+        gather.forward_far()
+
+
+def forward_kernel(dims, x_ref, cos_ref, sin_ref, *refs):
+    nz, plane, head_dim, q_cols, k_cols, v_cols, rows = dims
+    n_in = 6 if plane else 3
+    given, refs = refs[:n_in], refs[n_in:]
+    gains_ref, normed_t_ref, proj_ref, heads_ref, mixed_ref, full_ref, log_ref = refs[:7]
+    refs = refs[7:]
+    if plane:
+        qk_hbm, vo_hbm, gate_hbm, up_hbm, down_hbm = refs[:5]
+        refs = refs[5:]
+    w_qk, w_vo, normed, qkv, queries, keys, values, mix, local_sems, send_sems, recv_sems = refs
+    z, me = lax.axis_index("seq"), lax.axis_index("fsdp")
+    model = w_vo.shape[0]
+    tokens = x_ref.shape[0]
+    enter(me, z, nz, plane)
+    links = Links(send_sems, recv_sems)
+    local = []
+
+    def copy_here(source, target):
+        copy = pltpu.make_async_copy(source, target, local_sems.at[len(local)])
+        copy.start()
+        local.append(copy)
+        return copy
+
+    if plane:
+        own_qk, own_vo, own_gate, own_up, own_down, _ = given
+        half = own_down.shape[0] // 2
+        attention = [Gather(links, me, own_qk, w_qk, True), Gather(links, me, own_vo, w_vo, False)]
+        wide = [Gather(links, me, own_gate, gate_hbm, True), Gather(links, me, own_up, up_hbm, False)]
+        for gather in attention:
+            gather.begin()
+        here = [copy_here(g.own, g.block(0)) for g in attention]
+        down = []
+        for side in range(2):
+            g = Gather(links, me, own_down.at[pl.ds(side * half, half)], down_hbm.at[side], side == 0)
+            down.append(g)
+    else:
+        here = [copy_here(given[0], w_qk), copy_here(given[1], w_vo)]
+    x = x_ref[...].astype(F32)
+    unit = x * row_norm(x)
+    if plane:
+        forward_first(attention)
+        for gather in wide:
+            gather.begin()
+        for g in wide:
+            copy_here(g.own, g.block(0))
+        forward_far(attention)
+        for g in attention:
+            g.end()
+        wait_all(here)
+        stride = attention[0].rows
+        shard = w_vo.shape[0] // 8
+        gains = sum(w_qk[s * stride + shard : (s + 1) * stride].astype(F32) for s in range(8))
+        for s in range(8):
+            copy_here(w_qk.at[pl.ds(s * stride, shard)], qk_hbm.at[pl.ds(s * shard, shard)])
+        copy_here(w_vo, vo_hbm)
+    else:
+        stride = shard = model
+        wait_all(here)
+        gains = given[2][...].astype(F32)
+    gains_ref[...] = gains
+    normed[...] = (unit * gains[0:1, :model]).astype(BF)
+    width = 256
+    mask = head_mask(width, head_dim)
+    cos = jnp.concatenate([cos_ref[...]] * (width // 128), axis=1)
+    sin = jnp.concatenate([sin_ref[...]] * (width // 128), axis=1)
+
+    for start in range(0, q_cols + k_cols, width):
+        cols = slice(start, start + width)
+        if stride == shard:
+            proj = dot_nn(normed[...], w_qk[:, cols])
+        else:
+            weight = jnp.concatenate([w_qk[s * stride : s * stride + shard, cols] for s in range(8)], axis=0)
+            proj = dot_nn(normed[...], weight)
+        proj_ref[:, cols] = proj
+        scale = lax.rsqrt(head_sum(proj * proj, mask) * (1.0 / head_dim) + EPSILON)
+        head = proj * scale * gains_ref[1:2, cols]
+        qkv[:, cols] = (head * cos + partner(head, head_dim) * sin).astype(BF)
+    qkv[:, q_cols + k_cols :] = dot_nn(normed[...], w_vo[:, :v_cols]).astype(BF)
+
+    arrivals = []
+    for j in range(nz):
+        owner = z ^ j
+        base, at = 0, 0
+        for cols in (q_cols, k_cols, v_cols):
+            part = cols // nz
+            source = qkv.at[:, pl.ds(pl.multiple_of(base + owner * part, part), part)]
+            target = heads_ref.at[pl.ds(pl.multiple_of(z * tokens, tokens), tokens), pl.ds(at, part)]
+            if j == 0:
+                arrivals.append(copy_here(source, target))
+            else:
+                arrivals.append(links.start(source, target, {"seq": owner}))
+            base, at = base + cols, at + part
+    normed_t_ref[...] = normed[...].T
+    if plane:
+        forward_first(wide)
+        for gather in down:
+            gather.begin()
+        for g in down:
+            copy_here(g.own, g.block(0))
+    for i, copy in enumerate(arrivals):
+        if i < 3:
+            copy.wait()
+        else:
+            copy.wait_recv()
+
+    heads, seq_len, _ = queries.shape
+    kv_heads = keys.shape[0]
+    group = heads // kv_heads
+    split_heads(heads_ref, 0, queries)
+    split_heads(heads_ref, heads * head_dim, keys)
+    split_heads(heads_ref, (heads + kv_heads) * head_dim, values)
+    factor = head_dim**-0.5 * LOG2E
+    for r in range(seq_len // rows):
+        span = slice(r * rows, (r + 1) * rows)
+        reach = (r + 1) * rows
+
+        def one_head(h, _):
+            b = lax.div(h, group)
+            scores = dot_nt(queries[h, span], keys[b, :reach]) * factor
+            row = lax.broadcasted_iota(jnp.int32, scores.shape, 0) + r * rows
+            col = lax.broadcasted_iota(jnp.int32, scores.shape, 1)
+            probs = jnp.exp2(jnp.where(row >= col, scores, -1e30))
+            total = jnp.sum(probs, axis=1, keepdims=True)
+            full_ref[h, span] = dot_nn(probs.astype(BF), values[b, :reach]) * (1.0 / total)
+            log_ref[h, :, span] = jnp.broadcast_to(jnp.log2(total), (rows, 128)).T[0:8]
+            return 0
+
+        lax.fori_loop(0, heads, one_head, 0)
+    mix[...] = jnp.concatenate([full_ref[h].astype(BF) for h in range(heads)], axis=1)
+
+    back = []
+    part = mix.shape[1]
+    for j in range(nz):
+        owner = z ^ j
+        source = mix.at[pl.ds(pl.multiple_of(owner * tokens, tokens), tokens)]
+        target = mixed_ref.at[:, pl.ds(pl.multiple_of(z * part, part), part)]
+        if j == 0:
+            copy_here(source, target)
+        else:
+            back.append(links.start(source, target, {"seq": owner}))
+    if plane:
+        forward_far(wide)
+        forward_first(down)
+        forward_far(down)
+        for gather in wide + down:
+            gather.end()
+    for copy in back:
+        copy.wait_recv()
+    links.wait_sends()
+    for i, copy in enumerate(local):
+        if not any(copy is done for done in here + arrivals[:3]):
+            copy.wait()
 
 
 def load_heads(z, nz, blocks, scratch, sems, first):
@@ -157,52 +356,14 @@
         heads[h] = scratch[:, first + h * head_dim : first + (h + 1) * head_dim]
 
 
-def attend_kernel(dims, ids, *refs):
-    nz, rows = dims
-    blocks, outs = refs[:nz], refs[nz : 2 * nz]
-    full_ref, log_ref, scratch, queries, keys, values, sems = refs[2 * nz :]
-    z = ids[0]
-    wait_all(load_heads(z, nz, blocks, scratch, sems, 0))
-    heads, seq_len, head_dim = queries.shape
-    kv_heads = keys.shape[0]
-    group = heads // kv_heads
-    split_heads(scratch, 0, queries)
-    split_heads(scratch, heads * head_dim, keys)
-    split_heads(scratch, (heads + kv_heads) * head_dim, values)
-    scale = head_dim**-0.5 * LOG2E
-    for r in range(seq_len // rows):
-        span = slice(r * rows, (r + 1) * rows)
-        reach = (r + 1) * rows
-
-        def one_head(h, _):
-            b = lax.div(h, group)
-            scores = dot_nt(queries[h, span], keys[b, :reach]) * scale
-            row = lax.broadcasted_iota(jnp.int32, scores.shape, 0) + r * rows
-            col = lax.broadcasted_iota(jnp.int32, scores.shape, 1)
-            probs = jnp.exp2(jnp.where(row >= col, scores, -1e30))
-            total = jnp.sum(probs, axis=1, keepdims=True)
-            full_ref[h, span] = dot_nn(probs.astype(BF), values[b, :reach]) * (1.0 / total)
-            log_ref[h, :, span] = jnp.broadcast_to(jnp.log2(total), (rows, 128)).T[0:8]
-            return 0
-
-        lax.fori_loop(0, heads, one_head, 0)
-    tokens = outs[0].shape[0]
-    for j in range(nz):
-        first = pl.multiple_of((z ^ j) * tokens, tokens)
-        for h in range(heads):
-            outs[j][:, h * head_dim : (h + 1) * head_dim] = full_ref[h, pl.ds(first, tokens)].astype(BF)
-
-
 def attend_back_kernel(dims, ids, *refs):
     nz, rows, chunk = dims
-    blocks, grads = refs[:nz], refs[nz : 2 * nz]
-    full_ref, log_ref = refs[2 * nz : 2 * nz + 2]
-    outs = refs[2 * nz + 2 : 3 * nz + 2]
-    scratch, grad_scratch, queries, keys, values, grad, delta, q_grad, k_grad, v_grad, sems = refs[3 * nz + 2 :]
+    scratch, full_ref, log_ref = refs[:3]
+    grads, refs = refs[3 : 3 + nz], refs[3 + nz :]
+    outs, refs = refs[:nz], refs[nz:]
+    grad_scratch, queries, keys, values, grad, delta, q_grad, k_grad, v_grad, sems = refs
     z = ids[0]
-    copies = load_heads(z, nz, blocks, scratch, sems, 0)
-    copies += load_heads(z, nz, grads, grad_scratch, sems, nz)
-    wait_all(copies)
+    wait_all(load_heads(z, nz, grads, grad_scratch, sems, 0))
     heads, seq_len, head_dim = queries.shape
     kv_heads = keys.shape[0]
     group = heads // kv_heads
@@ -256,18 +417,6 @@
         outs[j][...] = jnp.concatenate(parts, axis=1)
 
 
-def load_columns(z, nz, blocks, whole, sems, first):
-    copies = []
-    width = blocks[0].shape[1]
-    for j in range(nz):
-        copy = pltpu.make_async_copy(
-            blocks[j], whole.at[:, pl.ds(pl.multiple_of((z ^ j) * width, width), width)], sems.at[first + j]
-        )
-        copy.start()
-        copies.append(copy)
-    return copies
-
-
 def norm_back(rows, gain, gradient):
     q = row_norm(rows)
     n = rows * q
@@ -275,47 +424,39 @@
     return q * (u - n * jnp.mean(u * n, axis=-1, keepdims=True)), jnp.sum(gradient * n, axis=0, keepdims=True)
 
 
-def feed_kernel(dims, ids, x_ref, dy_ref, gain_ref, *refs):
-    nz, n_out, n_ff, n_down, out_cols, width, groups = dims
-    mixed_blocks, refs = refs[:nz], refs[nz:]
-    out_pieces, refs = refs[:n_out], refs[n_out:]
-    gate_pieces, refs = refs[:n_ff], refs[n_ff:]
-    up_pieces, refs = refs[:n_ff], refs[n_ff:]
-    down_pieces, refs = refs[:n_down], refs[n_down:]
-    output_ref, middle_grad_ref, middle_low_ref, mixed_t_ref, normed_t_ref, gain_grad_ref = refs[:6]
-    grad_blocks, refs = refs[6 : 6 + nz], refs[6 + nz :]
+def feed_kernel(dims, ids, x_ref, dy_ref, gains_ref, mixed, *refs):
+    nz, out_cols, width, groups = dims
+    vo_hbm, gate_hbm, up_hbm, down_hbm = refs[:4]
+    output_ref, middle_grad_ref, middle_low_ref, mixed_t_ref, normed_t_ref, gain_grad_ref = refs[4:10]
+    grad_blocks, refs = refs[10 : 10 + nz], refs[10 + nz :]
     hidden_hbm, gate_grad_hbm, up_grad_hbm = refs[:3]
-    w_out, w_gate, w_up, w_down, mixed, middle, normed, back = refs[3:11]
+    w_out, w_gate, w_up, w_down, grad_low, middle, normed, back = refs[3:11]
     hidden_slot, gate_slot, up_slot, sems, slot_sems = refs[11:]
-    z, me = ids[0], ids[1]
-    at = 0
-    early = load_columns(z, nz, mixed_blocks, mixed, sems, at)
-    at += nz
-    early += start_pieces(me, out_pieces, w_out, sems, at, rows=w_out.shape[0] // n_out, cols=out_cols)
-    at += n_out
-    if n_down == 1:
-        down_copies = start_pieces(me, down_pieces, w_down, sems, at)
+    z = ids[0]
+    fetch = Fetch(sems)
+    model, hidden_cols = w_gate.shape
+    gain = gains_ref[2:3, :model]
+    early = [fetch.start(vo_hbm.at[:, pl.ds(*out_cols)], w_out)]
+    down_copies = []
+    if len(down_hbm.shape) == 2:
+        down_copies.append(fetch.start(down_hbm, w_down))
     else:
-        half = n_down // 2
-        rows = down_pieces[0].shape[0]
-        down_copies = start_pieces(me, down_pieces[:half], w_down, sems, at, stride=2 * rows)
-        down_copies += start_pieces(me, down_pieces[half:], w_down, sems, at + half, stride=2 * rows, base=rows)
-    at += n_down
-    hidden_cols = w_gate.shape[1]
+        half = hidden_cols // 16
+        for owner in range(8):
+            for side in range(2):
+                target = w_down.at[pl.ds((2 * owner + side) * half, half)]
+                down_copies.append(fetch.start(down_hbm.at[side, pl.ds(owner * half, half)], target))
     group_cols = hidden_cols // groups
     group_copies = []
     for g in range(groups):
-        cols = (g * group_cols, group_cols)
-        copies = start_pieces(me, gate_pieces, w_gate, sems, at, cols=cols, to_cols=cols)
-        copies += start_pieces(me, up_pieces, w_up, sems, at + n_ff, cols=cols, to_cols=cols)
-        at += 2 * n_ff
-        group_copies.append(copies)
+        cols = pl.ds(g * group_cols, group_cols)
+        group_copies.append([fetch.start(a.at[:, cols], b.at[:, cols]) for a, b in ((gate_hbm, w_gate), (up_hbm, w_up))])
     wait_all(early)
     x = x_ref[...].astype(F32)
     mixed_rows = mixed[...]
     mixed_t_ref[...] = mixed_rows.T
     middle_rows = x + dot_nn(mixed_rows, w_out[...])
-    normed_rows = (middle_rows * row_norm(middle_rows) * gain_ref[...]).astype(BF)
+    normed_rows = (middle_rows * row_norm(middle_rows) * gain).astype(BF)
     normed[...] = normed_rows
     normed_t_ref[...] = normed_rows.T
     middle[...] = middle_rows
@@ -362,14 +503,14 @@
         lax.fori_loop(g * per_group, (g + 1) * per_group, one_block, 0)
     output_ref[...] = middle[...].astype(BF)
     middle_rows = x_ref[...].astype(F32) + dot_nn(mixed[...], w_out[...])
-    part, gain_sum = norm_back(middle_rows, gain_ref[...], back[...])
+    part, gain_sum = norm_back(middle_rows, gain, back[...])
     gain_grad_ref[...] = gain_sum
     middle_grad = dy_ref[...].astype(F32) + part
     middle_grad_ref[...] = middle_grad
     middle_low = middle_grad.astype(BF)
     middle_low_ref[...] = middle_low
-    mixed[...] = dot_nt(middle_low, w_out[...]).astype(BF)
-    pack_blocks(z, nz, mixed, grad_blocks, (mixed.shape[1],))
+    grad_low[...] = dot_nt(middle_low, w_out[...]).astype(BF)
+    pack_blocks(z, nz, grad_low, grad_blocks, (grad_low.shape[1],))
     for f in (blocks - 2, blocks - 1):
         wait_all(slot_copies(f % 2, f))
 
@@ -428,27 +569,22 @@
     )(ids, left, right)
 
 
-def post_kernel(dims, ids, x_ref, middle_grad_ref, gain_ref, head_gain_ref, cos_ref, sin_ref, proj_ref, *refs):
-    nz, np_a, head_dim, q_cols, k_cols, v_cols = dims
+def post_kernel(dims, ids, x_ref, middle_grad_ref, gains_ref, cos_ref, sin_ref, proj_ref, *refs):
+    nz, head_dim, q_cols, k_cols, v_cols = dims
     blocks, refs = refs[:nz], refs[nz:]
-    a_pieces, b_pieces, refs = refs[:np_a], refs[np_a : 2 * np_a], refs[2 * np_a :]
-    input_grad_ref, first_ref, second_ref, gain_grad_ref, head_gain_grad_ref = refs[:5]
-    w_qk, w_v, qkv, sems = refs[5:]
-    z, me = ids[0], ids[1]
-    rows = w_qk.shape[0] // np_a
-    copies = start_pieces(me, a_pieces, w_qk, sems, 0, rows=rows)
-    copies += start_pieces(me, b_pieces, w_v, sems, np_a, rows=rows, cols=(0, v_cols))
+    qk_hbm, vo_hbm = refs[:2]
+    input_grad_ref, first_ref, second_ref, gain_grad_ref, head_gain_grad_ref = refs[2:7]
+    w_qk, w_v, qkv, sems = refs[7:]
+    z = ids[0]
+    fetch = Fetch(sems)
+    copies = [fetch.start(qk_hbm, w_qk), fetch.start(vo_hbm.at[:, pl.ds(0, v_cols)], w_v)]
     block_copies = []
     for j in range(nz):
         base, at = 0, 0
-        for i, width in enumerate((q_cols, k_cols, v_cols)):
+        for width in (q_cols, k_cols, v_cols):
             part = width // nz
             to = pl.multiple_of(base + (z ^ j) * part, part)
-            copy = pltpu.make_async_copy(
-                blocks[j].at[:, pl.ds(at, part)], qkv.at[:, pl.ds(to, part)], sems.at[2 * np_a + 3 * j + i]
-            )
-            copy.start()
-            block_copies.append(copy)
+            block_copies.append(fetch.start(blocks[j].at[:, pl.ds(at, part)], qkv.at[:, pl.ds(to, part)]))
             base, at = base + width, at + part
     wait_all(block_copies)
     width = 256
@@ -462,7 +598,7 @@
         proj = proj_ref[:, cols]
         scale = lax.rsqrt(head_sum(proj * proj, mask) * (1.0 / head_dim) + EPSILON)
         n = proj * scale
-        u = gradient * head_gain_ref[:, cols]
+        u = gradient * gains_ref[1:2, cols]
         head_gain_grad_ref[:, cols] = jnp.sum(gradient * n, axis=0, keepdims=True)
         low = (scale * (u - n * (head_sum(u * n, mask) * (1.0 / head_dim)))).astype(BF)
         qkv[:, cols] = low
@@ -470,7 +606,7 @@
     second_ref[...] = qkv[:, q_cols:]
     wait_all(copies)
     normed_grad = dot_nt(qkv[:, : q_cols + k_cols], w_qk[...]) + dot_nt(qkv[:, q_cols + k_cols :], w_v[...])
-    part, gain_sum = norm_back(x_ref[...].astype(F32), gain_ref[...], normed_grad)
+    part, gain_sum = norm_back(x_ref[...].astype(F32), gains_ref[0:1, : x_ref.shape[1]], normed_grad)
     gain_grad_ref[...] = gain_sum
     input_grad_ref[...] = (middle_grad_ref[...] + part).astype(BF)
 
@@ -481,20 +617,6 @@
 
 def swap(values, axis, size, bit):
     return lax.ppermute(values, axis, [(i, i ^ bit) for i in range(size)])
-
-
-def gather_plane(first, second):
-    near = {0: first, 2: swap(first, "fsdp", 8, 2), 4: swap(first, "fsdp", 8, 4)}
-    near[6] = swap(near[2], "fsdp", 8, 4)
-    far = {0: second, 4: swap(second, "fsdp", 8, 4), 2: swap(second, "fsdp", 8, 2)}
-    far[6] = swap(far[4], "fsdp", 8, 2)
-    both = []
-    for blocks in (near, far):
-        whole = dict(blocks)
-        for b in (0, 2, 4, 6):
-            whole[b + 1] = swap(blocks[b], "fsdp", 8, 1)
-        both.append([whole[b] for b in range(8)])
-    return both
 
 
 def reduce_plane(theirs, mine, x_first):
@@ -558,33 +680,28 @@
     hidden_cols = gate_weight.shape[1]
     seq_len = tokens * nz
 
-    gains = jnp.concatenate([attention_gain, query_gain, key_gain, feedforward_gain])
-    shard_rows = query_weight.shape[0]
     first = jnp.concatenate([query_weight, key_weight], axis=1)
     second = jnp.concatenate([value_weight, out_weight], axis=1)
-    if plane:
-        gain_rows = jnp.zeros((16, first.shape[1]), BF).at[0, : gains.shape[0]].set(gains)
-        qk_pieces, vo_pieces = gather_plane(jnp.concatenate([first, gain_rows]), second)
-        gate_pieces, up_pieces = gather_plane(gate_weight, up_weight)
-        half = down_weight.shape[0] // 2
-        upper, lower = gather_plane(down_weight[:half], down_weight[half:])
-        down_pieces = upper + lower
-        gains_all = flip_to_order(jnp.stack([p[shard_rows, : gains.shape[0]] for p in qk_pieces]), me)
+    wide_cols = q_cols + k_cols
+
+    def spread(values, count):
+        share = values.shape[0]
+        row = lax.dynamic_update_slice(jnp.zeros((share * fsdp,), BF), values, (me * share,))
+        return jnp.tile(row, count)
+
+    head_row = jnp.concatenate([spread(query_gain, q_cols // head_dim), spread(key_gain, k_cols // head_dim)])
+    fill = jnp.zeros((wide_cols - model,), BF)
+    gain_rows = [jnp.concatenate([spread(attention_gain, 1), fill]), head_row]
+    gain_rows += [jnp.concatenate([spread(feedforward_gain, 1), fill])] + [jnp.zeros((wide_cols,), BF)] * 13
+    gain_rows = jnp.stack(gain_rows)
+    if plane:
+        given = [jnp.concatenate([first, gain_rows]), second, gate_weight, up_weight, down_weight]
+        given.append(jnp.zeros((8, 128), F32))
     else:
         gather = functools.partial(lax.all_gather, axis_name="fsdp", axis=0, tiled=True)
-        qk_pieces, vo_pieces = [gather(first)], [gather(second)]
-        gate_pieces, up_pieces, down_pieces = [gather(gate_weight)], [gather(up_weight)], [gather(down_weight)]
-        gains_all = lax.all_gather(gains, "fsdp", axis=0)
-    gains_all = gains_all.astype(F32)
-    n_a, n_h = attention_gain.shape[0], query_gain.shape[0]
-    cuts = (n_a, n_a + n_h, n_a + 2 * n_h)
-    attention_scale = gains_all[:, : cuts[0]].reshape(1, -1)
-    query_scale = gains_all[:, cuts[0] : cuts[1]].reshape(1, -1)
-    key_scale = gains_all[:, cuts[1] : cuts[2]].reshape(1, -1)
-    feed_scale = gains_all[:, cuts[2] :].reshape(1, -1)
-    head_scale = jnp.concatenate(
-        [jnp.tile(query_scale, (1, q_cols // head_dim)), jnp.tile(key_scale, (1, k_cols // head_dim))], axis=1
-    )
+        qk_full, vo_full, gate_full = gather(first), gather(second), gather(gate_weight)
+        up_full, down_full = gather(up_weight), gather(down_weight)
+        given = [qk_full, vo_full, lax.psum(gain_rows.astype(F32), "fsdp")]
 
     half_dim = head_dim // 2
     freqs = ROPE_BASE ** (-jnp.arange(half_dim, dtype=F32) / half_dim)
@@ -593,27 +710,8 @@
     cosine = jnp.tile(cosine, (1, 128 // half_dim))
     sine = jnp.tile(jnp.concatenate([-sine, sine], axis=1), (1, 128 // head_dim))
 
-    np_a = len(qk_pieces)
-    dims = (nz, np_a, head_dim, q_cols, k_cols, v_cols)
+    dims = (nz, plane, head_dim, q_cols, k_cols, v_cols, min(256, seq_len))
     block_cols = (q_cols + k_cols + v_cols) // nz
-    qkv_scratch = [
-        pltpu.VMEM((model, q_cols + k_cols), BF),
-        pltpu.VMEM((model, v_cols), BF),
-        pltpu.VMEM((tokens, q_cols + k_cols + v_cols), BF),
-    ]
-    proj_flops = 2 * tokens * model * (q_cols + k_cols + v_cols)
-    normed_t, proj, *blocks = call(
-        functools.partial(pre_kernel, dims),
-        [shape_of((model, tokens), BF), shape_of((tokens, q_cols + k_cols), F32)]
-        + [shape_of((tokens, block_cols), BF)] * nz,
-        [SMEM] + [VMEM] * 5 + [ANY] * (2 * np_a),
-        [VMEM] * (2 + nz),
-        qkv_scratch + [pltpu.SemaphoreType.DMA((2 * np_a,))],
-        proj_flops,
-        12 * 2**20,
-    )(ids, x, attention_scale, head_scale, cosine, sine, *qk_pieces, *vo_pieces)
-    blocks = [blocks[0]] + [swap(blocks[j], "seq", nz, j) for j in range(1, nz)]
-
     mixed_cols = heads * head_dim
     head_scratch = [
         pltpu.VMEM((heads, seq_len, head_dim), BF),
@@ -621,24 +719,55 @@
         pltpu.VMEM((kv_heads, seq_len, head_dim), BF),
     ]
     attend_flops = 2 * heads * seq_len * seq_len * head_dim
-    *mixed, full, logs = call(
-        functools.partial(attend_kernel, (nz, min(256, seq_len))),
-        [shape_of((tokens, mixed_cols), BF)] * nz
-        + [shape_of((heads, seq_len, head_dim), F32), shape_of((heads, 8, seq_len), F32)],
-        [SMEM] + [ANY] * nz,
-        [VMEM] * (nz + 2),
-        [pltpu.VMEM((seq_len, block_cols), BF)] + head_scratch + [pltpu.SemaphoreType.DMA((nz,))],
-        4 * attend_flops,
-        8 * 2**20,
-    )(ids, *blocks)
-    mixed = [mixed[0]] + [swap(mixed[j], "seq", nz, j) for j in range(1, nz)]
-
-    n_ff, n_down = len(gate_pieces), len(down_pieces)
+    proj_flops = 2 * tokens * model * (q_cols + k_cols + v_cols)
+    outs = [
+        shape_of((16, wide_cols), F32),
+        shape_of((model, tokens), BF),
+        shape_of((tokens, wide_cols), F32),
+        shape_of((seq_len, block_cols), BF),
+        shape_of((tokens, q_cols), BF),
+        shape_of((heads, seq_len, head_dim), F32),
+        shape_of((heads, 8, seq_len), F32),
+    ]
+    n_links = 3 * (nz - 1) + nz - 1
+    qk_rows = model
+    if plane:
+        hidden = gate_weight.shape[1]
+        outs += [shape_of((model, wide_cols), BF), shape_of((model, v_cols + model), BF)]
+        outs += [shape_of((model, hidden), BF)] * 2 + [shape_of((2, hidden // 2, model), BF)]
+        n_links += 6 * 7
+        qk_rows += 8 * 16
+    got = call(
+        functools.partial(forward_kernel, dims),
+        outs,
+        [VMEM] * 3 + ([ANY] * 5 + [VMEM] if plane else [ANY] * 2 + [VMEM]),
+        [VMEM] * 7 + [ANY] * (len(outs) - 7),
+        [
+            pltpu.VMEM((qk_rows, wide_cols), BF),
+            pltpu.VMEM((model, v_cols + model), BF),
+            pltpu.VMEM((tokens, model), BF),
+            pltpu.VMEM((tokens, q_cols + k_cols + v_cols), BF),
+        ]
+        + head_scratch
+        + [
+            pltpu.VMEM((seq_len, mixed_cols), BF),
+            pltpu.SemaphoreType.DMA((24,)),
+            pltpu.SemaphoreType.DMA((n_links,)),
+            pltpu.SemaphoreType.DMA((n_links,)),
+        ],
+        proj_flops + 4 * attend_flops,
+        60 * 2**20,
+        collective=1,
+    )(x, cosine, sine, *given)
+    gains, normed_t, proj, head_rows, mixed, full, logs = got[:7]
+    if plane:
+        qk_full, vo_full, gate_full, up_full, down_full = got[7:]
+
     width = 512
     groups = 3
     rows_model = lambda kind: shape_of((tokens, model), kind)
     feed_out = call(
-        functools.partial(feed_kernel, (nz, np_a, n_ff, n_down, (v_cols, model), width, groups)),
+        functools.partial(feed_kernel, (nz, (v_cols, model), width, groups)),
         [
             rows_model(BF),
             rows_model(F32),
@@ -650,7 +779,7 @@
         + [shape_of((tokens, mixed_cols), BF)] * nz
         + [shape_of((hidden_cols, tokens), BF)]
         + [shape_of((tokens, hidden_cols), BF)] * 2,
-        [SMEM] + [VMEM] * 3 + [ANY] * (nz + np_a + 2 * n_ff + n_down),
+        [SMEM] + [VMEM] * 4 + [ANY] * 4,
         [VMEM] * (6 + nz) + [ANY] * 3,
         [
             pltpu.VMEM((q_cols, model), BF),
@@ -664,12 +793,12 @@
             pltpu.VMEM((2, width, tokens), BF),
             pltpu.VMEM((2, tokens, width), BF),
             pltpu.VMEM((2, tokens, width), BF),
-            pltpu.SemaphoreType.DMA((nz + np_a + n_down + 2 * n_ff * groups,)),
+            pltpu.SemaphoreType.DMA((17 + 2 * groups,)),
             pltpu.SemaphoreType.DMA((2, 3)),
         ],
         12 * tokens * model * hidden_cols,
         50 * 2**20,
-    )(ids, x, dy, feed_scale, *mixed, *vo_pieces, *gate_pieces, *up_pieces, *down_pieces)
+    )(ids, x, dy, gains, mixed, vo_full, gate_full, up_full, down_full)
     output, middle_grad, middle_low, mixed_t, normed_two_t, feed_gain_part = feed_out[:6]
     mixed_grad = feed_out[6 : 6 + nz]
     hidden_t, gate_grad, up_grad = feed_out[6 + nz :]
@@ -700,9 +829,9 @@
     grads = call(
         functools.partial(attend_back_kernel, (nz, min(256, seq_len), min(1024, seq_len))),
         [shape_of((tokens, block_cols), BF)] * nz,
-        [SMEM] + [ANY] * (2 * nz) + [VMEM] * 2,
+        [SMEM] + [VMEM] * 3 + [ANY] * nz,
         [VMEM] * nz,
-        [pltpu.VMEM((seq_len, block_cols), BF), pltpu.VMEM((seq_len, mixed_cols), BF)]
+        [pltpu.VMEM((seq_len, mixed_cols), BF)]
         + head_scratch
         + [
             pltpu.VMEM((heads, seq_len, head_dim), BF),
@@ -710,15 +839,15 @@
             pltpu.VMEM((heads, seq_len, head_dim), F32),
             pltpu.VMEM((kv_heads, seq_len, head_dim), BF),
             pltpu.VMEM((kv_heads, seq_len, head_dim), BF),
-            pltpu.SemaphoreType.DMA((2 * nz,)),
+            pltpu.SemaphoreType.DMA((nz,)),
         ],
         10 * attend_flops,
         20 * 2**20,
-    )(ids, *blocks, *mixed_grad, full, logs)
+    )(ids, head_rows, full, logs, *mixed_grad)
     grads = [grads[0]] + [swap(grads[j], "seq", nz, j) for j in range(1, nz)]
 
     input_grad, q_grad, kv_grad, attention_gain_part, head_gain_part = call(
-        functools.partial(post_kernel, dims),
+        functools.partial(post_kernel, (nz, head_dim, q_cols, k_cols, v_cols)),
         [
             rows_model(BF),
             shape_of((tokens, q_cols), BF),
@@ -726,12 +855,17 @@
             shape_of((1, model), F32),
             shape_of((1, q_cols + k_cols), F32),
         ],
-        [SMEM] + [VMEM] * 7 + [ANY] * (nz + 2 * np_a),
+        [SMEM] + [VMEM] * 6 + [ANY] * (nz + 2),
         [VMEM] * 5,
-        qkv_scratch + [pltpu.SemaphoreType.DMA((2 * np_a + 3 * nz,))],
+        [
+            pltpu.VMEM((model, wide_cols), BF),
+            pltpu.VMEM((model, v_cols), BF),
+            pltpu.VMEM((tokens, wide_cols + v_cols), BF),
+            pltpu.SemaphoreType.DMA((2 + 3 * nz,)),
+        ],
         proj_flops,
         14 * 2**20,
-    )(ids, x, middle_grad, attention_scale, head_scale, cosine, sine, proj, *grads, *qk_pieces, *vo_pieces)
+    )(ids, x, middle_grad, gains, cosine, sine, proj, *grads, qk_full, vo_full)
     if plane:
         q_t, q_m = weight_grad(ids, normed_t, q_grad, chips)
         kv_t, kv_m = weight_grad(ids, normed_t, kv_grad, chips)
@@ -751,6 +885,8 @@
         gain_shard = sum_line(reduce_plane(ordered[:, 1], ordered[:, 0], True)).reshape(-1)
     else:
         gain_shard = sum_line(scatter(gain_parts).reshape(-1))
+    n_a, n_h = attention_gain.shape[0], query_gain.shape[0]
+    cuts = (n_a, n_a + n_h, n_a + 2 * n_h)
     wide = lambda v: v.astype(F32)
     return (
         output.reshape(inputs.shape),

time: 770 us -> 736 us (0.956)
  Pallas kernels: 180 us -> 304 us
  waiting for transfers between devices: 395 us -> 287 us
  starting transfers between devices: 144 us -> 91.3 us
    pallas_call x4 -> x3, Pallas kernels: 95.9 us -> 220 us  [the longest x1 159 us: per_device(): call(functools.partial(forward_kernel, dims), outs, [VMEM] * 3 + ([ANY] *...]
    ppermute x78 -> x30, waiting for transfers between devices: 256 us -> 146 us  [swap(): return lax.ppermute(values, axis, [(i, i ^ bit) for i in range(size)])]
    ppermute x78 -> x30, starting transfers between devices: 84.3 us -> 29.8 us  [swap(): return lax.ppermute(values, axis, [(i, i ^ bit) for i in range(size)])]
  transfers between devices with their start and end apart: 102 -> 54, of which waited for: 48 -> 23; matrix products, arithmetic and copies ran while one was open for 4% -> 3% of each run, Pallas kernels for 10% -> 6%
where the time goes in v2:
time: 736 us; the launch traced here: 727 us
  Pallas kernels  304 us (41%)
  waiting for transfers between devices  287 us (39%)
  starting transfers between devices  91.3 us (12%)
  other arithmetic  27.3 us (4%)
  local copies, waits for them, and re-layouts  15 us (2%)
    pallas_call x1, Pallas kernels, per_device(): call(functools.partial(forward_kernel, dims), outs, [VMEM] * 3 + ([ANY] *...  159 us
    ppermute x30, waiting for transfers between devices, swap(): return lax.ppermute(values, axis, [(i, i ^ bit) for i in range(size)])  146 us
    ppermute x8, waiting for transfers between devices, sum_line(): outer = lax.ppermute(total, 'seq', [(1, 0), (2, 3)])  70.3 us
    ppermute x8, waiting for transfers between devices, sum_line(): inner = add(values, lax.ppermute(values, 'seq', [(0, 1), (3, 2)]))  69.9 us
    pallas_call x1, Pallas kernels, per_device(): call(functools.partial(feed_kernel, (nz, (v_cols, model), width, groups))...  47.2 us
    ppermute x8, starting transfers between devices, sum_line(): inner = add(values, lax.ppermute(values, 'seq', [(0, 1), (3, 2)]))  45.2 us
    pallas_call x6, Pallas kernels, weight_grad(): call(functools.partial(weight_grad_kernel, (chips, parts)), outs, [SMEM,...  43.4 us
    pallas_call x1, Pallas kernels, per_device(): call(functools.partial(attend_back_kernel, (nz, min(256, seq_len), min(10...  40.8 us
  transfers between devices with their start and end apart: 54, of which 23 were waited for; matrix products, arithmetic and copies ran while one was open for 3% of the time, Pallas kernels for 6%

profile of v2, /device:TPU:0, one launch (start us, length us, event | category | flops | bytes accessed | tf_op | source)
XLA Modules:
  0.0 726.6 jit_solution(17829224063717625844)
XLA Ops:
  8.6 2.6 concatenate.49.refs_0_
  11.9 159.1 %shard_map.237 = (f32[16,1536]{1,0:T(8,128)}, bf16[1024,512]{1,0:T(8,128)(2,1)}, f32[512,1536]{1,0:T(8,128)}, bf16[2048,512]{1,0:T(8,128)(2,1)}, bf16[512,1024]{...) custom-call(bf16[512,1024]{1,0:T(8,128)(2,1)} %bitcast.113, ...), custom_call_target="tpu_custom_call" | custom-call | flops 10737418240 | bytes 62914560 | tf_op jit(solution)/shard_map/pallas_call | solution.py:740
  171.0 47.2 %shard_map.238 = (bf16[512,1024]{1,0:T(8,128)(2,1)}, f32[512,1024]{1,0:T(8,128)}, bf16[512,1024]{1,0:T(8,128)(2,1)}, bf16[1024,512]{1,0:T(8,128)(2,1)}, bf16[102...) custom-call(s32[2]{0:T(128)} %pad_add_fusion.ids, ...), custom_call_target="tpu_custom_call" | custom-call | flops 28991029248 | bytes 52428800 | tf_op jit(solution)/shard_map/pallas_call | solution.py:769
  218.9 1.4 collective-permute-start.1
  220.3 2.4 collective-permute-start.2
  222.7 9.0 %collective-permute-done.refs_4_ = bf16[512,256]{1,0:T(8,128)(2,1)S(1)} collective-permute-done((bf16[512,256]{1,0:T(8,128)(2,1)}, bf16[512,256]{1,0:T(8,128)(2,1)S(1)}, u32[]{:S(2)}, u32[]{:S(2)}) %collective-permute-start) | collective-permute-done | bytes 262176 | tf_op jit(solution)/shard_map/ppermute | solution.py:619
  231.7 8.7 %collective-permute-done.1.refs_5_ = bf16[512,256]{1,0:T(8,128)(2,1)S(1)} collective-permute-done((bf16[512,256]{1,0:T(8,128)(2,1)}, bf16[512,256]{1,0:T(8,128)(2,1)S(1)}, u32[]{:S(2)}, u32[]{:S(2)}) %collective-permute-start.1) | collective-permute-done | bytes 262176 | tf_op jit(solution)/shard_map/ppermute | solution.py:619
  241.2 40.8 %shard_map.239 = (bf16[512,512]{1,0:T(8,128)(2,1)}, bf16[512,512]{1,0:T(8,128)(2,1)}, bf16[512,512]{1,0:T(8,128)(2,1)}, bf16[512,512]{1,0:T(8,128)(2,1)}) custom-call(s32[2]{0:T(128)} %pad_add_fusion.ids, bf16[2048,512]{1,0:T(8,128)(2,1)} %get-tuple-element.70.refs_0_, f32[4,2048,64]{2,1,0:T(8,128)} %get-tuple-element.71.refs_1_, ...), custom_call_target="tpu_custom_call" | custom-call | flops 21474836480 | bytes 20971520 | tf_op jit(solution)/shard_map/pallas_call | solution.py:829
  282.0 5.4 collective-permute-start.3
  287.5 2.4 collective-permute-start.5
  289.9 18.9 %collective-permute-done.3.refs_1_ = bf16[512,512]{1,0:T(8,128)(2,1)S(1)} collective-permute-done((bf16[512,512]{1,0:T(8,128)(2,1)}, bf16[512,512]{1,0:T(8,128)(2,1)S(1)}, u32[]{:S(2)}, u32[]{:S(2)}) %collective-permute-start.3) | collective-permute-done | bytes 524320 | tf_op jit(solution)/shard_map/ppermute | solution.py:619
  308.8 17.1 %collective-permute-done.4.refs_2_ = bf16[512,512]{1,0:T(8,128)(2,1)S(1)} collective-permute-done((bf16[512,512]{1,0:T(8,128)(2,1)}, bf16[512,512]{1,0:T(8,128)(2,1)S(1)}, u32[]{:S(2)}, u32[]{:S(2)}) %collective-permute-start.4) | collective-permute-done | bytes 524320 | tf_op jit(solution)/shard_map/ppermute | solution.py:619
  326.8 13.6 %shard_map.240 = (bf16[512,1024]{1,0:T(8,128)(2,1)}, bf16[512,1024]{1,0:T(8,128)(2,1)}, bf16[512,1024]{1,0:T(8,128)(2,1)}, f32[1,1024]{1,0:T(1,128)}, f32[1,1536]{1,0:T(1,128)}) custom-call(s32[2]{0:T(128)} %pad_add_fusion.ids, bf16[512,1024]{1,0:T(8,128)(2,1)} %bitcast.115, f32[512,1024]{1,0:T(8,128)} %get-tuple-element.68.middle_grad_ref, ...), custom_call_target="tpu_custom_call" | custom-call | flops 2147483648 | bytes 14680064 | tf_op jit(solution)/shard_map/pallas_call | solution.py:849
  343.3 3.8 shard_map.243
  348.4 9.8 %shard_map.246 = (bf16[4,288,1024]{2,1,0:T(8,128)(2,1)}, bf16[4,288,1024]{2,1,0:T(8,128)(2,1)}, bf16[4,288,1024]{2,1,0:T(8,128)(2,1)}, bf16[4,288,1024]{2,1,0:T(8,128)(2,1)}) custom-call(s32[2]{0:T(128)} %pad_add_fusion.ids, bf16[4608,512]{1,0:T(8,128)(2,1)} %get-tuple-element.104.left_ref, bf16[512,1024]{1,0:T(8,128)(2,1)} %bitcast.126), custom_call_target="tpu_custom_call" | custom-call | flops 4831838208 | bytes 15204352 | tf_op jit(solution)/shard_map/pallas_call | solution.py:560
  359.2 11.1 %shard_map.245 = (bf16[4,128,4608]{2,1,0:T(8,128)(2,1)}, bf16[4,128,4608]{2,1,0:T(8,128)(2,1)}) custom-call(s32[2]{0:T(128)} %pad_add_fusion.ids, bf16[1024,512]{1,0:T(8,128)(2,1)} %get-tuple-element.97.left_ref, bf16[512,4608]{1,0:T(8,128)(2,1)} %get-tuple-element.101.right_ref), custom_call_target="tpu_custom_call" | custom-call | flops 4831838208 | bytes 15204352 | tf_op jit(solution)/shard_map/pallas_call | solution.py:560
  370.3 11.6 %collective-permute-start.27 = (f32[1,272]{1,0:T(1,128)S(1)}, f32[1,272]{1,0:T(1,128)S(1)}, u32[]{:S(2)}, u32[]{:S(2)}) collective-permute-start(f32[1,272]{1,0:T(1,128)S(1)} %fusion.25), channel_id=1, source_target_pairs={{0,8},{24,16},{1,9},{25,17},{2,10},{26,18},{3,11},{27,19},{4,12},{... | collective-permute-start | bytes 3272 | tf_op jit(solution)/shard_map/ppermute | solution.py:640
  384.1 1.3 collective-permute-start.19
  385.4 11.0 %shard_map.244 = (bf16[4,128,4608]{2,1,0:T(8,128)(2,1)}, bf16[4,128,4608]{2,1,0:T(8,128)(2,1)}) custom-call(s32[2]{0:T(128)} %pad_add_fusion.ids, bf16[1024,512]{1,0:T(8,128)(2,1)} %get-tuple-element.97.left_ref, bf16[512,4608]{1,0:T(8,128)(2,1)} %get-tuple-element.98.right_ref), custom_call_target="tpu_custom_call" | custom-call | flops 4831838208 | bytes 15204352 | tf_op jit(solution)/shard_map/pallas_call | solution.py:560
  397.0 4.0 shard_map.242
  401.0 1.3 collective-permute-start.29
  402.3 3.8 shard_map.241
  407.9 1.6 collective-permute-start.20
  410.6 6.0 collective-permute-done.20
  417.8 4.2 collective-permute-start.21
  422.2 5.9 collective-permute-done.21
  428.1 1.5 collective-permute-start.13
  431.6 1.3 collective-permute-start.23
  432.9 1.7 add_convert_fusion.30
  434.7 7.0 collective-permute-done.13
  442.6 1.4 collective-permute-start.14
  446.2 28.7 %collective-permute-done.14 = bf16[128,1024]{1,0:T(8,128)(2,1)S(1)} collective-permute-done((bf16[128,1024]{1,0:T(8,128)(2,1)S(1)}, bf16[128,1024]{1,0:T(8,128)(2,1)S(1)}, u32[]{:S(2)}, u32[]{:S(2)}) %collective-permute-start.14) | collective-permute-done | bytes 262176 | tf_op jit(solution)/shard_map/ppermute | solution.py:619
  475.7 11.9 %collective-permute-start.15 = (bf16[128,1024]{1,0:T(8,128)(2,1)S(1)}, bf16[128,1024]{1,0:T(8,128)(2,1)S(1)}, u32[]{:S(2)}, u32[]{:S(2)}) collective-permute-start(bf16[128,1024]{1,0:T(8,128)(2,1)S(1)} %fusion.13), channel_id=1, source_target_pairs={{0,8},{24,16},{1,9},{25,17},{2,10},{26,18},{3,11},{27,19},{4,12},{... | collective-permute-start | bytes 786440 | tf_op jit(solution)/shard_map/ppermute | solution.py:640
  488.7 2.8 collective-permute-done.15
  491.5 4.4 collective-permute-start.9
  496.7 1.4 fusion.9
  498.1 1.6 collective-permute-start.44
  501.6 9.6 %collective-permute-done.44 = bf16[288,1024]{1,0:T(8,128)(2,1)S(1)} collective-permute-done((bf16[288,1024]{1,0:T(8,128)(2,1)S(1)}, bf16[288,1024]{1,0:T(8,128)(2,1)S(1)}, u32[]{:S(2)}, u32[]{:S(2)}) %collective-permute-start.44) | collective-permute-done | bytes 589856 | tf_op jit(solution)/shard_map/ppermute | solution.py:619
  511.2 1.3 collective-permute-start.17
  512.5 1.6 fusion.7
  514.2 4.7 collective-permute-start.45
  519.3 1.3 collective-permute-start.51
  520.7 1.3 collective-permute-start.11
  522.1 10.5 %collective-permute-done.45 = bf16[288,1024]{1,0:T(8,128)(2,1)S(1)} collective-permute-done((bf16[288,1024]{1,0:T(8,128)(2,1)S(1)}, bf16[288,1024]{1,0:T(8,128)(2,1)S(1)}, u32[]{:S(2)}, u32[]{:S(2)}) %collective-permute-start.45) | collective-permute-done | bytes 589856 | tf_op jit(solution)/shard_map/ppermute | solution.py:640
  533.5 7.3 %collective-permute-done.51 = bf16[288,1024]{1,0:T(8,128)(2,1)S(1)} collective-permute-done((bf16[288,1024]{1,0:T(8,128)(2,1)S(1)}, bf16[288,1024]{1,0:T(8,128)(2,1)S(1)}, u32[]{:S(2)}, u32[]{:S(2)}) %collective-permute-start.51) | collective-permute-done | bytes 589856 | tf_op jit(solution)/shard_map/ppermute | solution.py:640
  545.2 1.3 collective-permute-start.47
  546.8 1.5 collective-permute-start.53
  550.0 9.7 %collective-permute-done.47 = bf16[288,1024]{1,0:T(8,128)(2,1)S(1)} collective-permute-done((bf16[288,1024]{1,0:T(8,128)(2,1)S(1)}, bf16[288,1024]{1,0:T(8,128)(2,1)S(1)}, u32[]{:S(2)}, u32[]{:S(2)}) %collective-permute-start.47) | collective-permute-done | bytes 589856 | tf_op jit(solution)/shard_map/ppermute | solution.py:642
  559.7 12.4 %collective-permute-done.53 = bf16[288,1024]{1,0:T(8,128)(2,1)S(1)} collective-permute-done((bf16[288,1024]{1,0:T(8,128)(2,1)S(1)}, bf16[288,1024]{1,0:T(8,128)(2,1)S(1)}, u32[]{:S(2)}, u32[]{:S(2)}) %collective-permute-start.53) | collective-permute-done | bytes 589856 | tf_op jit(solution)/shard_map/ppermute | solution.py:642
  572.2 1.7 maximum_convert_fusion
  573.9 18.5 %collective-permute-done.37 = bf16[2,128,4608]{2,1,0:T(8,128)(2,1)S(1)} collective-permute-done((bf16[2,128,4608]{2,1,0:T(8,128)(2,1)S(1)}, bf16[2,128,4608]{2,1,0:T(8,128)(2,1)S(1)}, u32[]{:S(2)}, u32[]{:S(2)}) %collective-permute-start.37) | collective-permute-done | bytes 2359328 | tf_op jit(solution)/shard_map/ppermute | solution.py:619
  593.5 3.0 collective-permute-done.31
  597.0 1.9 collective-permute-start.32
  598.9 19.5 %collective-permute-done.38 = bf16[128,4608]{1,0:T(8,128)(2,1)S(1)} collective-permute-done((bf16[128,4608]{1,0:T(8,128)(2,1)S(1)}, bf16[128,4608]{1,0:T(8,128)(2,1)S(1)}, u32[]{:S(2)}, u32[]{:S(2)}) %collective-permute-start.38) | collective-permute-done | bytes 1179680 | tf_op jit(solution)/shard_map/ppermute | solution.py:619
  619.0 5.7 collective-permute-start.39
  625.3 1.4 collective-permute-start.33
  626.7 24.4 %collective-permute-done.39 = bf16[128,4608]{1,0:T(8,128)(2,1)S(1)} collective-permute-done((bf16[128,4608]{1,0:T(8,128)(2,1)S(1)}, bf16[128,4608]{1,0:T(8,128)(2,1)S(1)}, u32[]{:S(2)}, u32[]{:S(2)}) %collective-permute-start.39) | collective-permute-done | bytes 1179680 | tf_op jit(solution)/shard_map/ppermute | solution.py:640
  652.0 18.9 %collective-permute-done.33 = bf16[128,4608]{1,0:T(8,128)(2,1)S(1)} collective-permute-done((bf16[128,4608]{1,0:T(8,128)(2,1)S(1)}, bf16[128,4608]{1,0:T(8,128)(2,1)S(1)}, u32[]{:S(2)}, u32[]{:S(2)}) %collective-permute-start.33) | collective-permute-done | bytes 1179680 | tf_op jit(solution)/shard_map/ppermute | solution.py:640
  672.3 1.3 collective-permute-start.41
  673.9 1.3 collective-permute-start.35
  675.2 28.9 %collective-permute-done.41 = bf16[128,4608]{1,0:T(8,128)(2,1)S(1)} collective-permute-done((bf16[128,4608]{1,0:T(8,128)(2,1)S(1)}, bf16[128,4608]{1,0:T(8,128)(2,1)S(1)}, u32[]{:S(2)}, u32[]{:S(2)}) %collective-permute-start.41) | collective-permute-done | bytes 1179680 | tf_op jit(solution)/shard_map/ppermute | solution.py:642
  704.0 1.6 select_convert_fusion
  705.6 19.0 %collective-permute-done.35 = bf16[128,4608]{1,0:T(8,128)(2,1)S(1)} collective-permute-done((bf16[128,4608]{1,0:T(8,128)(2,1)S(1)}, bf16[128,4608]{1,0:T(8,128)(2,1)S(1)}, u32[]{:S(2)}, u32[]{:S(2)}) %collective-permute-start.35) | collective-permute-done | bytes 1179680 | tf_op jit(solution)/shard_map/ppermute | solution.py:642
  724.6 1.6 select_convert_fusion.1
  (206 shorter events, 45.7 us)
Async XLA Ops:
  0.6 6.5 copy-start.9
  218.2 13.4 %collective-permute-start = (bf16[512,256]{1,0:T(8,128)(2,1)}, bf16[512,256]{1,0:T(8,128)(2,1)S(1)}, u32[]{:S(2)}, u32[]{:S(2)}) collective-permute-start(bf16[512,256]{1,0:T(8,128)(2,1)} %get-tuple-element.74), channel_id=1, source_target_pairs={{0,8},{8,0},{16,24},{24,16},{1,9},{9,1},{17,25},{25,17},{2,10},{10... | collective-permute-start | bytes 786440 | tf_op jit(solution)/shard_map/ppermute | solution.py:619
  218.9 21.5 %collective-permute-start.1 = (bf16[512,256]{1,0:T(8,128)(2,1)}, bf16[512,256]{1,0:T(8,128)(2,1)S(1)}, u32[]{:S(2)}, u32[]{:S(2)}) collective-permute-start(bf16[512,256]{1,0:T(8,128)(2,1)} %get-tuple-element.75), channel_id=1, source_target_pairs={{0,16},{8,24},{16,0},{24,8},{1,17},{9,25},{17,1},{25,9},{2,18},{10... | collective-permute-start | bytes 786440 | tf_op jit(solution)/shard_map/ppermute | solution.py:619
  220.3 20.1 %collective-permute-start.2 = (bf16[512,256]{1,0:T(8,128)(2,1)}, bf16[512,256]{1,0:T(8,128)(2,1)S(1)}, u32[]{:S(2)}, u32[]{:S(2)}) collective-permute-start(bf16[512,256]{1,0:T(8,128)(2,1)} %get-tuple-element.76), channel_id=1, source_target_pairs={{0,24},{8,16},{16,8},{24,0},{1,25},{9,17},{17,9},{25,1},{2,26},{10... | collective-permute-start | bytes 786440 | tf_op jit(solution)/shard_map/ppermute | solution.py:619
  231.7 8.7 %copy-start.14 = (bf16[512,256]{1,0:T(8,128)(2,1)}, bf16[512,256]{1,0:T(8,128)(2,1)S(1)}, u32[]{:S(2)}) copy-start(bf16[512,256]{1,0:T(8,128)(2,1)S(1)} %collective-permute-done.refs_4_) | copy-start | bytes 786436
  282.0 26.8 %collective-permute-start.3 = (bf16[512,512]{1,0:T(8,128)(2,1)}, bf16[512,512]{1,0:T(8,128)(2,1)S(1)}, u32[]{:S(2)}, u32[]{:S(2)}) collective-permute-start(bf16[512,512]{1,0:T(8,128)(2,1)} %get-tuple-element.78), channel_id=1, source_target_pairs={{0,8},{8,0},{16,24},{24,16},{1,9},{9,1},{17,25},{25,17},{2,10},{10... | collective-permute-start | bytes 1572872 | tf_op jit(solution)/shard_map/ppermute | solution.py:619
  287.4 38.4 %collective-permute-start.4 = (bf16[512,512]{1,0:T(8,128)(2,1)}, bf16[512,512]{1,0:T(8,128)(2,1)S(1)}, u32[]{:S(2)}, u32[]{:S(2)}) collective-permute-start(bf16[512,512]{1,0:T(8,128)(2,1)} %get-tuple-element.79), channel_id=1, source_target_pairs={{0,16},{8,24},{16,0},{24,8},{1,17},{9,25},{17,1},{25,9},{2,18},{10... | collective-permute-start | bytes 1572872 | tf_op jit(solution)/shard_map/ppermute | solution.py:619
  287.5 38.4 %collective-permute-start.5 = (bf16[512,512]{1,0:T(8,128)(2,1)}, bf16[512,512]{1,0:T(8,128)(2,1)S(1)}, u32[]{:S(2)}, u32[]{:S(2)}) collective-permute-start(bf16[512,512]{1,0:T(8,128)(2,1)} %get-tuple-element.80), channel_id=1, source_target_pairs={{0,24},{8,16},{16,8},{24,0},{1,25},{9,17},{17,9},{25,1},{2,26},{10... | collective-permute-start | bytes 1572872 | tf_op jit(solution)/shard_map/ppermute | solution.py:619
  308.8 17.1 %copy-start.6 = (bf16[512,512]{1,0:T(8,128)(2,1)}, bf16[512,512]{1,0:T(8,128)(2,1)S(1)}, u32[]{:S(2)}) copy-start(bf16[512,512]{1,0:T(8,128)(2,1)S(1)} %collective-permute-done.3.refs_1_) | copy-start | bytes 1572868
  326.8 15.4 %copy-start.13 = (f32[1,1024]{1,0:T(1,128)S(1)}, f32[1,1024]{1,0:T(1,128)}, u32[]{:S(2)}) copy-start(f32[1,1024]{1,0:T(1,128)} %get-tuple-element.96) | copy-start | bytes 12292
  343.2 4.4 collective-permute-start.24
  347.1 34.9 %collective-permute-start.18 = (bf16[4,128,1024]{2,1,0:T(8,128)(2,1)}, bf16[4,128,1024]{2,1,0:T(8,128)(2,1)S(1)}, u32[]{:S(2)}, u32[]{:S(2)}) collective-permute-start(bf16[4,128,1024]{2,1,0:T(8,128)(2,1)} %get-tuple-element.93), channel_id=1, source_target_pairs={{0,1},{1,0},{2,3},{3,2},{4,5},{5,4},{6,7},{7,6},{8,9},{9,8},{10,11... | collective-permute-start | bytes 3145736 | tf_op jit(solution)/shard_map/ppermute | solution.py:619
  347.6 11.1 %collective-permute-start.25 = (f32[2,1,272]{2,1,0:T(1,128)S(1)}, f32[2,1,272]{2,1,0:T(1,128)S(1)}, u32[]{:S(2)}, u32[]{:S(2)}) collective-permute-start(f32[2,1,272]{2,1,0:T(1,128)S(1)} %pad_maximum_fusion.12), channel_id=1, source_target_pairs={{0,2},{1,3},{2,0},{3,1},{4,6},{5,7},{6,4},{7,5},{8,10},{9,11},{10,... | collective-permute-start | bytes 6536 | tf_op jit(solution)/shard_map/ppermute | solution.py:619
  358.1 73.4 %collective-permute-start.42 = (bf16[4,288,1024]{2,1,0:T(8,128)(2,1)}, bf16[4,288,1024]{2,1,0:T(8,128)(2,1)}, u32[]{:S(2)}, u32[]{:S(2)}) collective-permute-start(bf16[4,288,1024]{2,1,0:T(8,128)(2,1)} %get-tuple-element.106), channel_id=1, source_target_pairs={{0,1},{1,0},{2,3},{3,2},{4,5},{5,4},{6,7},{7,6},{8,9},{9,8},{10,11... | collective-permute-start | bytes 7077896 | tf_op jit(solution)/shard_map/ppermute | solution.py:619
  358.2 84.4 %collective-permute-start.48 = (bf16[4,288,1024]{2,1,0:T(8,128)(2,1)}, bf16[4,288,1024]{2,1,0:T(8,128)(2,1)S(1)}, u32[]{:S(2)}, u32[]{:S(2)}) collective-permute-start(bf16[4,288,1024]{2,1,0:T(8,128)(2,1)} %get-tuple-element.108), channel_id=1, source_target_pairs={{0,1},{1,0},{2,3},{3,2},{4,5},{5,4},{6,7},{7,6},{8,9},{9,8},{10,11... | collective-permute-start | bytes 7077896 | tf_op jit(solution)/shard_map/ppermute | solution.py:619
  358.7 11.6 %collective-permute-start.26 = (f32[1,272]{1,0:T(1,128)S(1)}, f32[1,272]{1,0:T(1,128)S(1)}, u32[]{:S(2)}, u32[]{:S(2)}) collective-permute-start(f32[1,272]{1,0:T(1,128)S(1)} %fusion.22), channel_id=1, source_target_pairs={{0,4},{1,5},{2,6},{3,7},{4,0},{5,1},{6,2},{7,3},{8,12},{9,13},{10,... | collective-permute-start | bytes 3272 | tf_op jit(solution)/shard_map/ppermute | solution.py:619
  359.2 23.8 %copy-start.4 = (bf16[4,128,1024]{2,1,0:T(8,128)(2,1)S(1)}, bf16[4,128,1024]{2,1,0:T(8,128)(2,1)}, u32[]{:S(2)}) copy-start(bf16[4,128,1024]{2,1,0:T(8,128)(2,1)} %get-tuple-element.92) | copy-start | bytes 3145732
  370.3 26.0 %collective-permute-start.27 = (f32[1,272]{1,0:T(1,128)S(1)}, f32[1,272]{1,0:T(1,128)S(1)}, u32[]{:S(2)}, u32[]{:S(2)}) collective-permute-start(f32[1,272]{1,0:T(1,128)S(1)} %fusion.25), channel_id=1, source_target_pairs={{0,8},{24,16},{1,9},{25,17},{2,10},{26,18},{3,11},{27,19},{4,12},{... | collective-permute-start | bytes 3272 | tf_op jit(solution)/shard_map/ppermute | solution.py:640
  384.1 22.6 %collective-permute-start.19 = (bf16[2,128,1024]{2,1,0:T(8,128)(2,1)}, bf16[2,128,1024]{2,1,0:T(8,128)(2,1)}, u32[]{:S(2)}, u32[]{:S(2)}) collective-permute-start(bf16[2,128,1024]{2,1,0:T(8,128)(2,1)} %pad_maximum_fusion.6), channel_id=1, source_target_pairs={{0,2},{1,3},{2,0},{3,1},{4,6},{5,7},{6,4},{7,5},{8,10},{9,11},{10,... | collective-permute-start | bytes 1572872 | tf_op jit(solution)/shard_map/ppermute | solution.py:619
  396.3 4.7 collective-permute-start.28
  401.0 16.8 %collective-permute-start.12 = (bf16[4,128,1024]{2,1,0:T(8,128)(2,1)}, bf16[4,128,1024]{2,1,0:T(8,128)(2,1)S(1)}, u32[]{:S(2)}, u32[]{:S(2)}) collective-permute-start(bf16[4,128,1024]{2,1,0:T(8,128)(2,1)} %get-tuple-element.89), channel_id=1, source_target_pairs={{0,1},{1,0},{2,3},{3,2},{4,5},{5,4},{6,7},{7,6},{8,9},{9,8},{10,11... | collective-permute-start | bytes 3145736 | tf_op jit(solution)/shard_map/ppermute | solution.py:619
  401.0 5.5 collective-permute-start.29
  406.5 23.2 %collective-permute-start.6 = (bf16[4,128,1024]{2,1,0:T(8,128)(2,1)}, bf16[4,128,1024]{2,1,0:T(8,128)(2,1)S(1)}, u32[]{:S(2)}, u32[]{:S(2)}) collective-permute-start(bf16[4,128,1024]{2,1,0:T(8,128)(2,1)} %get-tuple-element.86), channel_id=1, source_target_pairs={{0,1},{1,0},{2,3},{3,2},{4,5},{5,4},{6,7},{7,6},{8,9},{9,8},{10,11... | collective-permute-start | bytes 3145736 | tf_op jit(solution)/shard_map/ppermute | solution.py:619
  406.6 15.3 %copy-start.3 = (bf16[4,128,1024]{2,1,0:T(8,128)(2,1)S(1)}, bf16[4,128,1024]{2,1,0:T(8,128)(2,1)}, u32[]{:S(2)}) copy-start(bf16[4,128,1024]{2,1,0:T(8,128)(2,1)} %get-tuple-element.88) | copy-start | bytes 3145732
  407.9 8.7 %collective-permute-start.20 = (bf16[128,1024]{1,0:T(8,128)(2,1)S(1)}, bf16[128,1024]{1,0:T(8,128)(2,1)S(1)}, u32[]{:S(2)}, u32[]{:S(2)}) collective-permute-start(bf16[128,1024]{1,0:T(8,128)(2,1)S(1)} %fusion.20), channel_id=1, source_target_pairs={{0,4},{1,5},{2,6},{3,7},{4,0},{5,1},{6,2},{7,3},{8,12},{9,13},{10,... | collective-permute-start | bytes 786440 | tf_op jit(solution)/shard_map/ppermute | solution.py:619
  416.6 125.4 %collective-permute-start.36 = (bf16[4,128,4608]{2,1,0:T(8,128)(2,1)}, bf16[4,128,4608]{2,1,0:T(8,128)(2,1)S(1)}, u32[]{:S(2)}, u32[]{:S(2)}) collective-permute-start(bf16[4,128,4608]{2,1,0:T(8,128)(2,1)} %get-tuple-element.103), channel_id=1, source_target_pairs={{0,1},{1,0},{2,3},{3,2},{4,5},{5,4},{6,7},{7,6},{8,9},{9,8},{10,11... | collective-permute-start | bytes 14155784 | tf_op jit(solution)/shard_map/ppermute | solution.py:619
  417.8 10.4 %collective-permute-start.21 = (bf16[128,1024]{1,0:T(8,128)(2,1)S(1)}, bf16[128,1024]{1,0:T(8,128)(2,1)S(1)}, u32[]{:S(2)}, u32[]{:S(2)}) collective-permute-start(bf16[128,1024]{1,0:T(8,128)(2,1)S(1)} %fusion.12), channel_id=1, source_target_pairs={{0,8},{24,16},{1,9},{25,17},{2,10},{26,18},{3,11},{27,19},{4,12},{... | collective-permute-start | bytes 786440 | tf_op jit(solution)/shard_map/ppermute | solution.py:640
  422.2 8.3 %copy-start.2 = (bf16[4,128,1024]{2,1,0:T(8,128)(2,1)S(1)}, bf16[4,128,1024]{2,1,0:T(8,128)(2,1)}, u32[]{:S(2)}) copy-start(bf16[4,128,1024]{2,1,0:T(8,128)(2,1)} %get-tuple-element.85) | copy-start | bytes 3145732
  428.1 13.6 %collective-permute-start.13 = (bf16[2,128,1024]{2,1,0:T(8,128)(2,1)S(1)}, bf16[2,128,1024]{2,1,0:T(8,128)(2,1)S(1)}, u32[]{:S(2)}, u32[]{:S(2)}) collective-permute-start(bf16[2,128,1024]{2,1,0:T(8,128)(2,1)S(1)} %pad_maximum_fusion.5), channel_id=1, source_target_pairs={{0,4},{1,5},{2,6},{3,7},{4,0},{5,1},{6,2},{7,3},{8,12},{9,13},{10,... | collective-permute-start | bytes 1572872 | tf_op jit(solution)/shard_map/ppermute | solution.py:619
  429.7 1.0 collective-permute-start.22
  430.7 14.2 %collective-permute-start.7 = (bf16[2,128,1024]{2,1,0:T(8,128)(2,1)S(1)}, bf16[2,128,1024]{2,1,0:T(8,128)(2,1)S(1)}, u32[]{:S(2)}, u32[]{:S(2)}) collective-permute-start(bf16[2,128,1024]{2,1,0:T(8,128)(2,1)S(1)} %pad_maximum_fusion.4), channel_id=1, source_target_pairs={{0,2},{1,3},{2,0},{3,1},{4,6},{5,7},{6,4},{7,5},{8,10},{9,11},{10,... | collective-permute-start | bytes 1572872 | tf_op jit(solution)/shard_map/ppermute | solution.py:619
  431.6 44.1 %collective-permute-start.23 = (bf16[128,1024]{1,0:T(8,128)(2,1)S(1)}, bf16[128,1024]{1,0:T(8,128)(2,1)S(1)}, u32[]{:S(2)}, u32[]{:S(2)}) collective-permute-start(bf16[128,1024]{1,0:T(8,128)(2,1)S(1)} %add_convert_fusion.38), channel_id=1, source_target_pairs={{8,0},{16,24},{9,1},{17,25},{10,2},{18,26},{11,3},{19,27},{12,4},{... | collective-permute-start | bytes 786440 | tf_op jit(solution)/shard_map/ppermute | solution.py:642
  434.6 9.3 %copy-start = (bf16[4,288,1024]{2,1,0:T(8,128)(2,1)S(1)}, bf16[4,288,1024]{2,1,0:T(8,128)(2,1)}, u32[]{:S(2)}) copy-start(bf16[4,288,1024]{2,1,0:T(8,128)(2,1)} %get-tuple-element.107) | copy-start | bytes 7077892
  441.7 54.3 %collective-permute-start.43 = (bf16[2,288,1024]{2,1,0:T(8,128)(2,1)S(1)}, bf16[2,288,1024]{2,1,0:T(8,128)(2,1)S(1)}, u32[]{:S(2)}, u32[]{:S(2)}) collective-permute-start(bf16[2,288,1024]{2,1,0:T(8,128)(2,1)S(1)} %pad_maximum_fusion.2), channel_id=1, source_target_pairs={{0,2},{1,3},{2,0},{3,1},{4,6},{5,7},{6,4},{7,5},{8,10},{9,11},{10,... | collective-permute-start | bytes 3538952 | tf_op jit(solution)/shard_map/ppermute | solution.py:619
  442.6 32.4 %collective-permute-start.14 = (bf16[128,1024]{1,0:T(8,128)(2,1)S(1)}, bf16[128,1024]{1,0:T(8,128)(2,1)S(1)}, u32[]{:S(2)}, u32[]{:S(2)}) collective-permute-start(bf16[128,1024]{1,0:T(8,128)(2,1)S(1)} %fusion.18), channel_id=1, source_target_pairs={{0,2},{1,3},{2,0},{3,1},{4,6},{5,7},{6,4},{7,5},{8,10},{9,11},{10,... | collective-permute-start | bytes 786440 | tf_op jit(solution)/shard_map/ppermute | solution.py:619
  444.9 53.1 %collective-permute-start.49 = (bf16[2,288,1024]{2,1,0:T(8,128)(2,1)S(1)}, bf16[2,288,1024]{2,1,0:T(8,128)(2,1)S(1)}, u32[]{:S(2)}, u32[]{:S(2)}) collective-permute-start(bf16[2,288,1024]{2,1,0:T(8,128)(2,1)S(1)} %pad_maximum_fusion.3), channel_id=1, source_target_pairs={{0,4},{1,5},{2,6},{3,7},{4,0},{5,1},{6,2},{7,3},{8,12},{9,13},{10,... | collective-permute-start | bytes 3538952 | tf_op jit(solution)/shard_map/ppermute | solution.py:619
  475.0 13.5 %collective-permute-start.8 = (bf16[128,1024]{1,0:T(8,128)(2,1)S(1)}, bf16[128,1024]{1,0:T(8,128)(2,1)S(1)}, u32[]{:S(2)}, u32[]{:S(2)}) collective-permute-start(bf16[128,1024]{1,0:T(8,128)(2,1)S(1)} %fusion.16), channel_id=1, source_target_pairs={{0,4},{1,5},{2,6},{3,7},{4,0},{5,1},{6,2},{7,3},{8,12},{9,13},{10,... | collective-permute-start | bytes 786440 | tf_op jit(solution)/shard_map/ppermute | solution.py:619
  475.7 15.8 %collective-permute-start.15 = (bf16[128,1024]{1,0:T(8,128)(2,1)S(1)}, bf16[128,1024]{1,0:T(8,128)(2,1)S(1)}, u32[]{:S(2)}, u32[]{:S(2)}) collective-permute-start(bf16[128,1024]{1,0:T(8,128)(2,1)S(1)} %fusion.13), channel_id=1, source_target_pairs={{0,8},{24,16},{1,9},{25,17},{2,10},{26,18},{3,11},{27,19},{4,12},{... | collective-permute-start | bytes 786440 | tf_op jit(solution)/shard_map/ppermute | solution.py:640
  488.5 54.4 %collective-permute-start.30 = (bf16[4,128,4608]{2,1,0:T(8,128)(2,1)}, bf16[4,128,4608]{2,1,0:T(8,128)(2,1)S(1)}, u32[]{:S(2)}, u32[]{:S(2)}) collective-permute-start(bf16[4,128,4608]{2,1,0:T(8,128)(2,1)} %get-tuple-element.100), channel_id=1, source_target_pairs={{0,1},{1,0},{2,3},{3,2},{4,5},{5,4},{6,7},{7,6},{8,9},{9,8},{10,11... | collective-permute-start | bytes 14155784 | tf_op jit(solution)/shard_map/ppermute | solution.py:619
  491.5 8.4 %collective-permute-start.9 = (bf16[128,1024]{1,0:T(8,128)(2,1)S(1)}, bf16[128,1024]{1,0:T(8,128)(2,1)S(1)}, u32[]{:S(2)}, u32[]{:S(2)}) collective-permute-start(bf16[128,1024]{1,0:T(8,128)(2,1)S(1)} %fusion.14), channel_id=1, source_target_pairs={{0,8},{24,16},{1,9},{25,17},{2,10},{26,18},{3,11},{27,19},{4,12},{... | collective-permute-start | bytes 786440 | tf_op jit(solution)/shard_map/ppermute | solution.py:640
  496.0 4.8 collective-permute-start.16
  498.1 13.1 %collective-permute-start.44 = (bf16[288,1024]{1,0:T(8,128)(2,1)S(1)}, bf16[288,1024]{1,0:T(8,128)(2,1)S(1)}, u32[]{:S(2)}, u32[]{:S(2)}) collective-permute-start(bf16[288,1024]{1,0:T(8,128)(2,1)S(1)} %fusion.9), channel_id=1, source_target_pairs={{0,4},{1,5},{2,6},{3,7},{4,0},{5,1},{6,2},{7,3},{8,12},{9,13},{10,... | collective-permute-start | bytes 1769480 | tf_op jit(solution)/shard_map/ppermute | solution.py:619
  499.9 14.2 %collective-permute-start.50 = (bf16[288,1024]{1,0:T(8,128)(2,1)S(1)}, bf16[288,1024]{1,0:T(8,128)(2,1)S(1)}, u32[]{:S(2)}, u32[]{:S(2)}) collective-permute-start(bf16[288,1024]{1,0:T(8,128)(2,1)S(1)} %fusion.11), channel_id=1, source_target_pairs={{0,2},{1,3},{2,0},{3,1},{4,6},{5,7},{6,4},{7,5},{8,10},{9,11},{10,... | collective-permute-start | bytes 1769480 | tf_op jit(solution)/shard_map/ppermute | solution.py:619
  500.8 18.5 %collective-permute-start.10 = (bf16[128,1024]{1,0:T(8,128)(2,1)S(1)}, bf16[128,1024]{1,0:T(8,128)(2,1)S(1)}, u32[]{:S(2)}, u32[]{:S(2)}) collective-permute-start(bf16[128,1024]{1,0:T(8,128)(2,1)S(1)} %add_convert_fusion.51), channel_id=1, source_target_pairs={{8,16},{16,8},{9,17},{17,9},{10,18},{18,10},{11,19},{19,11},{12,20... | collective-permute-start | bytes 786440 | tf_op jit(solution)/shard_map/ppermute | solution.py:641
  511.2 9.5 %collective-permute-start.17 = (bf16[128,1024]{1,0:T(8,128)(2,1)S(1)}, bf16[128,1024]{1,0:T(8,128)(2,1)S(1)}, u32[]{:S(2)}, u32[]{:S(2)}) collective-permute-start(bf16[128,1024]{1,0:T(8,128)(2,1)S(1)} %add_convert_fusion.44), channel_id=1, source_target_pairs={{8,0},{16,24},{9,1},{17,25},{10,2},{18,26},{11,3},{19,27},{12,4},{... | collective-permute-start | bytes 786440 | tf_op jit(solution)/shard_map/ppermute | solution.py:642
  512.5 29.5 %slice-start = ((s8[4718592]{0:T(1024)(128)(4,1)}), s8[4194304]{0:T(1024)(128)(4,1)S(1)}, s32[]{:S(2)}) async-start(s8[4718592]{0:T(1024)(128)(4,1)} %bitcast.109), calls=%async_computation | async-start | bytes 8388608
  514.1 27.8 %slice-start.1 = ((s8[4718592]{0:T(1024)(128)(4,1)}), s8[524288]{0:T(1024)(128)(4,1)S(1)}, s32[]{:S(2)}) async-start(s8[4718592]{0:T(1024)(128)(4,1)} %bitcast.109), calls=%async_computation.1 | async-start | bytes 1048576
  514.2 18.5 %collective-permute-start.45 = (bf16[288,1024]{1,0:T(8,128)(2,1)S(1)}, bf16[288,1024]{1,0:T(8,128)(2,1)S(1)}, u32[]{:S(2)}, u32[]{:S(2)}) collective-permute-start(bf16[288,1024]{1,0:T(8,128)(2,1)S(1)} %fusion.7), channel_id=1, source_target_pairs={{0,8},{24,16},{1,9},{25,17},{2,10},{26,18},{3,11},{27,19},{4,12},{... | collective-permute-start | bytes 1769480 | tf_op jit(solution)/shard_map/ppermute | solution.py:640
  519.3 21.5 %collective-permute-start.51 = (bf16[288,1024]{1,0:T(8,128)(2,1)S(1)}, bf16[288,1024]{1,0:T(8,128)(2,1)S(1)}, u32[]{:S(2)}, u32[]{:S(2)}) collective-permute-start(bf16[288,1024]{1,0:T(8,128)(2,1)S(1)} %fusion.6), channel_id=1, source_target_pairs={{0,8},{24,16},{1,9},{25,17},{2,10},{26,18},{3,11},{27,19},{4,12},{... | collective-permute-start | bytes 1769480 | tf_op jit(solution)/shard_map/ppermute | solution.py:640
  520.7 28.4 %collective-permute-start.11 = (bf16[128,1024]{1,0:T(8,128)(2,1)S(1)}, bf16[128,1024]{1,0:T(8,128)(2,1)S(1)}, u32[]{:S(2)}, u32[]{:S(2)}) collective-permute-start(bf16[128,1024]{1,0:T(8,128)(2,1)S(1)} %add_convert_fusion.50), channel_id=1, source_target_pairs={{8,0},{16,24},{9,1},{17,25},{10,2},{18,26},{11,3},{19,27},{12,4},{... | collective-permute-start | bytes 786440 | tf_op jit(solution)/shard_map/ppermute | solution.py:642
  532.8 12.1 %collective-permute-start.46 = (bf16[288,1024]{1,0:T(8,128)(2,1)S(1)}, bf16[288,1024]{1,0:T(8,128)(2,1)S(1)}, u32[]{:S(2)}, u32[]{:S(2)}) collective-permute-start(bf16[288,1024]{1,0:T(8,128)(2,1)S(1)} %add_convert_fusion.27), channel_id=1, source_target_pairs={{8,16},{16,8},{9,17},{17,9},{10,18},{18,10},{11,19},{19,11},{12,20... | collective-permute-start | bytes 1769480 | tf_op jit(solution)/shard_map/ppermute | solution.py:641
  541.1 5.4 collective-permute-start.52
  542.8 49.6 %collective-permute-start.37 = (bf16[2,128,4608]{2,1,0:T(8,128)(2,1)S(1)}, bf16[2,128,4608]{2,1,0:T(8,128)(2,1)S(1)}, u32[]{:S(2)}, u32[]{:S(2)}) collective-permute-start(bf16[2,128,4608]{2,1,0:T(8,128)(2,1)S(1)} %pad_maximum_fusion.1), channel_id=1, source_target_pairs={{0,4},{1,5},{2,6},{3,7},{4,0},{5,1},{6,2},{7,3},{8,12},{9,13},{10,... | collective-permute-start | bytes 7077896 | tf_op jit(solution)/shard_map/ppermute | solution.py:619
  544.2 52.4 %collective-permute-start.31 = (bf16[2,128,4608]{2,1,0:T(8,128)(2,1)S(1)}, bf16[2,128,4608]{2,1,0:T(8,128)(2,1)S(1)}, u32[]{:S(2)}, u32[]{:S(2)}) collective-permute-start(bf16[2,128,4608]{2,1,0:T(8,128)(2,1)S(1)} %pad_maximum_fusion), channel_id=1, source_target_pairs={{0,2},{1,3},{2,0},{3,1},{4,6},{5,7},{6,4},{7,5},{8,10},{9,11},{10,... | collective-permute-start | bytes 7077896 | tf_op jit(solution)/shard_map/ppermute | solution.py:619
  545.2 14.4 %collective-permute-start.47 = (bf16[288,1024]{1,0:T(8,128)(2,1)S(1)}, bf16[288,1024]{1,0:T(8,128)(2,1)S(1)}, u32[]{:S(2)}, u32[]{:S(2)}) collective-permute-start(bf16[288,1024]{1,0:T(8,128)(2,1)S(1)} %add_convert_fusion.26), channel_id=1, source_target_pairs={{8,0},{16,24},{9,1},{17,25},{10,2},{18,26},{11,3},{19,27},{12,4},{... | collective-permute-start | bytes 1769480 | tf_op jit(solution)/shard_map/ppermute | solution.py:642
  546.8 25.4 %collective-permute-start.53 = (bf16[288,1024]{1,0:T(8,128)(2,1)S(1)}, bf16[288,1024]{1,0:T(8,128)(2,1)S(1)}, u32[]{:S(2)}, u32[]{:S(2)}) collective-permute-start(bf16[288,1024]{1,0:T(8,128)(2,1)S(1)} %add_convert_fusion.20), channel_id=1, source_target_pairs={{8,0},{16,24},{9,1},{17,25},{10,2},{18,26},{11,3},{19,27},{12,4},{... | collective-permute-start | bytes 1769480 | tf_op jit(solution)/shard_map/ppermute | solution.py:642
  592.8 25.6 %collective-permute-start.38 = (bf16[128,4608]{1,0:T(8,128)(2,1)S(1)}, bf16[128,4608]{1,0:T(8,128)(2,1)S(1)}, u32[]{:S(2)}, u32[]{:S(2)}) collective-permute-start(bf16[128,4608]{1,0:T(8,128)(2,1)S(1)} %fusion.5), channel_id=1, source_target_pairs={{0,2},{1,3},{2,0},{3,1},{4,6},{5,7},{6,4},{7,5},{8,10},{9,11},{10,... | collective-permute-start | bytes 3538952 | tf_op jit(solution)/shard_map/ppermute | solution.py:619
  597.0 27.7 %collective-permute-start.32 = (bf16[128,4608]{1,0:T(8,128)(2,1)S(1)}, bf16[128,4608]{1,0:T(8,128)(2,1)S(1)}, u32[]{:S(2)}, u32[]{:S(2)}) collective-permute-start(bf16[128,4608]{1,0:T(8,128)(2,1)S(1)} %fusion.3), channel_id=1, source_target_pairs={{0,4},{1,5},{2,6},{3,7},{4,0},{5,1},{6,2},{7,3},{8,12},{9,13},{10,... | collective-permute-start | bytes 3538952 | tf_op jit(solution)/shard_map/ppermute | solution.py:619
  619.0 32.1 %collective-permute-start.39 = (bf16[128,4608]{1,0:T(8,128)(2,1)S(1)}, bf16[128,4608]{1,0:T(8,128)(2,1)S(1)}, u32[]{:S(2)}, u32[]{:S(2)}) collective-permute-start(bf16[128,4608]{1,0:T(8,128)(2,1)S(1)} %fusion), channel_id=1, source_target_pairs={{0,8},{24,16},{1,9},{25,17},{2,10},{26,18},{3,11},{27,19},{4,12},{... | collective-permute-start | bytes 3538952 | tf_op jit(solution)/shard_map/ppermute | solution.py:640
  625.3 45.7 %collective-permute-start.33 = (bf16[128,4608]{1,0:T(8,128)(2,1)S(1)}, bf16[128,4608]{1,0:T(8,128)(2,1)S(1)}, u32[]{:S(2)}, u32[]{:S(2)}) collective-permute-start(bf16[128,4608]{1,0:T(8,128)(2,1)S(1)} %fusion.1), channel_id=1, source_target_pairs={{0,8},{24,16},{1,9},{25,17},{2,10},{26,18},{3,11},{27,19},{4,12},{... | collective-permute-start | bytes 3538952 | tf_op jit(solution)/shard_map/ppermute | solution.py:640
  651.3 20.7 %collective-permute-start.40 = (bf16[128,4608]{1,0:T(8,128)(2,1)S(1)}, bf16[128,4608]{1,0:T(8,128)(2,1)S(1)}, u32[]{:S(2)}, u32[]{:S(2)}) collective-permute-start(bf16[128,4608]{1,0:T(8,128)(2,1)S(1)} %add_convert_fusion.5), channel_id=1, source_target_pairs={{8,16},{16,8},{9,17},{17,9},{10,18},{18,10},{11,19},{19,11},{12,20... | collective-permute-start | bytes 3538952 | tf_op jit(solution)/shard_map/ppermute | solution.py:641
  671.3 2.3 collective-permute-start.34
  672.3 31.7 %collective-permute-start.41 = (bf16[128,4608]{1,0:T(8,128)(2,1)S(1)}, bf16[128,4608]{1,0:T(8,128)(2,1)S(1)}, u32[]{:S(2)}, u32[]{:S(2)}) collective-permute-start(bf16[128,4608]{1,0:T(8,128)(2,1)S(1)} %add_convert_fusion.4), channel_id=1, source_target_pairs={{8,0},{16,24},{9,1},{17,25},{10,2},{18,26},{11,3},{19,27},{12,4},{... | collective-permute-start | bytes 3538952 | tf_op jit(solution)/shard_map/ppermute | solution.py:642
  673.9 50.7 %collective-permute-start.35 = (bf16[128,4608]{1,0:T(8,128)(2,1)S(1)}, bf16[128,4608]{1,0:T(8,128)(2,1)S(1)}, u32[]{:S(2)}, u32[]{:S(2)}) collective-permute-start(bf16[128,4608]{1,0:T(8,128)(2,1)S(1)} %add_convert_fusion.10), channel_id=1, source_target_pairs={{8,0},{16,24},{9,1},{17,25},{10,2},{18,26},{11,3},{19,27},{12,4},{... | collective-permute-start | bytes 3538952 | tf_op jit(solution)/shard_map/ppermute | solution.py:642
  (11 other events, 20.4 us)

commit v3 on v2

v3 whole, which is shorter than its diff:
```python
import functools

import jax
import jax.numpy as jnp
from jax import lax
from jax.experimental import pallas as pl
from jax.experimental.pallas import tpu as pltpu
from jax.sharding import PartitionSpec as P

EPSILON = 1e-05
ROPE_BASE = 1000000.0
LOG2E = 1.4426950408889634
BF = jnp.bfloat16
F32 = jnp.float32
VMEM = pl.BlockSpec(memory_space=pltpu.VMEM)
SMEM = pl.BlockSpec(memory_space=pltpu.SMEM)
ANY = pl.BlockSpec(memory_space=pl.ANY)
VMEM_BYTES = 62 * 2**20


def dot_nn(a, b):
    return lax.dot_general(a, b, (((1,), (0,)), ((), ())), preferred_element_type=F32)


def dot_nt(a, b):
    return lax.dot_general(a, b, (((1,), (1,)), ((), ())), preferred_element_type=F32)


def dot_tn(a, b):
    return lax.dot_general(a, b, (((0,), (0,)), ((), ())), preferred_element_type=F32)


def shape_of(shape, dtype):
    return jax.ShapeDtypeStruct(shape, dtype)


def call(kernel, outs, in_specs, out_specs, scratch, flops, moved, collective=None, **more):
    params = {} if collective is None else {"collective_id": collective, "has_side_effects": True}
    return pl.pallas_call(
        kernel,
        out_shape=outs,
        in_specs=in_specs,
        out_specs=out_specs,
        scratch_shapes=scratch,
        compiler_params=pltpu.CompilerParams(vmem_limit_bytes=VMEM_BYTES, **params),
        cost_estimate=pl.CostEstimate(flops=flops, bytes_accessed=moved, transcendentals=0),
        **more,
    )


def row_norm(values):
    return lax.rsqrt(jnp.mean(values * values, axis=-1, keepdims=True) + EPSILON)


class Fetch:
    def __init__(self, sems):
        self.sems, self.used = sems, 0

    def start(self, source, target):
        copy = pltpu.make_async_copy(source, target, self.sems.at[self.used])
        copy.start()
        self.used += 1
        return copy


def wait_all(copies):
    for copy in copies:
        copy.wait()


def head_mask(width, head_dim):
    rows = lax.broadcasted_iota(jnp.int32, (width, width), 0) // head_dim
    cols = lax.broadcasted_iota(jnp.int32, (width, width), 1) // head_dim
    return (rows == cols).astype(BF)


def head_sum(values, mask):
    high = values.astype(BF)
    rest = (values - high.astype(F32)).astype(BF)
    return dot_nn(high, mask) + dot_nn(rest, mask)


def partner(values, head_dim):
    half = head_dim // 2
    width = values.shape[-1]
    lane = lax.broadcasted_iota(jnp.int32, values.shape, 1)
    after = pltpu.roll(values, width - half, 1)
    before = pltpu.roll(values, half, 1)
    return jnp.where(lane % head_dim < half, after, before)


def pack_blocks(z, nz, source, blocks, widths):
    for j, block in enumerate(blocks):
        owner = z ^ j
        base, at = 0, 0
        for width in widths:
            part = width // nz
            block[:, at : at + part] = source[:, pl.ds(pl.multiple_of(base + owner * part, part), part)]
            base, at = base + width, at + part


class Links:
    def __init__(self, send_sems, recv_sems):
        self.sems, self.used, self.started = (send_sems, recv_sems), 0, []

    def reserve(self, count):
        self.used += count
        return self.used - count

    def copy(self, source, target, device, at=None):
        at = self.reserve(1) if at is None else at
        return pltpu.make_async_remote_copy(
            src_ref=source,
            dst_ref=target,
            send_sem=self.sems[0].at[at],
            recv_sem=self.sems[1].at[at],
            device_id=device,
            device_id_type=pl.DeviceIdType.MESH,
        )

    def start(self, source, target, device):
        copy = self.copy(source, target, device)
        copy.start()
        self.started.append(copy)
        return copy

    def wait_sends(self):
        for copy in self.started:
            copy.wait_send()


def enter(me, z, nz, plane):
    barrier = pltpu.get_barrier_semaphore()
    peers = [{"seq": z ^ j} for j in range(1, nz)]
    if plane:
        peers += [{"fsdp": me ^ bit} for bit in (1, 2, 4)]
    for peer in peers:
        pl.semaphore_signal(barrier, inc=1, device_id=peer, device_id_type=pl.DeviceIdType.MESH)
    pl.semaphore_wait(barrier, len(peers))


class Gather:
    def __init__(self, links, me, own, whole, x_first):
        self.links, self.me, self.own, self.whole = links, me, own, whole
        self.rows = own.shape[0]
        self.near, self.other = (2, 4) if x_first else (4, 2)

    def block(self, b):
        return self.whole.at[pl.ds(pl.multiple_of((self.me ^ b) * self.rows, self.rows), self.rows)]

    def pass_on(self, b, bit):
        source = self.own if b == 0 else self.block(b)
        return self.links.start(source, self.block(b), {"fsdp": self.me ^ bit})

    def begin(self):
        self.first = self.pass_on(0, self.near)
        self.second = self.pass_on(0, self.other)
        self.to_core = [self.pass_on(0, 1)]

    def forward_first(self):
        self.first.wait_recv()
        self.far = self.pass_on(self.near, self.other)
        self.to_core.append(self.pass_on(self.near, 1))

    def forward_second(self):
        self.second.wait_recv()
        self.to_core.append(self.pass_on(self.other, 1))

    def forward_far(self):
        self.far.wait_recv()
        self.to_core.append(self.pass_on(self.near + self.other, 1))

    def end(self):
        for copy in self.to_core:
            copy.wait_recv()


def forward_first(gathers):
    for gather in gathers:
        gather.forward_first()
    for gather in gathers:
        gather.forward_second()


def forward_far(gathers):
    for gather in gathers:
        gather.forward_far()


def forward_kernel(dims, x_ref, cos_ref, sin_ref, *refs):
    nz, plane, head_dim, q_cols, k_cols, v_cols, rows = dims
    n_in = 5 if plane else 3
    given, refs = refs[:n_in], refs[n_in:]
    gains_ref, proj_ref, heads_ref, mixed_ref, log_ref, normed_t_hbm = refs[:6]
    refs = refs[6:]
    if plane:
        qk_hbm, vo_hbm, gate_hbm, up_hbm, down_hbm = refs[:5]
        refs = refs[5:]
    w_qk, w_vo, normed, normed_t, qkv, queries, keys, values, full, mix, local_sems, send_sems, recv_sems = refs
    z, me = lax.axis_index("seq"), lax.axis_index("fsdp")
    model = w_vo.shape[0]
    tokens = x_ref.shape[0]
    enter(me, z, nz, plane)
    links = Links(send_sems, recv_sems)
    local = []

    def copy_here(source, target):
        copy = pltpu.make_async_copy(source, target, local_sems.at[len(local)])
        copy.start()
        local.append(copy)
        return copy

    if plane:
        own_qk, own_vo, own_gate, own_up, own_down = given
        half = own_down.shape[0] // 2
        attention = [Gather(links, me, own_qk, w_qk, True), Gather(links, me, own_vo, w_vo, False)]
        wide = [Gather(links, me, own_gate, gate_hbm, True), Gather(links, me, own_up, up_hbm, False)]
        for gather in attention:
            gather.begin()
        here = [copy_here(g.own, g.block(0)) for g in attention]
        down = []
        for side in range(2):
            g = Gather(links, me, own_down.at[pl.ds(side * half, half)], down_hbm.at[side], side == 0)
            down.append(g)
    else:
        here = [copy_here(given[0], w_qk), copy_here(given[1], w_vo)]
    x = x_ref[...].astype(F32)
    unit = x * row_norm(x)
    if plane:
        forward_first(attention)
        for gather in wide:
            gather.begin()
        for g in wide:
            copy_here(g.own, g.block(0))
        forward_far(attention)
        for g in attention:
            g.end()
        wait_all(here)
        stride = attention[0].rows
        shard = w_vo.shape[0] // 8
        gains = sum(w_qk[s * stride + shard : (s + 1) * stride].astype(F32) for s in range(8))
        for s in range(8):
            copy_here(w_qk.at[pl.ds(s * stride, shard)], qk_hbm.at[pl.ds(s * shard, shard)])
        copy_here(w_vo, vo_hbm)
    else:
        stride = shard = model
        wait_all(here)
        gains = given[2][...].astype(F32)
    gains_ref[...] = gains
    normed[...] = (unit * gains[0:1, :model]).astype(BF)
    width = 256
    mask = head_mask(width, head_dim)
    cos = jnp.concatenate([cos_ref[...]] * (width // 128), axis=1)
    sin = jnp.concatenate([sin_ref[...]] * (width // 128), axis=1)

    for start in range(0, q_cols + k_cols, width):
        cols = slice(start, start + width)
        if stride == shard:
            proj = dot_nn(normed[...], w_qk[:, cols])
        else:
            weight = jnp.concatenate([w_qk[s * stride : s * stride + shard, cols] for s in range(8)], axis=0)
            proj = dot_nn(normed[...], weight)
        proj_ref[:, cols] = proj
        scale = lax.rsqrt(head_sum(proj * proj, mask) * (1.0 / head_dim) + EPSILON)
        head = proj * scale * gains_ref[1:2, cols]
        qkv[:, cols] = (head * cos + partner(head, head_dim) * sin).astype(BF)
    qkv[:, q_cols + k_cols :] = dot_nn(normed[...], w_vo[:, :v_cols]).astype(BF)

    arrivals = []
    for j in range(nz):
        owner = z ^ j
        base, at = 0, 0
        for cols in (q_cols, k_cols, v_cols):
            part = cols // nz
            source = qkv.at[:, pl.ds(pl.multiple_of(base + owner * part, part), part)]
            target = heads_ref.at[pl.ds(pl.multiple_of(z * tokens, tokens), tokens), pl.ds(at, part)]
            if j == 0:
                arrivals.append(copy_here(source, target))
            else:
                arrivals.append(links.start(source, target, {"seq": owner}))
            base, at = base + cols, at + part
    normed_t[...] = normed[...].T
    if plane:
        to_core = both_cores(links, copy_here, me, normed_t, normed_t_hbm, 1)
        forward_first(wide)
        for gather in down:
            gather.begin()
        for g in down:
            copy_here(g.own, g.block(0))
    else:
        copy_here(normed_t, normed_t_hbm)
    for i, copy in enumerate(arrivals):
        if i < 3:
            copy.wait()
        else:
            copy.wait_recv()

    heads, seq_len, _ = queries.shape
    kv_heads = keys.shape[0]
    group = heads // kv_heads
    split_heads(heads_ref, 0, queries)
    split_heads(heads_ref, heads * head_dim, keys)
    split_heads(heads_ref, (heads + kv_heads) * head_dim, values)
    factor = head_dim**-0.5 * LOG2E
    part = mix.shape[1]
    first_back = links.reserve(nz)
    own_mix = local_sems.shape[0] - 1
    for r in range(seq_len // rows):
        span = slice(r * rows, (r + 1) * rows)
        reach = (r + 1) * rows

        def one_head(h, _):
            b = lax.div(h, group)
            scores = dot_nt(queries[h, span], keys[b, :reach]) * factor
            row = lax.broadcasted_iota(jnp.int32, scores.shape, 0) + r * rows
            col = lax.broadcasted_iota(jnp.int32, scores.shape, 1)
            probs = jnp.exp2(jnp.where(row >= col, scores, -1e30))
            total = jnp.sum(probs, axis=1, keepdims=True)
            full[h, span] = (dot_nn(probs.astype(BF), values[b, :reach]) * (1.0 / total)).astype(BF)
            log_ref[h, :, span] = jnp.broadcast_to(jnp.log2(total), (rows, 128)).T[0:8]
            return 0

        lax.fori_loop(0, heads, one_head, 0)
        if reach % tokens == 0:
            t = reach // tokens - 1
            mine = slice(t * tokens, reach)
            mix[mine] = jnp.concatenate([full[h, mine] for h in range(heads)], axis=1)
            target = mixed_ref.at[:, pl.ds(pl.multiple_of(z * part, part), part)]

            @pl.when(z == t)
            def _():
                pltpu.make_async_copy(mix.at[mine], target, local_sems.at[own_mix]).start()

            @pl.when(z != t)
            def _():
                links.copy(mix.at[mine], target, {"seq": t}, at=first_back + (z ^ t)).start()

    if plane:
        forward_far(wide)
        forward_first(down)
        forward_far(down)
        for gather in wide + down:
            gather.end()
        to_core.wait_recv()
    here_rows = mix.at[pl.ds(0, tokens)]
    here_cols = mixed_ref.at[:, pl.ds(0, part)]
    pltpu.make_async_copy(here_rows, here_cols, local_sems.at[own_mix]).wait()
    for j in range(1, nz):
        copy = links.copy(here_rows, here_cols, {"seq": z ^ j}, at=first_back + j)
        copy.wait_recv()
        copy.wait_send()
    links.wait_sends()
    for copy in local:
        if not any(copy is done for done in here + arrivals[:3]):
            copy.wait()


def both_cores(links, copy_here, me, source, target, axis):
    size = source.shape[axis]
    here = pl.ds(pl.multiple_of(lax.rem(me, 2) * size, size), size)
    place = target.at[here] if axis == 0 else target.at[:, here]
    copy_here(source, place)
    return links.start(source, place, {"fsdp": me ^ 1})


def split_heads(scratch, first, heads):
    head_dim = heads.shape[-1]
    for h in range(heads.shape[0]):
        heads[h] = scratch[:, first + h * head_dim : first + (h + 1) * head_dim]


def attend_back(dims, heads_ref, grads_ref, log_ref, delta_ref, packed, scratch, after):
    rows, chunk = dims
    queries, keys, values, grad, q_grad, k_grad, v_grad = scratch
    heads, seq_len, head_dim = queries.shape
    kv_heads = keys.shape[0]
    group = heads // kv_heads
    split_heads(heads_ref, 0, queries)
    split_heads(heads_ref, heads * head_dim, keys)
    split_heads(heads_ref, (heads + kv_heads) * head_dim, values)
    split_heads(grads_ref, 0, grad)
    factor = head_dim**-0.5
    scale = factor * LOG2E
    for h in range(heads):
        q_grad[h] = jnp.zeros((seq_len, head_dim), F32)
    for at in range(seq_len // rows):
        span = slice(at * rows, (at + 1) * rows)

        def one_head(b, _):
            key, value = keys[b, span], values[b, span]
            key_total = jnp.zeros((rows, head_dim), F32)
            value_total = jnp.zeros((rows, head_dim), F32)
            for g in range(group):
                h = b * group + g
                for first in range(at * rows, seq_len, chunk):
                    last = min(first + chunk, seq_len)
                    part = slice(first, last)
                    query, out_grad = queries[h, part], grad[h, part]
                    scores = dot_nt(key, query) * scale - log_ref[h, 0:1, part]
                    if first == at * rows:
                        key_at = lax.broadcasted_iota(jnp.int32, scores.shape, 0) + at * rows
                        query_at = lax.broadcasted_iota(jnp.int32, scores.shape, 1) + first
                        scores = jnp.where(query_at >= key_at, scores, -1e30)
                    probs = jnp.exp2(scores)
                    prob_grad = dot_nt(value, out_grad)
                    score_grad = (probs * (prob_grad - delta_ref[h, 0:1, part])).astype(BF)
                    value_total = value_total + dot_nn(probs.astype(BF), out_grad)
                    key_total = key_total + dot_nn(score_grad, query)
                    q_grad[h, part] = q_grad[h, part] + dot_tn(score_grad, key)
            k_grad[b, span] = (key_total * factor).astype(BF)
            v_grad[b, span] = value_total.astype(BF)
            return 0

        lax.fori_loop(0, kv_heads, one_head, 0)
        parts = [(q_grad[h, span] * factor).astype(BF) for h in range(heads)]
        parts += [k_grad[b, span] for b in range(kv_heads)] + [v_grad[b, span] for b in range(kv_heads)]
        packed[span] = jnp.concatenate(parts, axis=1)
        after(at)


def attend_back_scratch(heads, kv_heads, seq_len, head_dim):
    rows = lambda count, kind: pltpu.VMEM((count, seq_len, head_dim), kind)
    return [rows(heads, BF), rows(kv_heads, BF), rows(kv_heads, BF), rows(heads, BF), rows(heads, F32), rows(kv_heads, BF), rows(kv_heads, BF)]


def attend_back_kernel(dims, heads_ref, grads_ref, log_ref, delta_ref, packed, *scratch):
    attend_back(dims, heads_ref, grads_ref, log_ref, delta_ref, packed, scratch, lambda at: None)


def norm_back(rows, gain, gradient):
    q = row_norm(rows)
    n = rows * q
    u = gradient * gain
    return q * (u - n * jnp.mean(u * n, axis=-1, keepdims=True)), jnp.sum(gradient * n, axis=0, keepdims=True)


def feed_kernel(dims, x_ref, dy_ref, gains_ref, mixed, *refs):
    nz, plane, head_dim, out_cols, width, groups = dims
    vo_hbm, gate_hbm, up_hbm, down_hbm = refs[:4]
    output_ref, middle_grad_ref, middle_low_ref, gain_grad_ref, grad_low, delta_ref = refs[4:10]
    mixed_t_hbm, normed_t_hbm, hidden_hbm, gate_grad_hbm, up_grad_hbm, dy_hbm = refs[10:16]
    w_out, w_gate, w_up, w_down, transposed, middle, normed, back = refs[16:24]
    hidden_slot, gate_slot, up_slot, sems, slot_sems, send_sems, recv_sems, slot_sends, block_recvs = refs[24:]
    me = lax.axis_index("fsdp")
    tokens = x_ref.shape[0]
    core = lax.rem(me, 2) if plane else 0
    place = pl.ds(pl.multiple_of(core * tokens, tokens), tokens)
    sibling = {"fsdp": me ^ 1}
    links = Links(send_sems, recv_sems)
    if plane:
        barrier = pltpu.get_barrier_semaphore()
        pl.semaphore_signal(barrier, inc=1, device_id=sibling, device_id_type=pl.DeviceIdType.MESH)
        pl.semaphore_wait(barrier, 1)
    local, to_core = [], []

    def share(source, target):
        local.append(fetch.start(source, target))
        if plane:
            to_core.append(links.start(source, target, sibling))

    fetch = Fetch(sems)
    model, hidden_cols = w_gate.shape
    gain = gains_ref[2:3, :model]
    early = [fetch.start(vo_hbm.at[:, pl.ds(*out_cols)], w_out)]
    down_copies = []
    if len(down_hbm.shape) == 2:
        down_copies.append(fetch.start(down_hbm, w_down))
    else:
        half = hidden_cols // 16
        for owner in range(8):
            for side in range(2):
                target = w_down.at[pl.ds((2 * owner + side) * half, half)]
                down_copies.append(fetch.start(down_hbm.at[side, pl.ds(owner * half, half)], target))
    group_cols = hidden_cols // groups
    group_copies = []
    for g in range(groups):
        cols = pl.ds(g * group_cols, group_cols)
        group_copies.append([fetch.start(a.at[:, cols], b.at[:, cols]) for a, b in ((gate_hbm, w_gate), (up_hbm, w_up))])
    wait_all(early)
    x = x_ref[...].astype(F32)
    mixed_rows = mixed[...]
    transposed[0] = mixed_rows.T
    share(transposed.at[0], mixed_t_hbm.at[:, place])
    share(dy_ref, dy_hbm.at[place])
    middle_rows = x + dot_nn(mixed_rows, w_out[...])
    normed_rows = (middle_rows * row_norm(middle_rows) * gain).astype(BF)
    normed[...] = normed_rows
    transposed[1] = normed_rows.T
    share(transposed.at[1], normed_t_hbm.at[:, place])
    middle[...] = middle_rows
    back[...] = jnp.zeros(back.shape, F32)
    wait_all(down_copies)

    def slot_places(f):
        here = pl.ds(pl.multiple_of(f * width, width), width)
        return (
            (hidden_slot, hidden_hbm.at[here, place]),
            (gate_slot, gate_grad_hbm.at[place, here]),
            (up_slot, up_grad_hbm.at[place, here]),
        )

    def slot_copies(slot, f):
        return [
            pltpu.make_async_copy(s.at[slot], target, slot_sems.at[slot, i]) for i, (s, target) in enumerate(slot_places(f))
        ]

    def slot_links(slot, f):
        if not plane:
            return []
        return [
            pltpu.make_async_remote_copy(
                src_ref=s.at[slot],
                dst_ref=target,
                send_sem=slot_sends.at[slot, i],
                recv_sem=block_recvs.at[f, i],
                device_id=sibling,
                device_id_type=pl.DeviceIdType.MESH,
            )
            for i, (s, target) in enumerate(slot_places(f))
        ]

    def wait_slot(slot, f):
        wait_all(slot_copies(slot, f))
        for copy in slot_links(slot, f):
            copy.wait_send()

    def one_block(f, _):
        slot = lax.rem(f, 2)
        here = pl.ds(pl.multiple_of(f * width, width), width)

        @pl.when(f >= 2)
        def _():
            wait_slot(slot, f - 2)

        gate = dot_nn(normed[...], w_gate[:, here])
        up = dot_nn(normed[...], w_up[:, here])
        hidden_grad = dot_nt(dy_ref[...], w_down[here])
        s = 1.0 / (1.0 + jnp.exp(-gate))
        silu = gate * s
        hidden = (silu * up).astype(BF)
        gate_grad = (hidden_grad * up * (s * (1.0 + gate * (1.0 - s)))).astype(BF)
        up_grad = (hidden_grad * silu).astype(BF)
        hidden_slot[slot] = hidden.T
        gate_slot[slot] = gate_grad
        up_slot[slot] = up_grad
        for copy in slot_copies(slot, f) + slot_links(slot, f):
            copy.start()
        middle[...] = middle[...] + dot_nn(hidden, w_down[here])
        back[...] = back[...] + (dot_nt(gate_grad, w_gate[:, here]) + dot_nt(up_grad, w_up[:, here]))
        return 0

    blocks = hidden_cols // width
    per_group = blocks // groups
    for g in range(groups):
        wait_all(group_copies[g])
        lax.fori_loop(g * per_group, (g + 1) * per_group, one_block, 0)
    output_ref[...] = middle[...].astype(BF)
    middle_rows = x_ref[...].astype(F32) + dot_nn(mixed[...], w_out[...])
    part, gain_sum = norm_back(middle_rows, gain, back[...])
    gain_grad_ref[...] = gain_sum
    middle_grad = dy_ref[...].astype(F32) + part
    middle_grad_ref[...] = middle_grad
    middle_low = middle_grad.astype(BF)
    middle_low_ref[...] = middle_low
    mixed_grad = dot_nt(middle_low, w_out[...]).astype(BF)
    grad_low[...] = mixed_grad
    product = mixed_grad.astype(F32) * mixed[...].astype(F32)
    heads = mixed.shape[1] // head_dim // nz
    row = lax.broadcasted_iota(jnp.int32, (8 * nz, mixed.shape[1]), 0)
    col = lax.broadcasted_iota(jnp.int32, (8 * nz, mixed.shape[1]), 1)
    pick = ((col // head_dim == (row // 8) * heads + row % 8) & (row % 8 < heads)).astype(BF)
    high = product.astype(BF)
    delta_ref[...] = dot_nt(pick, high) + dot_nt(pick, (product - high.astype(F32)).astype(BF))
    for f in (blocks - 2, blocks - 1):
        wait_slot(f % 2, f)
    if plane:
        for f in range(blocks):
            for copy in slot_links(f % 2, f):
                copy.wait_recv()
        for copy in to_core:
            copy.wait_recv()
        links.wait_sends()
    wait_all(local)


def weight_grad_kernel(left_ref, right_ref, out_ref):
    out_ref[...] = dot_nn(left_ref[...], right_ref[...]).astype(BF)


def weight_grad(left, right, width=256):
    rows, tokens = left.shape
    cols = right.shape[1]
    return call(
        weight_grad_kernel,
        shape_of((rows, cols), BF),
        [pl.BlockSpec((rows, tokens), lambda n: (0, 0)), pl.BlockSpec((tokens, width), lambda n: (0, n))],
        pl.BlockSpec((rows, width), lambda n: (0, n)),
        [],
        2 * rows * tokens * cols,
        2 * (rows * tokens + tokens * cols + rows * cols),
        grid=(cols // width,),
    )(left, right)


def project_back(dims, x, middle_grad, gains_ref, cos_ref, sin_ref, proj_ref, qkv, weights, outs):
    head_dim, wide_cols = dims
    w_qk, w_v = weights
    input_grad_ref, gain_grad_ref, head_gain_grad_ref = outs
    width = 256
    mask = head_mask(width, head_dim)
    cos = jnp.concatenate([cos_ref[...]] * (width // 128), axis=1)
    sin = jnp.concatenate([sin_ref[...]] * (width // 128), axis=1)
    for start in range(0, wide_cols, width):
        cols = slice(start, start + width)
        rotated = qkv[:, cols].astype(F32)
        gradient = rotated * cos - partner(rotated, head_dim) * sin
        proj = proj_ref[:, cols]
        scale = lax.rsqrt(head_sum(proj * proj, mask) * (1.0 / head_dim) + EPSILON)
        n = proj * scale
        u = gradient * gains_ref[1:2, cols]
        head_gain_grad_ref[:, cols] = jnp.sum(gradient * n, axis=0, keepdims=True)
        qkv[:, cols] = (scale * (u - n * (head_sum(u * n, mask) * (1.0 / head_dim)))).astype(BF)

    def finish():
        normed_grad = dot_nt(qkv[:, :wide_cols], w_qk[...]) + dot_nt(qkv[:, wide_cols:], w_v[...])
        part, gain_sum = norm_back(x[...].astype(F32), gains_ref[0:1, : x.shape[1]], normed_grad)
        gain_grad_ref[...] = gain_sum
        input_grad_ref[...] = (middle_grad[...] + part).astype(BF)

    return finish


def post_kernel(dims, x_ref, middle_grad_ref, gains_ref, cos_ref, sin_ref, proj_ref, grads_ref, qk_ref, v_ref, *refs):
    input_grad_ref, qkv, gain_grad_ref, head_gain_grad_ref = refs
    qkv[...] = grads_ref[...]
    outs = (input_grad_ref, gain_grad_ref, head_gain_grad_ref)
    project_back(
        dims, x_ref, middle_grad_ref, gains_ref, cos_ref, sin_ref, proj_ref, qkv, (qk_ref, v_ref), outs
    )()


class Reduce:
    def __init__(self, links, fetch, me, z, x_first, away, kept, first, second, inward, across, out):
        self.links, self.fetch, self.me, self.z = links, fetch, me, z
        self.away, self.kept, self.out = away, kept, out
        self.bits = (2, 4) if x_first else (4, 2)
        order = (1, 3, 0, 2) if x_first else (2, 3, 0, 1)
        self.slots = {r: (away if i < 2 else kept, i % 2) for i, r in enumerate(order)}
        self.arrived, self.second, self.inward, self.across = first, second, inward, across
        self.outer, self.inner = (z == 0) | (z == 3), (z == 1) | (z == 2)
        self.one = links.copy(away, first, {"fsdp": me ^ self.bits[0]})
        self.two = links.copy(kept.at[1], second, {"fsdp": me ^ self.bits[1]})
        self.three = links.copy(kept.at[0], inward, {"seq": z ^ 1})
        self.four = links.copy(kept.at[0], across, {"seq": z ^ 3})
        self.five = links.copy(kept.at[1], out, {"seq": z ^ 1})

    def put(self, r, cols, values):
        ref, i = self.slots[r]
        ref[i, :, cols] = values

    def rows_of(self):
        rows = self.kept.shape[1]
        step = 32 if rows % 32 == 0 else 16
        return rows // step, step

    def by_rows(self, work):
        count, step = self.rows_of()

        def body(i, _):
            work(pl.ds(pl.multiple_of(i * step, step), step))
            return 0

        lax.fori_loop(0, count, body, 0)

    def begin(self):
        self.one.start()

    def fold_one(self):
        self.one.wait_recv()
        self.one.wait_send()
        load = self.fetch.start(self.arrived, self.away)
        load.wait()

        def work(rows):
            for i in range(2):
                self.kept[i, rows] = self.kept[i, rows] + self.away[i, rows]

        self.by_rows(work)
        self.two.start()

    def fold_two(self):
        self.two.wait_recv()

        def work(rows):
            self.kept[0, rows] = self.kept[0, rows] + self.second[rows]

        self.by_rows(work)

        @pl.when(self.outer)
        def _():
            self.three.start()

    def fold_three(self):
        @pl.when(self.inner)
        def _():
            self.three.wait_recv()

            def work(rows):
                self.kept[0, rows] = self.kept[0, rows] + self.inward[rows]

            self.by_rows(work)
            self.four.start()

    def fold_four(self):
        self.two.wait_send()
        here = pltpu.make_async_copy(self.kept.at[1], self.out, self.fetch.sems.at[self.fetch.used])
        self.fetch.used += 1

        @pl.when(self.inner)
        def _():
            self.four.wait_recv()

            def work(rows):
                self.kept[1, rows] = self.kept[0, rows] + self.across[rows]

            self.by_rows(work)
            self.five.start()
            here.start()

        self.here = here

    def end(self):
        @pl.when(self.inner)
        def _():
            self.four.wait_send()
            self.five.wait_send()
            self.here.wait()

        @pl.when(self.outer)
        def _():
            self.three.wait_send()
            self.five.wait_recv()


def each(reduces, step):
    for reduce in reduces:
        getattr(reduce, step)()


class Total:
    def __init__(self, links, me, z, sums, arrived):
        self.sums, self.arrived = sums, arrived
        peers = [{"fsdp": me ^ 1}, {"fsdp": me ^ 2}, {"fsdp": me ^ 4}, {"seq": z ^ 1}, {"seq": z ^ 2}]
        self.copies = [links.copy(sums.at[i], arrived.at[i], peer) for i, peer in enumerate(peers)]

    def begin(self, at):
        self.copies[at].start()

    def fold(self, at):
        self.copies[at].wait_recv()
        self.sums[at + 1] = self.sums[at] + self.arrived[at]

    def end(self):
        for copy in self.copies:
            copy.wait_send()


def backward_kernel(dims, gains_ref, cos_ref, sin_ref, heads_ref, log_ref, grad_low, delta_own, low_ref, feed_gain_ref, *refs):
    nz, head_dim, cols, attend_dims, names = dims
    q_cols, k_cols, v_cols = cols
    given, refs = refs[:12], refs[12:]
    x_hbm, middle_grad_hbm, proj_hbm, hidden_hbm, dy_hbm, normed_two_hbm = given[:6]
    gate_hbm, up_hbm, mixed_hbm, normed_hbm, qk_hbm, vo_hbm = given[6:]
    input_grad_ref, totals_ref = refs[:2]
    n = len(names)
    finals, refs = dict(zip(names, refs[2 : 2 + n])), refs[2 + n :]
    firsts, refs = dict(zip(names, refs[:n])), refs[n:]
    low_hbm, refs = refs[0], refs[1:]
    aways, refs = dict(zip(names, refs[:n])), refs[n:]
    kepts, refs = dict(zip(names, refs[:n])), refs[n:]
    seconds, refs = dict(zip(names, refs[:n])), refs[n:]
    inwards, refs = dict(zip(names, refs[:n])), refs[n:]
    acrosses, refs = dict(zip(names, refs[:n])), refs[n:]
    grads, delta, qkv, other_qkv, sums, sum_arrived, gain_grad, head_gain_grad, sems, send_sems, recv_sems = refs
    z, me = lax.axis_index("seq"), lax.axis_index("fsdp")
    chip, core = lax.div(me, 2), lax.rem(me, 2)
    enter(me, z, nz, True)
    links, fetch = Links(send_sems, recv_sems), Fetch(sems)
    tokens = grad_low.shape[0]
    late = []

    def copy_here(source, target):
        copy = fetch.start(source, target)
        late.append(copy)
        return copy

    part = grad_low.shape[1] // nz
    my_rows = pl.ds(pl.multiple_of(z * tokens, tokens), tokens)
    arrivals = []
    for j in range(nz):
        owner = z ^ j
        pairs = [(grad_low.at[:, pl.ds(pl.multiple_of(owner * part, part), part)], grads.at[my_rows])]
        pairs.append((delta_own.at[pl.ds(pl.multiple_of(owner * 8, 8), 8)], delta.at[:, my_rows]))
        for source, target in pairs:
            if j == 0:
                copy_here(source, target)
            else:
                arrivals.append(links.start(source, target, {"seq": owner}))
    low_arrival = both_cores(links, copy_here, me, low_ref, low_hbm, 0)
    reduces = {}
    for name in names:
        x_first = name in ("down0", "gate0", "up0", "out0", "q")
        reduces[name] = Reduce(
            links, fetch, me, z, x_first, aways[name], kepts[name], firsts[name], seconds[name], inwards[name],
            acrosses[name], finals[name],
        )
    down, gate, up, out = ([reduces[kind + str(i)] for i in range(2)] for kind in ("down", "gate", "up", "out"))
    last = [reduces["q"], reduces["kv"]]
    total = Total(links, me, z, sums, sum_arrived)
    qkv_link = links.copy(qkv, other_qkv, {"fsdp": me ^ 1})
    chips = 4
    step = 256

    def my_blocks(source, target, rows):
        copies = []
        for r in range(chips):
            owner = (chip ^ r) * 2 + core
            copies.append(fetch.start(source.at[pl.ds(pl.multiple_of(owner * rows, rows), rows)], target.at[pl.ds(r * rows, rows)]))
        return copies

    def weight_grads(hidden, dy, normed_two, right, mixed, low):
        half = down[0].kept.shape[1]
        shard = gate[0].kept.shape[1]
        width = right.shape[2]
        ready = my_blocks(hidden_hbm, hidden, 2 * half) + [fetch.start(dy_hbm, dy)]
        ready_two = my_blocks(normed_two_hbm, normed_two, shard)
        chunks = [
            (source, units, c) for source, units in ((gate_hbm, gate), (up_hbm, up)) for c in range(source.shape[1] // width)
        ]
        loads = {}

        def load(i):
            if i < len(chunks):
                source, _, c = chunks[i]
                loads[i] = fetch.start(source.at[:, pl.ds(c * width, width)], right.at[i % 2])

        load(0)
        load(1)
        ready_out = my_blocks(mixed_hbm, mixed, shard)
        wait_all(ready)

        def down_block(i, _):
            here = pl.ds(pl.multiple_of(i * step, step), step)
            for r in range(chips):
                got = dot_nn(hidden[2 * r * half : 2 * (r + 1) * half], dy[:, here]).astype(BF)
                for side in range(2):
                    down[side].put(r, here, got[side * half : (side + 1) * half])
            return 0

        lax.fori_loop(0, dy.shape[1] // step, down_block, 0)
        each(down, "begin")
        wait_all(ready_two)
        per_unit = gate[0].kept.shape[2] // width
        for i, (source, units, c) in enumerate(chunks):
            loads[i].wait()
            unit = units[c // per_unit]
            base = (c % per_unit) * width

            def wide_block(k, _):
                here = pl.ds(pl.multiple_of(k * step, step), step)
                to = pl.ds(pl.multiple_of(base + k * step, step), step)
                got = dot_nn(normed_two[...], right[i % 2, :, here]).astype(BF)
                for r in range(chips):
                    unit.put(r, to, got[r * shard : (r + 1) * shard])
                return 0

            lax.fori_loop(0, width // step, wide_block, 0)
            load(i + 2)
            if source is gate_hbm and (c + 1) % per_unit == 0:
                unit.begin()
        low_arrival.wait_recv()
        late[-1].wait()
        late.pop()
        fetch.start(low_hbm, low).wait()
        wait_all(ready_out)
        cols_out = out[0].kept.shape[2]
        for start in range(0, low.shape[1], step):
            got = dot_nn(mixed[...], low[:, start : start + step]).astype(BF)
            to = slice(start % cols_out, start % cols_out + step)
            for r in range(chips):
                out[start // cols_out].put(r, to, got[r * shard : (r + 1) * shard])

    half = kepts["down0"].shape[1]
    shard = kepts["gate0"].shape[1]
    both = 2 * tokens
    model = low_ref.shape[1]
    wide_part = kepts["gate0"].shape[2] // 3
    pl.run_scoped(
        weight_grads,
        pltpu.VMEM((2 * chips * half, both), BF),
        pltpu.VMEM((both, model), BF),
        pltpu.VMEM((chips * shard, both), BF),
        pltpu.VMEM((2, both, wide_part), BF),
        pltpu.VMEM((chips * shard, both), BF),
        pltpu.VMEM((both, model), BF),
    )
    for copy in arrivals:
        copy.wait_recv()
    wait_all(late)
    del late[:]

    seq_len, block_cols = heads_ref.shape
    rows, _ = attend_dims
    first_back = links.reserve(3 * nz)
    own_back = fetch.used
    fetch.used += 3
    widths = [c // nz for c in cols]
    bases = [0, q_cols, q_cols + k_cols]

    def pieces(source_rows, packed):
        at = 0
        for i in range(3):
            yield i, packed.at[source_rows, pl.ds(at, widths[i])], qkv.at[
                :, pl.ds(pl.multiple_of(bases[i] + z * widths[i], widths[i]), widths[i])
            ]
            at += widths[i]

    def attention(packed, delta_rows, *scratch):
        for h in range(delta_rows.shape[0]):
            delta_rows[h] = jnp.broadcast_to(delta[h : h + 1], (8, seq_len))

        def after(at):
            reach = (at + 1) * rows
            if reach % tokens == 0:
                t = reach // tokens - 1
                mine = pl.ds(t * tokens, tokens)

                @pl.when(z == t)
                def _():
                    for i, source, target in pieces(mine, packed):
                        pltpu.make_async_copy(source, target, sems.at[own_back + i]).start()

                @pl.when(z != t)
                def _():
                    for i, source, target in pieces(mine, packed):
                        links.copy(source, target, {"seq": t}, at=first_back + 3 * (z ^ t) + i).start()

            if at == 0:
                each(down, "fold_one")
                each(up, "begin")
                each(out, "begin")
            if at == 3:
                each(gate, "fold_one")

        attend_back(attend_dims, heads_ref, grads, log_ref, delta_rows, packed, scratch, after)
        each(down, "fold_two")
        for i, source, target in pieces(pl.ds(0, tokens), packed):
            pltpu.make_async_copy(source, target, sems.at[own_back + i]).wait()
            for j in range(1, nz):
                copy = links.copy(source, target, {"seq": z ^ j}, at=first_back + 3 * j + i)
                copy.wait_recv()
                copy.wait_send()

    heads = log_ref.shape[0]
    kv_heads = k_cols // head_dim // nz
    pl.run_scoped(
        attention,
        pltpu.VMEM((seq_len, block_cols), BF),
        pltpu.VMEM((heads, 8, seq_len), F32),
        *attend_back_scratch(heads, kv_heads, seq_len, head_dim),
    )

    def projections(w_qk, w_v, proj, x, middle_grad, normed, grads_out):
        ready = [fetch.start(proj_hbm, proj)]
        ready_two = [
            fetch.start(a, b)
            for a, b in ((qk_hbm, w_qk), (vo_hbm.at[:, pl.ds(0, v_cols)], w_v), (x_hbm, x), (middle_grad_hbm, middle_grad))
        ]
        ready_three = my_blocks(normed_hbm, normed, shard)
        wait_all(ready)
        outs = (input_grad_ref, gain_grad, head_gain_grad)
        finish = project_back(
            (head_dim, q_cols + k_cols), x, middle_grad, gains_ref, cos_ref, sin_ref, proj, qkv, (w_qk, w_v), outs
        )
        qkv_link.start()
        each(up, "fold_one")
        each(out, "fold_one")
        each(down, "fold_three")
        wait_all(ready_two)
        finish()
        row = jnp.concatenate([gain_grad[...], head_gain_grad[...], feed_gain_ref[...]], axis=1)
        sums[0] = jnp.broadcast_to(row, sums.shape[1:])
        total.begin(0)
        qkv_link.wait()
        wait_all(ready_three)
        mine = normed[:, pl.ds(pl.multiple_of(core * tokens, tokens), tokens)]
        theirs = normed[:, pl.ds(pl.multiple_of((1 - core) * tokens, tokens), tokens)]
        cols_out = last[0].kept.shape[2]
        for start in range(0, qkv.shape[1], step):
            here = slice(start, start + step)
            got = (dot_nn(mine, qkv[:, here]) + dot_nn(theirs, other_qkv[:, here])).astype(BF)
            to = slice(start % cols_out, start % cols_out + step)
            for r in range(chips):
                last[start // cols_out].put(r, to, got[r * shard : (r + 1) * shard])

    pl.run_scoped(
        projections,
        pltpu.VMEM((model, q_cols + k_cols), BF),
        pltpu.VMEM((model, v_cols), BF),
        pltpu.VMEM((tokens, q_cols + k_cols), F32),
        pltpu.VMEM((tokens, model), BF),
        pltpu.VMEM((tokens, model), F32),
        pltpu.VMEM((chips * shard, both), BF),
        pltpu.VMEM((8, 128), F32),
    )
    each(last, "begin")
    total.fold(0)
    total.begin(1)
    each(gate, "fold_two")
    total.fold(1)
    total.begin(2)
    each(out, "fold_two")
    each(last, "fold_one")
    total.fold(2)
    total.begin(3)
    each(up, "fold_two")
    each(down, "fold_four")
    each(gate, "fold_three")
    each(last, "fold_two")
    each(out, "fold_three")
    total.fold(3)
    total.begin(4)
    each(up, "fold_three")
    each(last, "fold_three")
    each(gate, "fold_four")
    each(out, "fold_four")
    total.fold(4)
    each(up, "fold_four")
    each(last, "fold_four")
    totals_ref[...] = sums[5]
    total.end()
    for name in names:
        reduces[name].end()
    links.wait_sends()


def add(a, b):
    return (a.astype(F32) + b.astype(F32)).astype(a.dtype)


def sum_line(values):
    size = lax.axis_size("seq")
    if size != 4:
        return lax.psum(values, "seq")
    z = lax.axis_index("seq")
    inner = add(values, lax.ppermute(values, "seq", [(0, 1), (3, 2)]))
    total = add(inner, lax.ppermute(inner, "seq", [(1, 2), (2, 1)]))
    outer = lax.ppermute(total, "seq", [(1, 0), (2, 3)])
    return jnp.where((z == 1) | (z == 2), total, outer)


def per_device(
    inputs,
    positions,
    cotangent,
    query_weight,
    key_weight,
    value_weight,
    out_weight,
    attention_gain,
    query_gain,
    key_gain,
    feedforward_gain,
    gate_weight,
    up_weight,
    down_weight,
):
    seqs, tokens, model = inputs.shape
    assert seqs == 1
    fsdp, nz = lax.axis_size("fsdp"), lax.axis_size("seq")
    me, z = lax.axis_index("fsdp"), lax.axis_index("seq")
    plane = fsdp == 8 and nz == 4
    both = 2 * tokens if plane else tokens
    x = inputs.reshape(tokens, model)
    dy = cotangent.reshape(tokens, model)
    head_dim = query_gain.shape[0] * fsdp
    q_cols, k_cols, v_cols = query_weight.shape[1], key_weight.shape[1], value_weight.shape[1]
    heads, kv_heads = q_cols // head_dim // nz, k_cols // head_dim // nz
    hidden_cols = gate_weight.shape[1]
    seq_len = tokens * nz

    first = jnp.concatenate([query_weight, key_weight], axis=1)
    second = jnp.concatenate([value_weight, out_weight], axis=1)
    wide_cols = q_cols + k_cols

    def spread(values, count):
        share = values.shape[0]
        row = lax.dynamic_update_slice(jnp.zeros((share * fsdp,), BF), values, (me * share,))
        return jnp.tile(row, count)

    head_row = jnp.concatenate([spread(query_gain, q_cols // head_dim), spread(key_gain, k_cols // head_dim)])
    fill = jnp.zeros((wide_cols - model,), BF)
    gain_rows = [jnp.concatenate([spread(attention_gain, 1), fill]), head_row]
    gain_rows += [jnp.concatenate([spread(feedforward_gain, 1), fill])] + [jnp.zeros((wide_cols,), BF)] * 13
    gain_rows = jnp.stack(gain_rows)
    if plane:
        given = [jnp.concatenate([first, gain_rows]), second, gate_weight, up_weight, down_weight]
    else:
        gather = functools.partial(lax.all_gather, axis_name="fsdp", axis=0, tiled=True)
        qk_full, vo_full, gate_full = gather(first), gather(second), gather(gate_weight)
        up_full, down_full = gather(up_weight), gather(down_weight)
        given = [qk_full, vo_full, lax.psum(gain_rows.astype(F32), "fsdp")]

    half_dim = head_dim // 2
    freqs = ROPE_BASE ** (-jnp.arange(half_dim, dtype=F32) / half_dim)
    angles = positions.reshape(tokens).astype(F32)[:, None] * freqs[None, :]
    cosine, sine = jnp.cos(angles), jnp.sin(angles)
    cosine = jnp.tile(cosine, (1, 128 // half_dim))
    sine = jnp.tile(jnp.concatenate([-sine, sine], axis=1), (1, 128 // head_dim))

    dims = (nz, plane, head_dim, q_cols, k_cols, v_cols, min(256, seq_len))
    block_cols = (q_cols + k_cols + v_cols) // nz
    mixed_cols = heads * head_dim
    head_scratch = [
        pltpu.VMEM((heads, seq_len, head_dim), BF),
        pltpu.VMEM((kv_heads, seq_len, head_dim), BF),
        pltpu.VMEM((kv_heads, seq_len, head_dim), BF),
    ]
    attend_flops = 2 * heads * seq_len * seq_len * head_dim
    proj_flops = 2 * tokens * model * (q_cols + k_cols + v_cols)
    outs = [
        shape_of((16, wide_cols), F32),
        shape_of((tokens, wide_cols), F32),
        shape_of((seq_len, block_cols), BF),
        shape_of((tokens, q_cols), BF),
        shape_of((heads, 8, seq_len), F32),
        shape_of((model, both), BF),
    ]
    n_links = 3 * (nz - 1) + nz + 1
    qk_rows = model
    if plane:
        hidden = gate_weight.shape[1]
        outs += [shape_of((model, wide_cols), BF), shape_of((model, v_cols + model), BF)]
        outs += [shape_of((model, hidden), BF)] * 2 + [shape_of((2, hidden // 2, model), BF)]
        n_links += 6 * 7
        qk_rows += 8 * 16
    got = call(
        functools.partial(forward_kernel, dims),
        outs,
        [VMEM] * 3 + ([ANY] * 5 if plane else [ANY] * 2 + [VMEM]),
        [VMEM] * 5 + [ANY] * (len(outs) - 5),
        [
            pltpu.VMEM((qk_rows, wide_cols), BF),
            pltpu.VMEM((model, v_cols + model), BF),
            pltpu.VMEM((tokens, model), BF),
            pltpu.VMEM((model, tokens), BF),
            pltpu.VMEM((tokens, q_cols + k_cols + v_cols), BF),
        ]
        + head_scratch
        + [
            pltpu.VMEM((heads, seq_len, head_dim), BF),
            pltpu.VMEM((seq_len, mixed_cols), BF),
            pltpu.SemaphoreType.DMA((24,)),
            pltpu.SemaphoreType.DMA((n_links,)),
            pltpu.SemaphoreType.DMA((n_links,)),
        ],
        proj_flops + 4 * attend_flops,
        60 * 2**20,
        collective=1,
    )(x, cosine, sine, *given)
    gains, proj, head_rows, mixed, logs, normed_t = got[:6]
    if plane:
        qk_full, vo_full, gate_full, up_full, down_full = got[6:]

    width = 512
    groups = 3
    rows_model = lambda kind: shape_of((tokens, model), kind)
    feed_out = call(
        functools.partial(feed_kernel, (nz, plane, head_dim, (v_cols, model), width, groups)),
        [
            rows_model(BF),
            rows_model(F32),
            rows_model(BF),
            shape_of((1, model), F32),
            shape_of((tokens, q_cols), BF),
            shape_of((8 * nz, tokens), F32),
            shape_of((q_cols, both), BF),
            shape_of((model, both), BF),
            shape_of((hidden_cols, both), BF),
            shape_of((both, hidden_cols), BF),
            shape_of((both, hidden_cols), BF),
            shape_of((both, model), BF),
        ],
        [VMEM] * 4 + [ANY] * 4,
        [VMEM] * 6 + [ANY] * 6,
        [
            pltpu.VMEM((q_cols, model), BF),
            pltpu.VMEM((model, hidden_cols), BF),
            pltpu.VMEM((model, hidden_cols), BF),
            pltpu.VMEM((hidden_cols, model), BF),
            pltpu.VMEM((2, model, tokens), BF),
            pltpu.VMEM((tokens, model), F32),
            pltpu.VMEM((tokens, model), BF),
            pltpu.VMEM((tokens, model), F32),
            pltpu.VMEM((2, width, tokens), BF),
            pltpu.VMEM((2, tokens, width), BF),
            pltpu.VMEM((2, tokens, width), BF),
            pltpu.SemaphoreType.DMA((20 + 2 * groups,)),
            pltpu.SemaphoreType.DMA((2, 3)),
            pltpu.SemaphoreType.DMA((3,)),
            pltpu.SemaphoreType.DMA((3,)),
            pltpu.SemaphoreType.DMA((2, 3)),
            pltpu.SemaphoreType.DMA((hidden_cols // width, 3)),
        ],
        12 * tokens * model * hidden_cols,
        50 * 2**20,
        collective=2 if plane else None,
    )(x, dy, gains, mixed, vo_full, gate_full, up_full, down_full)
    output, middle_grad, middle_low, feed_gain_part, mixed_grad, delta = feed_out[:6]
    mixed_t, normed_two_t, hidden_t, gate_grad, up_grad, dy_both = feed_out[6:]

    attend_dims = (min(256, seq_len), min(1024, seq_len))
    attend_scratch = attend_back_scratch(heads, kv_heads, seq_len, head_dim)
    if plane:
        down_rows, down_cols = down_weight.shape
        blocks = {"down0": (down_rows // 2, down_cols), "down1": (down_rows // 2, down_cols)}
        for name in ("gate0", "gate1", "up0", "up1"):
            blocks[name] = (gate_weight.shape[0], hidden_cols // 2)
        blocks["out0"] = blocks["out1"] = (out_weight.shape[0], model // 2)
        blocks["q"] = blocks["kv"] = (query_weight.shape[0], q_cols)
        assert k_cols + v_cols == q_cols
        names = tuple(blocks)
        pairs = [(2,) + shape for shape in blocks.values()]
        total_cols = model + wide_cols + model
        n_links = 2 * (nz - 1) + 3 * nz + 2 + 5 * len(names) + 5
        n_copies = 2 + 1 + 4 * 4 + 16 + 3 + 6 + 4 + 2 * len(names)
        got = call(
            functools.partial(backward_kernel, (nz, head_dim, (q_cols, k_cols, v_cols), attend_dims, names)),
            [rows_model(BF), shape_of((8, total_cols), F32)]
            + [shape_of(shape, BF) for shape in blocks.values()]
            + [shape_of(shape, BF) for shape in pairs]
            + [shape_of((both, model), BF)],
            [VMEM] * 9 + [ANY] * 12,
            [VMEM] * 2 + [ANY] * (2 * len(names) + 1),
            [pltpu.VMEM(shape, BF) for shape in pairs] * 2
            + [pltpu.VMEM(shape, BF) for shape in blocks.values()] * 3
            + [
                pltpu.VMEM((seq_len, mixed_cols), BF),
                pltpu.VMEM((8, seq_len), F32),
                pltpu.VMEM((tokens, q_cols + k_cols + v_cols), BF),
                pltpu.VMEM((tokens, q_cols + k_cols + v_cols), BF),
                pltpu.VMEM((6, 8, total_cols), F32),
                pltpu.VMEM((5, 8, total_cols), F32),
                pltpu.VMEM((1, model), F32),
                pltpu.VMEM((1, wide_cols), F32),
                pltpu.SemaphoreType.DMA((n_copies,)),
                pltpu.SemaphoreType.DMA((n_links,)),
                pltpu.SemaphoreType.DMA((n_links,)),
            ],
            10 * attend_flops + 2 * tokens * model * (3 * hidden_cols + 3 * (q_cols + k_cols)),
            100 * 2**20,
            collective=3,
        )(
            gains, cosine, sine, head_rows, logs, mixed_grad, delta, middle_low, feed_gain_part, x, middle_grad, proj,
            hidden_t, dy_both, normed_two_t, gate_grad, up_grad, mixed_t, normed_t, qk_full, vo_full,
        )
        input_grad, totals = got[:2]
        shards = {name: value.astype(F32) for name, value in zip(names, got[2:])}
        down_shard = jnp.concatenate([shards["down0"], shards["down1"]])
        gate_shard, up_shard, out_shard = (
            jnp.concatenate([shards[kind + "0"], shards[kind + "1"]], axis=1) for kind in ("gate", "up", "out")
        )
        q_shard, kv_shard = shards["q"], shards["kv"]
        totals = totals[0]
    else:
        exchange = functools.partial(lax.all_to_all, axis_name="seq", tiled=True)
        grad_rows = exchange(mixed_grad, split_axis=1, concat_axis=0)
        delta_rows = exchange(delta, split_axis=0, concat_axis=1)
        packed = call(
            functools.partial(attend_back_kernel, attend_dims),
            shape_of((seq_len, block_cols), BF),
            [VMEM] * 4,
            VMEM,
            attend_scratch,
            10 * attend_flops,
            20 * 2**20,
        )(head_rows, grad_rows, logs, jnp.broadcast_to(delta_rows[:heads, None], (heads, 8, seq_len)))
        cuts = (mixed_cols, mixed_cols + k_cols // nz)
        parts = (packed[:, : cuts[0]], packed[:, cuts[0] : cuts[1]], packed[:, cuts[1] :])
        qkv = jnp.concatenate([exchange(part, split_axis=0, concat_axis=1) for part in parts], axis=1)
        input_grad, qkv, gain_part, head_gain_part = call(
            functools.partial(post_kernel, (head_dim, wide_cols)),
            [
                rows_model(BF),
                shape_of((tokens, wide_cols + v_cols), BF),
                shape_of((1, model), F32),
                shape_of((1, wide_cols), F32),
            ],
            [VMEM] * 9,
            [VMEM] * 4,
            [],
            proj_flops,
            14 * 2**20,
        )(x, middle_grad, gains, cosine, sine, proj, qkv, qk_full, vo_full[:, :v_cols])

        def reduce(left, right):
            return sum_line(lax.psum_scatter(weight_grad(left, right), "fsdp", scatter_dimension=0, tiled=True)).astype(F32)

        down_shard, gate_shard = reduce(hidden_t, dy), reduce(normed_two_t, gate_grad)
        up_shard, out_shard = reduce(normed_two_t, up_grad), reduce(mixed_t, middle_low)
        qkv_shard = reduce(normed_t, qkv)
        q_shard, kv_shard = qkv_shard[:, :q_cols], qkv_shard[:, q_cols:]
        totals = lax.psum(jnp.concatenate([gain_part, head_gain_part, feed_gain_part], axis=1)[0], ("seq", "fsdp"))

    q_total = totals[model : model + q_cols].reshape(-1, head_dim).sum(axis=0)
    k_total = totals[model + q_cols : model + wide_cols].reshape(-1, head_dim).sum(axis=0)

    def share(values):
        size = values.shape[0] // fsdp
        return lax.dynamic_slice(values, (me * size,), (size,))

    return (
        output.reshape(inputs.shape),
        input_grad.reshape(inputs.shape),
        q_shard,
        kv_shard[:, :k_cols],
        kv_shard[:, k_cols:],
        out_shard,
        share(totals[:model]),
        share(q_total),
        share(k_total),
        share(totals[model + wide_cols :]),
        gate_shard,
        up_shard,
        down_shard,
    )


def solution(mesh):
    tokens, rows, row = P("fsdp", "seq", None), P("fsdp", None), P("fsdp")
    in_specs = (tokens, P("fsdp", "seq"), tokens) + (rows,) * 4 + (row,) * 4 + (rows,) * 3
    out_specs = (tokens, tokens) + (rows,) * 4 + (row,) * 4 + (rows,) * 3
    return jax.shard_map(per_device, mesh=mesh, in_specs=in_specs, out_specs=out_specs, check_vma=False)
```

time: 736 us -> 528 us (0.72)
  the two profiles are of different devices: /device:TPU:0 before, /device:TPU:24 now
where the time goes in v3:
time: 528 us; the launch traced here: 519 us
  Pallas kernels  492 us (93%)
  local copies, waits for them, and re-layouts  16.1 us (3%)
  other arithmetic  9.91 us (2%)
    pallas_call x1, Pallas kernels, per_device(): call(functools.partial(backward_kernel, (nz, head_dim, (q_cols, k_cols, v...  287 us
    pallas_call x1, Pallas kernels, per_device(): call(functools.partial(forward_kernel, dims), outs, [VMEM] * 3 + ([ANY] *...  154 us
    pallas_call x1, Pallas kernels, per_device(): call(functools.partial(feed_kernel, (nz, plane, head_dim, (v_cols, model)...  51 us

profile of v3, /device:TPU:24, one launch (start us, length us, event | category | flops | bytes accessed | tf_op | source)
XLA Modules:
  0.0 518.9 jit_solution(11564561400205881943)
XLA Ops:
  0.6 0.0 copy-start.9
  0.7 0.0 copy-start.11
  0.7 0.0 copy-start.10
  0.7 0.0 copy-start.8
  0.7 0.9 dynamic_update_slice.18
  1.6 0.8 dynamic_update_slice.17
  2.5 0.1 tile.46
  2.6 0.7 convert_element_type.24
  3.3 0.8 dynamic_update_slice.16
  4.1 0.8 dynamic_update_slice.19
  5.0 0.1 tile.44
  5.1 0.3 fusion
  5.5 0.8 copy.28.sin_ref
  6.3 0.8 copy.27.cos_ref
  7.2 0.0 copy-done.10
  7.2 0.0 copy-done.8
  7.2 2.6 concatenate.58.refs_0_
  9.9 0.0 copy-done.9
  9.9 0.0 copy-done.11
  9.9 0.8 pad_maximum_fusion.1.refs_1_
  10.7 153.7 %shard_map.237 = (f32[16,1536]{1,0:T(8,128)}, f32[512,1536]{1,0:T(8,128)}, bf16[2048,512]{1,0:T(8,128)(2,1)}, bf16[512,1024]{1,0:T(8,128)(2,1)}, f32[4,8,2048]{2...) custom-call(bf16[512,1024]{1,0:T(8,128)(2,1)} %bitcast.17, ...), custom_call_target="tpu_custom_call" | custom-call | flops 10737418240 | bytes 62914560 | tf_op jit(solution)/shard_map/pallas_call | solution.py:1147
  164.4 51.0 %shard_map.238 = (bf16[512,1024]{1,0:T(8,128)(2,1)}, f32[512,1024]{1,0:T(8,128)}, bf16[512,1024]{1,0:T(8,128)(2,1)}, f32[1,1024]{1,0:T(1,128)}, bf16[512,1024]{1...) custom-call(bf16[512,1024]{1,0:T(8,128)(2,1)} %bitcast.18, ...), custom_call_target="tpu_custom_call" | custom-call | flops 28991029248 | bytes 52428800 | tf_op jit(solution)/shard_map/pallas_call | solution.py:1178
  215.4 286.9 %shard_map.239 = (bf16[512,1024]{1,0:T(8,128)(2,1)}, f32[8,3584]{1,0:T(8,128)}, bf16[288,1024]{1,0:T(8,128)(2,1)}, bf16[288,1024]{1,0:T(8,128)(2,1)}, bf16[128,2...) custom-call(f32[16,1536]{1,0:T(8,128)} %get-tuple-element.48.gains_r, ...), custom_call_target="tpu_custom_call" | custom-call | flops 40802189312 | bytes 104857600 | tf_op jit(solution)/shard_map/pallas_call | solution.py:1237
  502.3 0.0 copy-start.6
  502.3 0.0 copy-start.7
  502.3 0.8 slice_reduce_fusion.1
  503.1 0.8 fusion.2
  503.9 0.5 dynamic-slice_bitcast_fusion
  504.5 0.1 reshape.114
  504.6 0.6 dynamic_slice.19
  505.1 0.1 reshape.113
  505.2 0.6 dynamic_slice.18
  505.8 1.8 convert_element_type.26
  507.6 1.8 maximum_convert_fusion.3
  509.4 0.0 copy-start.2
  509.4 0.0 copy-start.3
  509.4 0.0 copy-start.4
  509.4 0.0 copy-start.5
  509.4 2.0 fusion.1
  511.4 0.0 copy-done.6
  511.4 0.0 copy-done.7
  511.4 1.7 maximum_convert_fusion.2
  513.1 0.0 copy-done.2
  513.1 0.0 copy-done.3
  513.1 0.0 copy-done.4
  513.1 0.0 copy-done.5
  513.1 0.0 copy-start
  513.1 2.7 maximum_convert_fusion
  515.9 0.0 copy-start.1
  515.9 0.0 copy-done
  515.9 1.0 copy.39
  516.8 0.6 copy-done.1
  517.5 1.0 copy.40
  (22 shorter events, 0.2 us)
Async XLA Ops:
  0.6 9.2 %copy-start.9 = (bf16[128,1024]{1,0:T(8,128)(2,1)S(1)}, bf16[128,1024]{1,0:T(8,128)(2,1)}, u32[]{:S(2)}) copy-start(bf16[128,1024]{1,0:T(8,128)(2,1)} %param.20) | copy-start | bytes 786436
  0.7 9.2 %copy-start.11 = (bf16[128,512]{1,0:T(8,128)(2,1)S(1)}, bf16[128,512]{1,0:T(8,128)(2,1)}, u32[]{:S(2)}) copy-start(bf16[128,512]{1,0:T(8,128)(2,1)} %param.19) | copy-start | bytes 393220
  0.7 6.5 %copy-start.10 = (bf16[128,512]{1,0:T(8,128)(2,1)S(1)}, bf16[128,512]{1,0:T(8,128)(2,1)}, u32[]{:S(2)}) copy-start(bf16[128,512]{1,0:T(8,128)(2,1)} %param.18) | copy-start | bytes 393220
  0.7 6.5 %copy-start.8 = (bf16[128,1024]{1,0:T(8,128)(2,1)S(1)}, bf16[128,1024]{1,0:T(8,128)(2,1)}, u32[]{:S(2)}) copy-start(bf16[128,1024]{1,0:T(8,128)(2,1)} %param.17) | copy-start | bytes 786436
  502.3 9.1 %copy-start.6 = (bf16[288,1024]{1,0:T(8,128)(2,1)S(1)}, bf16[288,1024]{1,0:T(8,128)(2,1)}, u32[]{:S(2)}) copy-start(bf16[288,1024]{1,0:T(8,128)(2,1)} %get-tuple-element.81) | copy-start | bytes 1769476
  502.3 9.1 %copy-start.7 = (bf16[288,1024]{1,0:T(8,128)(2,1)S(1)}, bf16[288,1024]{1,0:T(8,128)(2,1)}, u32[]{:S(2)}) copy-start(bf16[288,1024]{1,0:T(8,128)(2,1)} %get-tuple-element.82) | copy-start | bytes 1769476
  509.4 3.7 copy-start.2
  509.4 3.7 copy-start.3
  509.4 3.7 copy-start.4
  509.4 3.7 copy-start.5
  513.1 2.8 copy-start
  515.9 1.6 copy-start.1

commit v4 on v3

v4 whole, which is shorter than its diff:
```python
import functools

import jax
import jax.numpy as jnp
from jax import lax
from jax.experimental import pallas as pl
from jax.experimental.pallas import tpu as pltpu
from jax.sharding import PartitionSpec as P

EPSILON = 1e-05
ROPE_BASE = 1000000.0
LOG2E = 1.4426950408889634
BF = jnp.bfloat16
F32 = jnp.float32
VMEM = pl.BlockSpec(memory_space=pltpu.VMEM)
SMEM = pl.BlockSpec(memory_space=pltpu.SMEM)
ANY = pl.BlockSpec(memory_space=pl.ANY)
VMEM_BYTES = 62 * 2**20


def dot_nn(a, b):
    return lax.dot_general(a, b, (((1,), (0,)), ((), ())), preferred_element_type=F32)


def dot_nt(a, b):
    return lax.dot_general(a, b, (((1,), (1,)), ((), ())), preferred_element_type=F32)


def dot_tn(a, b):
    return lax.dot_general(a, b, (((0,), (0,)), ((), ())), preferred_element_type=F32)


def shape_of(shape, dtype):
    return jax.ShapeDtypeStruct(shape, dtype)


def call(kernel, outs, in_specs, out_specs, scratch, flops, moved, collective=None, **more):
    params = {} if collective is None else {"collective_id": collective, "has_side_effects": True}
    return pl.pallas_call(
        kernel,
        out_shape=outs,
        in_specs=in_specs,
        out_specs=out_specs,
        scratch_shapes=scratch,
        compiler_params=pltpu.CompilerParams(vmem_limit_bytes=VMEM_BYTES, **params),
        cost_estimate=pl.CostEstimate(flops=flops, bytes_accessed=moved, transcendentals=0),
        **more,
    )


def row_norm(values):
    return lax.rsqrt(jnp.mean(values * values, axis=-1, keepdims=True) + EPSILON)


class Fetch:
    def __init__(self, sems):
        self.sems, self.used = sems, 0

    def copy(self, source, target):
        self.used += 1
        return pltpu.make_async_copy(source, target, self.sems.at[self.used - 1])

    def start(self, source, target):
        copy = self.copy(source, target)
        copy.start()
        return copy


def wait_all(copies):
    for copy in copies:
        copy.wait()


def head_mask(width, head_dim):
    rows = lax.broadcasted_iota(jnp.int32, (width, width), 0) // head_dim
    cols = lax.broadcasted_iota(jnp.int32, (width, width), 1) // head_dim
    return (rows == cols).astype(BF)


def head_sum(values, mask):
    high = values.astype(BF)
    rest = (values - high.astype(F32)).astype(BF)
    return dot_nn(high, mask) + dot_nn(rest, mask)


def key_lanes(shape, head_dim):
    return lax.broadcasted_iota(jnp.int32, shape, 1) % (2 * head_dim) < head_dim


def partner(values, head_dim):
    half = head_dim // 2
    width = values.shape[-1]
    lane = lax.broadcasted_iota(jnp.int32, values.shape, 1)
    after = pltpu.roll(values, width - half, 1)
    before = pltpu.roll(values, half, 1)
    return jnp.where(lane % head_dim < half, after, before)


class Links:
    def __init__(self, send_sems, recv_sems):
        self.sems, self.used, self.started = (send_sems, recv_sems), 0, []

    def reserve(self, count):
        self.used += count
        return self.used - count

    def copy(self, source, target, device, at=None):
        at = self.reserve(1) if at is None else at
        return pltpu.make_async_remote_copy(
            src_ref=source,
            dst_ref=target,
            send_sem=self.sems[0].at[at],
            recv_sem=self.sems[1].at[at],
            device_id=device,
            device_id_type=pl.DeviceIdType.MESH,
        )

    def start(self, source, target, device):
        copy = self.copy(source, target, device)
        copy.start()
        self.started.append(copy)
        return copy

    def wait_sends(self):
        for copy in self.started:
            copy.wait_send()


def enter(me, z, nz, plane):
    barrier = pltpu.get_barrier_semaphore()
    peers = [{"seq": z ^ j} for j in range(1, nz)]
    if plane:
        peers += [{"fsdp": me ^ bit} for bit in (1, 2, 4)]
    for peer in peers:
        pl.semaphore_signal(barrier, inc=1, device_id=peer, device_id_type=pl.DeviceIdType.MESH)
    pl.semaphore_wait(barrier, len(peers))


class Gather:
    def __init__(self, links, me, own, whole, x_first, stride=None, base=0):
        self.links, self.me, self.own, self.whole = links, me, own, whole
        self.rows = own.shape[0]
        self.stride, self.base = self.rows if stride is None else stride, base
        self.near, self.other = (2, 4) if x_first else (4, 2)

    def block(self, b):
        return self.whole.at[pl.ds(pl.multiple_of((self.me ^ b) * self.stride + self.base, 16), self.rows)]

    def pass_on(self, b, bit):
        source = self.own if b == 0 else self.block(b)
        return self.links.start(source, self.block(b), {"fsdp": self.me ^ bit})

    def begin(self):
        self.first = self.pass_on(0, self.near)
        self.second = self.pass_on(0, self.other)
        self.to_core = [self.pass_on(0, 1)]

    def forward_first(self):
        self.first.wait_recv()
        self.far = self.pass_on(self.near, self.other)
        self.to_core.append(self.pass_on(self.near, 1))

    def forward_second(self):
        self.second.wait_recv()
        self.to_core.append(self.pass_on(self.other, 1))

    def forward_far(self):
        self.far.wait_recv()
        self.to_core.append(self.pass_on(self.near + self.other, 1))

    def end(self):
        for copy in self.to_core:
            copy.wait_recv()


def begin(gathers, copy_here=None):
    for gather in gathers:
        gather.begin()
    return [copy_here(gather.own, gather.block(0)) for gather in gathers]


def forward_first(gathers):
    for gather in gathers:
        gather.forward_first()
    for gather in gathers:
        gather.forward_second()


def forward_far(gathers):
    for gather in gathers:
        gather.forward_far()


def end(gathers):
    for gather in gathers:
        gather.end()


def forward_kernel(dims, x_ref, dy_ref, cos_ref, sin_ref, *refs):
    nz, plane, head_dim, widths, rows, width, groups = dims
    n_in = 5 if plane else 6
    given, refs = refs[:n_in], refs[n_in:]
    gains_ref, heads_ref, log_ref, output_ref, middle_grad_ref, middle_low_ref, gain_grad_ref, grad_low, delta_ref = refs[:9]
    refs = refs[9:]
    proj_hbm, normed_t_hbm, mixed_t_hbm, normed_two_hbm, hidden_hbm, gate_grad_hbm, up_grad_hbm, dy_hbm = refs[:8]
    refs = refs[8:]
    if plane:
        first_hbm, second_hbm, gate_hbm, up_hbm, down_hbm = refs[:5]
        refs = refs[5:]
    else:
        gate_hbm, up_hbm, down_hbm = given[3:]
    w_first, w_second, w_out, normed, transposed, proj, qkv, queries, keys, values, full, mix, mixed = refs[:13]
    w_gate, w_up, w_down, middle, total, back, hidden_slot, gate_slot, up_slot = refs[13:22]
    local_sems, weight_sems, slot_sems, send_sems, recv_sems, slot_sends, block_recvs = refs[22:]
    z, me = lax.axis_index("seq"), lax.axis_index("fsdp")
    model = w_second.shape[0]
    hidden_cols = gate_hbm.shape[1]
    tokens = x_ref.shape[0]
    enter(me, z, nz, plane)
    links = Links(send_sems, recv_sems)
    local = []
    to_core = []
    core = lax.rem(me, 2) if plane else 0
    place = pl.ds(pl.multiple_of(core * tokens, tokens), tokens)
    sibling = {"fsdp": me ^ 1}

    def copy_here(source, target):
        copy = pltpu.make_async_copy(source, target, local_sems.at[len(local)])
        copy.start()
        local.append(copy)
        return copy

    def share(source, target):
        copy_here(source, target)
        if plane:
            to_core.append(links.start(source, target, sibling))

    if plane:
        own_first, own_second, own_gate, own_up, own_down = given
        half = own_down.shape[0] // 2
        attention = [Gather(links, me, own_first, w_first, True), Gather(links, me, own_second, w_second, False)]
        here = begin(attention, copy_here)
        down = [
            Gather(links, me, own_down.at[pl.ds(side * half, half)], down_hbm, side == 0, 2 * half, side * half)
            for side in range(2)
        ]
        wide, at = [], 0
        for count in groups:
            cols = pl.ds(at * width, count * width)
            pair = ((own_gate, gate_hbm, True), (own_up, up_hbm, False))
            wide.append([Gather(links, me, own.at[:, cols], whole.at[:, cols], first) for own, whole, first in pair])
            at += count
    else:
        here = [copy_here(given[0], w_first), copy_here(given[1], w_second)]
    x = x_ref[...].astype(F32)
    unit = x * row_norm(x)
    if plane:
        forward_first(attention)
        here_down = begin(down, copy_here)
        forward_far(attention)
        end(attention)
        wait_all(here)
        stride = attention[0].rows
        shard = model // 8
        gains = sum(w_first[s * stride + shard : (s + 1) * stride].astype(F32) for s in range(8))
        for s in range(8):
            copy_here(w_first.at[pl.ds(s * stride, shard)], first_hbm.at[pl.ds(s * shard, shard)])
        copy_here(w_second, second_hbm)
    else:
        stride = shard = model
        wait_all(here)
        gains = given[2][...].astype(F32)
    out_half = model // 2
    for s in range(model // shard):
        source = w_first.at[pl.ds(s * stride, shard), pl.ds(w_first.shape[1] - out_half, out_half)]
        copy_here(source, w_out.at[pl.ds(s * shard, shard), pl.ds(0, out_half)])
    copy_here(w_second.at[:, pl.ds(w_second.shape[1] - out_half, out_half)], w_out.at[:, pl.ds(out_half, out_half)])
    out_copies = local[-model // shard - 1 :]
    gains_ref[...] = gains
    normed[...] = (unit * gains[0:1, :model]).astype(BF)
    chunk = 256
    mask = head_mask(chunk, head_dim)
    cos = jnp.concatenate([cos_ref[...]] * (chunk // 128), axis=1)
    sin = jnp.concatenate([sin_ref[...]] * (chunk // 128), axis=1)
    part_cols = nz * sum(widths)
    parts = qkv.shape[1] // part_cols
    my_rows = pl.ds(pl.multiple_of(z * tokens, tokens), tokens)
    arrivals = []
    for b in range(parts):
        for start in range(0, part_cols, chunk):
            cols = slice(start, start + chunk)
            if b == 1 or stride == shard:
                weight = (w_first, w_second)[b][:, cols]
            else:
                weight = jnp.concatenate([w_first[s * stride : s * stride + shard, cols] for s in range(8)], axis=0)
            got = dot_nn(normed[...], weight)
            here_cols = slice(b * part_cols + start, b * part_cols + start + chunk)
            proj[:, here_cols] = got
            scale = lax.rsqrt(head_sum(got * got, mask) * (1.0 / head_dim) + EPSILON)
            head = got * scale * gains_ref[1:2, cols]
            head = head * cos + partner(head, head_dim) * sin
            if start >= nz * widths[0]:
                head = jnp.where(key_lanes(head.shape, head_dim), head, got)
            qkv[:, here_cols] = head.astype(BF)
        arrived = []
        for j in range(nz):
            owner = z ^ j
            for i, size in enumerate(widths):
                base = b * part_cols + i * nz * widths[0]
                source = qkv.at[:, pl.ds(pl.multiple_of(base + owner * size, size), size)]
                target = heads_ref.at[my_rows, pl.ds(b * sum(widths) + i * widths[0], size)]
                if j == 0:
                    arrived.append(copy_here(source, target))
                else:
                    arrived.append(links.start(source, target, {"seq": owner}))
        arrivals.append(arrived)
    copy_here(proj, proj_hbm)
    transposed[0] = normed[...].T
    share(transposed.at[0], normed_t_hbm.at[:, place])
    share(dy_ref, dy_hbm.at[place])
    if plane:
        here_wide = [begin(wide[0], copy_here)]
        forward_first(down)
        here_wide.append(begin(wide[1], copy_here))
    group, seq_len, _ = queries.shape
    factor = head_dim**-0.5 * LOG2E
    arriving, here_mixed = [], []
    for b in range(parts):
        for i, copy in enumerate(arrivals[b]):
            if i < 2:
                copy.wait()
            else:
                copy.wait_recv()
        first = b * sum(widths)
        for g in range(group):
            queries[g] = heads_ref[:, first + g * head_dim : first + (g + 1) * head_dim]
        first += widths[0]
        keys[...] = heads_ref[:, first : first + head_dim]
        values[...] = heads_ref[:, first + head_dim : first + 2 * head_dim]
        for r in range(seq_len // rows):
            span = slice(r * rows, (r + 1) * rows)
            reach = (r + 1) * rows

            def one_head(g, _):
                scores = dot_nt(queries[g, span], keys[:reach]) * factor
                row = lax.broadcasted_iota(jnp.int32, scores.shape, 0) + r * rows
                col = lax.broadcasted_iota(jnp.int32, scores.shape, 1)
                probs = jnp.exp2(jnp.where(row >= col, scores, -1e30))
                total = jnp.sum(probs, axis=1, keepdims=True)
                full[g, span] = (dot_nn(probs.astype(BF), values[:reach]) * (1.0 / total)).astype(BF)
                log_ref[b * group + g, :, span] = jnp.broadcast_to(jnp.log2(total), (rows, 128)).T[0:8]
                return 0

            lax.fori_loop(0, group, one_head, 0)
        mix[b] = jnp.concatenate([full[g] for g in range(group)], axis=1)
        for j in range(nz):
            owner = z ^ j
            source = mix.at[b, pl.ds(pl.multiple_of(owner * tokens, tokens), tokens)]
            to = pl.multiple_of((z * parts + b) * widths[0], widths[0])
            target = mixed.at[:, pl.ds(to, widths[0])]
            if j == 0:
                here_mixed.append(copy_here(source, target))
            else:
                arriving.append(links.start(source, target, {"seq": owner}))
        if plane and b == 0:
            forward_first(wide[0])
            here_wide.append(begin(wide[2], copy_here))
    if plane:
        forward_far(down)
        forward_first(wide[1])
        here_wide.append(begin(wide[3], copy_here))
        forward_far(wide[0])
    for copy in arriving:
        copy.wait_recv()
    wait_all(here_mixed + out_copies)

    gain = gains_ref[2:3, :model]
    middle_rows = x_ref[...].astype(F32) + dot_nn(mixed[...], w_out[...])
    middle[...] = middle_rows
    total[...] = middle_rows
    normed_rows = (middle_rows * row_norm(middle_rows) * gain).astype(BF)
    normed[...] = normed_rows
    transposed[1] = normed_rows.T
    share(transposed.at[1], normed_two_hbm.at[:, place])
    transposed[2] = mixed[...].T
    share(transposed.at[2], mixed_t_hbm.at[:, place])
    back[...] = jnp.zeros(back.shape, F32)

    def slot_places(f):
        here = pl.ds(pl.multiple_of(f * width, width), width)
        return (
            (hidden_slot, hidden_hbm.at[here, place]),
            (gate_slot, gate_grad_hbm.at[place, here]),
            (up_slot, up_grad_hbm.at[place, here]),
        )

    def slot_copies(slot, f):
        return [
            pltpu.make_async_copy(s.at[slot], target, slot_sems.at[slot, i]) for i, (s, target) in enumerate(slot_places(f))
        ]

    def slot_links(slot, f):
        if not plane:
            return []
        return [
            pltpu.make_async_remote_copy(
                src_ref=s.at[slot],
                dst_ref=target,
                send_sem=slot_sends.at[slot, i],
                recv_sem=block_recvs.at[f, i],
                device_id=sibling,
                device_id_type=pl.DeviceIdType.MESH,
            )
            for i, (s, target) in enumerate(slot_places(f))
        ]

    def wait_slot(slot, f):
        wait_all(slot_copies(slot, f))
        for copy in slot_links(slot, f):
            copy.wait_send()

    def weight_copies(f):
        here = pl.ds(pl.multiple_of(f * width, width), width)
        slot = lax.rem(f, 2)
        pairs = ((gate_hbm.at[:, here], w_gate), (up_hbm.at[:, here], w_up), (down_hbm.at[here], w_down))
        return [
            pltpu.make_async_copy(source, target.at[slot], weight_sems.at[slot, i])
            for i, (source, target) in enumerate(pairs)
        ]

    def one_block(last, f, _):
        slot = lax.rem(f, 2)

        @pl.when(f + 1 < last)
        def _():
            for copy in weight_copies(f + 1):
                copy.start()

        wait_all(weight_copies(f))

        @pl.when(f >= 2)
        def _():
            wait_slot(slot, f - 2)

        gate = dot_nn(normed[...], w_gate[slot])
        up = dot_nn(normed[...], w_up[slot])
        hidden_grad = dot_nt(dy_ref[...], w_down[slot])
        s = 1.0 / (1.0 + jnp.exp(-gate))
        silu = gate * s
        hidden = (silu * up).astype(BF)
        gate_grad = (hidden_grad * up * (s * (1.0 + gate * (1.0 - s)))).astype(BF)
        up_grad = (hidden_grad * silu).astype(BF)
        hidden_slot[slot] = hidden.T
        gate_slot[slot] = gate_grad
        up_slot[slot] = up_grad
        for copy in slot_copies(slot, f) + slot_links(slot, f):
            copy.start()
        total[...] = total[...] + dot_nn(hidden, w_down[slot])
        back[...] = back[...] + (dot_nt(gate_grad, w_gate[slot]) + dot_nt(up_grad, w_up[slot]))
        return 0

    blocks = hidden_cols // width
    at = 0
    if plane:
        end(down)
        wait_all(here_down)
    for g, count in enumerate(groups):
        if plane:
            if g + 1 < len(groups):
                if g > 0:
                    forward_first(wide[g + 1])
            if g > 0:
                forward_far(wide[g])
            end(wide[g])
            wait_all(here_wide[g])
        for copy in weight_copies(at):
            copy.start()
        lax.fori_loop(at, at + count, functools.partial(one_block, at + count), 0)
        at += count
    output_ref[...] = total[...].astype(BF)
    part, gain_sum = norm_back(middle[...], gain, back[...])
    gain_grad_ref[...] = gain_sum
    middle_grad = dy_ref[...].astype(F32) + part
    middle_grad_ref[...] = middle_grad
    middle_low = middle_grad.astype(BF)
    middle_low_ref[...] = middle_low
    mixed_grad = dot_nt(middle_low, w_out[...]).astype(BF)
    grad_low[...] = mixed_grad
    product = mixed_grad.astype(F32) * mixed[...].astype(F32)
    heads = mixed.shape[1] // head_dim // nz
    row = lax.broadcasted_iota(jnp.int32, (8 * nz, mixed.shape[1]), 0)
    col = lax.broadcasted_iota(jnp.int32, (8 * nz, mixed.shape[1]), 1)
    pick = ((col // head_dim == (row // 8) * heads + row % 8) & (row % 8 < heads)).astype(BF)
    high = product.astype(BF)
    delta_ref[...] = dot_nt(pick, high) + dot_nt(pick, (product - high.astype(F32)).astype(BF))
    for f in (blocks - 2, blocks - 1):
        wait_slot(f % 2, f)
    if plane:
        for f in range(blocks):
            for copy in slot_links(f % 2, f):
                copy.wait_recv()
        for copy in to_core:
            copy.wait_recv()
        links.wait_sends()
    done = here + out_copies + here_mixed + [c for arrived in arrivals for c in arrived[:2]]
    if plane:
        done += here_down + [c for copies in here_wide for c in copies]
    for copy in local:
        if not any(copy is other for other in done):
            copy.wait()


def both_cores(links, copy_here, me, source, target, axis):
    size = source.shape[axis]
    here = pl.ds(pl.multiple_of(lax.rem(me, 2) * size, size), size)
    place = target.at[here] if axis == 0 else target.at[:, here]
    copy_here(source, place)
    return links.start(source, place, {"fsdp": me ^ 1})


def attend_back(dims, b, heads_ref, grads_ref, log_ref, delta_ref, packed, scratch, after):
    rows, chunk = dims
    queries, keys, values, grad, q_grad, k_grad, v_grad = scratch
    group, seq_len, head_dim = queries.shape
    first = b * (group + 2) * head_dim
    for g in range(group):
        queries[g] = heads_ref[:, first + g * head_dim : first + (g + 1) * head_dim]
        at = (b * group + g) * head_dim
        grad[g] = grads_ref[:, at : at + head_dim]
        q_grad[g] = jnp.zeros((seq_len, head_dim), F32)
    first += group * head_dim
    keys[...] = heads_ref[:, first : first + head_dim]
    values[...] = heads_ref[:, first + head_dim : first + 2 * head_dim]
    factor = head_dim**-0.5
    scale = factor * LOG2E
    for at in range(seq_len // rows):
        span = slice(at * rows, (at + 1) * rows)
        key, value = keys[span], values[span]
        k_grad[span] = jnp.zeros((rows, head_dim), F32)
        v_grad[span] = jnp.zeros((rows, head_dim), F32)

        def one_head(g, _):
            key_total = jnp.zeros((rows, head_dim), F32)
            value_total = jnp.zeros((rows, head_dim), F32)
            for start in range(at * rows, seq_len, chunk):
                part = slice(start, min(start + chunk, seq_len))
                query, out_grad = queries[g, part], grad[g, part]
                scores = dot_nt(key, query) * scale - log_ref[b * group + g, 0:1, part]
                if start == at * rows:
                    key_at = lax.broadcasted_iota(jnp.int32, scores.shape, 0) + at * rows
                    query_at = lax.broadcasted_iota(jnp.int32, scores.shape, 1) + start
                    scores = jnp.where(query_at >= key_at, scores, -1e30)
                probs = jnp.exp2(scores)
                prob_grad = dot_nt(value, out_grad)
                score_grad = (probs * (prob_grad - delta_ref[b * group + g, 0:1, part])).astype(BF)
                value_total = value_total + dot_nn(probs.astype(BF), out_grad)
                key_total = key_total + dot_nn(score_grad, query)
                q_grad[g, part] = q_grad[g, part] + dot_tn(score_grad, key)
            k_grad[span] = k_grad[span] + key_total
            v_grad[span] = v_grad[span] + value_total
            return 0

        lax.fori_loop(0, group, one_head, 0)
        parts = [(q_grad[g, span] * factor).astype(BF) for g in range(group)]
        parts += [(k_grad[span] * factor).astype(BF), v_grad[span].astype(BF)]
        packed[span] = jnp.concatenate(parts, axis=1)
        after(at)


def attend_back_scratch(group, seq_len, head_dim):
    many = lambda kind: pltpu.VMEM((group, seq_len, head_dim), kind)
    one = lambda kind: pltpu.VMEM((seq_len, head_dim), kind)
    return [many(BF), one(BF), one(BF), many(BF), many(F32), one(F32), one(F32)]


def attend_back_kernel(dims, heads_ref, grads_ref, log_ref, delta_ref, packed, *scratch):
    for b in range(packed.shape[0]):
        attend_back(dims, b, heads_ref, grads_ref, log_ref, delta_ref, packed.at[b], scratch, lambda at: None)


def norm_back(rows, gain, gradient):
    q = row_norm(rows)
    n = rows * q
    u = gradient * gain
    return q * (u - n * jnp.mean(u * n, axis=-1, keepdims=True)), jnp.sum(gradient * n, axis=0, keepdims=True)


def weight_grad_kernel(left_ref, right_ref, out_ref):
    out_ref[...] = dot_nn(left_ref[...], right_ref[...]).astype(BF)


def weight_grad(left, right, width=256):
    rows, tokens = left.shape
    cols = right.shape[1]
    return call(
        weight_grad_kernel,
        shape_of((rows, cols), BF),
        [pl.BlockSpec((rows, tokens), lambda n: (0, 0)), pl.BlockSpec((tokens, width), lambda n: (0, n))],
        pl.BlockSpec((rows, width), lambda n: (0, n)),
        [],
        2 * rows * tokens * cols,
        2 * (rows * tokens + tokens * cols + rows * cols),
        grid=(cols // width,),
    )(left, right)


def project_back(dims, b, gains_ref, cos_ref, sin_ref, proj_ref, qkv, head_gain_grad_ref):
    nz, head_dim, widths = dims
    part_cols = nz * sum(widths)
    width = 256
    mask = head_mask(width, head_dim)
    cos = jnp.concatenate([cos_ref[...]] * (width // 128), axis=1)
    sin = jnp.concatenate([sin_ref[...]] * (width // 128), axis=1)
    for start in range(0, part_cols, width):
        cols = slice(b * part_cols + start, b * part_cols + start + width)
        rotated = qkv[:, cols].astype(F32)
        gradient = rotated * cos - partner(rotated, head_dim) * sin
        proj = proj_ref[:, cols]
        scale = lax.rsqrt(head_sum(proj * proj, mask) * (1.0 / head_dim) + EPSILON)
        n = proj * scale
        u = gradient * gains_ref[1:2, start : start + width]
        head_gain_grad_ref[:, cols] = jnp.sum(gradient * n, axis=0, keepdims=True)
        back = scale * (u - n * (head_sum(u * n, mask) * (1.0 / head_dim)))
        if start >= nz * widths[0]:
            back = jnp.where(key_lanes(back.shape, head_dim), back, rotated)
        qkv[:, cols] = back.astype(BF)


def input_back(x_ref, middle_grad_ref, gains_ref, qkv, weight, input_grad_ref, gain_grad_ref):
    normed_grad = dot_nt(qkv[...], weight[...])
    part, gain_sum = norm_back(x_ref[...].astype(F32), gains_ref[0:1, : x_ref.shape[1]], normed_grad)
    gain_grad_ref[...] = gain_sum
    input_grad_ref[...] = (middle_grad_ref[...] + part).astype(BF)


def post_kernel(dims, x_ref, middle_grad_ref, gains_ref, cos_ref, sin_ref, proj_ref, grads_ref, weight_ref, *refs):
    input_grad_ref, qkv, gain_grad_ref, head_gain_grad_ref = refs
    nz, _, widths = dims
    qkv[...] = grads_ref[...]
    for b in range(qkv.shape[1] // (nz * sum(widths))):
        project_back(dims, b, gains_ref, cos_ref, sin_ref, proj_ref, qkv, head_gain_grad_ref)
    input_back(x_ref, middle_grad_ref, gains_ref, qkv, weight_ref, input_grad_ref, gain_grad_ref)


class Reduce:
    def __init__(self, links, fetch, me, z, x_first, away, kept, first, second, inward, across, out):
        self.links, self.fetch, self.me, self.z = links, fetch, me, z
        self.away, self.kept, self.out = away, kept, out
        self.bits = (2, 4) if x_first else (4, 2)
        order = (1, 3, 0, 2) if x_first else (2, 3, 0, 1)
        self.slots = {r: (away if i < 2 else kept, i % 2) for i, r in enumerate(order)}
        self.arrived, self.second, self.inward, self.across = first, second, inward, across
        self.outer, self.inner = (z == 0) | (z == 3), (z == 1) | (z == 2)
        self.one = links.copy(away, first, {"fsdp": me ^ self.bits[0]})
        self.two = links.copy(kept.at[1], second, {"fsdp": me ^ self.bits[1]})
        self.three = links.copy(kept.at[0], inward, {"seq": z ^ 1})
        self.four = links.copy(kept.at[0], across, {"seq": z ^ 3})
        self.five = links.copy(kept.at[1], out, {"seq": z ^ 1})
        self.here = fetch.copy(kept.at[1], out)
        self.load = fetch.copy(first, away)

    def put(self, r, cols, values):
        ref, i = self.slots[r]
        ref[i, :, cols] = values

    def rows_of(self):
        rows = self.kept.shape[1]
        step = 32 if rows % 32 == 0 else 16
        return rows // step, step

    def by_rows(self, work):
        count, step = self.rows_of()

        def body(i, _):
            work(pl.ds(pl.multiple_of(i * step, step), step))
            return 0

        lax.fori_loop(0, count, body, 0)

    def begin(self):
        self.one.start()

    def load_one(self):
        self.one.wait_recv()
        self.one.wait_send()
        self.load.start()

    def fold_one(self):
        self.load.wait()

        def work(rows):
            for i in range(2):
                self.kept[i, rows] = self.kept[i, rows] + self.away[i, rows]

        self.by_rows(work)
        self.two.start()

    def fold_two(self):
        self.two.wait_recv()

        def work(rows):
            self.kept[0, rows] = self.kept[0, rows] + self.second[rows]

        self.by_rows(work)

        @pl.when(self.outer)
        def _():
            self.three.start()

    def fold_three(self):
        @pl.when(self.inner)
        def _():
            self.three.wait_recv()

            def work(rows):
                self.kept[0, rows] = self.kept[0, rows] + self.inward[rows]

            self.by_rows(work)
            self.four.start()

    def fold_four(self):
        self.two.wait_send()

        @pl.when(self.inner)
        def _():
            self.four.wait_recv()

            def work(rows):
                self.kept[1, rows] = self.kept[0, rows] + self.across[rows]

            self.by_rows(work)
            self.five.start()
            self.here.start()

    def end(self):
        @pl.when(self.inner)
        def _():
            self.four.wait_send()
            self.five.wait_send()
            self.here.wait()

        @pl.when(self.outer)
        def _():
            self.three.wait_send()
            self.five.wait_recv()


def each(reduces, step):
    if step == "fold_one":
        each(reduces, "load_one")
    for reduce in reduces:
        getattr(reduce, step)()


class Total:
    def __init__(self, links, me, z, sums, arrived):
        self.sums, self.arrived = sums, arrived
        peers = [{"fsdp": me ^ 1}, {"fsdp": me ^ 2}, {"fsdp": me ^ 4}, {"seq": z ^ 1}, {"seq": z ^ 2}]
        self.copies = [links.copy(sums.at[i], arrived.at[i], peer) for i, peer in enumerate(peers)]

    def begin(self, at):
        self.copies[at].start()

    def fold(self, at):
        self.copies[at].wait_recv()
        self.sums[at + 1] = self.sums[at] + self.arrived[at]

    def end(self):
        for copy in self.copies:
            copy.wait_send()


def backward_kernel(dims, gains_ref, cos_ref, sin_ref, heads_ref, log_ref, grad_low, delta_own, low_ref, feed_gain_ref, *refs):
    nz, head_dim, widths, attend_dims, names = dims
    given, refs = refs[:12], refs[12:]
    x_hbm, middle_grad_hbm, proj_hbm, hidden_hbm, dy_hbm, normed_two_hbm = given[:6]
    gate_hbm, up_hbm, mixed_hbm, normed_hbm, first_hbm, second_hbm = given[6:]
    input_grad_ref, totals_ref = refs[:2]
    n = len(names)
    finals, refs = dict(zip(names, refs[2 : 2 + n])), refs[2 + n :]
    firsts, refs = dict(zip(names, refs[:n])), refs[n:]
    low_hbm, refs = refs[0], refs[1:]
    aways, refs = dict(zip(names, refs[:n])), refs[n:]
    kepts, refs = dict(zip(names, refs[:n])), refs[n:]
    seconds, refs = dict(zip(names, refs[:n])), refs[n:]
    inwards, refs = dict(zip(names, refs[:n])), refs[n:]
    acrosses, refs = dict(zip(names, refs[:n])), refs[n:]
    grads, delta, qkv, other_qkv, sums, sum_arrived, gain_grad, head_gain_grad, sems, send_sems, recv_sems = refs
    z, me = lax.axis_index("seq"), lax.axis_index("fsdp")
    chip, core = lax.div(me, 2), lax.rem(me, 2)
    enter(me, z, nz, True)
    links, fetch = Links(send_sems, recv_sems), Fetch(sems)
    tokens = grad_low.shape[0]
    seq_len, block_cols = heads_ref.shape
    part_cols = nz * sum(widths)
    parts = qkv.shape[1] // part_cols
    late = []

    def copy_here(source, target):
        copy = fetch.start(source, target)
        late.append(copy)
        return copy

    my_rows = pl.ds(pl.multiple_of(z * tokens, tokens), tokens)
    arrivals = []
    for b in range(parts):
        arrived = []
        for j in range(nz):
            owner = z ^ j
            from_cols = pl.ds(pl.multiple_of((owner * parts + b) * widths[0], widths[0]), widths[0])
            pairs = [(grad_low.at[:, from_cols], grads.at[my_rows, pl.ds(b * widths[0], widths[0])])]
            if b == 0:
                pairs.append((delta_own.at[pl.ds(pl.multiple_of(owner * 8, 8), 8)], delta.at[:, my_rows]))
            for source, target in pairs:
                if j == 0:
                    copy_here(source, target)
                else:
                    arrived.append(links.start(source, target, {"seq": owner}))
        arrivals.append(arrived)
    low_arrival = both_cores(links, copy_here, me, low_ref, low_hbm, 0)
    reduces = {}
    for name in names:
        reduces[name] = Reduce(
            links, fetch, me, z, name[-1] == "x", aways[name], kepts[name], firsts[name], seconds[name], inwards[name],
            acrosses[name], finals[name],
        )
    down = [[reduces[f"down{c}{way}"] for way in "xy"] for c in range(2)]
    gate, up = [reduces["gate0x"], reduces["gate1y"], reduces["gate2x"]], [reduces["up0y"], reduces["up1x"], reduces["up2y"]]
    wide = [gate[:2], [gate[2], up[0]], up[1:]]
    out = [reduces["outx"], reduces["outy"]]
    last = [[reduces[f"last{b}{way}"] for way in "xy"] for b in range(parts)]
    total = Total(links, me, z, sums, sum_arrived)
    part_cols_of = lambda b: pl.ds(b * part_cols, part_cols)
    qkv_links = [
        links.copy(qkv.at[:, part_cols_of(b)], other_qkv.at[:, part_cols_of(b)], {"fsdp": me ^ 1}) for b in range(parts)
    ]
    chips = 4
    step = 256
    half = down[0][0].kept.shape[1]
    shard = gate[0].kept.shape[1]
    both = 2 * tokens
    model = low_ref.shape[1]

    def my_blocks(source, target, rows):
        copies = []
        for r in range(chips):
            owner = (chip ^ r) * 2 + core
            copies.append(fetch.start(source.at[pl.ds(pl.multiple_of(owner * rows, rows), rows)], target.at[pl.ds(r * rows, rows)]))
        return copies

    def wide_grads(places, left, right):
        width = right.shape[2]
        chunks = [
            (source, (first + c) * width, unit, c * width)
            for source, first, unit in places
            for c in range(unit.kept.shape[2] // width)
        ]
        count = len(chunks)
        loads = [
            fetch.copy(source.at[:, pl.ds(at, width)], right.at[c % 2]) for c, (source, at, _, _) in enumerate(chunks)
        ]
        loads[0].start()
        loads[1].start()
        for c in range(count):
            loads[c].wait()
            _, _, unit, base = chunks[c]

            def block(k, _):
                here = pl.ds(pl.multiple_of(k * step, step), step)
                to = pl.ds(pl.multiple_of(base + k * step, step), step)
                got = dot_nn(left[...], right[c % 2, :, here]).astype(BF)
                for r in range(chips):
                    unit.put(r, to, got[r * shard : (r + 1) * shard])
                return 0

            lax.fori_loop(0, width // step, block, 0)
            if c + 2 < count:
                loads[c + 2].start()

    def early_grads(hidden, dy, normed_two, right, mixed, low):
        ready = my_blocks(hidden_hbm, hidden, 2 * half) + [fetch.start(dy_hbm, dy)]
        ready_two = my_blocks(normed_two_hbm, normed_two, shard)
        ready_three = my_blocks(mixed_hbm, mixed, shard)
        wait_all(ready)
        cols = down[0][0].kept.shape[2]
        for c in range(2):

            def down_block(i, _):
                to = pl.ds(pl.multiple_of(i * step, step), step)
                here = pl.ds(pl.multiple_of(c * cols + i * step, step), step)
                for r in range(chips):
                    got = dot_nn(hidden[2 * r * half : 2 * (r + 1) * half], dy[:, here]).astype(BF)
                    for side in range(2):
                        down[c][side].put(r, to, got[side * half : (side + 1) * half])
                return 0

            lax.fori_loop(0, cols // step, down_block, 0)
            each(down[c], "begin")
        wait_all(ready_two)
        per_unit = gate[0].kept.shape[2] // right.shape[2]
        wide_grads([(gate_hbm, i * per_unit, gate[i]) for i in range(3)] + [(up_hbm, 0, up[0])], normed_two, right)
        low_arrival.wait_recv()
        wait_all(late)
        del late[:]
        ready_three.append(fetch.start(low_hbm, low))
        wait_all(ready_three)
        cols = out[0].kept.shape[2]
        for start in range(0, low.shape[1], step):
            got = dot_nn(mixed[...], low[:, start : start + step]).astype(BF)
            for r in range(chips):
                out[start // cols].put(r, slice(start % cols, start % cols + step), got[r * shard : (r + 1) * shard])
        each(down[0], "fold_one")

    def late_grads(normed_two, right):
        wait_all(my_blocks(normed_two_hbm, normed_two, shard))
        per_unit = up[0].kept.shape[2] // right.shape[2]
        wide_grads([(up_hbm, i * per_unit, up[i]) for i in (1, 2)], normed_two, right)

    wide_part = gate[0].kept.shape[2] // 2
    pl.run_scoped(
        early_grads,
        pltpu.VMEM((2 * chips * half, both), BF),
        pltpu.VMEM((both, model), BF),
        pltpu.VMEM((chips * shard, both), BF),
        pltpu.VMEM((2, both, wide_part), BF),
        pltpu.VMEM((chips * shard, both), BF),
        pltpu.VMEM((both, model), BF),
    )

    heads = log_ref.shape[0]
    group = heads // parts
    first_back = links.reserve(parts * 2 * nz)
    own_back = fetch.used
    fetch.used += parts * 2

    def back_copies(b, packed):
        for i, width in enumerate(widths):
            base = b * part_cols + i * nz * widths[0]
            target = qkv.at[:, pl.ds(pl.multiple_of(base + z * width, width), width)]
            for j in range(nz):
                owner = z ^ j
                rows = pl.ds(pl.multiple_of(owner * tokens, tokens), tokens)
                source = packed.at[b, rows, pl.ds(i * widths[0], width)]
                if j == 0:
                    yield j, pltpu.make_async_copy(source, target, sems.at[own_back + 2 * b + i])
                else:
                    yield j, links.copy(source, target, {"seq": owner}, at=first_back + (2 * b + i) * nz + j)

    def attention(packed, delta_rows, *scratch):
        def after_first(at):
            if at == 3:
                each(down[1], "fold_one")
                each(wide[0], "begin")

        def after_second(at):
            if at == 1:
                each(down[0], "fold_two")
            if at == 3:
                each(down[1], "fold_two")

        for b, after in enumerate((after_first, after_second)):
            for copy in arrivals[b]:
                copy.wait_recv()
            if b == 0:
                for h in range(heads):
                    delta_rows[h] = jnp.broadcast_to(delta[h : h + 1], (8, seq_len))
            attend_back(attend_dims, b, heads_ref, grads, log_ref, delta_rows, packed.at[b], scratch, after)
            for _, copy in back_copies(b, packed):
                copy.start()
        pl.run_scoped(
            late_grads,
            pltpu.VMEM((chips * shard, both), BF),
            pltpu.VMEM((2, both, wide_part), BF),
        )
        each(wide[0], "fold_one")
        each(wide[1], "begin")
        each(wide[2], "begin")
        each(down[0], "fold_three")
        for b in range(parts):
            for j, copy in back_copies(b, packed):
                if j == 0:
                    copy.wait()
                else:
                    copy.wait_recv()
            project(b)
            if b == 0:
                each(down[1], "fold_three")
                each(wide[0], "fold_two")
        each(wide[1], "fold_one")
        for b in range(parts):
            for j, copy in back_copies(b, packed):
                if j:
                    copy.wait_send()

    def project(b):
        def inner(proj):
            cols = part_cols_of(b)
            fetch.start(proj_hbm.at[:, cols], proj.at[:, cols]).wait()
            project_back((nz, head_dim, widths), b, gains_ref, cos_ref, sin_ref, proj, qkv, head_gain_grad)
            qkv_links[b].start()

        pl.run_scoped(inner, pltpu.VMEM((tokens, parts * part_cols), F32))

    pl.run_scoped(
        attention,
        pltpu.VMEM((parts, seq_len, sum(widths)), BF),
        pltpu.VMEM((heads, 8, seq_len), F32),
        *attend_back_scratch(group, seq_len, head_dim),
    )

    def projections(weight, x, middle_grad, normed):
        ready = my_blocks(normed_hbm, normed, shard)
        ready_two = [fetch.start(x_hbm, x), fetch.start(middle_grad_hbm, middle_grad)]
        for b, source in enumerate((first_hbm, second_hbm)):
            ready_two.append(fetch.start(source.at[:, pl.ds(0, part_cols)], weight.at[:, part_cols_of(b)]))
        wait_all(ready)
        mine = normed[:, pl.ds(pl.multiple_of(core * tokens, tokens), tokens)]
        theirs = normed[:, pl.ds(pl.multiple_of((1 - core) * tokens, tokens), tokens)]
        for b in range(parts):
            qkv_links[b].wait()
            cols = last[b][0].kept.shape[2]
            for start in range(0, part_cols, step):
                here = slice(b * part_cols + start, b * part_cols + start + step)
                got = (dot_nn(mine, qkv[:, here]) + dot_nn(theirs, other_qkv[:, here])).astype(BF)
                for r in range(chips):
                    last[b][start // cols].put(r, slice(start % cols, start % cols + step), got[r * shard : (r + 1) * shard])
            each(last[b], "begin")
        each(out, "begin")
        wait_all(ready_two)
        input_back(x, middle_grad, gains_ref, qkv, weight, input_grad_ref, gain_grad)
        row = jnp.concatenate([gain_grad[...], head_gain_grad[...], feed_gain_ref[...]], axis=1)
        sums[0] = jnp.broadcast_to(row, sums.shape[1:])
        total.begin(0)

    pl.run_scoped(
        projections,
        pltpu.VMEM((model, parts * part_cols), BF),
        pltpu.VMEM((tokens, model), BF),
        pltpu.VMEM((tokens, model), F32),
        pltpu.VMEM((chips * shard, both), BF),
    )
    each(down[0], "fold_four")
    each(down[1], "fold_four")
    total.fold(0)
    total.begin(1)
    each(wide[0], "fold_three")
    each(wide[2], "fold_one")
    each(wide[1], "fold_two")
    total.fold(1)
    total.begin(2)
    each(last[0], "fold_one")
    each(last[1], "fold_one")
    each(out, "fold_one")
    each(wide[2], "fold_two")
    total.fold(2)
    total.begin(3)
    each(wide[0], "fold_four")
    each(last[0], "fold_two")
    each(last[1], "fold_two")
    each(out, "fold_two")
    total.fold(3)
    total.begin(4)
    each(wide[1], "fold_three")
    each(wide[2], "fold_three")
    each(wide[1], "fold_four")
    each(last[0], "fold_three")
    each(last[1], "fold_three")
    each(out, "fold_three")
    total.fold(4)
    each(wide[2], "fold_four")
    each(last[0], "fold_four")
    each(last[1], "fold_four")
    each(out, "fold_four")
    totals_ref[...] = sums[5]
    total.end()
    for name in names:
        reduces[name].end()
    links.wait_sends()


def add(a, b):
    return (a.astype(F32) + b.astype(F32)).astype(a.dtype)


def sum_line(values):
    size = lax.axis_size("seq")
    if size != 4:
        return lax.psum(values, "seq")
    z = lax.axis_index("seq")
    inner = add(values, lax.ppermute(values, "seq", [(0, 1), (3, 2)]))
    total = add(inner, lax.ppermute(inner, "seq", [(1, 2), (2, 1)]))
    outer = lax.ppermute(total, "seq", [(1, 0), (2, 3)])
    return jnp.where((z == 1) | (z == 2), total, outer)


def per_device(
    inputs,
    positions,
    cotangent,
    query_weight,
    key_weight,
    value_weight,
    out_weight,
    attention_gain,
    query_gain,
    key_gain,
    feedforward_gain,
    gate_weight,
    up_weight,
    down_weight,
):
    seqs, tokens, model = inputs.shape
    assert seqs == 1
    fsdp, nz = lax.axis_size("fsdp"), lax.axis_size("seq")
    me, z = lax.axis_index("fsdp"), lax.axis_index("seq")
    plane = fsdp == 8 and nz == 4
    both = 2 * tokens if plane else tokens
    x = inputs.reshape(tokens, model)
    dy = cotangent.reshape(tokens, model)
    head_dim = query_gain.shape[0] * fsdp
    q_cols, k_cols, v_cols = query_weight.shape[1], key_weight.shape[1], value_weight.shape[1]
    heads, kv_heads = q_cols // head_dim // nz, k_cols // head_dim // nz
    hidden_cols = gate_weight.shape[1]
    seq_len = tokens * nz

    group, parts = heads // kv_heads, kv_heads
    widths = (group * head_dim, 2 * head_dim)
    part_cols = nz * sum(widths)
    assert parts == 2

    def by_parts(query, key, value):
        rows = query.shape[0]
        q = query.reshape(rows, nz, parts, widths[0])
        kv = jnp.stack([v.reshape(rows, nz, parts, head_dim) for v in (key, value)], axis=3).reshape(rows, nz, parts, widths[1])
        return [jnp.concatenate([v[:, :, b].reshape(rows, -1) for v in (q, kv)], axis=1) for b in range(parts)]

    first, second = by_parts(query_weight, key_weight, value_weight)
    half_out = model // 2
    first = jnp.concatenate([first, out_weight[:, :half_out]], axis=1)
    second = jnp.concatenate([second, out_weight[:, half_out:]], axis=1)
    first_cols = first.shape[1]

    def spread(values):
        share = values.shape[0]
        return lax.dynamic_update_slice(jnp.zeros((share * fsdp,), BF), values, (me * share,))

    def gain_row(values):
        return jnp.concatenate([values, jnp.zeros((first_cols - values.shape[0],), BF)])

    key_row = jnp.concatenate([spread(key_gain), jnp.zeros((head_dim,), BF)])
    head_row = jnp.concatenate([jnp.tile(spread(query_gain), nz * group), jnp.tile(key_row, nz)])
    gain_rows = [gain_row(spread(attention_gain)), gain_row(head_row), gain_row(spread(feedforward_gain))]
    gain_rows = jnp.stack(gain_rows + [jnp.zeros((first_cols,), BF)] * 13)
    if plane:
        given = [jnp.concatenate([first, gain_rows]), second, gate_weight, up_weight, down_weight]
    else:
        gather = functools.partial(lax.all_gather, axis_name="fsdp", axis=0, tiled=True)
        first_full, second_full, gate_full = gather(first), gather(second), gather(gate_weight)
        up_full, down_full = gather(up_weight), gather(down_weight)
        given = [first_full, second_full, lax.psum(gain_rows.astype(F32), "fsdp"), gate_full, up_full, down_full]

    half_dim = head_dim // 2
    freqs = ROPE_BASE ** (-jnp.arange(half_dim, dtype=F32) / half_dim)
    angles = positions.reshape(tokens).astype(F32)[:, None] * freqs[None, :]
    cosine, sine = jnp.cos(angles), jnp.sin(angles)
    cosine = jnp.tile(cosine, (1, 128 // half_dim))
    sine = jnp.tile(jnp.concatenate([-sine, sine], axis=1), (1, 128 // head_dim))

    width = 512
    blocks = hidden_cols // width
    sizes = (blocks - 6, 3, 2, 1)
    block_cols = parts * sum(widths)
    mixed_cols = heads * head_dim
    attend_flops = 2 * heads * seq_len * seq_len * head_dim
    proj_flops = 2 * tokens * model * parts * part_cols
    rows_model = lambda kind: shape_of((tokens, model), kind)
    outs = [
        shape_of((16, first_cols), F32),
        shape_of((seq_len, block_cols), BF),
        shape_of((heads, 8, seq_len), F32),
        rows_model(BF),
        rows_model(F32),
        rows_model(BF),
        shape_of((1, model), F32),
        shape_of((tokens, q_cols), BF),
        shape_of((8 * nz, tokens), F32),
        shape_of((tokens, parts * part_cols), F32),
        shape_of((model, both), BF),
        shape_of((q_cols, both), BF),
        shape_of((model, both), BF),
        shape_of((hidden_cols, both), BF),
        shape_of((both, hidden_cols), BF),
        shape_of((both, hidden_cols), BF),
        shape_of((both, model), BF),
    ]
    n_links = parts * 3 * (nz - 1)
    first_rows = model
    if plane:
        outs += [shape_of((model, first_cols), BF)] * 2
        outs += [shape_of((model, hidden_cols), BF)] * 2 + [shape_of((hidden_cols, model), BF)]
        n_links += (4 + 2 * len(sizes)) * 7 + 4
        first_rows += 8 * 16
    many = lambda count: pltpu.VMEM((count, seq_len, head_dim), BF)
    one = pltpu.VMEM((seq_len, head_dim), BF)
    got = call(
        functools.partial(forward_kernel, (nz, plane, head_dim, widths, min(256, seq_len), width, sizes)),
        outs,
        [VMEM] * 4 + ([ANY] * 5 if plane else [ANY] * 2 + [VMEM] + [ANY] * 3),
        [VMEM] * 9 + [ANY] * (len(outs) - 9),
        [
            pltpu.VMEM((first_rows, first_cols), BF),
            pltpu.VMEM((model, first_cols), BF),
            pltpu.VMEM((q_cols, model), BF),
            pltpu.VMEM((tokens, model), BF),
            pltpu.VMEM((3, model, tokens), BF),
            pltpu.VMEM((tokens, parts * part_cols), F32),
            pltpu.VMEM((tokens, parts * part_cols), BF),
            many(group),
            one,
            one,
            many(group),
            pltpu.VMEM((parts, seq_len, widths[0]), BF),
            pltpu.VMEM((tokens, q_cols), BF),
            pltpu.VMEM((2, model, width), BF),
            pltpu.VMEM((2, model, width), BF),
            pltpu.VMEM((2, width, model), BF),
            pltpu.VMEM((tokens, model), F32),
            pltpu.VMEM((tokens, model), F32),
            pltpu.VMEM((tokens, model), F32),
            pltpu.VMEM((2, width, tokens), BF),
            pltpu.VMEM((2, tokens, width), BF),
            pltpu.VMEM((2, tokens, width), BF),
            pltpu.SemaphoreType.DMA((48,)),
            pltpu.SemaphoreType.DMA((2, 3)),
            pltpu.SemaphoreType.DMA((2, 3)),
            pltpu.SemaphoreType.DMA((n_links,)),
            pltpu.SemaphoreType.DMA((n_links,)),
            pltpu.SemaphoreType.DMA((2, 3)),
            pltpu.SemaphoreType.DMA((blocks, 3)),
        ],
        proj_flops + 4 * attend_flops + 12 * tokens * model * hidden_cols,
        100 * 2**20,
        collective=1,
    )(x, dy, cosine, sine, *given)
    gains, head_rows, logs, output, middle_grad, middle_low, feed_gain_part, mixed_grad, delta = got[:9]
    proj, normed_t, mixed_t, normed_two_t, hidden_t, gate_grad, up_grad, dy_both = got[9:17]
    if plane:
        first_full, second_full = got[17:19]

    attend_dims = (min(256, seq_len), min(1024, seq_len))
    attend_scratch = attend_back_scratch(group, seq_len, head_dim)
    if plane:
        down_rows, down_cols = down_weight.shape
        blocks = {f"down{c}{way}": (down_rows // 2, down_cols // 2) for c in range(2) for way in "xy"}
        wide_names = ("gate0x", "gate1y", "gate2x", "up0y", "up1x", "up2y")
        blocks |= {name: (gate_weight.shape[0], hidden_cols // 3) for name in wide_names}
        blocks |= {"out" + way: (out_weight.shape[0], model // 2) for way in "xy"}
        blocks |= {f"last{b}{way}": (query_weight.shape[0], part_cols // 2) for b in range(parts) for way in "xy"}
        names = tuple(blocks)
        pairs = [(2,) + shape for shape in blocks.values()]
        total_cols = model + parts * part_cols + model
        n_links = 3 * (nz - 1) + 2 * parts * nz + 1 + parts + 5 * len(names) + 5
        n_copies = 64 + 2 * len(names)
        got = call(
            functools.partial(backward_kernel, (nz, head_dim, widths, attend_dims, names)),
            [rows_model(BF), shape_of((8, total_cols), F32)]
            + [shape_of(shape, BF) for shape in blocks.values()]
            + [shape_of(shape, BF) for shape in pairs]
            + [shape_of((both, model), BF)],
            [VMEM] * 9 + [ANY] * 12,
            [VMEM] * 2 + [ANY] * (2 * len(names) + 1),
            [pltpu.VMEM(shape, BF) for shape in pairs] * 2
            + [pltpu.VMEM(shape, BF) for shape in blocks.values()] * 3
            + [
                pltpu.VMEM((seq_len, mixed_cols), BF),
                pltpu.VMEM((8, seq_len), F32),
                pltpu.VMEM((tokens, parts * part_cols), BF),
                pltpu.VMEM((tokens, parts * part_cols), BF),
                pltpu.VMEM((6, 8, total_cols), F32),
                pltpu.VMEM((5, 8, total_cols), F32),
                pltpu.VMEM((1, model), F32),
                pltpu.VMEM((1, parts * part_cols), F32),
                pltpu.SemaphoreType.DMA((n_copies,)),
                pltpu.SemaphoreType.DMA((n_links,)),
                pltpu.SemaphoreType.DMA((n_links,)),
            ],
            10 * attend_flops + 2 * tokens * model * (3 * hidden_cols + 3 * (q_cols + k_cols)),
            100 * 2**20,
            collective=3,
        )(
            gains, cosine, sine, head_rows, logs, mixed_grad, delta, middle_low, feed_gain_part, x, middle_grad, proj,
            hidden_t, dy_both, normed_two_t, gate_grad, up_grad, mixed_t, normed_t, first_full, second_full,
        )
        input_grad, totals = got[:2]
        shards = {name: value.astype(F32) for name, value in zip(names, got[2:])}
        down_shard = jnp.concatenate(
            [jnp.concatenate([shards["down0" + way], shards["down1" + way]], axis=1) for way in "xy"]
        )
        gate_shard, up_shard, out_shard = (
            jnp.concatenate([shards[name] for name in names if name.startswith(kind)], axis=1)
            for kind in ("gate", "up", "out")
        )
        part_shards = [(shards[f"last{b}x"], shards[f"last{b}y"]) for b in range(parts)]
        totals = totals[0]
    else:
        exchange = functools.partial(lax.all_to_all, axis_name="seq", tiled=True)
        grad_rows = exchange(mixed_grad, split_axis=1, concat_axis=0)
        delta_rows = exchange(delta, split_axis=0, concat_axis=1)
        packed = call(
            functools.partial(attend_back_kernel, attend_dims),
            shape_of((parts, seq_len, sum(widths)), BF),
            [VMEM] * 4,
            VMEM,
            attend_scratch,
            10 * attend_flops,
            20 * 2**20,
        )(head_rows, grad_rows, logs, jnp.broadcast_to(delta_rows[:heads, None], (heads, 8, seq_len)))
        pieces = [piece for b in range(parts) for piece in (packed[b, :, : widths[0]], packed[b, :, widths[0] :])]
        qkv = jnp.concatenate([exchange(piece, split_axis=0, concat_axis=1) for piece in pieces], axis=1)
        weight = jnp.concatenate([first_full[:, :part_cols], second_full[:, :part_cols]], axis=1)
        input_grad, qkv, gain_part, head_gain_part = call(
            functools.partial(post_kernel, (nz, head_dim, widths)),
            [
                rows_model(BF),
                shape_of((tokens, parts * part_cols), BF),
                shape_of((1, model), F32),
                shape_of((1, parts * part_cols), F32),
            ],
            [VMEM] * 8,
            [VMEM] * 4,
            [],
            proj_flops,
            14 * 2**20,
        )(x, middle_grad, gains, cosine, sine, proj, qkv, weight)

        def reduce(left, right):
            return sum_line(lax.psum_scatter(weight_grad(left, right), "fsdp", scatter_dimension=0, tiled=True)).astype(F32)

        down_shard, gate_shard = reduce(hidden_t, dy), reduce(normed_two_t, gate_grad)
        up_shard, out_shard = reduce(normed_two_t, up_grad), reduce(mixed_t, middle_low)
        qkv_shard = reduce(normed_t, qkv)
        section = nz * widths[0]
        part_shards = [
            (qkv_shard[:, b * part_cols : b * part_cols + section], qkv_shard[:, b * part_cols + section : (b + 1) * part_cols])
            for b in range(parts)
        ]
        totals = lax.psum(jnp.concatenate([gain_part, head_gain_part, feed_gain_part], axis=1)[0], ("seq", "fsdp"))

    shard_rows = query_weight.shape[0]
    q_shard = jnp.stack([q.reshape(shard_rows, nz, widths[0]) for q, _ in part_shards], axis=2).reshape(shard_rows, -1)
    kv_shard = jnp.stack([kv.reshape(shard_rows, nz, 2, head_dim) for _, kv in part_shards], axis=2)
    k_shard, v_shard = (kv_shard[:, :, :, i].reshape(shard_rows, -1) for i in range(2))

    head_totals = totals[model : model + parts * part_cols].reshape(parts, part_cols)
    q_total = head_totals[:, : nz * widths[0]].reshape(-1, head_dim).sum(axis=0)
    k_total = head_totals[:, nz * widths[0] :].reshape(-1, 2, head_dim)[:, 0].sum(axis=0)

    def share(values):
        size = values.shape[0] // fsdp
        return lax.dynamic_slice(values, (me * size,), (size,))

    return (
        output.reshape(inputs.shape),
        input_grad.reshape(inputs.shape),
        q_shard,
        k_shard,
        v_shard,
        out_shard,
        share(totals[:model]),
        share(q_total),
        share(k_total),
        share(totals[model + parts * part_cols :]),
        gate_shard,
        up_shard,
        down_shard,
    )


def solution(mesh):
    tokens, rows, row = P("fsdp", "seq", None), P("fsdp", None), P("fsdp")
    in_specs = (tokens, P("fsdp", "seq"), tokens) + (rows,) * 4 + (row,) * 4 + (rows,) * 3
    out_specs = (tokens, tokens) + (rows,) * 4 + (row,) * 4 + (rows,) * 3
    return jax.shard_map(per_device, mesh=mesh, in_specs=in_specs, out_specs=out_specs, check_vma=False)
```

time: 528 us -> 478 us (0.905)
  the two profiles are of different devices: /device:TPU:24 before, /device:TPU:0 now
where the time goes in v4:
time: 478 us; the launch traced here: 469 us
  Pallas kernels  434 us (91%)
  local copies, waits for them, and re-layouts  24.9 us (5%)
  other arithmetic  7.83 us (2%)
    pallas_call x1, Pallas kernels, per_device(): call(functools.partial(backward_kernel, (nz, head_dim, widths, attend_dim...  252 us
    pallas_call x1, Pallas kernels, per_device(): call(functools.partial(forward_kernel, (nz, plane, head_dim, widths, min(...  182 us

profile of v4, /device:TPU:0, one launch (start us, length us, event | category | flops | bytes accessed | tf_op | source)
XLA Modules:
  0.0 468.6 jit_solution(3532303054895101600)
XLA Ops:
  0.7 0.9 dynamic_update_slice.16
  1.5 0.9 dynamic_update_slice.15
  2.4 0.1 tile.44
  2.5 0.7 convert_element_type.9
  3.2 0.8 dynamic_update_slice.14
  4.1 0.8 dynamic_update_slice.17
  4.9 1.0 copy.71
  6.0 0.0 copy-start.12
  6.0 1.1 copy.72
  7.1 0.0 copy-start.13
  7.2 0.1 copy.92
  7.3 0.1 copy.91
  7.4 0.3 fusion
  7.8 0.8 copy.78.sin_ref
  8.6 0.8 copy.77.cos_ref
  9.5 0.0 copy-done.12
  9.5 0.2 reshape.120
  9.6 1.5 slice_reduce_fusion
  11.2 0.0 copy-done.13
  11.2 0.8 pad_maximum_fusion
  12.0 2.6 concatenate.70.refs_0_
  14.7 182.4 %shard_map.237 = (f32[16,1536]{1,0:T(8,128)}, bf16[2048,512]{1,0:T(8,128)(2,1)}, f32[4,8,2048]{2,1,0:T(8,128)}, bf16[512,1024]{1,0:T(8,128)(2,1)}, f32[512,1024]...) custom-call(bf16[512,1024]{1,0:T(8,128)(2,1)} %bitcast.51, ...), custom_call_target="tpu_custom_call" | custom-call | flops 39728447488 | bytes 104857600 | tf_op jit(solution)/shard_map/pallas_call | solution.py:1205
  197.1 251.9 %shard_map.238 = (bf16[512,1024]{1,0:T(8,128)(2,1)}, f32[8,4096]{1,0:T(8,128)}, bf16[288,512]{1,0:T(8,128)(2,1)}, bf16[288,512]{1,0:T(8,128)(2,1)}, bf16[288,512...) custom-call(f32[16,1536]{1,0:T(8,128)} %get-tuple-element.51.gains_r, ...), custom_call_target="tpu_custom_call" | custom-call | flops 40802189312 | bytes 104857600 | tf_op jit(solution)/shard_map/pallas_call | solution.py:1264
  449.0 0.9 slice_reduce_fusion.2
  449.9 0.8 fusion.4
  450.7 0.5 dynamic-slice_bitcast_fusion
  451.2 0.5 dynamic-slice_bitcast_fusion.1
  451.7 0.1 reshape.128
  451.9 0.6 dynamic_slice.19
  452.4 0.1 reshape.127
  452.5 0.6 dynamic_slice.18
  453.1 0.9 stack_reshape.24
  454.1 0.9 stack_reshape.25
  455.1 1.0 copy.84
  456.1 1.0 copy.85
  457.2 0.0 copy-start.14
  457.3 0.0 copy-start.15
  457.3 0.8 copy.90
  458.1 0.8 copy.89
  459.0 0.2 copy.83
  459.2 1.0 copy.88
  460.2 0.0 copy-done.14
  460.2 0.0 copy-done.15
  460.2 0.0 copy-start.4
  460.2 0.8 maximum_convert_fusion.5
  461.1 0.0 copy-done.5
  461.1 0.0 copy-done.6
  461.1 0.0 copy-done.7
  461.1 1.6 maximum_convert_fusion
  462.7 0.0 copy-done.2
  462.7 0.0 copy-done.3
  462.7 0.0 copy-done.4
  462.7 0.0 copy-start.9
  462.8 0.0 copy-start.10
  462.8 0.0 copy-start.11
  462.8 1.6 maximum_convert_fusion.1
  464.4 0.0 copy-done.8
  464.4 0.0 copy-done.9
  464.4 0.0 copy-done.10
  464.4 0.0 copy-start
  464.4 0.0 copy-start.1
  464.4 1.7 maximum_convert_fusion.2
  466.2 1.0 copy.110
  467.1 1.0 copy.111
  (47 shorter events, 0.6 us)
Async XLA Ops:
  6.0 3.5 copy-start.12
  7.1 4.0 copy-start.13
  457.2 3.0 copy-start.14
  457.3 3.0 copy-start.15
  458.1 3.0 copy-start.5
  458.1 3.0 copy-start.6
  458.1 3.0 copy-start.7
  460.2 2.5 copy-start.2
  460.2 2.5 copy-start.3
  460.2 2.5 copy-start.4
  462.7 1.7 copy-start.8
  462.7 1.7 copy-start.9
  462.8 1.7 copy-start.10
  462.8 1.7 copy-start.11
  464.4 1.7 copy-start
  464.4 2.7 copy-start.1

commit v5 on v4

--- a/solution.py
+++ b/solution.py
@@ -115,10 +115,13 @@
             device_id_type=pl.DeviceIdType.MESH,
         )
 
+    def plan(self, source, target, device):
+        self.started.append(self.copy(source, target, device))
+        return self.started[-1]
+
     def start(self, source, target, device):
-        copy = self.copy(source, target, device)
+        copy = self.plan(source, target, device)
         copy.start()
-        self.started.append(copy)
         return copy
 
     def wait_sends(self):
@@ -141,42 +144,43 @@
         self.links, self.me, self.own, self.whole = links, me, own, whole
         self.rows = own.shape[0]
         self.stride, self.base = self.rows if stride is None else stride, base
-        self.near, self.other = (2, 4) if x_first else (4, 2)
+        near, other = (2, 4) if x_first else (4, 2)
+        self.first, self.second = self.pass_on(0, near), self.pass_on(0, other)
+        self.far = self.pass_on(near, other)
+        self.to_core = [self.pass_on(b, 1) for b in (0, near, other, near + other)]
 
     def block(self, b):
         return self.whole.at[pl.ds(pl.multiple_of((self.me ^ b) * self.stride + self.base, 16), self.rows)]
 
     def pass_on(self, b, bit):
         source = self.own if b == 0 else self.block(b)
-        return self.links.start(source, self.block(b), {"fsdp": self.me ^ bit})
+        return self.links.plan(source, self.block(b), {"fsdp": self.me ^ bit})
 
     def begin(self):
-        self.first = self.pass_on(0, self.near)
-        self.second = self.pass_on(0, self.other)
-        self.to_core = [self.pass_on(0, 1)]
+        for copy in (self.first, self.second, self.to_core[0]):
+            copy.start()
 
     def forward_first(self):
         self.first.wait_recv()
-        self.far = self.pass_on(self.near, self.other)
-        self.to_core.append(self.pass_on(self.near, 1))
+        self.far.start()
+        self.to_core[1].start()
 
     def forward_second(self):
         self.second.wait_recv()
-        self.to_core.append(self.pass_on(self.other, 1))
+        self.to_core[2].start()
 
     def forward_far(self):
         self.far.wait_recv()
-        self.to_core.append(self.pass_on(self.near + self.other, 1))
+        self.to_core[3].start()
 
     def end(self):
         for copy in self.to_core:
             copy.wait_recv()
 
 
-def begin(gathers, copy_here=None):
+def begin(gathers):
     for gather in gathers:
         gather.begin()
-    return [copy_here(gather.own, gather.block(0)) for gather in gathers]
 
 
 def forward_first(gathers):
@@ -211,7 +215,8 @@
         gate_hbm, up_hbm, down_hbm = given[3:]
     w_first, w_second, w_out, normed, transposed, proj, qkv, queries, keys, values, full, mix, mixed = refs[:13]
     w_gate, w_up, w_down, middle, total, back, hidden_slot, gate_slot, up_slot = refs[13:22]
-    local_sems, weight_sems, slot_sems, send_sems, recv_sems, slot_sends, block_recvs = refs[22:]
+    local_sems, weight_sems, slot_sems, send_sems, recv_sems, slot_sends, block_recvs = refs[22:29]
+    own_slots = refs[29:]
     z, me = lax.axis_index("seq"), lax.axis_index("fsdp")
     model = w_second.shape[0]
     hidden_cols = gate_hbm.shape[1]
@@ -238,17 +243,26 @@
     if plane:
         own_first, own_second, own_gate, own_up, own_down = given
         half = own_down.shape[0] // 2
-        attention = [Gather(links, me, own_first, w_first, True), Gather(links, me, own_second, w_second, False)]
-        here = begin(attention, copy_here)
+        part_cols = nz * sum(widths)
+        both = ((own_first, w_first, True), (own_second, w_second, False))
+
+        def columns(pairs, start, size):
+            cols = pl.ds(start, size)
+            return [Gather(links, me, own.at[:, cols], whole.at[:, cols], x_first) for own, whole, x_first in pairs]
+
+        attention = columns(both, 0, part_cols)
+        outward = columns(both, part_cols, own_first.shape[1] - part_cols)
+        begin(attention)
+        here = [copy_here(gather.own, gather.block(0)) for gather in attention + outward]
+        own_places = [(own_gate, own_slots[0], gate_hbm), (own_up, own_slots[1], up_hbm), (own_down, own_slots[2], down_hbm)]
+        own_loads = [copy_here(own, slot) for own, slot, _ in own_places]
         down = [
             Gather(links, me, own_down.at[pl.ds(side * half, half)], down_hbm, side == 0, 2 * half, side * half)
             for side in range(2)
         ]
         wide, at = [], 0
         for count in groups:
-            cols = pl.ds(at * width, count * width)
-            pair = ((own_gate, gate_hbm, True), (own_up, up_hbm, False))
-            wide.append([Gather(links, me, own.at[:, cols], whole.at[:, cols], first) for own, whole, first in pair])
+            wide.append(columns(((own_gate, gate_hbm, True), (own_up, up_hbm, False)), at * width, count * width))
             at += count
     else:
         here = [copy_here(given[0], w_first), copy_here(given[1], w_second)]
@@ -256,26 +270,24 @@
     unit = x * row_norm(x)
     if plane:
         forward_first(attention)
-        here_down = begin(down, copy_here)
+        begin(outward)
+        begin(down)
         forward_far(attention)
         end(attention)
         wait_all(here)
         stride = attention[0].rows
         shard = model // 8
-        gains = sum(w_first[s * stride + shard : (s + 1) * stride].astype(F32) for s in range(8))
-        for s in range(8):
-            copy_here(w_first.at[pl.ds(s * stride, shard)], first_hbm.at[pl.ds(s * shard, shard)])
-        copy_here(w_second, second_hbm)
+        gains = sum(w_first[s * stride + shard : (s + 1) * stride, :part_cols].astype(F32) for s in range(8))
     else:
         stride = shard = model
         wait_all(here)
-        gains = given[2][...].astype(F32)
-    out_half = model // 2
-    for s in range(model // shard):
-        source = w_first.at[pl.ds(s * stride, shard), pl.ds(w_first.shape[1] - out_half, out_half)]
-        copy_here(source, w_out.at[pl.ds(s * shard, shard), pl.ds(0, out_half)])
-    copy_here(w_second.at[:, pl.ds(w_second.shape[1] - out_half, out_half)], w_out.at[:, pl.ds(out_half, out_half)])
-    out_copies = local[-model // shard - 1 :]
+        gains = given[2][:, : nz * sum(widths)].astype(F32)
+    if plane:
+        wait_all(own_loads)
+        own_stores = []
+        for own, slot, whole in own_places:
+            count = own.shape[0]
+            own_stores.append(copy_here(slot, whole.at[pl.ds(pl.multiple_of(me * count, count), count)]))
     gains_ref[...] = gains
     normed[...] = (unit * gains[0:1, :model]).astype(BF)
     chunk = 256
@@ -284,6 +296,7 @@
     sin = jnp.concatenate([sin_ref[...]] * (chunk // 128), axis=1)
     part_cols = nz * sum(widths)
     parts = qkv.shape[1] // part_cols
+    out_half = model // 2
     my_rows = pl.ds(pl.multiple_of(z * tokens, tokens), tokens)
     arrivals = []
     for b in range(parts):
@@ -319,9 +332,8 @@
     share(transposed.at[0], normed_t_hbm.at[:, place])
     share(dy_ref, dy_hbm.at[place])
     if plane:
-        here_wide = [begin(wide[0], copy_here)]
-        forward_first(down)
-        here_wide.append(begin(wide[1], copy_here))
+        forward_first(outward)
+        begin(wide[0])
     group, seq_len, _ = queries.shape
     factor = head_dim**-0.5 * LOG2E
     arriving, here_mixed = [], []
@@ -363,12 +375,28 @@
             else:
                 arriving.append(links.start(source, target, {"seq": owner}))
         if plane and b == 0:
+            forward_far(outward)
+            forward_first(down)
+            end(outward)
+            for s in range(8):
+                copy_here(w_first.at[pl.ds(s * stride, shard)], first_hbm.at[pl.ds(s * shard, shard)])
+            copy_here(w_second, second_hbm)
             forward_first(wide[0])
-            here_wide.append(begin(wide[2], copy_here))
+            begin(wide[1])
+            begin(wide[2])
+        if b == 0:
+            out_copies = [
+                copy_here(
+                    w_first.at[pl.ds(s * stride, shard), pl.ds(part_cols, out_half)],
+                    w_out.at[pl.ds(s * shard, shard), pl.ds(0, out_half)],
+                )
+                for s in range(model // shard)
+            ]
+            out_copies.append(copy_here(w_second.at[:, pl.ds(part_cols, out_half)], w_out.at[:, pl.ds(out_half, out_half)]))
     if plane:
         forward_far(down)
-        forward_first(wide[1])
-        here_wide.append(begin(wide[3], copy_here))
+        end(down)
+        wait_all(own_stores)
         forward_far(wide[0])
     for copy in arriving:
         copy.wait_recv()
@@ -428,14 +456,40 @@
             for i, (source, target) in enumerate(pairs)
         ]
 
-    def one_block(last, f, _):
+    blocks = hidden_cols // width
+    firsts = [sum(groups[:g]) for g in range(len(groups))]
+
+    ahead = [0, 0, firsts[min(1, len(firsts) - 1)] - 1] + firsts[2:]
+
+    def arrive(f):
+        for g in range(1, len(groups)):
+
+            @pl.when(f == ahead[g])
+            def _():
+                forward_first(wide[g])
+                if g + 2 < len(groups):
+                    begin(wide[g + 2])
+
+        for g in range(len(groups)):
+
+            @pl.when(f == firsts[g])
+            def _():
+                if g:
+                    forward_far(wide[g])
+                end(wide[g])
+
+    def one_block(f, _):
         slot = lax.rem(f, 2)
-
-        @pl.when(f + 1 < last)
-        def _():
-            for copy in weight_copies(f + 1):
+        if plane:
+            arrive(f)
+
+        def fetch(block):
+            for copy in weight_copies(block):
                 copy.start()
 
+        in_first = f < (firsts[1] if plane else blocks)
+        pl.when((f == 0) | ~in_first)(lambda: fetch(f))
+        pl.when(in_first & (f + 1 < (firsts[1] if plane else blocks)))(lambda: fetch(f + 1))
         wait_all(weight_copies(f))
 
         @pl.when(f >= 2)
@@ -459,24 +513,7 @@
         back[...] = back[...] + (dot_nt(gate_grad, w_gate[slot]) + dot_nt(up_grad, w_up[slot]))
         return 0
 
-    blocks = hidden_cols // width
-    at = 0
-    if plane:
-        end(down)
-        wait_all(here_down)
-    for g, count in enumerate(groups):
-        if plane:
-            if g + 1 < len(groups):
-                if g > 0:
-                    forward_first(wide[g + 1])
-            if g > 0:
-                forward_far(wide[g])
-            end(wide[g])
-            wait_all(here_wide[g])
-        for copy in weight_copies(at):
-            copy.start()
-        lax.fori_loop(at, at + count, functools.partial(one_block, at + count), 0)
-        at += count
+    lax.fori_loop(0, blocks, one_block, 0)
     output_ref[...] = total[...].astype(BF)
     part, gain_sum = norm_back(middle[...], gain, back[...])
     gain_grad_ref[...] = gain_sum
@@ -504,7 +541,7 @@
         links.wait_sends()
     done = here + out_copies + here_mixed + [c for arrived in arrivals for c in arrived[:2]]
     if plane:
-        done += here_down + [c for copies in here_wide for c in copies]
+        done += own_loads + own_stores
     for copy in local:
         if not any(copy is other for other in done):
             copy.wait()
@@ -518,7 +555,7 @@
     return links.start(source, place, {"fsdp": me ^ 1})
 
 
-def attend_back(dims, b, heads_ref, grads_ref, log_ref, delta_ref, packed, scratch, after):
+def attend_back(dims, b, heads_ref, grads_ref, log_ref, delta_ref, packed, scratch):
     rows, chunk = dims
     queries, keys, values, grad, q_grad, k_grad, v_grad = scratch
     group, seq_len, head_dim = queries.shape
@@ -564,7 +601,7 @@
         parts = [(q_grad[g, span] * factor).astype(BF) for g in range(group)]
         parts += [(k_grad[span] * factor).astype(BF), v_grad[span].astype(BF)]
         packed[span] = jnp.concatenate(parts, axis=1)
-        after(at)
+        yield at
 
 
 def attend_back_scratch(group, seq_len, head_dim):
@@ -575,7 +612,8 @@
 
 def attend_back_kernel(dims, heads_ref, grads_ref, log_ref, delta_ref, packed, *scratch):
     for b in range(packed.shape[0]):
-        attend_back(dims, b, heads_ref, grads_ref, log_ref, delta_ref, packed.at[b], scratch, lambda at: None)
+        for _ in attend_back(dims, b, heads_ref, grads_ref, log_ref, delta_ref, packed.at[b], scratch):
+            pass
 
 
 def norm_back(rows, gain, gradient):
@@ -615,7 +653,7 @@
         cols = slice(b * part_cols + start, b * part_cols + start + width)
         rotated = qkv[:, cols].astype(F32)
         gradient = rotated * cos - partner(rotated, head_dim) * sin
-        proj = proj_ref[:, cols]
+        proj = proj_ref[:, start : start + width]
         scale = lax.rsqrt(head_sum(proj * proj, mask) * (1.0 / head_dim) + EPSILON)
         n = proj * scale
         u = gradient * gains_ref[1:2, start : start + width]
@@ -638,7 +676,9 @@
     nz, _, widths = dims
     qkv[...] = grads_ref[...]
     for b in range(qkv.shape[1] // (nz * sum(widths))):
-        project_back(dims, b, gains_ref, cos_ref, sin_ref, proj_ref, qkv, head_gain_grad_ref)
+        part_cols = nz * sum(widths)
+        part = proj_ref.at[:, pl.ds(b * part_cols, part_cols)]
+        project_back(dims, b, gains_ref, cos_ref, sin_ref, part, qkv, head_gain_grad_ref)
     input_back(x_ref, middle_grad_ref, gains_ref, qkv, weight_ref, input_grad_ref, gain_grad_ref)
 
 
@@ -770,6 +810,29 @@
             copy.wait_send()
 
 
+EARLY = (
+    ("down0", "matmul"), ("down0", "begin"), ("out", "matmul"), ("out", "begin"), ("down1", "matmul"),
+    ("wide0", "matmul"), ("wide1", "matmul"),
+)
+MIDDLE = (
+    ("keys", 0, 0), ("down0", "fold_one"), ("keys", 0, 1), ("keys", 0, 2), ("down1", "begin"), ("keys", 0, 3),
+    ("down0", "fold_two"), ("wide1", "begin"), ("keys", 0, 4), ("keys", 0, 5), ("keys", 0, 6), ("keys", 0, 7),
+    ("keys", 1, 0), ("keys", 1, 1), ("keys", 1, 2), ("down1", "fold_one"), ("keys", 1, 3), ("keys", 1, 4),
+    ("keys", 1, 5), ("out", "fold_one"), ("keys", 1, 6), ("keys", 1, 7), ("wide1", "fold_one"), ("wide2", "matmul"),
+    ("wide2", "begin"), ("down1", "fold_two"), ("project", 0), ("down0", "fold_three"), ("wide1", "fold_two"),
+    ("last0", "matmul"), ("project", 1),
+)
+LATE = (
+    ("last0", "begin"), ("down1", "fold_three"), ("wide2", "fold_one"), ("down0", "fold_four"), ("last1", "matmul"),
+    ("last0", "fold_one"), ("wide1", "fold_three"), ("last1", "begin"), ("down1", "fold_four"), ("out", "fold_two"),
+    ("wide0", "begin"), ("out", "fold_three"), ("input",), ("wide2", "fold_two"), ("wide1", "fold_four"), ("total", 0),
+    ("wide2", "fold_three"), ("last0", "fold_two"), ("last1", "fold_one"), ("wide0", "fold_one"), ("total", 1),
+    ("out", "fold_four"), ("last1", "fold_two"), ("last0", "fold_three"), ("wide2", "fold_four"),
+    ("last1", "fold_three"), ("wide0", "fold_two"), ("last0", "fold_four"), ("total", 2), ("wide0", "fold_three"),
+    ("last1", "fold_four"), ("total", 3), ("wide0", "fold_four"), ("total", 4),
+)
+
+
 def backward_kernel(dims, gains_ref, cos_ref, sin_ref, heads_ref, log_ref, grad_low, delta_own, low_ref, feed_gain_ref, *refs):
     nz, head_dim, widths, attend_dims, names = dims
     given, refs = refs[:12], refs[12:]
@@ -785,7 +848,8 @@
     seconds, refs = dict(zip(names, refs[:n])), refs[n:]
     inwards, refs = dict(zip(names, refs[:n])), refs[n:]
     acrosses, refs = dict(zip(names, refs[:n])), refs[n:]
-    grads, delta, qkv, other_qkv, sums, sum_arrived, gain_grad, head_gain_grad, sems, send_sems, recv_sems = refs
+    grads, delta, qkv, other_qkv, normed_two, normed, sums, sum_arrived, gain_grad, head_gain_grad = refs[:10]
+    sems, send_sems, recv_sems = refs[10:]
     z, me = lax.axis_index("seq"), lax.axis_index("fsdp")
     chip, core = lax.div(me, 2), lax.rem(me, 2)
     enter(me, z, nz, True)
@@ -877,52 +941,92 @@
             if c + 2 < count:
                 loads[c + 2].start()
 
-    def early_grads(hidden, dy, normed_two, right, mixed, low):
-        ready = my_blocks(hidden_hbm, hidden, 2 * half) + [fetch.start(dy_hbm, dy)]
-        ready_two = my_blocks(normed_two_hbm, normed_two, shard)
-        ready_three = my_blocks(mixed_hbm, mixed, shard)
-        wait_all(ready)
-        cols = down[0][0].kept.shape[2]
-        for c in range(2):
-
-            def down_block(i, _):
-                to = pl.ds(pl.multiple_of(i * step, step), step)
-                here = pl.ds(pl.multiple_of(c * cols + i * step, step), step)
-                for r in range(chips):
-                    got = dot_nn(hidden[2 * r * half : 2 * (r + 1) * half], dy[:, here]).astype(BF)
-                    for side in range(2):
-                        down[c][side].put(r, to, got[side * half : (side + 1) * half])
-                return 0
-
-            lax.fori_loop(0, cols // step, down_block, 0)
-            each(down[c], "begin")
-        wait_all(ready_two)
-        per_unit = gate[0].kept.shape[2] // right.shape[2]
-        wide_grads([(gate_hbm, i * per_unit, gate[i]) for i in range(3)] + [(up_hbm, 0, up[0])], normed_two, right)
-        low_arrival.wait_recv()
-        wait_all(late)
-        del late[:]
-        ready_three.append(fetch.start(low_hbm, low))
-        wait_all(ready_three)
+    ready = {"two": my_blocks(normed_two_hbm, normed_two, shard), "one": my_blocks(normed_hbm, normed, shard)}
+
+    def ready_now(name):
+        wait_all(ready.pop(name, ()))
+
+    per_unit = 2
+    wide_part = gate[0].kept.shape[2] // per_unit
+    sides = {"gate": gate_hbm, "up": up_hbm}
+    wide_names = (("gate", 0), ("gate", 1), ("gate", 2), ("up", 0), ("up", 1), ("up", 2))
+
+    def wide_matmul(i, right):
+        ready_now("two")
+        pair = zip(wide_names[2 * i : 2 * i + 2], wide[i])
+        wide_grads([(sides[kind], at * per_unit, unit) for (kind, at), unit in pair], normed_two, right)
+
+    def out_matmul(mixed, low):
         cols = out[0].kept.shape[2]
         for start in range(0, low.shape[1], step):
             got = dot_nn(mixed[...], low[:, start : start + step]).astype(BF)
             for r in range(chips):
                 out[start // cols].put(r, slice(start % cols, start % cols + step), got[r * shard : (r + 1) * shard])
-        each(down[0], "fold_one")
-
-    def late_grads(normed_two, right):
-        wait_all(my_blocks(normed_two_hbm, normed_two, shard))
-        per_unit = up[0].kept.shape[2] // right.shape[2]
-        wide_grads([(up_hbm, i * per_unit, up[i]) for i in (1, 2)], normed_two, right)
-
-    wide_part = gate[0].kept.shape[2] // 2
+
+    def down_matmul(c, hidden, dy):
+        cols = down[0][0].kept.shape[2]
+
+        def block(i, _):
+            to = pl.ds(pl.multiple_of(i * step, step), step)
+            here = pl.ds(pl.multiple_of(c * cols + i * step, step), step)
+            for r in range(chips):
+                got = dot_nn(hidden[2 * r * half : 2 * (r + 1) * half], dy[:, here]).astype(BF)
+                for side in range(2):
+                    down[c][side].put(r, to, got[side * half : (side + 1) * half])
+            return 0
+
+        lax.fori_loop(0, cols // step, block, 0)
+
+    def last_matmul(b):
+        ready_now("one")
+        mine = normed[:, pl.ds(pl.multiple_of(core * tokens, tokens), tokens)]
+        theirs = normed[:, pl.ds(pl.multiple_of((1 - core) * tokens, tokens), tokens)]
+        qkv_links[b].wait()
+        cols = last[b][0].kept.shape[2]
+        for start in range(0, part_cols, step):
+            here = slice(b * part_cols + start, b * part_cols + start + step)
+            got = (dot_nn(mine, qkv[:, here]) + dot_nn(theirs, other_qkv[:, here])).astype(BF)
+            for r in range(chips):
+                last[b][start // cols].put(r, slice(start % cols, start % cols + step), got[r * shard : (r + 1) * shard])
+
+    pairs = {"out": out}
+    pairs |= {f"down{c}": down[c] for c in range(2)}
+    pairs |= {f"wide{i}": wide[i] for i in range(3)}
+    pairs |= {f"last{b}": last[b] for b in range(parts)}
+    right_shape = pltpu.VMEM((2, both, wide_part), BF)
+
+    def sum_step(name, what):
+        if what != "matmul":
+            each(pairs[name], what)
+        elif name[:4] == "last":
+            last_matmul(int(name[4]))
+        else:
+            pl.run_scoped(functools.partial(wide_matmul, int(name[4])), right_shape)
+
+    def early(hidden, dy, right, mixed, low):
+        ready["down"] = my_blocks(hidden_hbm, hidden, 2 * half) + [fetch.start(dy_hbm, dy)]
+        ready["out"] = my_blocks(mixed_hbm, mixed, shard)
+        for name, what in EARLY:
+            if what != "matmul":
+                each(pairs[name], what)
+            elif name[:4] == "down":
+                ready_now("down")
+                down_matmul(int(name[4]), hidden, dy)
+            elif name == "out":
+                low_arrival.wait_recv()
+                wait_all(late)
+                del late[:]
+                ready["out"].append(fetch.start(low_hbm, low))
+                ready_now("out")
+                out_matmul(mixed, low)
+            else:
+                wide_matmul(int(name[4]), right)
+
     pl.run_scoped(
-        early_grads,
+        early,
         pltpu.VMEM((2 * chips * half, both), BF),
         pltpu.VMEM((both, model), BF),
-        pltpu.VMEM((chips * shard, both), BF),
-        pltpu.VMEM((2, both, wide_part), BF),
+        right_shape,
         pltpu.VMEM((chips * shard, both), BF),
         pltpu.VMEM((both, model), BF),
     )
@@ -946,136 +1050,145 @@
                 else:
                     yield j, links.copy(source, target, {"seq": owner}, at=first_back + (2 * b + i) * nz + j)
 
-    def attention(packed, delta_rows, *scratch):
-        def after_first(at):
-            if at == 3:
-                each(down[1], "fold_one")
-                each(wide[0], "begin")
-
-        def after_second(at):
-            if at == 1:
-                each(down[0], "fold_two")
-            if at == 3:
-                each(down[1], "fold_two")
-
-        for b, after in enumerate((after_first, after_second)):
-            for copy in arrivals[b]:
-                copy.wait_recv()
-            if b == 0:
-                for h in range(heads):
-                    delta_rows[h] = jnp.broadcast_to(delta[h : h + 1], (8, seq_len))
-            attend_back(attend_dims, b, heads_ref, grads, log_ref, delta_rows, packed.at[b], scratch, after)
-            for _, copy in back_copies(b, packed):
-                copy.start()
-        pl.run_scoped(
-            late_grads,
-            pltpu.VMEM((chips * shard, both), BF),
-            pltpu.VMEM((2, both, wide_part), BF),
-        )
-        each(wide[0], "fold_one")
-        each(wide[1], "begin")
-        each(wide[2], "begin")
-        each(down[0], "fold_three")
-        for b in range(parts):
+    def middle(packed, delta_rows, *scratch):
+        blocks = {}
+
+        def keys_step(b, at):
+            if at == 0:
+                for copy in arrivals[b]:
+                    copy.wait_recv()
+                if b == 0:
+                    for h in range(heads):
+                        delta_rows[h] = jnp.broadcast_to(delta[h : h + 1], (8, seq_len))
+                blocks[b] = attend_back(attend_dims, b, heads_ref, grads, log_ref, delta_rows, packed.at[b], scratch)
+            next(blocks[b])
+            if (at + 1) * attend_dims[0] == seq_len:
+                for _, copy in back_copies(b, packed):
+                    copy.start()
+
+        def project_step(b):
             for j, copy in back_copies(b, packed):
                 if j == 0:
                     copy.wait()
                 else:
                     copy.wait_recv()
-            project(b)
-            if b == 0:
-                each(down[1], "fold_three")
-                each(wide[0], "fold_two")
-        each(wide[1], "fold_one")
+
+            def inner(proj):
+                fetch.start(proj_hbm.at[:, part_cols_of(b)], proj).wait()
+                project_back((nz, head_dim, widths), b, gains_ref, cos_ref, sin_ref, proj, qkv, head_gain_grad)
+
+            pl.run_scoped(inner, pltpu.VMEM((tokens, part_cols), F32))
+            qkv_links[b].start()
+
+        for token in MIDDLE:
+            if token[0] == "keys":
+                keys_step(*token[1:])
+            elif token[0] == "project":
+                project_step(token[1])
+            else:
+                sum_step(*token)
         for b in range(parts):
             for j, copy in back_copies(b, packed):
                 if j:
                     copy.wait_send()
 
-    def project(b):
-        def inner(proj):
-            cols = part_cols_of(b)
-            fetch.start(proj_hbm.at[:, cols], proj.at[:, cols]).wait()
-            project_back((nz, head_dim, widths), b, gains_ref, cos_ref, sin_ref, proj, qkv, head_gain_grad)
-            qkv_links[b].start()
-
-        pl.run_scoped(inner, pltpu.VMEM((tokens, parts * part_cols), F32))
-
     pl.run_scoped(
-        attention,
+        middle,
         pltpu.VMEM((parts, seq_len, sum(widths)), BF),
         pltpu.VMEM((heads, 8, seq_len), F32),
         *attend_back_scratch(group, seq_len, head_dim),
     )
 
-    def projections(weight, x, middle_grad, normed):
-        ready = my_blocks(normed_hbm, normed, shard)
-        ready_two = [fetch.start(x_hbm, x), fetch.start(middle_grad_hbm, middle_grad)]
+    def input_step(weight, x, middle_grad):
+        copies = [fetch.start(x_hbm, x), fetch.start(middle_grad_hbm, middle_grad)]
         for b, source in enumerate((first_hbm, second_hbm)):
-            ready_two.append(fetch.start(source.at[:, pl.ds(0, part_cols)], weight.at[:, part_cols_of(b)]))
-        wait_all(ready)
-        mine = normed[:, pl.ds(pl.multiple_of(core * tokens, tokens), tokens)]
-        theirs = normed[:, pl.ds(pl.multiple_of((1 - core) * tokens, tokens), tokens)]
-        for b in range(parts):
-            qkv_links[b].wait()
-            cols = last[b][0].kept.shape[2]
-            for start in range(0, part_cols, step):
-                here = slice(b * part_cols + start, b * part_cols + start + step)
-                got = (dot_nn(mine, qkv[:, here]) + dot_nn(theirs, other_qkv[:, here])).astype(BF)
-                for r in range(chips):
-                    last[b][start // cols].put(r, slice(start % cols, start % cols + step), got[r * shard : (r + 1) * shard])
-            each(last[b], "begin")
-        each(out, "begin")
-        wait_all(ready_two)
+            copies.append(fetch.start(source.at[:, pl.ds(0, part_cols)], weight.at[:, part_cols_of(b)]))
+        wait_all(copies)
         input_back(x, middle_grad, gains_ref, qkv, weight, input_grad_ref, gain_grad)
         row = jnp.concatenate([gain_grad[...], head_gain_grad[...], feed_gain_ref[...]], axis=1)
         sums[0] = jnp.broadcast_to(row, sums.shape[1:])
-        total.begin(0)
-
-    pl.run_scoped(
-        projections,
-        pltpu.VMEM((model, parts * part_cols), BF),
-        pltpu.VMEM((tokens, model), BF),
-        pltpu.VMEM((tokens, model), F32),
-        pltpu.VMEM((chips * shard, both), BF),
-    )
-    each(down[0], "fold_four")
-    each(down[1], "fold_four")
-    total.fold(0)
-    total.begin(1)
-    each(wide[0], "fold_three")
-    each(wide[2], "fold_one")
-    each(wide[1], "fold_two")
-    total.fold(1)
-    total.begin(2)
-    each(last[0], "fold_one")
-    each(last[1], "fold_one")
-    each(out, "fold_one")
-    each(wide[2], "fold_two")
-    total.fold(2)
-    total.begin(3)
-    each(wide[0], "fold_four")
-    each(last[0], "fold_two")
-    each(last[1], "fold_two")
-    each(out, "fold_two")
-    total.fold(3)
-    total.begin(4)
-    each(wide[1], "fold_three")
-    each(wide[2], "fold_three")
-    each(wide[1], "fold_four")
-    each(last[0], "fold_three")
-    each(last[1], "fold_three")
-    each(out, "fold_three")
-    total.fold(4)
-    each(wide[2], "fold_four")
-    each(last[0], "fold_four")
-    each(last[1], "fold_four")
-    each(out, "fold_four")
+
+    for token in LATE:
+        if token[0] == "input":
+            pl.run_scoped(
+                input_step,
+                pltpu.VMEM((model, parts * part_cols), BF),
+                pltpu.VMEM((tokens, model), BF),
+                pltpu.VMEM((tokens, model), F32),
+            )
+            total.begin(0)
+        elif token[0] == "total":
+            total.fold(token[1])
+            if token[1] < 4:
+                total.begin(token[1] + 1)
+        else:
+            sum_step(*token)
     totals_ref[...] = sums[5]
     total.end()
     for name in names:
         reduces[name].end()
     links.wait_sends()
+
+
+def finish_kernel(dims, *refs):
+    names, nz, head_dim = dims
+    n = len(names)
+    output_in, input_grad_in = refs[:2]
+    shards, refs = dict(zip(names, refs[2 : 2 + n])), refs[2 + n :]
+    output, input_grad, q_out, k_out, v_out, out_out, gate_out, up_out, down_out = refs[:9]
+    slots, refs = dict(zip(names, refs[9 : 9 + n])), refs[9 + n :]
+    passing, q, k, v, out, gate, up, down, load_sems, store_sems = refs
+    fetch, store = Fetch(load_sems), Fetch(store_sems)
+    wide = [name for name in names if name[:4] in ("gate", "up0y", "up1x", "up2y")]
+    order = wide + [name for name in names if name not in wide]
+    loads = {name: fetch.start(shards[name], slots[name]) for name in order}
+    moves = [fetch.start(source, passing.at[i]) for i, source in enumerate((output_in, input_grad_in))]
+    stores = []
+
+    def place(name, target, row, col):
+        loads[name].wait()
+        rows, cols = slots[name].shape
+        target[row : row + rows, col : col + cols] = slots[name][...].astype(F32)
+
+    cols = slots["gate0x"].shape[1]
+    for target, done, pieces in (
+        (gate, gate_out, ("gate0x", "gate1y", "gate2x")),
+        (up, up_out, ("up0y", "up1x", "up2y")),
+    ):
+        for i, name in enumerate(pieces):
+            place(name, target, 0, i * cols)
+        stores.append(store.start(target, done))
+    rows, cols = slots["down0x"].shape
+    for c in range(2):
+        for i, way in enumerate("xy"):
+            place(f"down{c}{way}", down, i * rows, c * cols)
+    stores.append(store.start(down, down_out))
+    cols = slots["outx"].shape[1]
+    for i, way in enumerate("xy"):
+        place("out" + way, out, 0, i * cols)
+    stores.append(store.start(out, out_out))
+    parts = 2
+    width = q.shape[1] // (nz * parts)
+    for b in range(parts):
+        loads[f"last{b}x"].wait()
+        for i in range(nz):
+            to = (i * parts + b) * width
+            q[:, to : to + width] = slots[f"last{b}x"][:, i * width : (i + 1) * width].astype(F32)
+    stores.append(store.start(q, q_out))
+    for b in range(parts):
+        loads[f"last{b}y"].wait()
+    for i, target in enumerate((k, v)):
+        pieces = [
+            slots[f"last{b}y"][:, (2 * at + i) * head_dim : (2 * at + i + 1) * head_dim]
+            for at in range(nz)
+            for b in range(parts)
+        ]
+        target[...] = jnp.concatenate(pieces, axis=1).astype(F32)
+    stores += [store.start(k, k_out), store.start(v, v_out)]
+    for i, target in enumerate((output, input_grad)):
+        moves[i].wait()
+        stores.append(store.start(passing.at[i], target))
+    wait_all(stores)
 
 
 def add(a, b):
@@ -1140,15 +1253,16 @@
     second = jnp.concatenate([second, out_weight[:, half_out:]], axis=1)
     first_cols = first.shape[1]
 
-    def spread(values):
+    def spread(values, count=1):
         share = values.shape[0]
-        return lax.dynamic_update_slice(jnp.zeros((share * fsdp,), BF), values, (me * share,))
+        own = (jnp.arange(share * fsdp * count) % (share * fsdp)) // share == me
+        return jnp.where(own, jnp.tile(values, fsdp * count), jnp.zeros((), BF))
 
     def gain_row(values):
         return jnp.concatenate([values, jnp.zeros((first_cols - values.shape[0],), BF)])
 
     key_row = jnp.concatenate([spread(key_gain), jnp.zeros((head_dim,), BF)])
-    head_row = jnp.concatenate([jnp.tile(spread(query_gain), nz * group), jnp.tile(key_row, nz)])
+    head_row = jnp.concatenate([spread(query_gain, nz * group), jnp.tile(key_row, nz)])
     gain_rows = [gain_row(spread(attention_gain)), gain_row(head_row), gain_row(spread(feedforward_gain))]
     gain_rows = jnp.stack(gain_rows + [jnp.zeros((first_cols,), BF)] * 13)
     if plane:
@@ -1160,22 +1274,22 @@
         given = [first_full, second_full, lax.psum(gain_rows.astype(F32), "fsdp"), gate_full, up_full, down_full]
 
     half_dim = head_dim // 2
-    freqs = ROPE_BASE ** (-jnp.arange(half_dim, dtype=F32) / half_dim)
+    lane = jnp.arange(128)
+    freqs = ROPE_BASE ** (-(lane % half_dim).astype(F32) / half_dim)
     angles = positions.reshape(tokens).astype(F32)[:, None] * freqs[None, :]
-    cosine, sine = jnp.cos(angles), jnp.sin(angles)
-    cosine = jnp.tile(cosine, (1, 128 // half_dim))
-    sine = jnp.tile(jnp.concatenate([-sine, sine], axis=1), (1, 128 // head_dim))
+    cosine = jnp.cos(angles)
+    sine = jnp.sin(angles) * jnp.where(lane % head_dim < half_dim, -1.0, 1.0)[None, :]
 
     width = 512
     blocks = hidden_cols // width
-    sizes = (blocks - 6, 3, 2, 1)
+    sizes = (blocks - 6,) + (1,) * 6
     block_cols = parts * sum(widths)
     mixed_cols = heads * head_dim
     attend_flops = 2 * heads * seq_len * seq_len * head_dim
     proj_flops = 2 * tokens * model * parts * part_cols
     rows_model = lambda kind: shape_of((tokens, model), kind)
     outs = [
-        shape_of((16, first_cols), F32),
+        shape_of((16, part_cols), F32),
         shape_of((seq_len, block_cols), BF),
         shape_of((heads, 8, seq_len), F32),
         rows_model(BF),
@@ -1198,7 +1312,7 @@
     if plane:
         outs += [shape_of((model, first_cols), BF)] * 2
         outs += [shape_of((model, hidden_cols), BF)] * 2 + [shape_of((hidden_cols, model), BF)]
-        n_links += (4 + 2 * len(sizes)) * 7 + 4
+        n_links += (6 + 2 * len(sizes)) * 7 + 4
         first_rows += 8 * 16
     many = lambda count: pltpu.VMEM((count, seq_len, head_dim), BF)
     one = pltpu.VMEM((seq_len, head_dim), BF)
@@ -1237,7 +1351,8 @@
             pltpu.SemaphoreType.DMA((n_links,)),
             pltpu.SemaphoreType.DMA((2, 3)),
             pltpu.SemaphoreType.DMA((blocks, 3)),
-        ],
+        ]
+        + [pltpu.VMEM(w.shape, BF) for w in (gate_weight, up_weight, down_weight) if plane],
         proj_flops + 4 * attend_flops + 12 * tokens * model * hidden_cols,
         100 * 2**20,
         collective=1,
@@ -1276,6 +1391,8 @@
                 pltpu.VMEM((8, seq_len), F32),
                 pltpu.VMEM((tokens, parts * part_cols), BF),
                 pltpu.VMEM((tokens, parts * part_cols), BF),
+                pltpu.VMEM((model // 2, both), BF),
+                pltpu.VMEM((model // 2, both), BF),
                 pltpu.VMEM((6, 8, total_cols), F32),
                 pltpu.VMEM((5, 8, total_cols), F32),
                 pltpu.VMEM((1, model), F32),
@@ -1292,15 +1409,20 @@
             hidden_t, dy_both, normed_two_t, gate_grad, up_grad, mixed_t, normed_t, first_full, second_full,
         )
         input_grad, totals = got[:2]
-        shards = {name: value.astype(F32) for name, value in zip(names, got[2:])}
-        down_shard = jnp.concatenate(
-            [jnp.concatenate([shards["down0" + way], shards["down1" + way]], axis=1) for way in "xy"]
-        )
-        gate_shard, up_shard, out_shard = (
-            jnp.concatenate([shards[name] for name in names if name.startswith(kind)], axis=1)
-            for kind in ("gate", "up", "out")
-        )
-        part_shards = [(shards[f"last{b}x"], shards[f"last{b}y"]) for b in range(parts)]
+        slots = [pltpu.VMEM(shape, BF) for shape in blocks.values()]
+        out_shapes = [w.shape for w in (query_weight, key_weight, value_weight, out_weight, gate_weight, up_weight, down_weight)]
+        output, input_grad, q_shard, k_shard, v_shard, out_shard, gate_shard, up_shard, down_shard = call(
+            functools.partial(finish_kernel, (names, nz, head_dim)),
+            [rows_model(BF)] * 2 + [shape_of(shape, F32) for shape in out_shapes],
+            [ANY] * (2 + len(names)),
+            [ANY] * 9,
+            slots
+            + [pltpu.VMEM((2, tokens, model), BF)]
+            + [pltpu.VMEM(shape, F32) for shape in out_shapes]
+            + [pltpu.SemaphoreType.DMA((2 + len(names),)), pltpu.SemaphoreType.DMA((9,))],
+            0,
+            18 * 2**20,
+        )(output, input_grad, *got[2 : 2 + len(names)])
         totals = totals[0]
     else:
         exchange = functools.partial(lax.all_to_all, axis_name="seq", tiled=True)
@@ -1344,20 +1466,19 @@
             (qkv_shard[:, b * part_cols : b * part_cols + section], qkv_shard[:, b * part_cols + section : (b + 1) * part_cols])
             for b in range(parts)
         ]
+        shard_rows = query_weight.shape[0]
+        q_shard = jnp.stack([q.reshape(shard_rows, nz, widths[0]) for q, _ in part_shards], axis=2).reshape(shard_rows, -1)
+        kv_shard = jnp.stack([kv.reshape(shard_rows, nz, 2, head_dim) for _, kv in part_shards], axis=2)
+        k_shard, v_shard = (kv_shard[:, :, :, i].reshape(shard_rows, -1) for i in range(2))
         totals = lax.psum(jnp.concatenate([gain_part, head_gain_part, feed_gain_part], axis=1)[0], ("seq", "fsdp"))
-
-    shard_rows = query_weight.shape[0]
-    q_shard = jnp.stack([q.reshape(shard_rows, nz, widths[0]) for q, _ in part_shards], axis=2).reshape(shard_rows, -1)
-    kv_shard = jnp.stack([kv.reshape(shard_rows, nz, 2, head_dim) for _, kv in part_shards], axis=2)
-    k_shard, v_shard = (kv_shard[:, :, :, i].reshape(shard_rows, -1) for i in range(2))
 
     head_totals = totals[model : model + parts * part_cols].reshape(parts, part_cols)
     q_total = head_totals[:, : nz * widths[0]].reshape(-1, head_dim).sum(axis=0)
     k_total = head_totals[:, nz * widths[0] :].reshape(-1, 2, head_dim)[:, 0].sum(axis=0)
 
     def share(values):
-        size = values.shape[0] // fsdp
-        return lax.dynamic_slice(values, (me * size,), (size,))
+        own = jnp.arange(fsdp)[:, None] == me
+        return jnp.sum(jnp.where(own, values.reshape(fsdp, -1), 0.0), axis=0)
 
     return (
         output.reshape(inputs.shape),

time: 478 us -> 425 us (0.89); the launches traced: 469 us -> 421 us
  Pallas kernels: 434 us -> 404 us
  local copies, waits for them, and re-layouts: 24.9 us -> 10.4 us
    pallas_call x1, Pallas kernels: 252 us -> 216 us  [per_device(): call(functools.partial(backward_kernel, (nz, head_dim, widths, attend_dim...]
    concatenate x5 -> x0, other arithmetic: 5.86 us -> none  [the longest x3 4.13 us: per_device(): jnp.concatenate([shards[name] for name in names if name.startswith(kind)]...]
    pallas_call x0 -> x1, Pallas kernels: none -> 5.65 us  [per_device(): call(functools.partial(finish_kernel, (names, nz, head_dim)), [rows_model...]
where the time goes in v5:
time: 425 us; the launch traced here: 421 us
  Pallas kernels  404 us (95%)
  local copies, waits for them, and re-layouts  10.4 us (2%)
  other arithmetic  5.37 us (1%)
    pallas_call x1, Pallas kernels, per_device(): call(functools.partial(backward_kernel, (nz, head_dim, widths, attend_dim...  216 us
    pallas_call x1, Pallas kernels, per_device(): call(functools.partial(forward_kernel, (nz, plane, head_dim, widths, min(...  183 us

profile of v5, /device:TPU:0, one launch (start us, length us, event | category | flops | bytes accessed | tf_op | source)
XLA Modules:
  0.0 421.4 jit_solution(17323133576304993237)
XLA Ops:
  0.6 0.0 copy-start.1
  0.7 0.0 copy-start
  0.7 0.8 convert_element_type.17
  1.5 0.7 tile.24
  2.1 0.1 tile.50
  2.2 0.7 bitcast_select_fusion
  3.0 0.7 tile.22
  3.6 0.1 tile.23
  3.8 1.0 copy.31
  4.8 1.0 copy.32
  5.9 0.1 copy.38
  6.1 0.1 copy.37
  6.2 0.0 copy-done
  6.2 0.2 reshape.122
  6.4 1.5 slice_reduce_fusion
  7.9 0.0 copy-done.1
  7.9 0.8 pad_maximum_fusion
  8.8 2.8 concatenate.34.refs_0_
  11.6 1.8 fusion
  13.4 182.8 %shard_map.237 = (f32[16,1024]{1,0:T(8,128)}, bf16[2048,512]{1,0:T(8,128)(2,1)}, f32[4,8,2048]{2,1,0:T(8,128)}, bf16[512,1024]{1,0:T(8,128)(2,1)}, f32[512,1024]...) custom-call(bf16[512,1024]{1,0:T(8,128)(2,1)} %bitcast.39, ...), custom_call_target="tpu_custom_call" | custom-call | flops 39728447488 | bytes 104857600 | tf_op jit(solution)/shard_map/pallas_call | solution.py:1319
  196.2 216.0 %shard_map.238 = (bf16[512,1024]{1,0:T(8,128)(2,1)}, f32[8,4096]{1,0:T(8,128)}, bf16[288,512]{1,0:T(8,128)(2,1)}, bf16[288,512]{1,0:T(8,128)(2,1)}, bf16[288,512...) custom-call(f32[16,1024]{1,0:T(8,128)} %get-tuple-element.60.gains_r, ...), custom_call_target="tpu_custom_call" | custom-call | flops 40802189312 | bytes 104857600 | tf_op jit(solution)/shard_map/pallas_call | solution.py:1379
  412.2 0.9 slice_reduce_fusion.2
  413.1 0.8 fusion.22
  413.8 0.6 select_reduce_fusion
  414.5 0.1 reshape.128
  414.6 0.1 reshape.129
  414.6 0.1 reshape.130
  414.8 0.1 reshape.131
  414.8 0.6 select_reduce_fusion.1
  415.5 5.6 %shard_map.239 = (bf16[512,1024]{1,0:T(8,128)(2,1)}, bf16[512,1024]{1,0:T(8,128)(2,1)}, f32[128,1024]{1,0:T(8,128)}, f32[128,512]{1,0:T(8,128)}, f32[128,512]{1,...) custom-call(bf16[512,1024]{1,0:T(8,128)(2,1)} %get-tuple-element.59.refs_0_, ...), custom_call_target="tpu_custom_call" | custom-call | bytes 18874368 | tf_op jit(solution)/shard_map/pallas_call | solution.py:1414
  (26 shorter events, 0.3 us)
Async XLA Ops:
  0.6 7.3 %copy-start.1 = (bf16[128,1024]{1,0:T(8,128)(2,1)S(1)}, bf16[128,1024]{1,0:T(8,128)(2,1)}, u32[]{:S(2)}) copy-start(bf16[128,1024]{1,0:T(8,128)(2,1)} %param.20) | copy-start | bytes 786436
  0.7 5.5 %copy-start = (bf16[128,1024]{1,0:T(8,128)(2,1)S(1)}, bf16[128,1024]{1,0:T(8,128)(2,1)}, u32[]{:S(2)}) copy-start(bf16[128,1024]{1,0:T(8,128)(2,1)} %param.17) | copy-start | bytes 786436
